TPU v7x, 32 devices: a whole 2x2x4 slice. The times are simulated.
32 devices in a mesh: mp: 2 (over core), dp: 16 (over z, y, x).
Axes of the slice: x: 2, y: 2, z: 4, core: 2. Of those that a mesh axis runs over, the one named last changes fastest.
Arguments:
- tokens: bfloat16 [131072, 512], P('dp'), may hold values from -6 to 6
- norm1_gain: float32 [512], replicated, may hold values from 0.5 to 1.5
- norm1_bias: float32 [512], replicated, may hold values from -1.5 to 1.5
- w_query: bfloat16 [512, 512], P(None, 'mp'), may hold values from -0.25 to 0.25
- b_query: float32 [512], P('mp'), may hold values from -2.5 to 2.5
- w_key: bfloat16 [512, 512], P(None, 'mp'), may hold values from -0.25 to 0.25
- b_key: float32 [512], P('mp'), may hold values from -2.5 to 2.5
- w_value: bfloat16 [512, 512], P(None, 'mp'), may hold values from -0.25 to 0.25
- b_value: float32 [512], P('mp'), may hold values from -2.5 to 2.5
- w_out: bfloat16 [512, 512], P('mp'), may hold values from -2 to 2
- b_out: float32 [512], replicated, may hold values from -1.5 to 1.5
- norm2_gain: float32 [512], replicated, may hold values from 0.5 to 1.5
- norm2_bias: float32 [512], replicated, may hold values from -1.5 to 1.5
- w_up: bfloat16 [512, 2048], P(None, 'mp'), may hold values from -0.25 to 0.25
- b_up: float32 [2048], P('mp'), may hold values from -2.5 to 2.5
- w_down: bfloat16 [2048, 512], P('mp'), may hold values from -0.125 to 0.125
- b_down: float32 [512], replicated, may hold values from -1.5 to 1.5
- cotangent: bfloat16 [131072, 512], P('dp'), may hold values from -6 to 6
Outputs:
- layer_out: bfloat16 [131072, 512], P('dp')
- tokens_grad: bfloat16 [131072, 512], P('dp')
- norm1_gain_grad: float32 [512], replicated
- norm1_bias_grad: float32 [512], replicated
- w_query_grad: float32 [512, 512], P(None, 'mp')
- b_query_grad: float32 [512], P('mp')
- w_key_grad: float32 [512, 512], P(None, 'mp')
- b_key_grad: float32 [512], P('mp')
- w_value_grad: float32 [512, 512], P(None, 'mp')
- b_value_grad: float32 [512], P('mp')
- w_out_grad: float32 [512, 512], P('mp')
- b_out_grad: float32 [512], replicated
- norm2_gain_grad: float32 [512], replicated
- norm2_bias_grad: float32 [512], replicated
- w_up_grad: float32 [512, 2048], P(None, 'mp')
- b_up_grad: float32 [2048], P('mp')
- w_down_grad: float32 [2048, 512], P('mp')
- b_down_grad: float32 [512], replicated
All inputs are finite; a program needn't handle non-finite values.
Results may differ from a plain program's by a relative error of at most 0.025.
Values may be sent and summed in bfloat16 or wider, within the bound.
No kernel may reach another device: no remote copies, remote signals or barrier semaphores. Data moves between devices by JAX's collectives and lax.ppermute only.
A program may use at most 384 MiB of HBM per device.

v0:
```python
import math

import jax
import jax.numpy as jnp
from jax import lax
from jax.sharding import PartitionSpec as P

HEAD_DIM = 64
SEQ_LEN = 256


def for_sending(value):
    return jax.tree.map(lambda a: a.astype(jnp.bfloat16) if a.dtype == jnp.float32 else a, value)


def layer_norm(rows, gain, shift):
    center = rows - jnp.mean(rows, axis=1, keepdims=True)
    factor = lax.rsqrt(jnp.mean(center * center, axis=1, keepdims=True) + 1e-05)
    plain = center * factor
    return (plain * gain + shift, plain, factor)


def norm_back(grad, plain, factor, gain):
    scaled = grad * gain
    return factor * (
        scaled
        - jnp.mean(scaled, axis=1, keepdims=True)
        - plain * jnp.mean(scaled * plain, axis=1, keepdims=True)
    )


def lead_dot(left, right):
    return lax.dot_general(
        left, right, (((0,), (0,)), ((), ())), preferred_element_type=jnp.float32
    )


def tail_dot(left, right):
    return lax.dot_general(
        left, right, (((1,), (1,)), ((), ())), preferred_element_type=jnp.float32
    )


def layer_pass(
    tokens,
    cotangent,
    norm1_gain,
    norm1_bias,
    w_query,
    b_query,
    w_key,
    b_key,
    w_value,
    b_value,
    w_out,
    b_out,
    norm2_gain,
    norm2_bias,
    w_up,
    b_up,
    w_down,
    b_down,
):
    rows = tokens.shape[0]
    seqs = rows // SEQ_LEN
    local = w_query.shape[1]
    heads_here = local // HEAD_DIM
    scale = 1.0 / math.sqrt(HEAD_DIM)
    causal = lax.broadcasted_iota(jnp.int32, (SEQ_LEN, SEQ_LEN), 0) >= lax.broadcasted_iota(
        jnp.int32, (SEQ_LEN, SEQ_LEN), 1
    )
    inputs = tokens.astype(jnp.float32)
    normed1, plain1, factor1 = layer_norm(inputs, norm1_gain, norm1_bias)
    first = normed1.astype(jnp.bfloat16)

    def project(weight, shift):
        return (jnp.dot(first, weight, preferred_element_type=jnp.float32) + shift).astype(
            jnp.bfloat16
        )

    def split(matrix):
        return matrix.reshape(seqs, SEQ_LEN, heads_here, HEAD_DIM)

    query_h = split(project(w_query, b_query))
    keys_h = split(project(w_key, b_key))
    values_h = split(project(w_value, b_value))

    def magnitude_of():
        scores = (
            jnp.einsum("sihe,sjhe->shij", query_h, keys_h, preferred_element_type=jnp.float32)
            * scale
        )
        root = jnp.sqrt(scores * scores + 1.0)
        return (scores, root, jnp.where(causal, root, -jnp.inf))

    scores, root, magnitude = magnitude_of()
    top = jnp.max(magnitude, axis=-1, keepdims=True)
    expo = jnp.exp(magnitude - top)
    total = jnp.sum(expo, axis=-1, keepdims=True)
    logsum = top + jnp.log(total)
    signed = scores / root * (expo / total)
    mixed = (
        jnp.einsum(
            "shij,sjhe->sihe",
            signed.astype(jnp.bfloat16),
            values_h,
            preferred_element_type=jnp.float32,
        )
        .reshape(rows, local)
        .astype(jnp.bfloat16)
    )
    attn_part = jnp.dot(mixed, w_out, preferred_element_type=jnp.float32)
    attn_part = lax.psum(attn_part.astype(jnp.bfloat16), "mp").astype(jnp.float32)
    hidden1 = inputs + attn_part + b_out
    normed2, plain2, factor2 = layer_norm(hidden1, norm2_gain, norm2_bias)
    second = normed2.astype(jnp.bfloat16)
    upper = jnp.dot(second, w_up, preferred_element_type=jnp.float32) + b_up
    activ = jax.nn.gelu(upper, approximate=False).astype(jnp.bfloat16)
    ffout = jnp.dot(activ, w_down, preferred_element_type=jnp.float32)
    ffout = lax.psum(ffout.astype(jnp.bfloat16), "mp").astype(jnp.float32)
    layer_out = (hidden1 + ffout + b_down).astype(jnp.bfloat16)
    grad_out = cotangent.astype(jnp.float32)
    grad_act = tail_dot(cotangent, w_down)
    cdf_part = 0.5 * (1.0 + jax.scipy.special.erf(upper * (1.0 / math.sqrt(2.0))))
    density = jnp.exp(-0.5 * upper * upper) * (1.0 / math.sqrt(2.0 * math.pi))
    grad_up = (grad_act * (cdf_part + upper * density)).astype(jnp.bfloat16)
    grad_norm2 = tail_dot(grad_up, w_up)
    grad_norm2 = lax.psum(grad_norm2.astype(jnp.bfloat16), "mp").astype(jnp.float32)
    mlp_terms = (
        jnp.sum(grad_norm2 * plain2, axis=0),
        jnp.sum(grad_norm2, axis=0),
        lead_dot(second, grad_up),
        jnp.sum(grad_up.astype(jnp.float32), axis=0),
        lead_dot(activ, cotangent),
        jnp.sum(grad_out, axis=0),
    )
    grad_hidden = grad_out + norm_back(grad_norm2, plain2, factor2, norm2_gain)
    grad_attn = grad_hidden.astype(jnp.bfloat16)
    grad_mixed = tail_dot(grad_attn, w_out).astype(jnp.bfloat16)
    out_terms = (lead_dot(mixed, grad_attn), jnp.sum(grad_hidden, axis=0))
    grad_mixed_h = split(grad_mixed)
    scores, root, magnitude = magnitude_of()
    probs = jnp.exp(magnitude - logsum)
    smooth_sign = scores / root
    signed = smooth_sign * probs
    grad_signed = jnp.einsum(
        "sihe,sjhe->shij", grad_mixed_h, values_h, preferred_element_type=jnp.float32
    )
    row_dot = jnp.sum(signed * grad_signed, axis=-1, keepdims=True)
    slope = 1.0 / (root * root * root) + smooth_sign * smooth_sign
    grad_scores = (probs * grad_signed * slope - signed * row_dot).astype(jnp.bfloat16)
    grad_query = (
        (
            jnp.einsum("shij,sjhe->sihe", grad_scores, keys_h, preferred_element_type=jnp.float32)
            * scale
        )
        .reshape(rows, local)
        .astype(jnp.bfloat16)
    )
    grad_keys = (
        (
            jnp.einsum("shij,sihe->sjhe", grad_scores, query_h, preferred_element_type=jnp.float32)
            * scale
        )
        .reshape(rows, local)
        .astype(jnp.bfloat16)
    )
    grad_values = (
        jnp.einsum(
            "shij,sihe->sjhe",
            signed.astype(jnp.bfloat16),
            grad_mixed_h,
            preferred_element_type=jnp.float32,
        )
        .reshape(rows, local)
        .astype(jnp.bfloat16)
    )
    grad_norm1 = (
        tail_dot(grad_query, w_query) + tail_dot(grad_keys, w_key) + tail_dot(grad_values, w_value)
    )
    grad_norm1 = lax.psum(grad_norm1.astype(jnp.bfloat16), "mp").astype(jnp.float32)
    attn_terms = (
        jnp.sum(grad_norm1 * plain1, axis=0),
        jnp.sum(grad_norm1, axis=0),
        lead_dot(first, grad_query),
        jnp.sum(grad_query.astype(jnp.float32), axis=0),
        lead_dot(first, grad_keys),
        jnp.sum(grad_keys.astype(jnp.float32), axis=0),
        lead_dot(first, grad_values),
        jnp.sum(grad_values.astype(jnp.float32), axis=0),
        out_terms[0],
        out_terms[1],
    )
    tokens_grad = (grad_hidden + norm_back(grad_norm1, plain1, factor1, norm1_gain)).astype(
        jnp.bfloat16
    )
    return (layer_out, tokens_grad, attn_terms, mlp_terms)


def body(
    tokens,
    norm1_gain,
    norm1_bias,
    w_query,
    b_query,
    w_key,
    b_key,
    w_value,
    b_value,
    w_out,
    b_out,
    norm2_gain,
    norm2_bias,
    w_up,
    b_up,
    w_down,
    b_down,
    cotangent,
):
    layer_out, tokens_grad, attn_terms, mlp_terms = layer_pass(
        tokens,
        cotangent,
        norm1_gain,
        norm1_bias,
        w_query,
        b_query,
        w_key,
        b_key,
        w_value,
        b_value,
        w_out,
        b_out,
        norm2_gain,
        norm2_bias,
        w_up,
        b_up,
        w_down,
        b_down,
    )
    joined = jax.tree.map(
        lambda part: part.astype(jnp.float32),
        lax.psum(for_sending(tuple(attn_terms) + tuple(mlp_terms)), "dp"),
    )
    attn_terms = joined[:10]
    mlp_terms = joined[10:]
    return (layer_out, tokens_grad) + tuple(attn_terms) + tuple(mlp_terms)


def solution(mesh):
    return jax.shard_map(
        body,
        mesh=mesh,
        in_specs=(
            P("dp", None),
            P(),
            P(),
            P(None, "mp"),
            P("mp"),
            P(None, "mp"),
            P("mp"),
            P(None, "mp"),
            P("mp"),
            P("mp", None),
            P(),
            P(),
            P(),
            P(None, "mp"),
            P("mp"),
            P("mp", None),
            P(),
            P("dp", None),
        ),
        out_specs=(
            P("dp", None),
            P("dp", None),
            P(),
            P(),
            P(None, "mp"),
            P("mp"),
            P(None, "mp"),
            P("mp"),
            P(None, "mp"),
            P("mp"),
            P("mp", None),
            P(),
            P(),
            P(),
            P(None, "mp"),
            P("mp"),
            P("mp", None),
            P(),
        ),
        check_vma=False,
    )
```

profile of v0, /device:TPU:0, one launch (start us, length us, event | category | flops | bytes accessed | tf_op | source)
XLA Modules:
  0.0 994.1 jit_solution(10935919470891825407)
XLA Ops:
  7.4 4.7 convert_reduce_fusion
  12.1 6.2 fusion.42
  18.4 4.7 fusion.37
  23.1 3.4 copy-done.10
  26.5 4.3 fusion.55
  30.7 12.9 %reshape.126 = bf16[32,256,4,64]{3,2,1,0:T(4,128)(2,1)} reshape(bf16[8192,256]{1,0:T(8,128)(2,1)} %fusion.55) | data formatting | bytes 8388608 | tf_op jit(solution)/shard_map/reshape | solution.py:82
  43.6 12.4 %copy.52 = bf16[32,256,4,64]{1,3,2,0:T(8,128)(2,1)} copy(bf16[32,256,4,64]{3,2,1,0:T(4,128)(2,1)} %reshape.126) | data formatting | bytes 8388608 | tf_op jit(solution)/shard_map/reshape | solution.py:82
  56.0 7.7 fusion.56
  63.7 12.9 %reshape.125 = bf16[32,256,4,64]{3,2,1,0:T(4,128)(2,1)} reshape(bf16[8192,256]{1,0:T(8,128)(2,1)} %fusion.56) | data formatting | bytes 8388608 | tf_op jit(solution)/shard_map/reshape | solution.py:82
  76.6 12.4 %copy.51 = bf16[32,256,4,64]{1,3,2,0:T(8,128)(2,1)} copy(bf16[32,256,4,64]{3,2,1,0:T(4,128)(2,1)} %reshape.125) | data formatting | bytes 8388608 | tf_op jit(solution)/shard_map/reshape | solution.py:82
  88.9 7.7 fusion.57
  96.6 13.2 %reshape.124 = bf16[32,256,4,64]{3,2,1,0:T(4,128)(2,1)} reshape(bf16[8192,256]{1,0:T(8,128)(2,1)} %fusion.57) | data formatting | bytes 8388608 | tf_op jit(solution)/shard_map/reshape | solution.py:82
  109.8 12.4 %copy.53 = bf16[32,256,4,64]{1,3,2,0:T(8,128)(2,1)} copy(bf16[32,256,4,64]{3,2,1,0:T(4,128)(2,1)} %reshape.124) | data formatting | bytes 8388608 | tf_op jit(solution)/shard_map/reshape | solution.py:82
  122.2 25.0 %fusion.70 = (f32[32,4,256]{2,1,0:T(4,128)S(1)}, f32[32,4,256,256]{2,3,1,0:T(8,128)}) fusion(pred[256,256]{0,1:T(8,128)(4,1)S(1)} %iota_compare_fusion, bf16[32,256,4,64]{1,3,2,0:T(8,128)(2,1)} %copy.51, bf16[32,256,4,64]{1,3,2,0:T(8,128)(2,1)} %copy.52), kind=kOutput, calls=%fused_computation.106 | convolution fusion | flops 1115652096 | bytes 42139648 | tf_op jit(solution)/shard_map/sihe,sjhe->shij/dot_general | solution.py:90
  147.2 19.3 %fusion.23 = f32[32,4,256]{2,1,0:T(4,128)S(1)} fusion(f32[32,4,256]{2,1,0:T(4,128)S(1)} %get-tuple-element.46, f32[32,4,256,256]{2,3,1,0:T(8,128)} %get-tuple-element.47, pred[256,256]{0,1:T(8,128)(4,1)S(1)} %iota_compare_fusion), kind=kLoop, calls=%fused_computation.39 | loop fusion | flops 50298880 | bytes 33882112 | tf_op jit(solution)/shard_map/reduce_sum | solution.py:99
  166.5 33.5 %convert_bitcast_fusion = bf16[32,256,4,64]{1,3,2,0:T(8,128)(2,1)} fusion(bf16[32,256,4,64]{1,3,2,0:T(8,128)(2,1)} %copy.53, f32[32,4,256]{2,1,0:T(4,128)S(1)} %fusion.23, f32[32,4,256]{2,1,0:T(4,128)S(1)} %get-tuple-element.46, f32[32,4,256,256]{2,3,1,0:T(8,128)} %get-tuple-element.47, pred[256,256]{0,1:T(8,128)(4,1)S(1)} %iota_compare_fusion), kind=kOutput, calls=%fused_computation.98 | convolution fusion | flops 1151336448 | bytes 42270720 | tf_op jit(solution)/shard_map/shij,sjhe->sihe/dot_general | solution.py:103
  200.0 4.6 copy.55
  204.7 4.3 copy.80
  210.9 5.8 convolution_convert_fusion.2
  216.8 41.7 %all-reduce.8.cloned.1.call-done = bf16[8192,512]{1,0:T(8,128)(2,1)} async-done(((bf16[8192,512]{1,0:T(8,128)(2,1)}), bf16[8192,512]{1,0:T(8,128)(2,1)}) %all-reduce.8.cloned.1.call-update) | async-done | bytes 8388624 | tf_op jit(solution)/shard_map/psum | solution.py:113
  258.5 8.6 fusion.58
  267.1 9.3 multiply_reduce_fusion.1
  277.1 8.0 add_convert_fusion.2
  285.1 81.4 %fusion.2 = (bf16[8192,1024]{1,0:T(8,128)(2,1)}, f32[8192,1024]{1,0:T(8,128)}) fusion(f32[1024]{0:T(1024)S(1)} %copy-done.50, bf16[8192,512]{1,0:T(8,128)(2,1)S(1)} %add_convert_fusion.2, bf16[512,1024]{1,0:T(8,128)(2,1)S(1)} %copy-done), kind=kOutput, calls=%fused_computation.5 | convolution fusion | flops 9143582720 | bytes 59772928 | tf_op jit(solution)/shard_map/dot_general | solution.py:117
  366.5 23.6 %fusion.84 = (bf16[1024]{0:T(1024)(128)(2,1)}, bf16[8192,1024]{1,0:T(8,128)(2,1)}) fusion(f32[8192,1024]{1,0:T(8,128)} %get-tuple-element.49, f32[1024]{0:T(1024)S(1)} %copy-done.50, bf16[8192,512]{1,0:T(8,128)(2,1)S(1)} %copy-done.7, bf16[1024,512]{1,0:T(8,128)(2,1)S(1)} %copy-done.49), kind=kOutput, calls=%fused_computation.127 | convolution fusion | flops 8690596864 | bytes 59774976 | tf_op jit(solution)/shard_map/dot_general | solution.py:39
  390.2 17.0 %convolution_convert_fusion = bf16[8192,512]{1,0:T(8,128)(2,1)} fusion(bf16[8192,1024]{1,0:T(8,128)(2,1)} %get-tuple-element.59, bf16[512,1024]{1,0:T(8,128)(2,1)S(1)} %copy-done), kind=kOutput, calls=%fused_computation.82 | convolution fusion | flops 8594128896 | bytes 26214400 | tf_op jit(solution)/shard_map/dot_general | solution.py:39
  407.3 17.2 %convolution_convert_fusion.1 = bf16[8192,512]{1,0:T(8,128)(2,1)} fusion(bf16[8192,1024]{1,0:T(8,128)(2,1)} %get-tuple-element.48, bf16[1024,512]{1,0:T(8,128)(2,1)S(1)} %copy-done.49), kind=kOutput, calls=%fused_computation.83 | convolution fusion | flops 8594128896 | bytes 26214400 | tf_op jit(solution)/shard_map/dot_general | solution.py:119
  424.6 15.8 %convolution_convert_fusion.5 = bf16[512,1024]{1,0:T(8,128)(2,1)} fusion(bf16[8192,512]{1,0:T(8,128)(2,1)} %copy-done.11, bf16[8192,1024]{1,0:T(8,128)(2,1)} %get-tuple-element.59), kind=kOutput, calls=%fused_computation.101 | convolution fusion | flops 8590458880 | bytes 26214400 | tf_op jit(solution)/shard_map/dot_general | solution.py:33
  440.4 13.1 %convolution_convert_fusion.4 = bf16[1024,512]{1,0:T(8,128)(2,1)} fusion(bf16[8192,1024]{1,0:T(8,128)(2,1)S(1)} %bitcast.99, bf16[8192,512]{1,0:T(8,128)(2,1)} %param.35), kind=kOutput, calls=%fused_computation.100 | convolution fusion | flops 8590458880 | bytes 26214400 | tf_op jit(solution)/shard_map/dot_general | solution.py:33
  453.5 16.4 %fusion.47 = (bf16[512]{0:T(512)(128)(2,1)}, f32[8192]{0:T(1024)S(1)}, f32[8192]{0:T(1024)S(1)}) fusion(bf16[8192,512]{1,0:T(8,128)(2,1)} %all-reduce.10.cloned.1.call-done, f32[8192]{0:T(1024)S(1)} %copy-done.29, f32[8192]{0:T(1024)S(1)} %copy-done.19, f32[512]{0:T(512)S(1)} %copy-done.37, bf16[8192,512]{1,0:T(8,128)(2,1)} %all-reduce.8.cloned.1.call-done, ...), kind=kLoop, calls=%fused_computation.70 | loop fusion | flops 54509056 | bytes 25302016 | tf_op jit(solution)/shard_map/reduce_sum | solution.py:130
  470.0 12.5 %fusion.79 = (bf16[512]{0:T(512)(128)(2,1)}, f32[8192,512]{1,0:T(8,128)S(1)}) fusion(f32[8192]{0:T(1024)S(1)} %get-tuple-element.60, f32[8192]{0:T(1024)S(1)} %copy-done.19, f32[512]{0:T(512)S(1)} %copy-done.37, bf16[8192,512]{1,0:T(8,128)(2,1)} %all-reduce.8.cloned.1.call-done, bf16[8192,512]{1,0:T(8,128)(2,1)} %param.18, f32[8192]{0:T(1024)S(1)} %get-tuple-element.61, ...), kind=kLoop, calls=%fused_computation.123 | loop fusion | flops 62914048 | bytes 50467840 | tf_op jit(solution)/shard_map/reduce_sum | solution.py:140
  482.5 4.0 fusion.65
  488.4 4.3 convolution_convert_fusion.3
  492.7 12.9 %reshape.127 = bf16[32,256,4,64]{3,2,1,0:T(4,128)(2,1)} reshape(bf16[8192,256]{1,0:T(8,128)(2,1)} %convolution_convert_fusion.3) | data formatting | bytes 8388608 | tf_op jit(solution)/shard_map/reshape | solution.py:82
  505.6 12.3 %copy.57 = bf16[32,256,4,64]{1,3,2,0:T(8,128)(2,1)} copy(bf16[32,256,4,64]{3,2,1,0:T(4,128)(2,1)} %reshape.127) | data formatting | bytes 8388608 | tf_op jit(solution)/shard_map/reshape | solution.py:82
  518.0 31.5 %fusion.83 = (bf16[4,64]{1,0:T(4,128)(2,1)}, bf16[32,4,64,256]{3,2,1,0:T(8,128)(2,1)}) fusion(bf16[32,256,4,64]{1,3,2,0:T(8,128)(2,1)} %copy.57, f32[32,4,256]{2,1,0:T(4,128)S(1)} %bitcast.94, f32[32,4,256,256]{2,3,1,0:T(8,128)} %get-tuple-element.47, pred[256,256]{0,1:T(8,128)(4,1)S(1)} %copy-done.21), kind=kOutput, calls=%fused_computation.126 | convolution fusion | flops 1145044736 | bytes 42140160 | tf_op jit(solution)/shard_map/shij,sihe->sjhe/dot_general | solution.py:169
  549.5 33.2 %multiply_reduce_fusion = (f32[32,4,256]{2,1,0:T(4,128)S(1)}, f32[32,4,256,256]{2,3,1,0:T(8,128)}) fusion(f32[32,4,256]{2,1,0:T(4,128)S(1)} %bitcast.95, f32[32,4,256,256]{2,3,1,0:T(8,128)} %get-tuple-element.47, pred[256,256]{0,1:T(8,128)(4,1)S(1)} %copy-done.21, bf16[32,256,4,64]{1,3,2,0:T(8,128)(2,1)} %copy.57, bf16[32,256,4,64]{1,3,2,0:T(8,128)(2,1)S(1)} %copy-done.12), kind=kOutput, calls=%fused_computation.16 | convolution fusion | flops 1149206528 | bytes 75825152 | tf_op jit(solution)/shard_map/sihe,sjhe->shij/dot_general | solution.py:146
  582.7 34.6 %fusion.21 = bf16[32,4,256,256]{2,3,1,0:T(8,128)(2,1)} fusion(f32[32,4,256,256]{2,3,1,0:T(8,128)} %get-tuple-element.51, f32[32,4,256,256]{2,3,1,0:T(8,128)} %get-tuple-element.47, f32[32,4,256]{2,1,0:T(4,128)S(1)} %get-tuple-element.50, f32[32,4,256]{2,1,0:T(4,128)S(1)} %bitcast.96, pred[256,256]{0,1:T(8,128)(4,1)S(1)} %copy-done.21), kind=kLoop, calls=%fused_computation.36 | loop fusion | flops 142606336 | bytes 84213760 | tf_op jit(solution)/shard_map/convert_element_type | solution.py:151
  617.4 12.5 %fusion.82 = (bf16[4,64]{1,0:T(4,128)(2,1)S(1)}, bf16[32,4,64,256]{3,2,1,0:T(8,128)(2,1)}) fusion(bf16[32,256,4,64]{1,3,2,0:T(8,128)(2,1)} %copy.51, bf16[32,4,256,256]{2,3,1,0:T(8,128)(2,1)} %fusion.21), kind=kOutput, calls=%fused_computation.125 | convolution fusion | flops 1080033024 | bytes 25166336 | tf_op jit(solution)/shard_map/shij,sihe->sjhe/dot_general | solution.py:162
  629.9 10.2 %fusion.81 = (bf16[4,64]{1,0:T(4,128)(2,1)S(1)}, bf16[32,4,64,256]{3,2,1,0:T(8,128)(2,1)S(1)}) fusion(bf16[32,256,4,64]{1,3,2,0:T(8,128)(2,1)} %copy.52, bf16[32,4,256,256]{2,3,1,0:T(8,128)(2,1)} %fusion.21), kind=kOutput, calls=%fused_computation.124 | convolution fusion | flops 1080033024 | bytes 25166336 | tf_op jit(solution)/shard_map/shij,sjhe->sihe/dot_general | solution.py:154
  640.1 2.4 copy.61
  642.5 4.4 copy.81
  646.9 3.1 convolution_convert_fusion.8
  650.0 8.3 fusion.85
  658.3 2.5 copy.67
  660.8 4.3 copy.83
  665.1 2.0 copy-done.6
  667.1 3.1 convolution_convert_fusion.6
  670.2 2.7 copy.64
  672.8 4.3 copy.82
  677.1 2.0 copy-done.9
  679.1 3.1 convolution_convert_fusion.7
  682.3 11.0 %fusion.86 = f32[8192,512]{1,0:T(8,128)} fusion(bf16[8192,256]{0,1:T(8,128)(2,1)} %bitcast.87, bf16[512,256]{1,0:T(8,128)(2,1)S(1)} %copy-done.35), kind=kOutput, calls=%fused_computation.129 | convolution fusion | flops 2147483648 | bytes 21233664 | tf_op jit(solution)/shard_map/dot_general | solution.py:39
  693.2 17.4 %add_convert_fusion = bf16[8192,512]{1,0:T(8,128)(2,1)} fusion(f32[8192,512]{1,0:T(8,128)} %fusion.85, f32[8192,512]{1,0:T(8,128)} %fusion.86, bf16[8192,256]{0,1:T(8,128)(2,1)} %bitcast.79, bf16[512,256]{1,0:T(8,128)(2,1)S(1)} %copy-done.31), kind=kOutput, calls=%fused_computation.75 | convolution fusion | flops 2160066560 | bytes 46399488 | tf_op jit(solution)/shard_map/dot_general | solution.py:39
  710.7 4.6 reduce_sum.229
  715.6 4.6 reduce_sum.227
  720.2 112.7 %all-reduce.12.cloned.1.call-done = (bf16[512,256]{1,0:T(8,128)(2,1)}, bf16[512,256]{1,0:T(8,128)(2,1)}, bf16[512,256]{1,0:T(8,128)(2,1)}, bf16[256,512]{1,0:T(8...) async-done(((bf16[512,256]{1,0:T(8,128)(2,1)}, bf16[512,256]{1,0:T(8,128)(2,1)}, bf16[512,256]{1,0:T(8,128)(2,1)}, bf16[256,512]{1,0:T(8,128)(2,1)}, ...) | async-done | bytes 3145744 | tf_op jit(solution)/shard_map/psum | solution.py:242
  840.1 3.1 convert_element_type.256
  843.2 3.1 convert_element_type.259
  846.4 48.7 %all-reduce.14.cloned.1.call-done = (bf16[8192,512]{1,0:T(8,128)(2,1)}, bf16[8192,512]{1,0:T(8,128)(2,1)}) async-done(((bf16[8192,512]{1,0:T(8,128)(2,1)}, bf16[8192,512]{1,0:T(8,128)(2,1)}), (bf16[8192,512]{1,0:T(8,128)(2,1)}, bf16[8192,512]{1,0:T(8,128)(2,1)})) %all-reduce.14.cloned.1.call-update) | async-done | bytes 16777232 | tf_op jit(solution)/shard_map/psum | solution.py:120
  895.1 4.5 reduce_sum.218
  899.6 13.9 %fusion.49 = (bf16[512]{0:T(512)(128)(2,1)S(1)}, f32[8192]{0:T(1024)S(1)}, f32[8192]{0:T(1024)S(1)}) fusion(bf16[8192,512]{1,0:T(8,128)(2,1)} %param.18, bf16[8192,512]{1,0:T(8,128)(2,1)} %get-tuple-element.41, f32[8192]{0:T(1024)S(1)} %copy-done.23, f32[8192]{0:T(1024)S(1)} %copy-done.17, f32[512]{0:T(512)S(1)} %copy-done.40), kind=kLoop, calls=%fused_computation.72 | loop fusion | flops 41926144 | bytes 16911360 | tf_op jit(solution)/shard_map/reduce_sum | solution.py:183
  913.6 43.0 %all-reduce = (bf16[512]{0:T(512)(128)(2,1)S(1)}, bf16[512]{0:T(512)(128)(2,1)S(1)}, bf16[256]{0:T(256)(128)(2,1)S(1)}, bf16[256]{0:T(256)(128)(2,1)S(1)}, bf16[...) all-reduce(bf16[512]{0:T(512)(128)(2,1)S(1)} %get-tuple-element.20,, ...), channel_id=1, replica_groups=mesh['mp'=2,'dp'=16] {'dp'}, use_global_device_ids=true, to_apply=%region_16.17 | all-reduce | flops 4864 | bytes 19456 | tf_op jit(solution)/shard_map/psum | solution.py:242
  962.4 24.6 %fusion.41 = (bf16[8192,512]{1,0:T(8,128)(2,1)}, bf16[8192,512]{1,0:T(8,128)(2,1)}) fusion(f32[8192,512]{1,0:T(8,128)} %copy-done.2, bf16[8192,512]{1,0:T(8,128)(2,1)} %param.18, bf16[8192,512]{1,0:T(8,128)(2,1)} %get-tuple-element.41, f32[8192]{0:T(1024)S(1)} %broadcast_multiply_fusion, f32[8192]{0:T(1024)S(1)} %broadcast_multiply_fusion.1, ...), kind=kLoop, calls=%fused_computation.64 | loop fusion | flops 75497472 | bytes 67246080 | tf_op jit(solution)/shard_map/convert_element_type | solution.py:194
  (166 shorter events, 18.2 us)
Async XLA Ops:
  7.2 277.9 %copy-start = (bf16[512,1024]{1,0:T(8,128)(2,1)S(1)}, bf16[512,1024]{1,0:T(8,128)(2,1)}, u32[]{:S(2)}) copy-start(bf16[512,1024]{1,0:T(8,128)(2,1)} %param.31) | copy-start | bytes 3145732
  7.2 11.1 %copy-start.39 = (f32[512]{0:T(512)S(1)}, f32[512]{0:T(512)}, u32[]{:S(2)}) copy-start(f32[512]{0:T(512)} %param.19) | copy-start | bytes 6148
  7.2 11.1 %copy-start.46 = (f32[512]{0:T(512)S(1)}, f32[512]{0:T(512)}, u32[]{:S(2)}) copy-start(f32[512]{0:T(512)} %param.20) | copy-start | bytes 6148
  7.2 251.2 %all-reduce.8.cloned.1.call-start = ((), (), s32[]{:S(2)}) async-start(), calls=%async_computation | async-start | bytes 16777216 | tf_op jit(solution)/shard_map/psum | solution.py:113
  7.3 11.0 %slice-start = ((s8[8388608]{0:T(1024)(128)(4,1)}), s8[4194304]{0:T(1024)(128)(4,1)S(1)}, s32[]{:S(2)}) async-start(s8[8388608]{0:T(1024)(128)(4,1)} %bitcast.72), calls=%async_computation.4 | async-start | bytes 8388608
  7.3 159.1 %copy-start.20 = (pred[256,256]{0,1:T(8,128)(4,1)}, pred[256,256]{0,1:T(8,128)(4,1)S(1)}, u32[]{:S(2)}) copy-start(pred[256,256]{0,1:T(8,128)(4,1)S(1)} %iota_compare_fusion) | copy-start | bytes 196612
  7.3 19.1 %copy-start.34 = (bf16[512,256]{1,0:T(8,128)(2,1)S(1)}, bf16[512,256]{1,0:T(8,128)(2,1)}, u32[]{:S(2)}) copy-start(bf16[512,256]{1,0:T(8,128)(2,1)} %param.23) | copy-start | bytes 786436
  7.3 19.1 %copy-start.51 = (f32[256]{0:T(256)S(1)}, f32[256]{0:T(256)}, u32[]{:S(2)}) copy-start(f32[256]{0:T(256)} %param.24) | copy-start | bytes 3076
  12.1 6.2 slice-start.1
  12.1 10.9 %copy-start.16 = (f32[8192]{0:T(1024)}, f32[8192]{0:T(1024)S(1)}, u32[]{:S(2)}) copy-start(f32[8192]{0:T(1024)S(1)} %broadcast_multiply_fusion.5) | copy-start | bytes 98308
  18.3 4.7 copy-start.22
  26.4 29.5 %copy-start.32 = (bf16[512,256]{1,0:T(8,128)(2,1)S(1)}, bf16[512,256]{1,0:T(8,128)(2,1)}, u32[]{:S(2)}) copy-start(bf16[512,256]{1,0:T(8,128)(2,1)} %param.21) | copy-start | bytes 786436
  26.4 29.5 %copy-start.52 = (f32[256]{0:T(256)S(1)}, f32[256]{0:T(256)}, u32[]{:S(2)}) copy-start(f32[256]{0:T(256)} %param.22) | copy-start | bytes 3076
  56.0 33.0 %copy-start.30 = (bf16[512,256]{1,0:T(8,128)(2,1)S(1)}, bf16[512,256]{1,0:T(8,128)(2,1)}, u32[]{:S(2)}) copy-start(bf16[512,256]{1,0:T(8,128)(2,1)} %param.25) | copy-start | bytes 786436
  56.0 33.0 %copy-start.53 = (f32[256]{0:T(256)S(1)}, f32[256]{0:T(256)}, u32[]{:S(2)}) copy-start(f32[256]{0:T(256)} %param.26) | copy-start | bytes 3076
  147.2 19.3 %copy-start.24 = (f32[32,4,256]{2,1,0:T(4,128)}, f32[32,4,256]{2,1,0:T(4,128)S(1)}, u32[]{:S(2)}) copy-start(f32[32,4,256]{2,1,0:T(4,128)S(1)} %get-tuple-element.46) | copy-start | bytes 393220
  166.5 33.5 %copy-start.26 = (f32[32,4,256]{2,1,0:T(4,128)}, f32[32,4,256]{2,1,0:T(4,128)S(1)}, u32[]{:S(2)}) copy-start(f32[32,4,256]{2,1,0:T(4,128)S(1)} %fusion.23) | copy-start | bytes 393220
  200.0 10.9 %copy-start.14 = (bf16[256,512]{1,0:T(8,128)(2,1)S(1)}, bf16[256,512]{1,0:T(8,128)(2,1)}, u32[]{:S(2)}) copy-start(bf16[256,512]{1,0:T(8,128)(2,1)} %param.27) | copy-start | bytes 786436
  204.7 53.8 %copy-start.36 = (f32[512]{0:T(512)S(1)}, f32[512]{0:T(512)}, u32[]{:S(2)}) copy-start(f32[512]{0:T(512)} %param.28) | copy-start | bytes 6148
  216.7 60.3 %copy-start.41 = (f32[512]{0:T(512)S(1)}, f32[512]{0:T(512)}, u32[]{:S(2)}) copy-start(f32[512]{0:T(512)} %param.29) | copy-start | bytes 6148
  216.7 60.3 %copy-start.47 = (f32[512]{0:T(512)S(1)}, f32[512]{0:T(512)}, u32[]{:S(2)}) copy-start(f32[512]{0:T(512)} %param.30) | copy-start | bytes 6148
  216.8 236.7 %all-reduce.10.cloned.1.call-start = ((), (), s32[]{:S(2)}) async-start(), calls=%async_computation.1 | async-start | bytes 16777216 | tf_op jit(solution)/shard_map/psum | solution.py:128
  267.0 10.0 %slice-start.2 = ((s8[8388608]{0:T(1024)(128)(4,1)}), s8[4194304]{0:T(1024)(128)(4,1)S(1)}, s32[]{:S(2)}) async-start(s8[8388608]{0:T(1024)(128)(4,1)} %bitcast.74), calls=%async_computation.6 | async-start | bytes 8388608
  267.1 9.4 copy-start.18
  267.1 10.0 %slice-start.3 = ((s8[8388608]{0:T(1024)(128)(4,1)}), s8[4194304]{0:T(1024)(128)(4,1)S(1)}, s32[]{:S(2)}) async-start(s8[8388608]{0:T(1024)(128)(4,1)} %bitcast.74), calls=%async_computation.7 | async-start | bytes 8388608
  276.4 8.7 copy-start.50
  285.1 81.4 %copy-start.11 = (bf16[8192,512]{1,0:T(8,128)(2,1)}, bf16[8192,512]{1,0:T(8,128)(2,1)S(1)}, u32[]{:S(2)}) copy-start(bf16[8192,512]{1,0:T(8,128)(2,1)S(1)} %add_convert_fusion.2) | copy-start | bytes 25165828
  285.1 81.4 %copy-start.7 = (bf16[8192,512]{1,0:T(8,128)(2,1)S(1)}, bf16[8192,512]{1,0:T(8,128)(2,1)}, u32[]{:S(2)}) copy-start(bf16[8192,512]{1,0:T(8,128)(2,1)} %param.35) | copy-start | bytes 25165828
  285.1 81.4 %copy-start.49 = (bf16[1024,512]{1,0:T(8,128)(2,1)S(1)}, bf16[1024,512]{1,0:T(8,128)(2,1)}, u32[]{:S(2)}) copy-start(bf16[1024,512]{1,0:T(8,128)(2,1)} %param.33) | copy-start | bytes 3145732
  390.2 17.1 %copy-start.25 = (f32[32,4,256]{2,1,0:T(4,128)S(1)}, f32[32,4,256]{2,1,0:T(4,128)}, u32[]{:S(2)}) copy-start(f32[32,4,256]{2,1,0:T(4,128)} %copy-done.24) | copy-start | bytes 393220
  390.2 17.1 %copy-start.27 = (f32[32,4,256]{2,1,0:T(4,128)S(1)}, f32[32,4,256]{2,1,0:T(4,128)}, u32[]{:S(2)}) copy-start(f32[32,4,256]{2,1,0:T(4,128)} %copy-done.26) | copy-start | bytes 393220
  407.2 425.7 %all-reduce.12.cloned.1.call-start = ((), (), s32[]{:S(2)}) async-start(), calls=%async_computation.2 | async-start | bytes 6291456 | tf_op jit(solution)/shard_map/psum | solution.py:242
  407.3 33.1 %slice-start.6 = ((s8[16777216]{0:T(1024)(128)(4,1)}), s8[4194304]{0:T(1024)(128)(4,1)S(1)}, s32[]{:S(2)}) async-start(s8[16777216]{0:T(1024)(128)(4,1)} %bitcast.98), calls=%async_computation.10 | async-start | bytes 8388608
  407.3 33.0 %slice-start.7 = ((s8[16777216]{0:T(1024)(128)(4,1)}), s8[4194304]{0:T(1024)(128)(4,1)S(1)}, s32[]{:S(2)}) async-start(s8[16777216]{0:T(1024)(128)(4,1)} %bitcast.98), calls=%async_computation.11 | async-start | bytes 8388608
  407.3 33.0 %slice-start.8 = ((s8[16777216]{0:T(1024)(128)(4,1)}), s8[4194304]{0:T(1024)(128)(4,1)S(1)}, s32[]{:S(2)}) async-start(s8[16777216]{0:T(1024)(128)(4,1)} %bitcast.98), calls=%async_computation.12 | async-start | bytes 8388608
  424.6 15.8 %slice-start.9 = ((s8[16777216]{0:T(1024)(128)(4,1)}), s8[4194304]{0:T(1024)(128)(4,1)S(1)}, s32[]{:S(2)}) async-start(s8[16777216]{0:T(1024)(128)(4,1)} %bitcast.98), calls=%async_computation.13 | async-start | bytes 8388608
  440.4 13.1 %copy-start.19 = (f32[8192]{0:T(1024)S(1)}, f32[8192]{0:T(1024)}, u32[]{:S(2)}) copy-start(f32[8192]{0:T(1024)} %copy-done.18) | copy-start | bytes 98308
  440.4 13.1 %copy-start.29 = (f32[8192]{0:T(1024)S(1)}, f32[8192]{0:T(1024)}, u32[]{:S(2)}) copy-start(f32[8192]{0:T(1024)} %copy-done.28) | copy-start | bytes 98308
  440.4 13.1 %copy-start.37 = (f32[512]{0:T(512)S(1)}, f32[512]{0:T(512)}, u32[]{:S(2)}) copy-start(f32[512]{0:T(512)} %param.28) | copy-start | bytes 6148
  440.4 13.1 %copy-start.42 = (f32[512]{0:T(512)S(1)}, f32[512]{0:T(512)}, u32[]{:S(2)}) copy-start(f32[512]{0:T(512)} %param.29) | copy-start | bytes 6148
  453.5 16.5 %copy-start.3 = (bf16[8192,512]{1,0:T(8,128)(2,1)S(1)}, bf16[8192,512]{1,0:T(8,128)(2,1)}, u32[]{:S(2)}) copy-start(bf16[8192,512]{1,0:T(8,128)(2,1)} %all-reduce.10.cloned.1.call-done) | copy-start | bytes 25165828
  470.0 12.5 %copy-start.5 = (bf16[32,8,32,256]{3,1,2,0:T(8,128)(2,1)S(1)}, bf16[32,8,32,256]{3,1,2,0:T(8,128)(2,1)}, u32[]{:S(2)}) copy-start(bf16[32,8,32,256]{3,1,2,0:T(8,128)(2,1)} %copy-done.4) | copy-start | bytes 12582916
  482.5 5.9 copy-start.2
  482.5 5.9 copy-start.15
  492.7 25.2 %copy-start.21 = (pred[256,256]{0,1:T(8,128)(4,1)S(1)}, pred[256,256]{0,1:T(8,128)(4,1)}, u32[]{:S(2)}) copy-start(pred[256,256]{0,1:T(8,128)(4,1)} %copy-done.20) | copy-start | bytes 196612
  518.0 31.5 %copy-start.12 = (bf16[32,256,4,64]{1,3,2,0:T(8,128)(2,1)S(1)}, bf16[32,256,4,64]{1,3,2,0:T(8,128)(2,1)}, u32[]{:S(2)}) copy-start(bf16[32,256,4,64]{1,3,2,0:T(8,128)(2,1)} %copy.53) | copy-start | bytes 12582916
  640.1 6.8 slice-start.4
  640.1 9.9 copy-start.33
  642.5 4.4 slice-start.5
  646.9 11.4 %copy-start.13 = (bf16[32,4,64,256]{3,2,1,0:T(8,128)(2,1)S(1)}, bf16[32,4,64,256]{3,2,1,0:T(8,128)(2,1)}, u32[]{:S(2)}) copy-start(bf16[32,4,64,256]{3,2,1,0:T(8,128)(2,1)} %get-tuple-element.57) | copy-start | bytes 12582916
  658.3 11.8 %copy-start.8 = (bf16[32,4,64,256]{3,2,1,0:T(8,128)(2,1)S(1)}, bf16[32,4,64,256]{3,2,1,0:T(8,128)(2,1)}, u32[]{:S(2)}) copy-start(bf16[32,4,64,256]{3,2,1,0:T(8,128)(2,1)} %get-tuple-element.55) | copy-start | bytes 12582916
  670.1 12.1 %copy-start.35 = (bf16[512,256]{1,0:T(8,128)(2,1)S(1)}, bf16[512,256]{1,0:T(8,128)(2,1)}, u32[]{:S(2)}) copy-start(bf16[512,256]{1,0:T(8,128)(2,1)} %param.23) | copy-start | bytes 786436
  679.1 14.1 %copy-start.31 = (bf16[512,256]{1,0:T(8,128)(2,1)S(1)}, bf16[512,256]{1,0:T(8,128)(2,1)}, u32[]{:S(2)}) copy-start(bf16[512,256]{1,0:T(8,128)(2,1)} %param.25) | copy-start | bytes 786436
  682.2 212.8 %all-reduce.14.cloned.1.call-start = ((), (), s32[]{:S(2)}) async-start(), calls=%async_computation.3 | async-start | bytes 33554432 | tf_op jit(solution)/shard_map/psum | solution.py:120
  710.7 4.7 copy-start.54
  710.7 188.9 %copy-start.17 = (f32[8192]{0:T(1024)S(1)}, f32[8192]{0:T(1024)}, u32[]{:S(2)}) copy-start(f32[8192]{0:T(1024)} %copy-done.16) | copy-start | bytes 98308
  710.7 188.9 %copy-start.23 = (f32[8192]{0:T(1024)S(1)}, f32[8192]{0:T(1024)}, u32[]{:S(2)}) copy-start(f32[8192]{0:T(1024)} %copy-done.22) | copy-start | bytes 98308
  710.7 188.9 %copy-start.40 = (f32[512]{0:T(512)S(1)}, f32[512]{0:T(512)}, u32[]{:S(2)}) copy-start(f32[512]{0:T(512)} %param.19) | copy-start | bytes 6148
  836.5 77.1 %copy-start.43 = (bf16[512]{0:T(512)(128)(2,1)S(1)}, bf16[512]{0:T(512)(128)(2,1)}, u32[]{:S(2)}) copy-start(bf16[512]{0:T(512)(128)(2,1)} %get-tuple-element.18) | copy-start | bytes 3076
  836.5 77.1 %copy-start.44 = (bf16[512]{0:T(512)(128)(2,1)S(1)}, bf16[512]{0:T(512)(128)(2,1)}, u32[]{:S(2)}) copy-start(bf16[512]{0:T(512)(128)(2,1)} %get-tuple-element.42) | copy-start | bytes 3076
  836.5 77.2 %copy-start.48 = (bf16[1024]{0:T(1024)(128)(2,1)S(1)}, bf16[1024]{0:T(1024)(128)(2,1)}, u32[]{:S(2)}) copy-start(bf16[1024]{0:T(1024)(128)(2,1)} %get-tuple-element.58) | copy-start | bytes 6148
  836.5 125.9 %copy-start.38 = (f32[512]{0:T(512)S(1)}, f32[512]{0:T(512)}, u32[]{:S(2)}) copy-start(f32[512]{0:T(512)} %param.28) | copy-start | bytes 6148
  836.5 125.9 %copy-start.45 = (f32[512]{0:T(512)S(1)}, f32[512]{0:T(512)}, u32[]{:S(2)}) copy-start(f32[512]{0:T(512)} %param.34) | copy-start | bytes 6148
  962.4 24.7 %copy-start.1 = (bf16[512,1024]{1,0:T(8,128)(2,1)S(1)}, bf16[512,1024]{1,0:T(8,128)(2,1)}, u32[]{:S(2)}) copy-start(bf16[512,1024]{1,0:T(8,128)(2,1)} %param.31) | copy-start | bytes 3145732
  (5 other events, 10.0 us)
Sparse Core Ops, SparseCore 0:
  216.8 41.5 all-reduce.7
  407.3 40.0 all-reduce.9
  682.4 150.4 all-reduce.11
  836.1 58.9 all-reduce.13
where the time goes:
time: 1010 us; the launch traced here: 994 us
  matrix products  394 us (39%)
  waiting for transfers between devices  203 us (20%)
  other arithmetic  196 us (19%)
  local copies, waits for them, and re-layouts  143 us (14%)
  blocking collectives  43 us (4%)
  between operations  15.1 us (1%)
    psum x1, waiting for transfers between devices, body(): lax.psum(for_sending(tuple(attn_terms) + tuple(mlp_terms)), 'dp')  113 us
    reshape x8, local copies, waits for them, and re-layouts, split(): return matrix.reshape(seqs, SEQ_LEN, heads_here, HEAD_DIM)  101 us
    dot_general x6, matrix products, tail_dot(): lax.dot_general(left, right, (((1,), (1,)), ((), ())), preferred_element_...  81.7 us
    dot_general x1, matrix products, layer_pass(): upper = jnp.dot(second, w_up, preferred_element_type=jnp.float32) + b_up  81.4 us
    psum x1, waiting for transfers between devices, layer_pass(): ffout = lax.psum(ffout.astype(jnp.bfloat16), 'mp').astype(jnp.float32)  48.7 us
    psum x1, blocking collectives, body(): lax.psum(for_sending(tuple(attn_terms) + tuple(mlp_terms)), 'dp')  43 us
    dot_general x6, matrix products, lead_dot(): lax.dot_general(left, right, (((0,), (0,)), ((), ())), preferred_element_...  42.1 us
    psum x1, waiting for transfers between devices, layer_pass(): lax.psum(attn_part.astype(jnp.bfloat16), 'mp').astype(jnp.float32)  41.7 us
  transfers between devices with their start and end apart: 4, of which 3 were waited for; matrix products, arithmetic and copies ran while one was open for 10% of the time, Pallas kernels for 0%

commit v1 on v0

v1 whole, which is shorter than its diff:
```python
import functools
import math

import jax
import jax.numpy as jnp
from jax import lax
from jax.experimental import pallas as pl
from jax.experimental.pallas import tpu as pltpu
from jax.sharding import PartitionSpec as P

HEAD_DIM = 64
SEQ = 256
HALF = SEQ // 2
LANES = 128
BF = jnp.bfloat16
F32 = jnp.float32
VMEM_LIMIT = 60 * 1024 * 1024


def dot(left, right):
    return jnp.dot(left, right, preferred_element_type=F32)


def tail_dot(left, right):
    return lax.dot_general(left, right, (((1,), (1,)), ((), ())), preferred_element_type=F32)


def turned(block):
    return block.astype(F32).T.astype(BF)


def wide(column, lanes):
    return jnp.concatenate([column] * (lanes // LANES), axis=1)


def lane_fold(rows):
    total = rows[:, :LANES]
    for start in range(LANES, rows.shape[1], LANES):
        total = total + rows[:, start : start + LANES]
    return total


def norm_plain(x):
    center = x - jnp.mean(x, axis=0, keepdims=True)
    factor = lax.rsqrt(jnp.mean(center * center, axis=0, keepdims=True) + 1e-05)
    return center * factor, factor


def norm_back(grad, plain, factor, gain):
    scaled = grad * gain
    return factor * (
        scaled
        - jnp.mean(scaled, axis=0, keepdims=True)
        - plain * jnp.mean(scaled * plain, axis=0, keepdims=True)
    )


def upper_mask():
    return lax.broadcasted_iota(jnp.int32, (HALF, HALF), 0) <= lax.broadcasted_iota(
        jnp.int32, (HALF, HALF), 1
    )


def head_scores(keys, query):
    full = dot(keys.astype(F32).T.astype(BF), query)
    return full[:HALF, :HALF], full[:, HALF:]


def smooth(scores):
    square = scores * scores + 1.0
    inverse = lax.rsqrt(square)
    return inverse, square * inverse


def attend(scores, mask):
    inverse, root = smooth(scores)
    if scores.shape[0] > HALF:
        diag = jnp.where(mask, root[HALF:], -1e30)
        magnitude = jnp.concatenate([root[:HALF], diag], axis=0)
    else:
        magnitude = jnp.where(mask, root, -1e30)
    top = jnp.max(magnitude, axis=0, keepdims=True)
    expo = jnp.exp(magnitude - top)
    total = jnp.sum(expo, axis=0, keepdims=True)
    signed = (scores * inverse) * (expo * (1.0 / total))
    return signed, top + jnp.log(total)


def attn_kernel(seqs, *refs):
    (tok, wq0, wq1, wk0, wk1, wv0, wv1, wo0, wo1, vec) = refs[:10]
    (query_o, keys_o, values_o, mixed_o, logsum_o, hidden_o) = refs[10:16]
    wqkv_t, wo_t = refs[16:18]
    dim = tok.shape[1]
    lanes = seqs * SEQ

    @pl.when(pl.program_id(0) == 0)
    def _():
        part = dim // 2
        for index, ref in enumerate((wq0, wq1, wk0, wk1, wv0, wv1)):
            wqkv_t[index * part : (index + 1) * part, :] = turned(ref[...])
        wo_t[:, :part] = turned(wo0[...])
        wo_t[:, part:] = turned(wo1[...])

    x = tok[...].astype(F32).T
    plain, _ = norm_plain(x)
    first = (plain * wide(vec[0:dim, :], lanes) + wide(vec[dim : 2 * dim, :], lanes)).astype(BF)
    outs = []
    for index in range(3):
        made = dot(wqkv_t[index * dim : (index + 1) * dim, :], first)
        made = made + wide(vec[(2 + index) * dim : (3 + index) * dim, :], lanes)
        made = made.astype(BF)
        if index == 0:
            made = made * jnp.asarray(1.0 / math.sqrt(HEAD_DIM), BF)
        outs.append(made)
    query, keys, values = outs
    mask = upper_mask()
    heads = dim // HEAD_DIM
    mixed_all = []
    for s in range(seqs):
        span = slice(s * SEQ, (s + 1) * SEQ)
        query_o[s], keys_o[s], values_o[s] = query[:, span], keys[:, span], values[:, span]
        parts = []
        logs = []
        for h in range(heads):
            rows = slice(h * HEAD_DIM, (h + 1) * HEAD_DIM)
            near, far = head_scores(keys[rows, span], query[rows, span])
            signed_a, log_a = attend(near, mask)
            signed_b, log_b = attend(far, mask)
            v = values[rows, span]
            mixed_a = dot(v[:, :HALF], signed_a.astype(BF))
            mixed_b = dot(v, signed_b.astype(BF))
            parts.append(jnp.concatenate([mixed_a, mixed_b], axis=1))
            logs.append(jnp.concatenate([log_a, log_b], axis=1))
        mixed = jnp.concatenate(parts, axis=0).astype(BF)
        mixed_o[s] = mixed
        logsum_o[s] = jnp.concatenate(logs, axis=0)
        mixed_all.append(mixed)
    mixed = jnp.concatenate(mixed_all, axis=1)
    hidden = x + dot(wo_t[...], mixed) + wide(vec[5 * dim : 6 * dim, :], lanes)
    for s in range(seqs):
        hidden_o[s] = hidden[:, s * SEQ : (s + 1) * SEQ]


def mlp_kernel(seqs, block, *refs):
    (hid, cot, wu0, wu1, wd0, wd1, vec, bup) = refs[:8]
    (out_o, dhid_o, gup_o, gdown_o, gvec_o, gbup_o) = refs[8:14]
    wu_t, wd_t, gup, gdown = refs[14:18]
    dim = hid.shape[1]
    units = wu0.shape[1]
    lanes = seqs * SEQ
    step = pl.program_id(0)

    @pl.when(step == 0)
    def _():
        for index, (up, down) in enumerate(((wu0, wd0), (wu1, wd1))):
            wu_t[index * units : (index + 1) * units, :] = turned(up[...])
            wd_t[:, index * units : (index + 1) * units] = turned(down[...])
        gup[...] = jnp.zeros_like(gup)
        gdown[...] = jnp.zeros_like(gdown)
        gvec_o[...] = jnp.zeros_like(gvec_o)
        gbup_o[...] = jnp.zeros_like(gbup_o)

    hidden = jnp.concatenate([hid[s] for s in range(seqs)], axis=1)
    grad_out = cot[...].astype(F32).T
    grad_low = grad_out.astype(BF)
    gain = wide(vec[0:dim, :], lanes)
    plain, factor = norm_plain(hidden)
    second = (plain * gain + wide(vec[dim : 2 * dim, :], lanes)).astype(BF)
    ffout = None
    dnorm = None
    for start in range(0, 2 * units, block):
        span = slice(start, start + block)
        half, inner = divmod(start, units)
        up_ref, down_ref = ((wu0, wd0), (wu1, wd1))[half]
        inner = slice(inner, inner + block)
        upper = dot(wu_t[span, :], second) + wide(bup[span, :], lanes)
        dact = dot(down_ref[inner, :], grad_low)
        cdf = 0.5 * lax.erf(upper * (1.0 / math.sqrt(2.0))) + 0.5
        density = jnp.exp(-0.5 * (upper * upper)) * (1.0 / math.sqrt(2.0 * math.pi))
        act = (upper * cdf).astype(BF)
        dup_wide = dact * (cdf + upper * density)
        dup = dup_wide.astype(BF)
        gbup_o[span, :] += lane_fold(dup.astype(F32))
        out_part = dot(wd_t[:, span], act)
        dn_part = dot(up_ref[:, inner], dup)
        ffout = out_part if ffout is None else ffout + out_part
        dnorm = dn_part if dnorm is None else dnorm + dn_part
        gup[:, span] += tail_dot(second, dup)
        gdown[span, :] += tail_dot(act, grad_low)
    out = hidden + ffout + wide(vec[2 * dim : 3 * dim, :], lanes)
    out_o[...] = out.T.astype(BF)
    gvec_o[0:dim, :] += lane_fold(dnorm * plain)
    gvec_o[dim : 2 * dim, :] += lane_fold(dnorm)
    gvec_o[2 * dim : 3 * dim, :] += lane_fold(grad_out)
    dhidden = grad_out + norm_back(dnorm, plain, factor, gain)
    gvec_o[3 * dim : 4 * dim, :] += lane_fold(dhidden)
    for s in range(seqs):
        dhid_o[s] = dhidden[:, s * SEQ : (s + 1) * SEQ]

    @pl.when(step == pl.num_programs(0) - 1)
    def _():
        for half in range(2):
            span = slice(half * units, (half + 1) * units)
            gup_o[half] = gup[:, span].astype(BF)
            gdown_o[half] = gdown[span, :].astype(BF)


def grad_kernel(seqs, *refs):
    (tok, dhid, query_i, keys_i, values_i, mixed_i, logsum_i) = refs[:7]
    (wq0, wq1, wk0, wk1, wv0, wv1, wo0, wo1, vec) = refs[7:16]
    (tgrad_o, gqkv_o, gout_o, gvec_o) = refs[16:20]
    gqkv, gout = refs[20:22]
    dim = tok.shape[1]
    part = dim // 2
    lanes = seqs * SEQ
    step = pl.program_id(0)
    scale = 1.0 / math.sqrt(HEAD_DIM)

    @pl.when(step == 0)
    def _():
        gqkv[...] = jnp.zeros_like(gqkv)
        gout[...] = jnp.zeros_like(gout)
        gvec_o[...] = jnp.zeros_like(gvec_o)

    dhidden = jnp.concatenate([dhid[s] for s in range(seqs)], axis=1)
    dattn = dhidden.astype(BF)
    mixed = jnp.concatenate([mixed_i[s] for s in range(seqs)], axis=1)
    gout[...] += tail_dot(mixed, dattn)
    dmixed = jnp.concatenate([dot(wo0[...], dattn), dot(wo1[...], dattn)], axis=0).astype(BF)
    mask = upper_mask()
    heads = dim // HEAD_DIM
    zero = jnp.zeros((HALF, HALF), BF)
    dq_all, dk_all, dv_all = [], [], []
    for s in range(seqs):
        span = slice(s * SEQ, (s + 1) * SEQ)
        dq, dk, dv = [], [], []
        for h in range(heads):
            rows = slice(h * HEAD_DIM, (h + 1) * HEAD_DIM)
            q, k, v = query_i[s, rows, :], keys_i[s, rows, :], values_i[s, rows, :]
            dm = dmixed[rows, span]
            score_pair = head_scores(k, q)
            dsigned_pair = head_scores(v, dm)
            signed_low, dscores_low = [], []
            for index in range(2):
                scores, dsigned = score_pair[index], dsigned_pair[index]
                lse = logsum_i[s, h : h + 1, index * HALF : (index + 1) * HALF]
                inverse, root = smooth(scores)
                if index == 1:
                    diag = jnp.where(mask, root[HALF:], -1e30)
                    magnitude = jnp.concatenate([root[:HALF], diag], axis=0)
                else:
                    magnitude = jnp.where(mask, root, -1e30)
                probs = jnp.exp(magnitude - lse)
                sign = scores * inverse
                signed = sign * probs
                row_dot = jnp.sum(signed * dsigned, axis=0, keepdims=True)
                slope = inverse * inverse * inverse + sign * sign
                dscores = probs * dsigned * slope - signed * row_dot
                signed_low.append(signed.astype(BF))
                dscores_low.append(dscores.astype(BF))
            dq_a = dot(k[:, :HALF], dscores_low[0])
            dq_b = dot(k, dscores_low[1])
            dq.append(jnp.concatenate([dq_a, dq_b], axis=1))
            full = jnp.concatenate(
                [jnp.concatenate([dscores_low[0], zero], axis=0), dscores_low[1]], axis=1
            )
            dk.append(tail_dot(q, full))
            full = jnp.concatenate(
                [jnp.concatenate([signed_low[0], zero], axis=0), signed_low[1]], axis=1
            )
            dv.append(tail_dot(dm, full))
        dq_all.append((jnp.concatenate(dq, axis=0) * scale).astype(BF))
        dk_all.append(jnp.concatenate(dk, axis=0).astype(BF))
        dv_all.append(jnp.concatenate(dv, axis=0).astype(BF))
    x = tok[...].astype(F32).T
    gain = wide(vec[0:dim, :], lanes)
    plain, factor = norm_plain(x)
    first = (plain * gain + wide(vec[dim : 2 * dim, :], lanes)).astype(BF)
    dnorm = None
    weights = ((wq0, wq1), (wk0, wk1), (wv0, wv1))
    for index, group in enumerate((dq_all, dk_all, dv_all)):
        grad = jnp.concatenate(group, axis=1)
        gqkv[:, index * dim : (index + 1) * dim] += tail_dot(first, grad)
        gvec_o[(2 + index) * dim : (3 + index) * dim, :] += lane_fold(grad.astype(F32))
        for half in range(2):
            made = dot(weights[index][half][...], grad[half * part : (half + 1) * part])
            dnorm = made if dnorm is None else dnorm + made
    gvec_o[0:dim, :] += lane_fold(dnorm * plain)
    gvec_o[dim : 2 * dim, :] += lane_fold(dnorm)
    tgrad = dhidden + norm_back(dnorm, plain, factor, gain)
    tgrad_o[...] = tgrad.T.astype(BF)

    @pl.when(step == pl.num_programs(0) - 1)
    def _():
        for half in range(2):
            for index in range(3):
                start = index * dim + half * part
                gqkv_o[half, index] = gqkv[:, start : start + part].astype(BF)
            gout_o[half] = gout[half * part : (half + 1) * part, :].astype(BF)


def whole_vmem():
    return pl.BlockSpec(memory_space=pltpu.VMEM)


def seq_block(seqs, *dims):
    return pl.BlockSpec((seqs,) + dims, lambda i: (i,) + (0,) * len(dims))


def params():
    return pltpu.CompilerParams(
        dimension_semantics=("arbitrary",), vmem_limit_bytes=VMEM_LIMIT
    )


def attn_call(tokens, weights, vec, seqs):
    rows, dim = tokens.shape
    count = rows // SEQ
    heads = dim // HEAD_DIM
    feat = jax.ShapeDtypeStruct((count, dim, SEQ), BF)
    return pl.pallas_call(
        functools.partial(attn_kernel, seqs),
        grid=(count // seqs,),
        in_specs=[pl.BlockSpec((seqs * SEQ, dim), lambda i: (i, 0))] + [whole_vmem()] * 9,
        out_specs=[seq_block(seqs, dim, SEQ)] * 4
        + [seq_block(seqs, heads, SEQ), seq_block(seqs, dim, SEQ)],
        out_shape=[feat] * 4
        + [
            jax.ShapeDtypeStruct((count, heads, SEQ), F32),
            jax.ShapeDtypeStruct((count, dim, SEQ), F32),
        ],
        scratch_shapes=[pltpu.VMEM((3 * dim, dim), BF), pltpu.VMEM((dim, dim), BF)],
        compiler_params=params(),
        name="attn_forward",
    )(tokens, *weights, vec)


def mlp_call(hidden, cotangent, weights, vec, bup, seqs, block):
    rows, dim = cotangent.shape
    count = rows // SEQ
    units = weights[0].shape[1]
    return pl.pallas_call(
        functools.partial(mlp_kernel, seqs, block),
        grid=(count // seqs,),
        in_specs=[
            seq_block(seqs, dim, SEQ),
            pl.BlockSpec((seqs * SEQ, dim), lambda i: (i, 0)),
        ]
        + [whole_vmem()] * 6,
        out_specs=[
            pl.BlockSpec((seqs * SEQ, dim), lambda i: (i, 0)),
            seq_block(seqs, dim, SEQ),
        ]
        + [whole_vmem()] * 4,
        out_shape=[
            jax.ShapeDtypeStruct((rows, dim), BF),
            jax.ShapeDtypeStruct((count, dim, SEQ), F32),
            jax.ShapeDtypeStruct((2, dim, units), BF),
            jax.ShapeDtypeStruct((2, units, dim), BF),
            jax.ShapeDtypeStruct((4 * dim, LANES), F32),
            jax.ShapeDtypeStruct((2 * units, LANES), F32),
        ],
        scratch_shapes=[
            pltpu.VMEM((2 * units, dim), BF),
            pltpu.VMEM((dim, 2 * units), BF),
            pltpu.VMEM((dim, 2 * units), F32),
            pltpu.VMEM((2 * units, dim), F32),
        ],
        compiler_params=params(),
        name="feed_forward",
    )(hidden, cotangent, *weights, vec, bup)


def grad_call(tokens, dhidden, saved, weights, vec, seqs):
    rows, dim = tokens.shape
    count = rows // SEQ
    part = dim // 2
    heads = dim // HEAD_DIM
    return pl.pallas_call(
        functools.partial(grad_kernel, seqs),
        grid=(count // seqs,),
        in_specs=[pl.BlockSpec((seqs * SEQ, dim), lambda i: (i, 0))]
        + [seq_block(seqs, dim, SEQ)] * 5
        + [seq_block(seqs, heads, SEQ)]
        + [whole_vmem()] * 9,
        out_specs=[pl.BlockSpec((seqs * SEQ, dim), lambda i: (i, 0))] + [whole_vmem()] * 3,
        out_shape=[
            jax.ShapeDtypeStruct((rows, dim), BF),
            jax.ShapeDtypeStruct((2, 3, dim, part), BF),
            jax.ShapeDtypeStruct((2, part, dim), BF),
            jax.ShapeDtypeStruct((5 * dim, LANES), F32),
        ],
        scratch_shapes=[pltpu.VMEM((dim, 3 * dim), F32), pltpu.VMEM((dim, dim), F32)],
        compiler_params=params(),
        name="attn_backward",
    )(tokens, dhidden, *saved, *weights, vec)


def shifted(value, axis, count, shift):
    return lax.ppermute(value, axis, [(i, (i + shift) % count) for i in range(count)])


def gathered(value, count, axis):
    blocks = [value] + [shifted(value, "mp", count, -r) for r in range(1, count)]
    half = count // 2
    return [
        blocks[g * half] if half == 1 else jnp.concatenate(blocks[g * half : (g + 1) * half], axis)
        for g in range(2)
    ]


def added(left, right):
    return (left.astype(F32) + right.astype(F32)).astype(BF)


def halve_double(value, order):
    me = lax.axis_index("dp")
    count = lax.axis_size("dp")
    swap = lambda block, bit: lax.ppermute(block, "dp", [(i, i ^ bit) for i in range(count)])
    for bit in order:
        half = value.shape[0] // 2
        low, high = value[:half], value[half:]
        upper = (me & bit) != 0
        keep, send = jnp.where(upper, high, low), jnp.where(upper, low, high)
        value = added(keep, swap(send, bit))
    for bit in reversed(order):
        other = swap(value, bit)
        upper = (me & bit) != 0
        value = jnp.concatenate(
            [jnp.where(upper, other, value), jnp.where(upper, value, other)], axis=0
        )
    return value


def dp_sum(value, count):
    bits = [1 << b for b in range(count.bit_length() - 1)]
    rows = value.shape[0]
    unit = 16 * count
    third = -(-rows // (3 * unit)) * unit
    value = jnp.pad(value, ((0, 3 * third - rows), (0, 0)))
    parts = []
    for index in range(3):
        order = bits[index:] + bits[:index]
        parts.append(halve_double(value[index * third : (index + 1) * third], order))
    return jnp.concatenate(parts, axis=0)[:rows]


def body(mp, dp, *args):
    (tokens, gain1, shift1, wq, bq, wk, bk, wv, bv, wo, bo) = args[:11]
    (gain2, shift2, wu, bu, wd, bd, cotangent) = args[11:]
    rows, dim = tokens.shape
    local = wq.shape[1]
    units = wu.shape[1]
    own = rows // mp
    me = lax.axis_index("mp")

    weights = []
    for w in (wq, wk, wv):
        weights += gathered(w, mp, 1)
    weights += gathered(wo, mp, 0)
    mlp_weights = gathered(wu, mp, 1) + gathered(wd, mp, 0)
    small = jnp.concatenate([bq, bk, bv, bu])
    blocks = [small] + [shifted(small, "mp", mp, -r) for r in range(1, mp)]
    spread = lambda lo, hi: jnp.concatenate([b[lo:hi] for b in blocks])
    over = lambda vector: jnp.broadcast_to(vector[:, None], (vector.shape[0], LANES))
    vec1 = over(
        jnp.concatenate(
            [gain1, shift1]
            + [spread(i * local, (i + 1) * local) for i in range(3)]
            + [bo]
        )
    )
    vec2 = over(jnp.concatenate([gain2, shift2, bd]))
    bup = over(spread(3 * local, 3 * local + units))

    tok = lax.dynamic_slice_in_dim(tokens, me * own, own)
    cot = lax.dynamic_slice_in_dim(cotangent, me * own, own)
    saved = attn_call(tok, weights, vec1, 1)
    out, dhidden, gup, gdown, gvec2, gbup = mlp_call(
        saved[-1], cot, mlp_weights, vec2, bup, 1, 512
    )
    tgrad, gqkv, gout, gvec1 = grad_call(tok, dhidden, saved[:-1], weights, vec1, 1)

    def whole(part):
        full = jnp.zeros((rows, dim), BF)
        for r in range(mp):
            block = part if r == 0 else shifted(part, "mp", mp, r)
            full = lax.dynamic_update_slice_in_dim(full, block, ((me - r) % mp) * own, 0)
        return full

    gvec1 = jnp.sum(gvec1, axis=1)
    gvec2 = jnp.sum(gvec2, axis=1)
    gbup = jnp.sum(gbup, axis=1)
    same = jnp.concatenate([gvec2, gvec1[: 2 * dim]])
    per = mp // 2

    def piece(r):
        g, j = divmod(r, per)
        cols = slice(j * units, (j + 1) * units)
        lanes = slice(j * local, (j + 1) * local)
        bias = [gvec1[(2 + i) * dim + r * local : (2 + i) * dim + (r + 1) * local] for i in range(3)]
        vector = jnp.concatenate([same] + bias + [gbup[r * units : (r + 1) * units]])
        size = -(-vector.shape[0] // dim) * dim
        vector = jnp.pad(vector, (0, size - vector.shape[0])).reshape(-1, dim).astype(BF)
        qkv = [gqkv[g, i][:, lanes].reshape(-1, dim) for i in range(3)]
        return jnp.concatenate(
            [gup[g][:, cols].reshape(-1, dim), gdown[g][cols]]
            + qkv
            + [gout[g][lanes], vector],
            axis=0,
        )

    total = piece(0).astype(F32)
    for r in range(1, mp):
        total = total + shifted(piece(r), "mp", mp, r).astype(F32)
    total = dp_sum(total.astype(BF), dp).astype(F32)
    at = 0

    def take(count, shape):
        nonlocal at
        block = total[at : at + count]
        at += count
        return block.reshape(shape)

    g_up = take(units, (dim, units))
    g_down = take(units, (units, dim))
    g_qkv = [take(local, (dim, local)) for _ in range(3)]
    g_out = take(local, (local, dim))
    vector = total[at:].reshape(-1)
    g_same = [vector[i * dim : (i + 1) * dim] for i in range(6)]
    base = 6 * dim
    g_bias = [vector[base + i * local : base + (i + 1) * local] for i in range(3)]
    g_bup = vector[base + 3 * local : base + 3 * local + units]
    return (
        whole(out),
        whole(tgrad),
        g_same[4],
        g_same[5],
        g_qkv[0],
        g_bias[0],
        g_qkv[1],
        g_bias[1],
        g_qkv[2],
        g_bias[2],
        g_out,
        g_same[3],
        g_same[0],
        g_same[1],
        g_up,
        g_bup,
        g_down,
        g_same[2],
    )


def solution(mesh):
    split = P("dp", None)
    columns, some, lines = P(None, "mp"), P("mp"), P("mp", None)
    return jax.shard_map(
        functools.partial(body, mesh.shape["mp"], mesh.shape["dp"]),
        mesh=mesh,
        in_specs=(split, P(), P(), columns, some, columns, some, columns, some, lines, P())
        + (P(), P(), columns, some, lines, P(), split),
        out_specs=(split, split, P(), P(), columns, some, columns, some, columns, some, lines)
        + (P(), P(), P(), columns, some, lines, P()),
        check_vma=False,
    )
```

time: 1010 us -> 398 us (0.39); the launches traced: 994 us -> 397 us
  matrix products: 394 us -> 0 us
  Pallas kernels: 0 us -> 223 us
  other arithmetic: 196 us -> 13.1 us
  waiting for transfers between devices: 203 us -> 59 us
  local copies, waits for them, and re-layouts: 143 us -> 61 us
  blocking collectives: 43 us -> 0 us
  starting transfers between devices: 0.16 us -> 39.7 us
  between operations: 15.1 us -> 1.56 us
    dot_general x24 -> x0, matrix products: 394 us -> none  [the longest x6 81.7 us: tail_dot(): lax.dot_general(left, right, (((1,), (1,)), ((), ())), preferred_element_...]
    pallas_call x0 -> x3, Pallas kernels: none -> 223 us  [the longest x1 84.1 us: mlp_call(): pl.pallas_call(functools.partial(mlp_kernel, seqs, block), grid=(count //...]
    psum x4 -> x0, waiting for transfers between devices: 203 us -> none  [the longest x1 113 us: body(): lax.psum(for_sending(tuple(attn_terms) + tuple(mlp_terms)), 'dp')]
    reduce_sum x11 -> x3, other arithmetic: 105 us -> 3.77 us  [the longest x1 1.85 us: body(): gvec1 = jnp.sum(gvec1, axis=1)]
    reshape x8 -> x5, local copies, waits for them, and re-layouts: 101 us -> 5.33 us  [the longest x4 5.33 us: take(): return block.reshape(shape)]
    convert_element_type x20 -> x12, other arithmetic: 91.1 us -> 5.12 us  [the longest x2 3.68 us: body(): total = dp_sum(total.astype(BF), dp).astype(F32)]
    ppermute x0 -> x34, waiting for transfers between devices: none -> 59 us  [the longest x24 52.4 us: halve_double(): lax.ppermute(block, 'dp', [(i, i ^ bit) for i in range(count)])]
    psum x1 -> x0, blocking collectives: 43 us -> none  [body(): lax.psum(for_sending(tuple(attn_terms) + tuple(mlp_terms)), 'dp')]
  transfers between devices with their start and end apart: 4 -> 34, of which waited for: 3 -> 18; matrix products, arithmetic and copies ran while one was open for 10% -> 8% of each run, Pallas kernels for 0% -> 15%
where the time goes in v1:
time: 398 us; the launch traced here: 397 us
  Pallas kernels  223 us (56%)
  local copies, waits for them, and re-layouts  61 us (15%)
  waiting for transfers between devices  59 us (15%)
  starting transfers between devices  39.7 us (10%)
  other arithmetic  13.1 us (3%)
    pallas_call x1, Pallas kernels, mlp_call(): pl.pallas_call(functools.partial(mlp_kernel, seqs, block), grid=(count //...  84.1 us
    pallas_call x1, Pallas kernels, grad_call(): pl.pallas_call(functools.partial(grad_kernel, seqs), grid=(count // seqs,...  81 us
    pallas_call x1, Pallas kernels, attn_call(): pl.pallas_call(functools.partial(attn_kernel, seqs), grid=(count // seqs,...  57.8 us
    ppermute x24, waiting for transfers between devices, halve_double(): lax.ppermute(block, 'dp', [(i, i ^ bit) for i in range(count)])  52.4 us
    ppermute x24, starting transfers between devices, halve_double(): lax.ppermute(block, 'dp', [(i, i ^ bit) for i in range(count)])  36.8 us
    dynamic_update_slice x4, local copies, waits for them, and re-layouts, whole(): full = lax.dynamic_update_slice_in_dim(full, block, (me - r) % mp * own, 0)  11.8 us
    unnamed x83, local copies, waits for them, and re-layouts  10.9 us
    another operation x6, local copies, waits for them, and re-layouts, piece(): qkv = [gqkv[g, i][:, lanes].reshape(-1, dim) for i in range(3)]  8.57 us
  transfers between devices with their start and end apart: 34, of which 18 were waited for; matrix products, arithmetic and copies ran while one was open for 8% of the time, Pallas kernels for 15%

profile of v1, /device:TPU:0, one launch (start us, length us, event | category | flops | bytes accessed | tf_op | source)
XLA Modules:
  0.0 397.3 jit_solution(4447468971798394367)
XLA Ops:
  4.4 7.4 %constant_dynamic-slice_fusion = (bf16[4096,512]{1,0:T(8,128)(2,1)}, bf16[4096,512]{1,0:T(8,128)(2,1)}) fusion(bf16[8192,512]{1,0:T(8,128)(2,1)} %param.35, s32[]{:T(128)S(6)} %select_n.247, bf16[8192,512]{1,0:T(8,128)(2,1)} %param.18), kind=kLoop, calls=%fused_computation.92 | loop fusion | bytes 16777220 | tf_op jit(solution)/shard_map/dynamic_slice | solution.py:477
  12.7 2.3 collective-permute-done.3.refs_8_.refs_14_
  14.9 1.6 broadcast_in_dim.6.refs_9_.refs_15_
  16.6 57.8 %attn_forward.1 = (bf16[16,512,256]{2,1,0:T(8,128)(2,1)}, bf16[16,512,256]{2,1,0:T(8,128)(2,1)}, bf16[16,512,256]{2,1,0:T(8,128)(2,1)}, bf16[16,512,256]{2,1,0:T...) custom-call(bf16[4096,512]{1,0:T(8,128)(2,1)} %get-tuple-element.109.refs_0_, bf16[512,256]{1,0:T(8,128)(2,1)} %refs_7_.3, ...), custom_call_target="tpu_custom_call" | custom-call | tf_op jit(solution)/shard_map/attn_forward/pallas_call | solution.py:321
  74.4 1.3 broadcast_in_dim.8.refs_7_
  75.8 1.2 broadcast_in_dim.7.refs_6_
  76.9 84.1 %feed_forward.1 = (bf16[4096,512]{1,0:T(8,128)(2,1)}, f32[16,512,256]{2,1,0:T(8,128)}, bf16[2,512,1024]{2,1,0:T(8,128)(2,1)}, bf16[2,1024,512]{2,1,0:T(8,128)(2,...) custom-call(f32[16,512,256]{2,1,0:T(8,128)} %get-tuple-element.34.refs_0_, bf16[4096,512]{1,0:T(8,128)(2,1)} %get-tuple-element.108.refs_1_, ...), custom_call_target="tpu_custom_call" | custom-call | tf_op jit(solution)/shard_map/feed_forward/pallas_call | solution.py:342
  161.1 81.0 %attn_backward.1 = (bf16[4096,512]{1,0:T(8,128)(2,1)}, bf16[2,3,512,256]{3,2,1,0:T(8,128)(2,1)}, bf16[2,256,512]{2,1,0:T(8,128)(2,1)}, f32[2560,128]{1,0:T(8,128)}) custom-call(bf16[4096,512]{1,0:T(8,128)(2,1)} %get-tuple-element.109.refs_0_, f32[16,512,256]{2,1,0:T(8,128)} %get-tuple-element.36.refs_1_, bf16[16,512,256]{2,1,0:T(8,128)(2,1)} %get-tuple-element.37.refs_2_, ...), custom_call_target="tpu_custom_call" | custom-call | tf_op jit(solution)/shard_map/attn_backward/pallas_call | solution.py:379
  242.1 1.9 reduce_sum.28
  244.0 1.6 reduce_sum.27
  246.0 1.0 fusion.4
  247.0 0.8 reshape_squeeze.29
  247.8 1.7 fusion.3
  249.9 1.0 constant_dynamic-update-slice_fusion.12
  250.9 1.2 reshape_squeeze.24
  252.1 1.3 constant_dynamic-update-slice_fusion.6
  253.4 1.7 reshape_squeeze.30
  255.1 1.8 reshape_squeeze.31
  256.9 1.7 reshape_squeeze.25
  258.6 1.7 reshape_squeeze.26
  260.3 0.8 reshape_squeeze.27
  262.0 2.8 bitcast_dynamic-update-slice_fusion.1
  270.2 4.3 %collective-permute-done.9 = bf16[3082,512]{1,0:T(8,128)(2,1)} collective-permute-done((bf16[3082,512]{1,0:T(8,128)(2,1)}, bf16[3082,512]{1,0:T(8,128)(2,1)}, u32[]{:S(2)}, u32[]{:S(2)}) %collective-permute-start.9) | collective-permute-done | bytes 3156000 | tf_op jit(solution)/shard_map/ppermute | solution.py:400
  274.5 2.8 add_convert_fusion
  277.3 1.6 broadcast_select_fusion
  278.8 2.6 collective-permute-start.10
  281.5 1.5 collective-permute-start.18
  283.0 1.6 collective-permute-start.26
  286.3 2.8 constant_dynamic-update-slice_fusion.25
  289.1 7.9 %collective-permute-done.10 = bf16[640,512]{1,0:T(8,128)(2,1)S(1)} collective-permute-done((bf16[640,512]{1,0:T(8,128)(2,1)}, bf16[640,512]{1,0:T(8,128)(2,1)S(1)}, u32[]{:S(2)}, u32[]{:S(2)}) %collective-permute-start.10) | collective-permute-done | bytes 655392 | tf_op jit(solution)/shard_map/ppermute | solution.py:419
  296.9 1.5 collective-permute-done.18
  298.4 1.0 collective-permute-done.26
  299.4 0.8 add_convert_fusion.1
  300.3 2.6 collective-permute-start.27
  302.9 1.6 collective-permute-start.19
  305.2 11.7 %collective-permute-done.27 = bf16[320,512]{1,0:T(8,128)(2,1)S(1)} collective-permute-done((bf16[320,512]{1,0:T(8,128)(2,1)S(1)}, bf16[320,512]{1,0:T(8,128)(2,1)S(1)}, u32[]{:S(2)}, u32[]{:S(2)}) %collective-permute-start.27) | collective-permute-done | bytes 327712 | tf_op jit(solution)/shard_map/ppermute | solution.py:419
  317.8 0.8 collective-permute-start.20
  318.8 3.3 collective-permute-start.12
  322.0 2.7 constant_dynamic-update-slice_fusion.22
  324.8 5.8 %constant_dynamic-update-slice_fusion.24 = bf16[8192,512]{1,0:T(8,128)(2,1)S(1)} fusion(bf16[8192,512]{1,0:T(8,128)(2,1)S(1)} %constant_dynamic-update-slice_fusion.25, bf16[4096,512]{1,0:T(8,128)(2,1)} %collective-permute-done.7, s32[]{:T(128)S(6)} %select_n.251), kind=kLoop, calls=%fused_computation.90 | loop fusion | bytes 8388612 | tf_op jit(solution)/shard_map/dynamic_update_slice | solution.py:488
  330.7 0.9 collective-permute-start.29
  331.7 1.5 collective-permute-start.21
  333.4 1.8 collective-permute-done.29
  335.2 0.9 collective-permute-start.30
  336.3 1.5 collective-permute-start.22
  337.7 1.3 collective-permute-done.13
  339.8 1.5 collective-permute-start.31
  341.7 1.2 collective-permute-start.23
  342.9 3.5 collective-permute-done.14
  346.6 3.6 collective-permute-start.32
  350.2 3.4 collective-permute-done.15
  353.6 9.3 %collective-permute-start.16 = (bf16[320,512]{1,0:T(8,128)(2,1)S(1)}, bf16[320,512]{1,0:T(8,128)(2,1)S(1)}, u32[]{:S(2)}, u32[]{:S(2)}) collective-permute-start(bf16[320,512]{1,0:T(8,128)(2,1)S(1)} %pad_maximum_fusion.3), channel_id=1, source_target_pairs={{0,2},{1,3},{2,0},{3,1},{4,6},{5,7},{6,4},{7,5},{8,10},{9,11},{10,... | collective-permute-start | bytes 983048 | tf_op jit(solution)/shard_map/ppermute | solution.py:419
  363.1 4.9 %collective-permute-done.16 = bf16[320,512]{1,0:T(8,128)(2,1)S(1)} collective-permute-done((bf16[320,512]{1,0:T(8,128)(2,1)S(1)}, bf16[320,512]{1,0:T(8,128)(2,1)S(1)}, u32[]{:S(2)}, u32[]{:S(2)}) %collective-permute-start.16) | collective-permute-done | bytes 327712 | tf_op jit(solution)/shard_map/ppermute | solution.py:419
  368.2 1.9 collective-permute-done.24
  371.2 7.6 %collective-permute-done.17 = bf16[640,512]{1,0:T(8,128)(2,1)S(1)} collective-permute-done((bf16[640,512]{1,0:T(8,128)(2,1)S(1)}, bf16[640,512]{1,0:T(8,128)(2,1)S(1)}, u32[]{:S(2)}, u32[]{:S(2)}) %collective-permute-start.17) | collective-permute-done | bytes 655392 | tf_op jit(solution)/shard_map/ppermute | solution.py:419
  379.1 4.4 %collective-permute-done.25 = bf16[640,512]{1,0:T(8,128)(2,1)S(1)} collective-permute-done((bf16[640,512]{1,0:T(8,128)(2,1)S(1)}, bf16[640,512]{1,0:T(8,128)(2,1)S(1)}, u32[]{:S(2)}, u32[]{:S(2)}) %collective-permute-start.25) | collective-permute-done | bytes 655392 | tf_op jit(solution)/shard_map/ppermute | solution.py:419
  384.7 0.9 slice_convert_fusion
  385.6 2.1 fusion.1
  387.7 1.6 fusion.2
  390.5 1.5 fusion
  392.0 1.7 reshape.68
  393.7 1.9 reshape.64
  395.6 0.9 reshape.66
  396.5 0.9 reshape.67
  (186 shorter events, 20.5 us)
Async XLA Ops:
  1.4 10.4 %collective-permute-start.4 = (f32[1792]{0:T(1024)S(1)}, f32[1792]{0:T(1024)S(1)}, u32[]{:S(2)}, u32[]{:S(2)}) collective-permute-start(f32[1792]{0:T(1024)S(1)} %pad_maximum_fusion.9), channel_id=1, source_target_pairs={{0,16},{16,0},{1,17},{17,1},{2,18},{18,2},{3,19},{19,3},{4,20},{20... | collective-permute-start | bytes 21512 | tf_op jit(solution)/shard_map/ppermute | solution.py:400
  1.9 10.1 %collective-permute-start = (bf16[512,256]{1,0:T(8,128)(2,1)}, bf16[512,256]{1,0:T(8,128)(2,1)S(1)}, u32[]{:S(2)}, u32[]{:S(2)}) collective-permute-start(bf16[512,256]{1,0:T(8,128)(2,1)} %refs_7_.3), channel_id=1, source_target_pairs={{0,16},{16,0},{1,17},{17,1},{2,18},{18,2},{3,19},{19,3},{4,20},{20... | collective-permute-start | bytes 786440 | tf_op jit(solution)/shard_map/ppermute | solution.py:400
  2.0 10.7 %collective-permute-start.1 = (bf16[512,256]{1,0:T(8,128)(2,1)}, bf16[512,256]{1,0:T(8,128)(2,1)S(1)}, u32[]{:S(2)}, u32[]{:S(2)}) collective-permute-start(bf16[512,256]{1,0:T(8,128)(2,1)} %refs_9_.1), channel_id=1, source_target_pairs={{0,16},{16,0},{1,17},{17,1},{2,18},{18,2},{3,19},{19,3},{4,20},{20... | collective-permute-start | bytes 786440 | tf_op jit(solution)/shard_map/ppermute | solution.py:400
  2.4 10.2 %collective-permute-start.2 = (bf16[512,256]{1,0:T(8,128)(2,1)}, bf16[512,256]{1,0:T(8,128)(2,1)S(1)}, u32[]{:S(2)}, u32[]{:S(2)}) collective-permute-start(bf16[512,256]{1,0:T(8,128)(2,1)} %refs_11_.1), channel_id=1, source_target_pairs={{0,16},{16,0},{1,17},{17,1},{2,18},{18,2},{3,19},{19,3},{4,20},{20... | collective-permute-start | bytes 786440 | tf_op jit(solution)/shard_map/ppermute | solution.py:400
  2.5 71.9 %collective-permute-start.5 = (bf16[512,1024]{1,0:T(8,128)(2,1)}, bf16[512,1024]{1,0:T(8,128)(2,1)S(1)}, u32[]{:S(2)}, u32[]{:S(2)}) collective-permute-start(bf16[512,1024]{1,0:T(8,128)(2,1)} %refs_2_.1), channel_id=1, source_target_pairs={{0,16},{16,0},{1,17},{17,1},{2,18},{18,2},{3,19},{19,3},{4,20},{20... | collective-permute-start | bytes 3145736 | tf_op jit(solution)/shard_map/ppermute | solution.py:400
  4.3 7.5 %copy-start.24 = (f32[512]{0:T(512)S(1)}, f32[512]{0:T(512)}, u32[]{:S(2)}) copy-start(f32[512]{0:T(512)} %param.34) | copy-start | bytes 6148
  4.3 7.5 %copy-start.25 = (f32[512]{0:T(512)S(1)}, f32[512]{0:T(512)}, u32[]{:S(2)}) copy-start(f32[512]{0:T(512)} %param.30) | copy-start | bytes 6148
  4.3 7.5 %copy-start.26 = (f32[512]{0:T(512)S(1)}, f32[512]{0:T(512)}, u32[]{:S(2)}) copy-start(f32[512]{0:T(512)} %param.29) | copy-start | bytes 6148
  4.3 7.5 %copy-start.21 = (f32[256]{0:T(256)S(1)}, f32[256]{0:T(256)}, u32[]{:S(2)}) copy-start(f32[256]{0:T(256)} %param.22) | copy-start | bytes 3076
  4.3 7.5 %copy-start.10 = (bf16[1024,512]{1,0:T(8,128)(2,1)S(1)}, bf16[1024,512]{1,0:T(8,128)(2,1)}, u32[]{:S(2)}) copy-start(bf16[1024,512]{1,0:T(8,128)(2,1)} %refs_4_.1) | copy-start | bytes 3145732
  4.3 7.7 %copy-start.22 = (f32[256]{0:T(256)S(1)}, f32[256]{0:T(256)}, u32[]{:S(2)}) copy-start(f32[256]{0:T(256)} %param.24) | copy-start | bytes 3076
  4.3 7.7 %copy-start.23 = (f32[256]{0:T(256)S(1)}, f32[256]{0:T(256)}, u32[]{:S(2)}) copy-start(f32[256]{0:T(256)} %param.26) | copy-start | bytes 3076
  4.3 7.7 %copy-start.5 = (bf16[256,512]{1,0:T(8,128)(2,1)S(1)}, bf16[256,512]{1,0:T(8,128)(2,1)}, u32[]{:S(2)}) copy-start(bf16[256,512]{1,0:T(8,128)(2,1)} %refs_13_.1) | copy-start | bytes 786436
  4.4 8.2 %copy-start.27 = (f32[512]{0:T(512)S(1)}, f32[512]{0:T(512)}, u32[]{:S(2)}) copy-start(f32[512]{0:T(512)} %param.28) | copy-start | bytes 6148
  4.4 8.2 %copy-start.20 = (f32[1024]{0:T(1024)S(1)}, f32[1024]{0:T(1024)}, u32[]{:S(2)}) copy-start(f32[1024]{0:T(1024)} %param.32) | copy-start | bytes 12292
  11.8 62.6 %collective-permute-start.6 = (bf16[1024,512]{1,0:T(8,128)(2,1)S(1)}, bf16[1024,512]{1,0:T(8,128)(2,1)}, u32[]{:S(2)}, u32[]{:S(2)}) collective-permute-start(bf16[1024,512]{1,0:T(8,128)(2,1)S(1)} %copy-done.10), channel_id=1, source_target_pairs={{0,16},{16,0},{1,17},{17,1},{2,18},{18,2},{3,19},{19,3},{4,20},{20... | collective-permute-start | bytes 3145736 | tf_op jit(solution)/shard_map/ppermute | solution.py:400
  12.1 4.5 %copy-start.6 = (bf16[512,256]{1,0:T(8,128)(2,1)}, bf16[512,256]{1,0:T(8,128)(2,1)S(1)}, u32[]{:S(2)}) copy-start(bf16[512,256]{1,0:T(8,128)(2,1)S(1)} %collective-permute-done.refs_2_.refs_8_) | copy-start | bytes 786436
  12.1 2.9 collective-permute-start.3
  12.6 3.9 copy-start.7
  12.7 3.9 copy-start.8
  14.9 1.6 copy-start.9
  74.4 2.5 copy-start.11
  161.1 84.5 %copy-start.12 = (f32[2048,128]{1,0:T(8,128)S(1)}, f32[2048,128]{1,0:T(8,128)}, u32[]{:S(2)}) copy-start(f32[2048,128]{1,0:T(8,128)} %get-tuple-element.49) | copy-start | bytes 3145732
  242.1 3.9 copy-start.4
  261.1 3.7 copy-start.13
  262.0 3.6 copy-start.18
  262.0 4.3 %copy-start.17 = (bf16[256,512]{1,0:T(8,128)(2,1)S(1)}, bf16[256,512]{1,0:T(8,128)(2,1)}, u32[]{:S(2)}) copy-start(bf16[256,512]{1,0:T(8,128)(2,1)} %reshape_squeeze.31) | copy-start | bytes 786436
  262.0 5.0 %copy-start.16 = (bf16[256,512]{1,0:T(8,128)(2,1)S(1)}, bf16[256,512]{1,0:T(8,128)(2,1)}, u32[]{:S(2)}) copy-start(bf16[256,512]{1,0:T(8,128)(2,1)} %reshape_squeeze.25) | copy-start | bytes 786436
  262.0 5.0 %copy-start.14 = (bf16[256,512]{1,0:T(8,128)(2,1)S(1)}, bf16[256,512]{1,0:T(8,128)(2,1)}, u32[]{:S(2)}) copy-start(bf16[256,512]{1,0:T(8,128)(2,1)} %reshape_squeeze.26) | copy-start | bytes 786436
  262.0 5.0 %copy-start.15 = (bf16[256,512]{1,0:T(8,128)(2,1)S(1)}, bf16[256,512]{1,0:T(8,128)(2,1)}, u32[]{:S(2)}) copy-start(bf16[256,512]{1,0:T(8,128)(2,1)} %reshape_squeeze.27) | copy-start | bytes 786436
  262.0 5.1 %copy-start.19 = (bf16[2,256,512]{2,1,0:T(8,128)(2,1)S(1)}, bf16[2,256,512]{2,1,0:T(8,128)(2,1)}, u32[]{:S(2)}) copy-start(bf16[2,256,512]{2,1,0:T(8,128)(2,1)} %get-tuple-element.46) | copy-start | bytes 1572868
  268.4 6.0 %collective-permute-start.9 = (bf16[3082,512]{1,0:T(8,128)(2,1)}, bf16[3082,512]{1,0:T(8,128)(2,1)}, u32[]{:S(2)}, u32[]{:S(2)}) collective-permute-start(bf16[3082,512]{1,0:T(8,128)(2,1)} %constant_dynamic-update-slice_fusion.8), channel_id=1, source_target_pairs={{0,16},{16,0},{1,17},{17,1},{2,18},{18,2},{3,19},{19,3},{4,20},{20... | collective-permute-start | bytes 9467912 | tf_op jit(solution)/shard_map/ppermute | solution.py:400
  269.6 52.4 %collective-permute-start.8 = (bf16[4096,512]{1,0:T(8,128)(2,1)}, bf16[4096,512]{1,0:T(8,128)(2,1)}, u32[]{:S(2)}, u32[]{:S(2)}) collective-permute-start(bf16[4096,512]{1,0:T(8,128)(2,1)} %get-tuple-element.42), channel_id=1, source_target_pairs={{0,16},{16,0},{1,17},{17,1},{2,18},{18,2},{3,19},{19,3},{4,20},{20... | collective-permute-start | bytes 12582920 | tf_op jit(solution)/shard_map/ppermute | solution.py:400
  270.0 54.8 %collective-permute-start.7 = (bf16[4096,512]{1,0:T(8,128)(2,1)}, bf16[4096,512]{1,0:T(8,128)(2,1)}, u32[]{:S(2)}, u32[]{:S(2)}) collective-permute-start(bf16[4096,512]{1,0:T(8,128)(2,1)} %get-tuple-element.35), channel_id=1, source_target_pairs={{0,16},{16,0},{1,17},{17,1},{2,18},{18,2},{3,19},{19,3},{4,20},{20... | collective-permute-start | bytes 12582920 | tf_op jit(solution)/shard_map/ppermute | solution.py:400
  278.8 18.1 %collective-permute-start.10 = (bf16[640,512]{1,0:T(8,128)(2,1)}, bf16[640,512]{1,0:T(8,128)(2,1)S(1)}, u32[]{:S(2)}, u32[]{:S(2)}) collective-permute-start(bf16[640,512]{1,0:T(8,128)(2,1)} %get-tuple-element.67), channel_id=1, source_target_pairs={{0,1},{1,0},{2,3},{3,2},{4,5},{5,4},{6,7},{7,6},{8,9},{9,8},{10,11... | collective-permute-start | bytes 1966088 | tf_op jit(solution)/shard_map/ppermute | solution.py:419
  281.5 16.9 %collective-permute-start.18 = (bf16[640,512]{1,0:T(8,128)(2,1)}, bf16[640,512]{1,0:T(8,128)(2,1)S(1)}, u32[]{:S(2)}, u32[]{:S(2)}) collective-permute-start(bf16[640,512]{1,0:T(8,128)(2,1)} %get-tuple-element.66), channel_id=1, source_target_pairs={{0,2},{1,3},{2,0},{3,1},{4,6},{5,7},{6,4},{7,5},{8,10},{9,11},{10,... | collective-permute-start | bytes 1966088 | tf_op jit(solution)/shard_map/ppermute | solution.py:419
  283.0 2.2 copy-start.3
  283.0 16.4 %collective-permute-start.26 = (bf16[640,512]{1,0:T(8,128)(2,1)S(1)}, bf16[640,512]{1,0:T(8,128)(2,1)S(1)}, u32[]{:S(2)}, u32[]{:S(2)}) collective-permute-start(bf16[640,512]{1,0:T(8,128)(2,1)S(1)} %get-tuple-element.65), channel_id=1, source_target_pairs={{0,4},{1,5},{2,6},{3,7},{4,0},{5,1},{6,2},{7,3},{8,12},{9,13},{10,... | collective-permute-start | bytes 1966088 | tf_op jit(solution)/shard_map/ppermute | solution.py:419
  300.3 16.6 %collective-permute-start.27 = (bf16[320,512]{1,0:T(8,128)(2,1)S(1)}, bf16[320,512]{1,0:T(8,128)(2,1)S(1)}, u32[]{:S(2)}, u32[]{:S(2)}) collective-permute-start(bf16[320,512]{1,0:T(8,128)(2,1)S(1)} %broadcast_select_fusion.5), channel_id=1, source_target_pairs={{0,8},{1,9},{2,10},{3,11},{4,12},{5,13},{6,14},{7,15},{8,0},{9,1},... | collective-permute-start | bytes 983048 | tf_op jit(solution)/shard_map/ppermute | solution.py:419
  302.9 14.7 %collective-permute-start.19 = (bf16[320,512]{1,0:T(8,128)(2,1)S(1)}, bf16[320,512]{1,0:T(8,128)(2,1)S(1)}, u32[]{:S(2)}, u32[]{:S(2)}) collective-permute-start(bf16[320,512]{1,0:T(8,128)(2,1)S(1)} %broadcast_select_fusion.8), channel_id=1, source_target_pairs={{0,4},{1,5},{2,6},{3,7},{4,0},{5,1},{6,2},{7,3},{8,12},{9,13},{10,... | collective-permute-start | bytes 983048 | tf_op jit(solution)/shard_map/ppermute | solution.py:419
  304.6 14.0 %collective-permute-start.11 = (bf16[320,512]{1,0:T(8,128)(2,1)S(1)}, bf16[320,512]{1,0:T(8,128)(2,1)S(1)}, u32[]{:S(2)}, u32[]{:S(2)}) collective-permute-start(bf16[320,512]{1,0:T(8,128)(2,1)S(1)} %broadcast_select_fusion.11), channel_id=1, source_target_pairs={{0,2},{1,3},{2,0},{3,1},{4,6},{5,7},{6,4},{7,5},{8,10},{9,11},{10,... | collective-permute-start | bytes 983048 | tf_op jit(solution)/shard_map/ppermute | solution.py:419
  317.0 13.6 %collective-permute-start.28 = (bf16[160,512]{1,0:T(8,128)(2,1)S(1)}, bf16[160,512]{1,0:T(8,128)(2,1)S(1)}, u32[]{:S(2)}, u32[]{:S(2)}) collective-permute-start(bf16[160,512]{1,0:T(8,128)(2,1)S(1)} %broadcast_select_fusion.14), channel_id=1, source_target_pairs={{0,1},{1,0},{2,3},{3,2},{4,5},{5,4},{6,7},{7,6},{8,9},{9,8},{10,11... | collective-permute-start | bytes 491528 | tf_op jit(solution)/shard_map/ppermute | solution.py:419
  317.8 13.8 %collective-permute-start.20 = (bf16[160,512]{1,0:T(8,128)(2,1)S(1)}, bf16[160,512]{1,0:T(8,128)(2,1)S(1)}, u32[]{:S(2)}, u32[]{:S(2)}) collective-permute-start(bf16[160,512]{1,0:T(8,128)(2,1)S(1)} %broadcast_select_fusion.17), channel_id=1, source_target_pairs={{0,8},{1,9},{2,10},{3,11},{4,12},{5,13},{6,14},{7,15},{8,0},{9,1},... | collective-permute-start | bytes 491528 | tf_op jit(solution)/shard_map/ppermute | solution.py:419
  318.8 14.4 %collective-permute-start.12 = (bf16[160,512]{1,0:T(8,128)(2,1)S(1)}, bf16[160,512]{1,0:T(8,128)(2,1)S(1)}, u32[]{:S(2)}, u32[]{:S(2)}) collective-permute-start(bf16[160,512]{1,0:T(8,128)(2,1)S(1)} %broadcast_select_fusion.20), channel_id=1, source_target_pairs={{0,4},{1,5},{2,6},{3,7},{4,0},{5,1},{6,2},{7,3},{8,12},{9,13},{10,... | collective-permute-start | bytes 491528 | tf_op jit(solution)/shard_map/ppermute | solution.py:419
  324.8 5.8 %copy-start.2 = (bf16[8192,512]{1,0:T(8,128)(2,1)}, bf16[8192,512]{1,0:T(8,128)(2,1)S(1)}, u32[]{:S(2)}) copy-start(bf16[8192,512]{1,0:T(8,128)(2,1)S(1)} %constant_dynamic-update-slice_fusion.22) | copy-start | bytes 25165828
  330.6 48.4 %copy-start.1 = (bf16[8192,512]{1,0:T(8,128)(2,1)}, bf16[8192,512]{1,0:T(8,128)(2,1)S(1)}, u32[]{:S(2)}) copy-start(bf16[8192,512]{1,0:T(8,128)(2,1)S(1)} %constant_dynamic-update-slice_fusion.24) | copy-start | bytes 25165828
  330.7 4.5 %collective-permute-start.29 = (bf16[80,512]{1,0:T(8,128)(2,1)S(1)}, bf16[80,512]{1,0:T(8,128)(2,1)S(1)}, u32[]{:S(2)}, u32[]{:S(2)}) collective-permute-start(bf16[80,512]{1,0:T(8,128)(2,1)S(1)} %broadcast_select_fusion.23), channel_id=1, source_target_pairs={{0,2},{1,3},{2,0},{3,1},{4,6},{5,7},{6,4},{7,5},{8,10},{9,11},{10,... | collective-permute-start | bytes 245768 | tf_op jit(solution)/shard_map/ppermute | solution.py:419
  331.7 4.5 %collective-permute-start.21 = (bf16[80,512]{1,0:T(8,128)(2,1)S(1)}, bf16[80,512]{1,0:T(8,128)(2,1)S(1)}, u32[]{:S(2)}, u32[]{:S(2)}) collective-permute-start(bf16[80,512]{1,0:T(8,128)(2,1)S(1)} %broadcast_select_fusion.26), channel_id=1, source_target_pairs={{0,1},{1,0},{2,3},{3,2},{4,5},{5,4},{6,7},{7,6},{8,9},{9,8},{10,11... | collective-permute-start | bytes 245768 | tf_op jit(solution)/shard_map/ppermute | solution.py:419
  333.3 5.7 %collective-permute-start.13 = (bf16[80,512]{1,0:T(8,128)(2,1)S(1)}, bf16[80,512]{1,0:T(8,128)(2,1)S(1)}, u32[]{:S(2)}, u32[]{:S(2)}) collective-permute-start(bf16[80,512]{1,0:T(8,128)(2,1)S(1)} %broadcast_select_fusion.29), channel_id=1, source_target_pairs={{0,8},{1,9},{2,10},{3,11},{4,12},{5,13},{6,14},{7,15},{8,0},{9,1},... | collective-permute-start | bytes 245768 | tf_op jit(solution)/shard_map/ppermute | solution.py:419
  335.2 4.5 %collective-permute-start.30 = (bf16[80,512]{1,0:T(8,128)(2,1)S(1)}, bf16[80,512]{1,0:T(8,128)(2,1)S(1)}, u32[]{:S(2)}, u32[]{:S(2)}) collective-permute-start(bf16[80,512]{1,0:T(8,128)(2,1)S(1)} %add_convert_fusion.10), channel_id=1, source_target_pairs={{0,2},{1,3},{2,0},{3,1},{4,6},{5,7},{6,4},{7,5},{8,10},{9,11},{10,... | collective-permute-start | bytes 245768 | tf_op jit(solution)/shard_map/ppermute | solution.py:419
  336.3 5.4 %collective-permute-start.22 = (bf16[80,512]{1,0:T(8,128)(2,1)S(1)}, bf16[80,512]{1,0:T(8,128)(2,1)S(1)}, u32[]{:S(2)}, u32[]{:S(2)}) collective-permute-start(bf16[80,512]{1,0:T(8,128)(2,1)S(1)} %add_convert_fusion.11), channel_id=1, source_target_pairs={{0,1},{1,0},{2,3},{3,2},{4,5},{5,4},{6,7},{7,6},{8,9},{9,8},{10,11... | collective-permute-start | bytes 245768 | tf_op jit(solution)/shard_map/ppermute | solution.py:419
  339.1 7.3 %collective-permute-start.14 = (bf16[80,512]{1,0:T(8,128)(2,1)S(1)}, bf16[80,512]{1,0:T(8,128)(2,1)S(1)}, u32[]{:S(2)}, u32[]{:S(2)}) collective-permute-start(bf16[80,512]{1,0:T(8,128)(2,1)S(1)} %add_convert_fusion.12), channel_id=1, source_target_pairs={{0,8},{1,9},{2,10},{3,11},{4,12},{5,13},{6,14},{7,15},{8,0},{9,1},... | collective-permute-start | bytes 245768 | tf_op jit(solution)/shard_map/ppermute | solution.py:419
  339.8 6.7 %collective-permute-start.31 = (bf16[160,512]{1,0:T(8,128)(2,1)S(1)}, bf16[160,512]{1,0:T(8,128)(2,1)S(1)}, u32[]{:S(2)}, u32[]{:S(2)}) collective-permute-start(bf16[160,512]{1,0:T(8,128)(2,1)S(1)} %pad_maximum_fusion.8), channel_id=1, source_target_pairs={{0,1},{1,0},{2,3},{3,2},{4,5},{5,4},{6,7},{7,6},{8,9},{9,8},{10,11... | collective-permute-start | bytes 491528 | tf_op jit(solution)/shard_map/ppermute | solution.py:419
  341.7 21.2 %collective-permute-start.23 = (bf16[160,512]{1,0:T(8,128)(2,1)S(1)}, bf16[160,512]{1,0:T(8,128)(2,1)S(1)}, u32[]{:S(2)}, u32[]{:S(2)}) collective-permute-start(bf16[160,512]{1,0:T(8,128)(2,1)S(1)} %pad_maximum_fusion.7), channel_id=1, source_target_pairs={{0,8},{1,9},{2,10},{3,11},{4,12},{5,13},{6,14},{7,15},{8,0},{9,1},... | collective-permute-start | bytes 491528 | tf_op jit(solution)/shard_map/ppermute | solution.py:419
  346.4 7.1 %collective-permute-start.15 = (bf16[160,512]{1,0:T(8,128)(2,1)S(1)}, bf16[160,512]{1,0:T(8,128)(2,1)S(1)}, u32[]{:S(2)}, u32[]{:S(2)}) collective-permute-start(bf16[160,512]{1,0:T(8,128)(2,1)S(1)} %pad_maximum_fusion.6), channel_id=1, source_target_pairs={{0,4},{1,5},{2,6},{3,7},{4,0},{5,1},{6,2},{7,3},{8,12},{9,13},{10,... | collective-permute-start | bytes 491528 | tf_op jit(solution)/shard_map/ppermute | solution.py:419
  346.6 24.3 %collective-permute-start.32 = (bf16[320,512]{1,0:T(8,128)(2,1)S(1)}, bf16[320,512]{1,0:T(8,128)(2,1)S(1)}, u32[]{:S(2)}, u32[]{:S(2)}) collective-permute-start(bf16[320,512]{1,0:T(8,128)(2,1)S(1)} %pad_maximum_fusion.5), channel_id=1, source_target_pairs={{0,8},{1,9},{2,10},{3,11},{4,12},{5,13},{6,14},{7,15},{8,0},{9,1},... | collective-permute-start | bytes 983048 | tf_op jit(solution)/shard_map/ppermute | solution.py:419
  353.6 14.3 %collective-permute-start.16 = (bf16[320,512]{1,0:T(8,128)(2,1)S(1)}, bf16[320,512]{1,0:T(8,128)(2,1)S(1)}, u32[]{:S(2)}, u32[]{:S(2)}) collective-permute-start(bf16[320,512]{1,0:T(8,128)(2,1)S(1)} %pad_maximum_fusion.3), channel_id=1, source_target_pairs={{0,2},{1,3},{2,0},{3,1},{4,6},{5,7},{6,4},{7,5},{8,10},{9,11},{10,... | collective-permute-start | bytes 983048 | tf_op jit(solution)/shard_map/ppermute | solution.py:419
  363.0 7.1 %collective-permute-start.24 = (bf16[320,512]{1,0:T(8,128)(2,1)S(1)}, bf16[320,512]{1,0:T(8,128)(2,1)S(1)}, u32[]{:S(2)}, u32[]{:S(2)}) collective-permute-start(bf16[320,512]{1,0:T(8,128)(2,1)S(1)} %pad_maximum_fusion.4), channel_id=1, source_target_pairs={{0,4},{1,5},{2,6},{3,7},{4,0},{5,1},{6,2},{7,3},{8,12},{9,13},{10,... | collective-permute-start | bytes 983048 | tf_op jit(solution)/shard_map/ppermute | solution.py:419
  368.1 10.7 %collective-permute-start.17 = (bf16[640,512]{1,0:T(8,128)(2,1)S(1)}, bf16[640,512]{1,0:T(8,128)(2,1)S(1)}, u32[]{:S(2)}, u32[]{:S(2)}) collective-permute-start(bf16[640,512]{1,0:T(8,128)(2,1)S(1)} %pad_maximum_fusion), channel_id=1, source_target_pairs={{0,1},{1,0},{2,3},{3,2},{4,5},{5,4},{6,7},{7,6},{8,9},{9,8},{10,11... | collective-permute-start | bytes 1966088 | tf_op jit(solution)/shard_map/ppermute | solution.py:419
  370.3 13.3 %collective-permute-start.25 = (bf16[640,512]{1,0:T(8,128)(2,1)S(1)}, bf16[640,512]{1,0:T(8,128)(2,1)S(1)}, u32[]{:S(2)}, u32[]{:S(2)}) collective-permute-start(bf16[640,512]{1,0:T(8,128)(2,1)S(1)} %pad_maximum_fusion.1), channel_id=1, source_target_pairs={{0,2},{1,3},{2,0},{3,1},{4,6},{5,7},{6,4},{7,5},{8,10},{9,11},{10,... | collective-permute-start | bytes 1966088 | tf_op jit(solution)/shard_map/ppermute | solution.py:419
  371.1 13.5 %collective-permute-start.33 = (bf16[640,512]{1,0:T(8,128)(2,1)S(1)}, bf16[640,512]{1,0:T(8,128)(2,1)S(1)}, u32[]{:S(2)}, u32[]{:S(2)}) collective-permute-start(bf16[640,512]{1,0:T(8,128)(2,1)S(1)} %pad_maximum_fusion.2), channel_id=1, source_target_pairs={{0,4},{1,5},{2,6},{3,7},{4,0},{5,1},{6,2},{7,3},{8,12},{9,13},{10,... | collective-permute-start | bytes 1966088 | tf_op jit(solution)/shard_map/ppermute | solution.py:419
  385.6 3.7 copy-start

commit v2 on v1

v2 whole, which is shorter than its diff:
```python
import functools
import math

import jax
import jax.numpy as jnp
from jax import lax
from jax.experimental import pallas as pl
from jax.experimental.pallas import tpu as pltpu
from jax.sharding import PartitionSpec as P

HEAD_DIM = 64
SEQ = 256
HALF = SEQ // 2
LANES = 128
BF = jnp.bfloat16
F32 = jnp.float32
VMEM_LIMIT = 60 * 1024 * 1024


def dot(left, right):
    return jnp.dot(left, right, preferred_element_type=F32)


def tail_dot(left, right):
    return lax.dot_general(left, right, (((1,), (1,)), ((), ())), preferred_element_type=F32)


def turned(block):
    return block.astype(F32).T.astype(BF)


def wide(column, lanes):
    return jnp.concatenate([column] * (lanes // LANES), axis=1)


def lane_fold(rows):
    total = rows[:, :LANES]
    for start in range(LANES, rows.shape[1], LANES):
        total = total + rows[:, start : start + LANES]
    return total


def as_row(sums):
    return jnp.sum(sums.T, axis=0, keepdims=True)


def norm_plain(x):
    center = x - jnp.mean(x, axis=0, keepdims=True)
    factor = lax.rsqrt(jnp.mean(center * center, axis=0, keepdims=True) + 1e-05)
    return center * factor, factor


def norm_back(grad, plain, factor, gain):
    scaled = grad * gain
    return factor * (
        scaled
        - jnp.mean(scaled, axis=0, keepdims=True)
        - plain * jnp.mean(scaled * plain, axis=0, keepdims=True)
    )


def upper_mask():
    return lax.broadcasted_iota(jnp.int32, (HALF, HALF), 0) <= lax.broadcasted_iota(
        jnp.int32, (HALF, HALF), 1
    )


def smooth(scores):
    square = scores * scores + 1.0
    inverse = lax.rsqrt(square)
    return inverse, square * inverse


def pair_diag(left, right):
    zero = jnp.zeros_like(left)
    return jnp.concatenate(
        [jnp.concatenate([left, zero], axis=1), jnp.concatenate([zero, right], axis=1)], axis=0
    )


def pair_near_far(rows):
    left, right = rows[:HEAD_DIM], rows[HEAD_DIM:]
    return (
        pair_diag(left[:, :HALF], right[:, :HALF]),
        pair_diag(left[:, HALF:], right[:, HALF:]),
    )


def attend(scores, mask):
    inverse, root = smooth(scores)
    if scores.shape[0] > HALF:
        diagonal = jnp.where(mask, root[HALF:], -1e30)
        magnitude = jnp.concatenate([root[:HALF], diagonal], axis=0)
    else:
        magnitude = jnp.where(mask, root, -1e30)
    top = jnp.max(magnitude, axis=0, keepdims=True)
    expo = jnp.exp(magnitude - top)
    probs = expo * (1.0 / jnp.sum(expo, axis=0, keepdims=True))
    sign = scores * inverse
    slope = inverse * inverse * inverse + sign * sign
    return (sign * probs).astype(BF), (probs * slope).astype(BF)


def attn_kernel(seqs, place, *refs):
    (tok, wq0, wq1, wk0, wk1, wv0, wv1, wo0, wo1, vec) = refs[:10]
    (query_o, keys_o, values_o, mixed_o, signed_o, slope_o, first_o, hidden_o) = refs[10:18]
    wqkv_t, wo_t = refs[18:20]
    dim = tok.shape[1]
    lanes = seqs * SEQ

    @pl.when(pl.program_id(0) == 0)
    def _():
        part = dim // 2
        for index, ref in enumerate((wq0, wq1, wk0, wk1, wv0, wv1)):
            wqkv_t[index * part : (index + 1) * part, :] = turned(ref[...])
        wo_t[:, :part] = turned(wo0[...])
        wo_t[:, part:] = turned(wo1[...])

    half = lax.broadcasted_iota(jnp.int32, (HALF, SEQ), 1)
    mask = lax.broadcasted_iota(jnp.int32, (HALF, SEQ), 0) <= jnp.where(half < HALF, half, half - HALF)
    pairs = dim // LANES
    x = tok[...].astype(F32).T
    plain, _ = norm_plain(x)
    first = (plain * wide(vec[0:dim, :], lanes) + wide(vec[dim : 2 * dim, :], lanes)).astype(BF)
    outs = []
    for index in range(3):
        made = dot(wqkv_t[index * dim : (index + 1) * dim, :], first)
        made = made + wide(vec[(2 + index) * dim : (3 + index) * dim, :], lanes)
        made = made.astype(BF)
        if index == 0:
            made = made * jnp.asarray(1.0 / math.sqrt(HEAD_DIM), BF)
        outs.append(made)
    query, keys, values = outs
    mixed_all = []
    for s in range(seqs):
        span = slice(s * SEQ, (s + 1) * SEQ)
        first_o[s] = first[:, span]
        k_nat = turned(keys[:, span])
        parts = []
        for p in range(pairs):
            rows = slice(p * LANES, (p + 1) * LANES)
            c, g = divmod(p, 2)
            query_o[s, c, g], keys_o[s, c, g] = query[rows, span], keys[rows, span]
            values_o[s, c, g] = values[rows, span]
            near_q, far_q = pair_near_far(query[rows, span])
            kp = k_nat[:, rows]
            near, near_g = attend(dot(kp[:HALF], near_q), mask)
            far, far_g = attend(dot(kp, far_q), mask)
            signed_o[s, c, g, :HALF], signed_o[s, c, g, HALF:] = near, far
            slope_o[s, c, g, :HALF], slope_o[s, c, g, HALF:] = near_g, far_g
            v = values[rows, span]
            near_m, far_m = dot(v[:, :HALF], near), dot(v, far)
            made = jnp.concatenate(
                [
                    jnp.concatenate([near_m[:HEAD_DIM, :HALF], far_m[:HEAD_DIM, :HALF]], axis=1),
                    jnp.concatenate([near_m[HEAD_DIM:, HALF:], far_m[HEAD_DIM:, HALF:]], axis=1),
                ],
                axis=0,
            ).astype(BF)
            mixed_o[s, c, g] = made
            parts.append(made)
        mixed_all.append(jnp.concatenate(parts, axis=0))
    mixed = jnp.concatenate(mixed_all, axis=1)
    hidden = x + dot(wo_t[...], mixed) + wide(vec[5 * dim : 6 * dim, :], lanes)
    for s in range(seqs):
        hidden_o[s] = hidden[:, s * SEQ : (s + 1) * SEQ]


def mlp_kernel(seqs, block, place, *refs):
    (hid, cot, wu0, wu1, wd0, wd1, vec, bup) = refs[:8]
    (out_o, low_o, grad_o, gvec_o) = refs[8:12]
    wu_t, wd_t, gup, gdown, gvec, gbup = refs[12:18]
    dim = hid.shape[1]
    units = wu0.shape[1]
    lanes = seqs * SEQ
    step = pl.program_id(0)

    @pl.when(step == 0)
    def _():
        for index, (up, down) in enumerate(((wu0, wd0), (wu1, wd1))):
            wu_t[index * units : (index + 1) * units, :] = turned(up[...])
            wd_t[:, index * units : (index + 1) * units] = turned(down[...])
        gup[...] = jnp.zeros_like(gup)
        gdown[...] = jnp.zeros_like(gdown)
        gvec[...] = jnp.zeros_like(gvec)
        gbup[...] = jnp.zeros_like(gbup)

    hidden = jnp.concatenate([hid[s] for s in range(seqs)], axis=1)
    grad_out = cot[...].astype(F32).T
    grad_low = grad_out.astype(BF)
    gain = wide(vec[0:dim, :], lanes)
    plain, factor = norm_plain(hidden)
    second = (plain * gain + wide(vec[dim : 2 * dim, :], lanes)).astype(BF)
    ffout = None
    dnorm = None
    for start in range(0, 2 * units, block):
        span = slice(start, start + block)
        half, inner = divmod(start, units)
        up_ref, down_ref = ((wu0, wd0), (wu1, wd1))[half]
        inner = slice(inner, inner + block)
        upper = dot(wu_t[span, :], second) + wide(bup[span, :], lanes)
        dact = dot(down_ref[inner, :], grad_low)
        cdf = 0.5 * lax.erf(upper * (1.0 / math.sqrt(2.0))) + 0.5
        density = jnp.exp(-0.5 * (upper * upper)) * (1.0 / math.sqrt(2.0 * math.pi))
        act = (upper * cdf).astype(BF)
        dup_wide = dact * (cdf + upper * density)
        dup = dup_wide.astype(BF)
        gbup[span, :] += lane_fold(dup.astype(F32))
        out_part = dot(wd_t[:, span], act)
        dn_part = dot(up_ref[:, inner], dup)
        ffout = out_part if ffout is None else ffout + out_part
        dnorm = dn_part if dnorm is None else dnorm + dn_part
        gup[:, span] += tail_dot(second, dup)
        gdown[span, :] += tail_dot(act, grad_low)
    out = hidden + ffout + wide(vec[2 * dim : 3 * dim, :], lanes)
    out_o[...] = out.T.astype(BF)
    gvec[0:dim, :] += lane_fold(dnorm * plain)
    gvec[dim : 2 * dim, :] += lane_fold(dnorm)
    gvec[2 * dim : 3 * dim, :] += lane_fold(grad_out)
    dhidden = grad_out + norm_back(dnorm, plain, factor, gain)
    gvec[3 * dim :, :] += lane_fold(dhidden)
    for s in range(seqs):
        low_o[s] = dhidden[:, s * SEQ : (s + 1) * SEQ].astype(BF)

    @pl.when(step == pl.num_programs(0) - 1)
    def _():
        for half in range(2):
            for index in range(units // dim):
                start = half * units + index * dim
                grad_o[half, index * dim : (index + 1) * dim, :] = gup[:, start : start + dim].astype(BF)
            grad_o[half, units:, :] = gdown[half * units : (half + 1) * units, :].astype(BF)
        for index in range(4):
            gvec_o[index : index + 1, :] = as_row(gvec[index * dim : (index + 1) * dim, :])
        for index in range(2 * units // dim):
            gvec_o[4 + index : 5 + index, :] = as_row(gbup[index * dim : (index + 1) * dim, :])


def grad_kernel(seqs, group, *refs):
    (low_i, first_i, query_i, keys_i, values_i, mixed_i, signed_i, slope_i) = refs[:8]
    wo0, wo1 = refs[8:10]
    (dq_o, dk_o, dv_o, grad_o, gvec_o) = refs[10:15]
    gqkv, gout, gb = refs[15:18]
    dim = low_i.shape[1]
    part = 2 * LANES
    step = pl.program_id(0)
    scale = 1.0 / math.sqrt(HEAD_DIM)

    @pl.when(step == 0)
    def _():
        gqkv[...] = jnp.zeros_like(gqkv)
        gout[...] = jnp.zeros_like(gout)
        gb[...] = jnp.zeros_like(gb)

    place = slice(group * LANES, (group + 1) * LANES)
    first = jnp.concatenate([first_i[s] for s in range(seqs)], axis=1)
    low = jnp.concatenate([low_i[s] for s in range(seqs)], axis=1)
    dmixed = jnp.concatenate([dot(wo0[place, :], low), dot(wo1[place, :], low)], axis=0).astype(BF)
    mixed = jnp.concatenate(
        [
            jnp.concatenate([mixed_i[s, 0, 0], mixed_i[s, 1, 0]], axis=0)
            for s in range(seqs)
        ],
        axis=1,
    )
    dq_all, dk_all, dv_all = [], [], []
    for s in range(seqs):
        span = slice(s * SEQ, (s + 1) * SEQ)
        dq, dk, dv = [], [], []
        for c in range(2):
            rows = slice(c * LANES, (c + 1) * LANES)
            q, k = query_i[s, c, 0], keys_i[s, c, 0]
            dm = dmixed[rows, span]
            v_nat = turned(values_i[s, c, 0])
            near_q, far_q = pair_near_far(q)
            near_m, far_m = pair_near_far(dm)
            low_pair = []
            for index in range(2):
                keys = slice(0, HALF) if index == 0 else slice(0, SEQ)
                block = slice(0, HALF) if index == 0 else slice(HALF, HALF + SEQ)
                dsigned = dot(v_nat[keys], (near_m, far_m)[index])
                signed = signed_i[s, c, 0, block].astype(F32)
                row_dot = jnp.sum(signed * dsigned, axis=0, keepdims=True)
                dscores = slope_i[s, c, 0, block].astype(F32) * dsigned - signed * row_dot
                low_pair.append(dscores.astype(BF))
            near, far = low_pair
            near_p, far_p = dot(k[:, :HALF], near), dot(k, far)
            dq.append(
                jnp.concatenate(
                    [
                        jnp.concatenate([near_p[:HEAD_DIM, :HALF], far_p[:HEAD_DIM, :HALF]], axis=1),
                        jnp.concatenate([near_p[HEAD_DIM:, HALF:], far_p[HEAD_DIM:, HALF:]], axis=1),
                    ],
                    axis=0,
                )
            )
            near_p, far_p = tail_dot(near, near_q), tail_dot(far, far_q)
            dk.append(jnp.concatenate([far_p[:HALF] + near_p, far_p[HALF:]], axis=0))
            near_p = tail_dot(signed_i[s, c, 0, :HALF], near_m)
            far_p = tail_dot(signed_i[s, c, 0, HALF:], far_m)
            dv.append(jnp.concatenate([far_p[:HALF] + near_p, far_p[HALF:]], axis=0))
        dq_all.append((jnp.concatenate(dq, axis=0) * scale).astype(BF))
        dk_all.append(jnp.concatenate(dk, axis=1).astype(BF))
        dv_all.append(jnp.concatenate(dv, axis=1).astype(BF))
        dq_o[s], dk_o[s], dv_o[s] = dq_all[s], dk_all[s], dv_all[s]
    gout[...] += tail_dot(mixed, low)
    dq, dk, dv = jnp.concatenate(dq_all, axis=1), jnp.concatenate(dk_all, axis=0), jnp.concatenate(dv_all, axis=0)
    gqkv[:, :part] += tail_dot(first, dq)
    gqkv[:, part : 2 * part] += dot(first, dk)
    gqkv[:, 2 * part :] += dot(first, dv)
    gb[:part, :] += lane_fold(dq.astype(F32))
    for index, block in ((2, dk), (3, dv)):
        total = jnp.sum(block.astype(F32).reshape(-1, 8, part), axis=0)
        gb[index * LANES : index * LANES + 8, :] += total[:, :LANES]
        gb[index * LANES + 8 : index * LANES + 16, :] += total[:, LANES:]

    @pl.when(step == pl.num_programs(0) - 1)
    def _():
        for c in range(2):
            for index in range(3):
                start = index * part + c * LANES
                grad_o[c, index * dim : (index + 1) * dim, :] = gqkv[:, start : start + LANES].astype(BF)
            for index in range(dim // LANES):
                start = 3 * dim + index * LANES
                grad_o[c, start : start + LANES, :] = gout[
                    c * LANES : (c + 1) * LANES, index * LANES : (index + 1) * LANES
                ].astype(BF)
            gvec_o[c : c + 1, :] = as_row(gb[c * LANES : (c + 1) * LANES, :])
            for index in (2, 3):
                rows = slice(index * LANES + 8 * c, index * LANES + 8 * c + 8)
                gvec_o[2 * index - 2 + c : 2 * index - 1 + c, :] = jnp.sum(gb[rows, :], axis=0, keepdims=True)


def input_kernel(seqs, place, *refs):
    tok, dhid, dq0, dk0, dv0, dq1, dk1, dv1 = refs[:8]
    wq0, wq1, wk0, wk1, wv0, wv1, vec = refs[8:15]
    tgrad_o, gvec_o = refs[15:17]
    gvec = refs[17]
    dim = tok.shape[1]

    @pl.when(pl.program_id(0) == 0)
    def _():
        gvec[...] = jnp.zeros_like(gvec)

    gain = wide(vec[0:dim, :], SEQ)
    for s in range(seqs):
        rows = slice(s * SEQ, (s + 1) * SEQ)
        dnorm = None
        for c, (wq, wk, wv) in enumerate(((wq0, wk0, wv0), (wq1, wk1, wv1))):
            lanes = slice(c * LANES, (c + 1) * LANES)
            dq = jnp.concatenate([dq0[s, lanes, :], dq1[s, lanes, :]], axis=0)
            dk = jnp.concatenate([dk0[s, :, lanes], dk1[s, :, lanes]], axis=1)
            dv = jnp.concatenate([dv0[s, :, lanes], dv1[s, :, lanes]], axis=1)
            made = dot(wq[...], dq) + tail_dot(wk[...], dk) + tail_dot(wv[...], dv)
            dnorm = made if dnorm is None else dnorm + made
        plain, factor = norm_plain(tok[rows, :].astype(F32).T)
        gvec[0:dim, :] += lane_fold(dnorm * plain)
        gvec[dim : 2 * dim, :] += lane_fold(dnorm)
        tgrad = dhid[s].astype(F32) + norm_back(dnorm, plain, factor, gain)
        tgrad_o[rows, :] = tgrad.T.astype(BF)

    @pl.when(pl.program_id(0) == pl.num_programs(0) - 1)
    def _():
        for index in range(2):
            gvec_o[index : index + 1, :] = as_row(gvec[index * dim : (index + 1) * dim, :])


def whole_vmem():
    return pl.BlockSpec(memory_space=pltpu.VMEM)


def seq_block(seqs, *dims):
    return pl.BlockSpec((seqs,) + dims, lambda i: (i,) + (0,) * len(dims))


def params():
    return pltpu.CompilerParams(
        dimension_semantics=("arbitrary",), vmem_limit_bytes=VMEM_LIMIT
    )


def prefetch(grid, in_specs, out_specs, scratch=()):
    return pltpu.PrefetchScalarGridSpec(
        num_scalar_prefetch=1, grid=grid, in_specs=in_specs, out_specs=out_specs, scratch_shapes=scratch
    )


def row_block(seqs, dim, steps):
    return pl.BlockSpec((seqs * SEQ, dim), lambda i, place: (place[0] * steps + i, 0))


def placed_seq_block(seqs, *dims):
    return pl.BlockSpec((seqs,) + dims, lambda i, place: (i,) + (0,) * len(dims))


def attn_call(place, tokens, own, weights, vec, seqs):
    dim = tokens.shape[1]
    count = own // SEQ
    steps = count // seqs
    feat = (2, 2, LANES, SEQ)
    wide_block = (2, 2, HALF + SEQ, SEQ)
    shape = jax.ShapeDtypeStruct
    return pl.pallas_call(
        functools.partial(attn_kernel, seqs),
        grid_spec=prefetch(
            (steps,),
            [row_block(seqs, dim, steps)] + [whole_vmem()] * 9,
            [placed_seq_block(seqs, *feat)] * 4
            + [placed_seq_block(seqs, *wide_block)] * 2
            + [placed_seq_block(seqs, dim, SEQ)] * 2,
            [pltpu.VMEM((3 * dim, dim), BF), pltpu.VMEM((dim, dim), BF)],
        ),
        out_shape=[shape((count,) + feat, BF)] * 4
        + [shape((count,) + wide_block, BF)] * 2
        + [shape((count, dim, SEQ), BF), shape((count, dim, SEQ), F32)],
        compiler_params=params(),
        name="attn_forward",
    )(place, tokens, *weights, vec)


def grad_call(group, low, first, saved, weights, seqs):
    count, dim = low.shape[:2]
    steps = count // seqs
    one = lambda *dims: pl.BlockSpec((seqs, 2, 1) + dims, lambda i: (i, 0, group, 0, 0))
    shape = jax.ShapeDtypeStruct
    part = 2 * LANES
    return pl.pallas_call(
        functools.partial(grad_kernel, seqs, group),
        grid=(steps,),
        in_specs=[seq_block(seqs, dim, SEQ)] * 2
        + [one(LANES, SEQ)] * 4
        + [one(HALF + SEQ, SEQ)] * 2
        + [whole_vmem()] * 2,
        out_specs=[seq_block(seqs, part, SEQ), seq_block(seqs, SEQ, part), seq_block(seqs, SEQ, part)]
        + [whole_vmem()] * 2,
        out_shape=[
            shape((count, part, SEQ), BF),
            shape((count, SEQ, part), BF),
            shape((count, SEQ, part), BF),
            shape((2, 4 * dim, LANES), BF),
            shape((8, LANES), F32),
        ],
        scratch_shapes=[
            pltpu.VMEM((dim, 3 * part), F32),
            pltpu.VMEM((part, dim), F32),
            pltpu.VMEM((4 * LANES, LANES), F32),
        ],
        compiler_params=params(),
        name="attn_backward",
    )(low, first, *saved, *weights)


def input_call(place, tokens, dhidden, pieces, weights, vec, seqs):
    dim = tokens.shape[1]
    count = dhidden.shape[0]
    steps = count // seqs
    part = 2 * LANES
    trio = [
        placed_seq_block(seqs, part, SEQ),
        placed_seq_block(seqs, SEQ, part),
        placed_seq_block(seqs, SEQ, part),
    ]
    return pl.pallas_call(
        functools.partial(input_kernel, seqs),
        grid_spec=prefetch(
            (steps,),
            [row_block(seqs, dim, steps), placed_seq_block(seqs, dim, SEQ)]
            + trio * 2
            + [whole_vmem()] * 7,
            [
                pl.BlockSpec((seqs * SEQ, dim), lambda i, place: (i, 0)),
                whole_vmem(),
            ],
            [pltpu.VMEM((2 * dim, LANES), F32)],
        ),
        out_shape=[
            jax.ShapeDtypeStruct((count * SEQ, dim), BF),
            jax.ShapeDtypeStruct((8, dim), F32),
        ],
        compiler_params=params(),
        name="input_grad",
    )(place, tokens, dhidden, *pieces, *weights, vec)


def mlp_call(place, hidden, cotangent, weights, vec, bup, seqs, block):
    count, dim = hidden.shape[:2]
    steps = count // seqs
    units = weights[0].shape[1]
    shape = jax.ShapeDtypeStruct
    return pl.pallas_call(
        functools.partial(mlp_kernel, seqs, block),
        grid_spec=prefetch(
            (steps,),
            [placed_seq_block(seqs, dim, SEQ), row_block(seqs, dim, steps)] + [whole_vmem()] * 6,
            [
                pl.BlockSpec((seqs * SEQ, dim), lambda i, place: (i, 0)),
                placed_seq_block(seqs, dim, SEQ),
            ]
            + [whole_vmem()] * 2,
            [
                pltpu.VMEM((2 * units, dim), BF),
                pltpu.VMEM((dim, 2 * units), BF),
                pltpu.VMEM((dim, 2 * units), F32),
                pltpu.VMEM((2 * units, dim), F32),
                pltpu.VMEM((4 * dim, LANES), F32),
                pltpu.VMEM((2 * units, LANES), F32),
            ],
        ),
        out_shape=[
            shape((count * SEQ, dim), BF),
            shape((count, dim, SEQ), BF),
            shape((2, 2 * units, dim), BF),
            shape((8, dim), F32),
        ],
        compiler_params=params(),
        name="feed_forward",
    )(place, hidden, cotangent, *weights, vec, bup)


def shifted(value, axis, count, shift):
    return lax.ppermute(value, axis, [(i, (i + shift) % count) for i in range(count)])


def gathered(value, count, axis):
    blocks = [value] + [shifted(value, "mp", count, -r) for r in range(1, count)]
    half = count // 2
    return [
        blocks[g * half] if half == 1 else jnp.concatenate(blocks[g * half : (g + 1) * half], axis)
        for g in range(2)
    ]


def total_of(blocks):
    total = blocks[0].astype(F32)
    for block in blocks[1:]:
        total = total + block.astype(F32)
    return total.astype(BF)


class DpSum:
    def __init__(self, count):
        self.count = count
        self.groups = []
        bit = 1
        while bit < count:
            size = min(4, count // bit)
            self.groups.append((bit, size))
            bit *= size

    def swap(self, value, distance):
        return lax.ppermute(value, "dp", [(i, i ^ distance) for i in range(self.count)])

    def place(self, bit, size):
        return (lax.axis_index("dp") // bit) % size

    def scatter(self, value, stage):
        bit, size = self.groups[stage]
        here = self.place(bit, size)
        parts = value.reshape(size, value.shape[0] // size, value.shape[1])
        pick = lambda m: lax.dynamic_index_in_dim(parts, here ^ m, 0, keepdims=False)
        return [pick(0)] + [self.swap(pick(m), m * bit) for m in range(1, size)]

    def gather(self, value, stage):
        bit, size = self.groups[stage]
        return [value] + [self.swap(value, m * bit) for m in range(1, size)]

    def join(self, blocks, stage):
        bit, size = self.groups[stage]
        here = self.place(bit, size)
        whole = jnp.zeros((size,) + blocks[0].shape, blocks[0].dtype)
        for m, block in enumerate(blocks):
            whole = lax.dynamic_update_index_in_dim(whole, block, here ^ m, 0)
        return whole.reshape(-1, blocks[0].shape[1])


def body(mp, dp, *args):
    (tokens, gain1, shift1, wq, bq, wk, bk, wv, bv, wo, bo) = args[:11]
    (gain2, shift2, wu, bu, wd, bd, cotangent) = args[11:]
    rows, dim = tokens.shape
    local = wq.shape[1]
    units = wu.shape[1]
    own = rows // mp
    per = mp // 2
    me = lax.axis_index("mp")
    place = me.astype(jnp.int32).reshape(1)
    tie = lax.optimization_barrier
    dp_sum = DpSum(dp)

    weights = []
    for w in (wq, wk, wv):
        weights += gathered(w, mp, 1)
    weights += gathered(wo, mp, 0)
    small = jnp.concatenate([bq, bk, bv, bu])
    blocks = [small] + [shifted(small, "mp", mp, -r) for r in range(1, mp)]
    mlp_weights = gathered(wu, mp, 1) + gathered(wd, mp, 0)
    spread = lambda lo, hi: jnp.concatenate([b[lo:hi] for b in blocks])
    over = lambda vector: jnp.broadcast_to(vector[:, None], (vector.shape[0], LANES))
    vec1 = over(
        jnp.concatenate(
            [gain1, shift1] + [spread(i * local, (i + 1) * local) for i in range(3)] + [bo]
        )
    )
    vec2 = over(jnp.concatenate([gain2, shift2, bd]))
    bup = over(spread(3 * local, 3 * local + units))

    def whole(part, others):
        full = jnp.zeros((rows, dim), BF)
        for r, block in enumerate([part] + others):
            full = lax.dynamic_update_slice_in_dim(full, block, ((me - r) % mp) * own, 0)
        return full

    def spread_out(part):
        return [shifted(part, "mp", mp, r) for r in range(1, mp)]

    def ff_piece(grad, r):
        g, j = divmod(r, per)
        if per == 1:
            return grad[g]
        up = grad[g, : per * units].reshape(-1, dim, dim)
        up = jnp.concatenate(list(up), axis=1)[:, j * units : (j + 1) * units]
        down = grad[g, per * units + j * units : per * units + (j + 1) * units]
        return jnp.concatenate([up.reshape(-1, dim), down], axis=0)

    def at_piece(grads, r):
        g, j = divmod(r, per)
        if per == 1:
            return jnp.concatenate([grad[g] for grad in grads], axis=0)
        parts = []
        for index in range(3):
            block = [grad[g, index * dim : (index + 1) * dim] for grad in grads]
            block = jnp.concatenate(block, axis=1)[:, j * local : (j + 1) * local]
            parts.append(block.reshape(-1, LANES))
        block = [grad[g, 3 * dim :].reshape(-1, LANES, LANES) for grad in grads]
        block = jnp.concatenate([jnp.concatenate(list(b), axis=1) for b in block], axis=0)
        parts.append(block[j * local : (j + 1) * local].reshape(-1, LANES))
        return jnp.concatenate(parts, axis=0)

    def mp_send(piece):
        return [piece(0)] + [shifted(piece(r), "mp", mp, r) for r in range(1, mp)]

    *saved, first, hidden = attn_call(place, tokens, own, weights, vec1, 2)
    hidden, mlp_weights = tie((hidden, mlp_weights))
    out, low, grad_ff, vec_ff = mlp_call(place, hidden, cotangent, mlp_weights, vec2, bup, 2, 512)

    ff = mp_send(lambda r: ff_piece(grad_ff, r))
    outs = spread_out(out)
    low, ff[0], out = tie((low, ff[0], out))
    dq0, dk0, dv0, grad0, vec_at0 = grad_call(0, low, first, saved, weights[6:], 2)
    ff, outs, dq0 = tie((ff, outs, dq0))
    ff = dp_sum.scatter(total_of(ff), 0)
    out_full = whole(out, outs)
    if per == 1:
        at0 = mp_send(lambda r: at_piece([grad0], r))
    low, ff[0] = tie((low, ff[0]))
    dq1, dk1, dv1, grad1, vec_at1 = grad_call(1, low, first, saved, weights[6:], 2)
    ff, dq1 = tie((ff, dq1))
    ff = dp_sum.scatter(total_of(ff), 1)
    if per == 1:
        at1 = mp_send(lambda r: at_piece([grad1], r))
    low, ff[0] = tie((low, ff[0]))
    tgrad, vec_in = input_call(
        place, tokens, low, [dq0, dk0, dv0, dq1, dk1, dv1], weights[:6], vec1, 2
    )
    tgrads = spread_out(tgrad)

    same = jnp.concatenate([vec_ff[:4].reshape(-1), vec_in[:2].reshape(-1)])
    gbup = vec_ff[4:].reshape(-1)
    bias = []
    for index in range(3):
        chunks = [v[2 * index + c] for c in range(2) for v in (vec_at0, vec_at1)]
        bias.append(jnp.concatenate(chunks))

    def vec_piece(r):
        vector = jnp.concatenate(
            [same] + [b[r * local : (r + 1) * local] for b in bias] + [gbup[r * units : (r + 1) * units]]
        )
        size = -(-vector.shape[0] // (16 * dp * LANES)) * (16 * dp * LANES)
        return jnp.pad(vector, (0, size - vector.shape[0])).reshape(-1, LANES).astype(BF)

    ff, tgrad = tie((ff, tgrad))
    if per == 1:
        vecs = mp_send(vec_piece)
        at = jnp.concatenate([total_of(at0), total_of(at1), total_of(vecs)], axis=0)
    else:
        at = total_of(
            mp_send(lambda r: jnp.concatenate([at_piece([grad0, grad1], r), vec_piece(r)], axis=0))
        )
    stages = len(dp_sum.groups)
    for stage in range(2, stages):
        ff = dp_sum.scatter(total_of(ff), stage)
    ff = total_of(ff)
    for stage in range(stages):
        at = total_of(dp_sum.scatter(at, stage))
    for stage in reversed(range(stages)):
        ff = dp_sum.join(dp_sum.gather(ff, stage), stage)
        at = dp_sum.join(dp_sum.gather(at, stage), stage)
    ff, at = ff.astype(F32), at.astype(F32)

    if per == 1:
        g_up = jnp.concatenate(list(ff[:units].reshape(-1, dim, dim)), axis=1)
        tall = 4 * dim
        halves = [at[:tall], at[tall : 2 * tall]]
        g_qkv = [
            jnp.concatenate([h[i * dim : (i + 1) * dim] for h in halves], axis=1) for i in range(3)
        ]
        g_out = jnp.concatenate(
            [
                jnp.concatenate(list(h[3 * dim :].reshape(-1, LANES, LANES)), axis=1)
                for h in halves
            ],
            axis=0,
        )
        used = 2 * tall
    else:
        g_up = ff[:units].reshape(dim, units)
        each = dim * local // LANES
        g_qkv = [at[i * each : (i + 1) * each].reshape(dim, local) for i in range(3)]
        g_out = at[3 * each : 4 * each].reshape(local, dim)
        used = 4 * each
    g_down = ff[units:]
    vector = at[used:].reshape(-1)
    g_same = [vector[i * dim : (i + 1) * dim] for i in range(6)]
    base = 6 * dim
    g_bias = [vector[base + i * local : base + (i + 1) * local] for i in range(3)]
    g_bup = vector[base + 3 * local : base + 3 * local + units]
    return (
        out_full,
        whole(tgrad, tgrads),
        g_same[4],
        g_same[5],
        g_qkv[0],
        g_bias[0],
        g_qkv[1],
        g_bias[1],
        g_qkv[2],
        g_bias[2],
        g_out,
        g_same[3],
        g_same[0],
        g_same[1],
        g_up,
        g_bup,
        g_down,
        g_same[2],
    )


def solution(mesh):
    split = P("dp", None)
    columns, some, lines = P(None, "mp"), P("mp"), P("mp", None)
    return jax.shard_map(
        functools.partial(body, mesh.shape["mp"], mesh.shape["dp"]),
        mesh=mesh,
        in_specs=(split, P(), P(), columns, some, columns, some, columns, some, lines, P())
        + (P(), P(), columns, some, lines, P(), split),
        out_specs=(split, split, P(), P(), columns, some, columns, some, columns, some, lines)
        + (P(), P(), P(), columns, some, lines, P()),
        check_vma=False,
    )
```

time: 398 us -> 340 us (0.85); the launches traced: 397 us -> 333 us
  Pallas kernels: 223 us -> 188 us
  waiting for transfers between devices: 59 us -> 36.9 us
  local copies, waits for them, and re-layouts: 61 us -> 48 us
  starting transfers between devices: 39.7 us -> 45.6 us
    pallas_call x3 -> x5, Pallas kernels: 223 us -> 188 us  [the longest x1 73.6 us: mlp_call(): pl.pallas_call(functools.partial(mlp_kernel, seqs, block), grid_spec=pref...]
    ppermute x24, waiting for transfers between devices: 52.4 us -> 36.8 us  [swap(): lax.ppermute(value, 'dp', [(i, i ^ distance) for i in range(self.count)])]
    another operation x10 -> x4, local copies, waits for them, and re-layouts: 11.2 us -> 1.29 us  [the longest x6 8.57 us: piece(): qkv = [gqkv[g, i][:, lanes].reshape(-1, dim) for i in range(3)]]
    squeeze x0 -> x9, local copies, waits for them, and re-layouts: none -> 9.79 us  [the longest x1 3.81 us: ff_piece(): return grad[g]]
    unnamed x83 -> x58, local copies, waits for them, and re-layouts: 10.9 us -> 18.5 us
    dynamic_slice x1 -> x0, local copies, waits for them, and re-layouts: 7.38 us -> none  [body(): cot = lax.dynamic_slice_in_dim(cotangent, me * own, own)]
    ppermute x10 -> x13, waiting for transfers between devices: 6.57 us -> 0.03 us  [shifted(): lax.ppermute(value, axis, [(i, (i + shift) % count) for i in range(count)])]
    reshape x5 -> x0, local copies, waits for them, and re-layouts: 5.33 us -> none  [the longest x4 5.33 us: take(): return block.reshape(shape)]
  transfers between devices with their start and end apart: 34 -> 37, of which waited for: 18 -> 8; matrix products, arithmetic and copies ran while one was open for 8% -> 13% of each run, Pallas kernels for 15% -> 34%
where the time goes in v2:
time: 340 us; the launch traced here: 333 us
  Pallas kernels  188 us (55%)
  local copies, waits for them, and re-layouts  48 us (14%)
  starting transfers between devices  45.6 us (13%)
  waiting for transfers between devices  36.9 us (11%)
  other arithmetic  13.2 us (4%)
    pallas_call x1, Pallas kernels, mlp_call(): pl.pallas_call(functools.partial(mlp_kernel, seqs, block), grid_spec=pref...  73.6 us
    pallas_call x2, Pallas kernels, grad_call(): pl.pallas_call(functools.partial(grad_kernel, seqs, group), grid=(steps,)...  49.1 us
    pallas_call x1, Pallas kernels, attn_call(): pl.pallas_call(functools.partial(attn_kernel, seqs), grid_spec=prefetch((...  47.6 us
    ppermute x24, starting transfers between devices, swap(): lax.ppermute(value, 'dp', [(i, i ^ distance) for i in range(self.count)])  42 us
    ppermute x24, waiting for transfers between devices, swap(): lax.ppermute(value, 'dp', [(i, i ^ distance) for i in range(self.count)])  36.8 us
    unnamed x58, local copies, waits for them, and re-layouts  18.5 us
    pallas_call x1, Pallas kernels, input_call(): pl.pallas_call(functools.partial(input_kernel, seqs), grid_spec=prefetch(...  17.8 us
    dynamic_update_slice x4, local copies, waits for them, and re-layouts, whole(): full = lax.dynamic_update_slice_in_dim(full, block, (me - r) % mp * own, 0)  8.29 us
  transfers between devices with their start and end apart: 37, of which 8 were waited for; matrix products, arithmetic and copies ran while one was open for 13% of the time, Pallas kernels for 34%

profile of v2, /device:TPU:0, one launch (start us, length us, event | category | flops | bytes accessed | tf_op | source)
XLA Modules:
  0.0 333.3 jit_solution(15007244263159799164)
XLA Ops:
  0.7 0.7 pad_maximum_fusion.5
  4.3 0.7 pad_maximum_fusion.6
  7.6 0.7 constant_dynamic-update-slice_fusion.10
  9.0 1.6 broadcast_in_dim.82.refs_9_.refs_14_
  10.7 47.6 %attn_forward.1 = (bf16[16,2,2,128,256]{4,3,2,1,0:T(8,128)(2,1)}, bf16[16,2,2,128,256]{4,3,2,1,0:T(8,128)(2,1)}, bf16[16,2,2,128,256]{4,3,2,1,0:T(8,128)(2,1)}, ...) custom-call(s32[1]{0:T(128)} %bitcast.place, ...), custom_call_target="tpu_custom_call" | custom-call | tf_op jit(solution)/shard_map/attn_forward/pallas_call | solution.py:402
  58.3 1.7 broadcast_in_dim.84.refs_7_
  60.1 1.2 broadcast_in_dim.83.refs_6_
  61.2 73.6 %feed_forward.1 = (bf16[4096,512]{1,0:T(8,128)(2,1)}, bf16[16,512,256]{2,1,0:T(8,128)(2,1)}, bf16[2,2048,512]{2,1,0:T(8,128)(2,1)}, f32[8,512]{1,0:T(8,128)}) custom-call(s32[1]{0:T(128)} %bitcast.place, f32[16,512,256]{2,1,0:T(8,128)} %get-tuple-element.69.refs_0_, bf16[8192,512]{1,0:T(8,128)(2,1)} %refs_1_.3, bf16[512,1024]{1,0:T(8,128)(2,1)} %refs_2_, ...), custom_call_target="tpu_custom_call" | custom-call | tf_op jit(solution)/shard_map/feed_forward/pallas_call | solution.py:489
  135.2 3.8 %slice_bitcast_fusion = (bf16[2048,512]{1,0:T(8,128)(2,1)}, bf16[2048,512]{1,0:T(8,128)(2,1)S(1)}) fusion(bf16[2,2048,512]{2,1,0:T(8,128)(2,1)} %get-tuple-element.75), kind=kLoop, calls=%fused_computation.2 | loop fusion | bytes 8388608 | tf_op jit(solution)/shard_map/squeeze | solution.py:617
  139.2 24.6 %attn_backward.2 = (bf16[16,256,256]{2,1,0:T(8,128)(2,1)}, bf16[16,256,256]{2,1,0:T(8,128)(2,1)}, bf16[16,256,256]{2,1,0:T(8,128)(2,1)}, bf16[2,2048,128]{2,1,0:T(8,128)(2,1)}, f32[8,128]{1,0:T(8,128)}) custom-call(bf16[16,512,256]{2,1,0:T(8,128)(2,1)} %get-tuple-element.99.refs_0_.refs_1_, bf16[16,512,256]{2,1,0:T(8,128)(2,1)} %get-tuple-element.80.refs_1_, ...), custom_call_target="tpu_custom_call" | custom-call | tf_op jit(solution)/shard_map/attn_backward/pallas_call | solution.py:426
  163.9 1.1 slice_bitcast_fusion.5
  165.4 0.7 convert.68
  167.7 1.6 copy-done.3
  170.8 3.8 %add_convert_fusion = bf16[2048,512]{1,0:T(8,128)(2,1)S(1)} fusion(bf16[2048,512]{1,0:T(8,128)(2,1)} %collective-permute-done.7, bf16[2048,512]{1,0:T(8,128)(2,1)S(1)} %get-tuple-element.89), kind=kLoop, calls=%fused_computation | loop fusion | flops 4194304 | bytes 6291456 | tf_op jit(solution)/shard_map/convert_element_type | solution.py:536
  174.5 1.2 dynamic-slice_bitcast_fusion
  175.7 2.7 collective-permute-start.10
  178.4 1.4 collective-permute-start.11
  179.9 24.5 %attn_backward.3 = (bf16[16,256,256]{2,1,0:T(8,128)(2,1)}, bf16[16,256,256]{2,1,0:T(8,128)(2,1)}, bf16[16,256,256]{2,1,0:T(8,128)(2,1)}, bf16[2,2048,128]{2,1,0:T(8,128)(2,1)}, f32[8,128]{1,0:T(8,128)}) custom-call(bf16[16,512,256]{2,1,0:T(8,128)(2,1)} %get-tuple-element.99.refs_0_.refs_1_, bf16[16,512,256]{2,1,0:T(8,128)(2,1)} %get-tuple-element.80.refs_1_, ...), custom_call_target="tpu_custom_call" | custom-call | tf_op jit(solution)/shard_map/attn_backward/pallas_call | solution.py:426
  204.4 1.9 slice_bitcast_fusion.4
  206.2 0.7 convert.69
  207.5 4.5 %constant_dynamic-update-slice_fusion.2 = bf16[8192,512]{1,0:T(8,128)(2,1)} fusion(bf16[8192,512]{1,0:T(8,128)(2,1)} %copy-done.1, bf16[4096,512]{1,0:T(8,128)(2,1)} %collective-permute-done.8, s32[]{:T(128)S(6)} %select_n.113), kind=kLoop, calls=%fused_computation.63 | loop fusion | bytes 8388612 | tf_op jit(solution)/shard_map/dynamic_update_slice | solution.py:608
  212.2 0.7 dynamic-slice_bitcast_fusion.7
  212.9 2.1 collective-permute-start.12
  215.0 2.6 collective-permute-start.13
  217.6 17.8 %input_grad.1 = (bf16[4096,512]{1,0:T(8,128)(2,1)}, f32[8,512]{1,0:T(8,128)}) custom-call(s32[1]{0:T(128)} %bitcast.place, bf16[8192,512]{1,0:T(8,128)(2,1)} %refs_0_.3, bf16[16,512,256]{2,1,0:T(8,128)(2,1)} %get-tuple-element.99.refs_0_.refs_1_, bf16[16,256,256]{2,1,0:T(8,128)(2,1)} %get-tuple-element.100.refs_2_, ...), custom_call_target="tpu_custom_call" | custom-call | tf_op jit(solution)/shard_map/input_grad/pallas_call | solution.py:462
  235.4 0.7 fusion.10
  238.6 0.9 dynamic-update-slice.11
  239.5 0.8 dynamic-update-slice.12
  240.3 0.8 dynamic-update-slice.13
  241.1 0.8 dynamic-update-slice.14
  242.0 0.8 dynamic-update-slice.15
  242.8 0.8 dynamic-update-slice.16
  244.0 1.8 collective-permute-start.19
  245.8 1.5 collective-permute-start.20
  247.7 1.0 collective-permute-start.31
  249.2 1.6 copy-done.2
  251.4 1.3 collective-permute-done.31
  252.8 2.4 collective-permute-start.32
  255.2 2.3 collective-permute-start.33
  257.4 2.7 collective-permute-done.20
  260.3 0.8 collective-permute-start.22
  261.1 3.5 %collective-permute-start.23 = (bf16[272,128]{1,0:T(8,128)(2,1)S(1)}, bf16[272,128]{1,0:T(8,128)(2,1)S(1)}, u32[]{:S(2)}, u32[]{:S(2)}) collective-permute-start(bf16[272,128]{1,0:T(8,128)(2,1)S(1)} %get-tuple-element.162), channel_id=1, source_target_pairs={{0,8},{1,9},{2,10},{3,11},{4,12},{5,13},{6,14},{7,15},{8,0},{9,1},... | collective-permute-start | bytes 208904 | tf_op jit(solution)/shard_map/ppermute | solution.py:550
  264.6 2.7 collective-permute-start.24
  267.3 4.0 %collective-permute-done.23 = bf16[272,128]{1,0:T(8,128)(2,1)S(1)} collective-permute-done((bf16[272,128]{1,0:T(8,128)(2,1)S(1)}, bf16[272,128]{1,0:T(8,128)(2,1)S(1)}, u32[]{:S(2)}, u32[]{:S(2)}) %collective-permute-start.23) | collective-permute-done | bytes 69664 | tf_op jit(solution)/shard_map/ppermute | solution.py:550
  271.4 1.5 collective-permute-start.25
  272.9 1.5 collective-permute-start.34
  274.5 1.5 collective-permute-start.35
  276.5 2.6 collective-permute-start.26
  279.2 3.3 collective-permute-done.26
  282.4 3.9 %collective-permute-start.27 = (bf16[272,128]{1,0:T(8,128)(2,1)S(1)}, bf16[272,128]{1,0:T(8,128)(2,1)S(1)}, u32[]{:S(2)}, u32[]{:S(2)}) collective-permute-start(bf16[272,128]{1,0:T(8,128)(2,1)S(1)} %get-tuple-element.121), channel_id=1, source_target_pairs={{0,12},{1,13},{2,14},{3,15},{4,8},{5,9},{6,10},{7,11},{8,4},{9,5},... | collective-permute-start | bytes 208904 | tf_op jit(solution)/shard_map/ppermute | solution.py:550
  286.3 2.3 collective-permute-done.27
  288.6 1.5 collective-permute-start.28
  290.6 12.8 %collective-permute-done.28 = bf16[1088,128]{1,0:T(8,128)(2,1)S(1)} collective-permute-done((bf16[1088,128]{1,0:T(8,128)(2,1)S(1)}, bf16[1088,128]{1,0:T(8,128)(2,1)S(1)}, u32[]{:S(2)}, u32[]{:S(2)}) %collective-permute-start.28) | collective-permute-done | bytes 278560 | tf_op jit(solution)/shard_map/ppermute | solution.py:550
  303.4 1.5 collective-permute-start.29
  305.0 5.4 %collective-permute-done.29 = bf16[1088,128]{1,0:T(8,128)(2,1)S(1)} collective-permute-done((bf16[1088,128]{1,0:T(8,128)(2,1)S(1)}, bf16[1088,128]{1,0:T(8,128)(2,1)S(1)}, u32[]{:S(2)}, u32[]{:S(2)}) %collective-permute-start.29) | collective-permute-done | bytes 278560 | tf_op jit(solution)/shard_map/ppermute | solution.py:550
  310.4 2.4 collective-permute-start.30
  312.8 5.0 %collective-permute-done.30 = bf16[1088,128]{1,0:T(8,128)(2,1)S(1)} collective-permute-done((bf16[1088,128]{1,0:T(8,128)(2,1)S(1)}, bf16[1088,128]{1,0:T(8,128)(2,1)S(1)}, u32[]{:S(2)}, u32[]{:S(2)}) %collective-permute-start.30) | collective-permute-done | bytes 278560 | tf_op jit(solution)/shard_map/ppermute | solution.py:550
  320.0 0.8 pad_maximum_fusion.4
  320.8 1.0 pad_maximum_fusion.2
  321.9 0.8 maximum_maximum_fusion
  323.4 1.6 slice.320
  325.2 1.5 pad_maximum_fusion
  326.7 2.7 constant_dynamic-update-slice_fusion
  329.4 3.4 %copy-done = bf16[8192,512]{1,0:T(8,128)(2,1)} copy-done((bf16[8192,512]{1,0:T(8,128)(2,1)}, bf16[8192,512]{1,0:T(8,128)(2,1)S(1)}, u32[]{:S(2)}) %copy-start) | copy-done | bytes 8388632
  (143 shorter events, 19.8 us)
Async XLA Ops:
  1.4 4.3 %collective-permute-start.4 = (f32[1792]{0:T(1024)S(1)}, f32[1792]{0:T(1024)S(1)}, u32[]{:S(2)}, u32[]{:S(2)}) collective-permute-start(f32[1792]{0:T(1024)S(1)} %pad_maximum_fusion.5), channel_id=1, source_target_pairs={{0,16},{16,0},{1,17},{17,1},{2,18},{18,2},{3,19},{19,3},{4,20},{20... | collective-permute-start | bytes 21512 | tf_op jit(solution)/shard_map/ppermute | solution.py:520
  1.9 5.3 %collective-permute-start.3 = (bf16[256,512]{1,0:T(8,128)(2,1)}, bf16[256,512]{1,0:T(8,128)(2,1)S(1)}, u32[]{:S(2)}, u32[]{:S(2)}) collective-permute-start(bf16[256,512]{1,0:T(8,128)(2,1)} %refs_8_.4), channel_id=1, source_target_pairs={{0,16},{16,0},{1,17},{17,1},{2,18},{18,2},{3,19},{19,3},{4,20},{20... | collective-permute-start | bytes 786440 | tf_op jit(solution)/shard_map/ppermute | solution.py:520
  2.0 7.0 %collective-permute-start = (bf16[512,256]{1,0:T(8,128)(2,1)}, bf16[512,256]{1,0:T(8,128)(2,1)S(1)}, u32[]{:S(2)}, u32[]{:S(2)}) collective-permute-start(bf16[512,256]{1,0:T(8,128)(2,1)} %refs_8_.5), channel_id=1, source_target_pairs={{0,16},{16,0},{1,17},{17,1},{2,18},{18,2},{3,19},{19,3},{4,20},{20... | collective-permute-start | bytes 786440 | tf_op jit(solution)/shard_map/ppermute | solution.py:520
  2.4 6.6 %collective-permute-start.1 = (bf16[512,256]{1,0:T(8,128)(2,1)}, bf16[512,256]{1,0:T(8,128)(2,1)S(1)}, u32[]{:S(2)}, u32[]{:S(2)}) collective-permute-start(bf16[512,256]{1,0:T(8,128)(2,1)} %refs_10_.1), channel_id=1, source_target_pairs={{0,16},{16,0},{1,17},{17,1},{2,18},{18,2},{3,19},{19,3},{4,20},{20... | collective-permute-start | bytes 786440 | tf_op jit(solution)/shard_map/ppermute | solution.py:520
  2.5 55.8 %collective-permute-start.5 = (bf16[512,1024]{1,0:T(8,128)(2,1)}, bf16[512,1024]{1,0:T(8,128)(2,1)S(1)}, u32[]{:S(2)}, u32[]{:S(2)}) collective-permute-start(bf16[512,1024]{1,0:T(8,128)(2,1)} %refs_2_), channel_id=1, source_target_pairs={{0,16},{16,0},{1,17},{17,1},{2,18},{18,2},{3,19},{19,3},{4,20},{20... | collective-permute-start | bytes 3145736 | tf_op jit(solution)/shard_map/ppermute | solution.py:520
  5.7 52.6 %collective-permute-start.6 = (bf16[1024,512]{1,0:T(8,128)(2,1)}, bf16[1024,512]{1,0:T(8,128)(2,1)S(1)}, u32[]{:S(2)}, u32[]{:S(2)}) collective-permute-start(bf16[1024,512]{1,0:T(8,128)(2,1)} %refs_4_), channel_id=1, source_target_pairs={{0,16},{16,0},{1,17},{17,1},{2,18},{18,2},{3,19},{19,3},{4,20},{20... | collective-permute-start | bytes 3145736 | tf_op jit(solution)/shard_map/ppermute | solution.py:520
  7.2 3.5 %copy-start.4 = (bf16[256,512]{1,0:T(8,128)(2,1)}, bf16[256,512]{1,0:T(8,128)(2,1)S(1)}, u32[]{:S(2)}) copy-start(bf16[256,512]{1,0:T(8,128)(2,1)S(1)} %collective-permute-done.3.refs_8_.refs_9_) | copy-start | bytes 786436
  7.2 1.8 collective-permute-start.2
  9.0 1.7 copy-start.9
  9.0 1.7 copy-start.10
  9.0 1.6 copy-start.11
  58.3 2.9 copy-start.5
  58.3 2.9 copy-start.6
  134.8 35.9 %collective-permute-start.8 = (bf16[4096,512]{1,0:T(8,128)(2,1)}, bf16[4096,512]{1,0:T(8,128)(2,1)}, u32[]{:S(2)}, u32[]{:S(2)}) collective-permute-start(bf16[4096,512]{1,0:T(8,128)(2,1)} %get-tuple-element.77), channel_id=1, source_target_pairs={{0,16},{16,0},{1,17},{17,1},{2,18},{18,2},{3,19},{19,3},{4,20},{20... | collective-permute-start | bytes 12582920 | tf_op jit(solution)/shard_map/ppermute | solution.py:520
  139.0 31.7 %collective-permute-start.7 = (bf16[2048,512]{1,0:T(8,128)(2,1)}, bf16[2048,512]{1,0:T(8,128)(2,1)}, u32[]{:S(2)}, u32[]{:S(2)}) collective-permute-start(bf16[2048,512]{1,0:T(8,128)(2,1)} %get-tuple-element.124), channel_id=1, source_target_pairs={{0,16},{16,0},{1,17},{17,1},{2,18},{18,2},{3,19},{19,3},{4,20},{20... | collective-permute-start | bytes 6291464 | tf_op jit(solution)/shard_map/ppermute | solution.py:520
  139.2 26.1 %copy-start.12 = (f32[8,512]{1,0:T(8,128)S(1)}, f32[8,512]{1,0:T(8,128)}, u32[]{:S(2)}) copy-start(f32[8,512]{1,0:T(8,128)} %get-tuple-element.110) | copy-start | bytes 49156
  165.0 5.0 %collective-permute-start.16 = (bf16[2048,128]{1,0:T(8,128)(2,1)S(1)}, bf16[2048,128]{1,0:T(8,128)(2,1)S(1)}, u32[]{:S(2)}, u32[]{:S(2)}) collective-permute-start(bf16[2048,128]{1,0:T(8,128)(2,1)S(1)} %slice_bitcast_fusion.5), channel_id=1, source_target_pairs={{0,16},{16,0},{1,17},{17,1},{2,18},{18,2},{3,19},{19,3},{4,20},{20... | collective-permute-start | bytes 1572872 | tf_op jit(solution)/shard_map/ppermute | solution.py:520
  167.2 2.2 copy-start.3
  169.4 1.2 copy-start.8
  169.9 5.8 %copy-start.1 = (bf16[8192,512]{1,0:T(8,128)(2,1)}, bf16[8192,512]{1,0:T(8,128)(2,1)S(1)}, u32[]{:S(2)}) copy-start(bf16[8192,512]{1,0:T(8,128)(2,1)S(1)} %constant_dynamic-update-slice_fusion.3) | copy-start | bytes 25165828
  175.7 36.2 %collective-permute-start.10 = (bf16[512,512]{1,0:T(8,128)(2,1)}, bf16[512,512]{1,0:T(8,128)(2,1)S(1)}, u32[]{:S(2)}, u32[]{:S(2)}) collective-permute-start(bf16[512,512]{1,0:T(8,128)(2,1)} %get-tuple-element.150), channel_id=1, source_target_pairs={{0,2},{1,3},{2,0},{3,1},{4,6},{5,7},{6,4},{7,5},{8,10},{9,11},{10,... | collective-permute-start | bytes 1572872 | tf_op jit(solution)/shard_map/ppermute | solution.py:550
  178.4 33.5 %collective-permute-start.11 = (bf16[512,512]{1,0:T(8,128)(2,1)}, bf16[512,512]{1,0:T(8,128)(2,1)S(1)}, u32[]{:S(2)}, u32[]{:S(2)}) collective-permute-start(bf16[512,512]{1,0:T(8,128)(2,1)} %get-tuple-element.149), channel_id=1, source_target_pairs={{0,3},{1,2},{2,1},{3,0},{4,7},{5,6},{6,5},{7,4},{8,11},{9,10},{10,... | collective-permute-start | bytes 1572872 | tf_op jit(solution)/shard_map/ppermute | solution.py:550
  179.8 32.1 %collective-permute-start.9 = (bf16[512,512]{1,0:T(8,128)(2,1)}, bf16[512,512]{1,0:T(8,128)(2,1)S(1)}, u32[]{:S(2)}, u32[]{:S(2)}) collective-permute-start(bf16[512,512]{1,0:T(8,128)(2,1)} %get-tuple-element.151), channel_id=1, source_target_pairs={{0,1},{1,0},{2,3},{3,2},{4,5},{5,4},{6,7},{7,6},{8,9},{9,8},{10,11... | collective-permute-start | bytes 1572872 | tf_op jit(solution)/shard_map/ppermute | solution.py:550
  206.2 31.7 %collective-permute-start.17 = (bf16[2048,128]{1,0:T(8,128)(2,1)}, bf16[2048,128]{1,0:T(8,128)(2,1)S(1)}, u32[]{:S(2)}, u32[]{:S(2)}) collective-permute-start(bf16[2048,128]{1,0:T(8,128)(2,1)} %slice_bitcast_fusion.4), channel_id=1, source_target_pairs={{0,16},{16,0},{1,17},{17,1},{2,18},{18,2},{3,19},{19,3},{4,20},{20... | collective-permute-start | bytes 1572872 | tf_op jit(solution)/shard_map/ppermute | solution.py:520
  212.9 32.9 %collective-permute-start.12 = (bf16[128,512]{1,0:T(8,128)(2,1)}, bf16[128,512]{1,0:T(8,128)(2,1)S(1)}, u32[]{:S(2)}, u32[]{:S(2)}) collective-permute-start(bf16[128,512]{1,0:T(8,128)(2,1)} %get-tuple-element.158), channel_id=1, source_target_pairs={{0,4},{1,5},{2,6},{3,7},{4,0},{5,1},{6,2},{7,3},{8,12},{9,13},{10,... | collective-permute-start | bytes 393224 | tf_op jit(solution)/shard_map/ppermute | solution.py:550
  215.0 32.3 %collective-permute-start.13 = (bf16[128,512]{1,0:T(8,128)(2,1)S(1)}, bf16[128,512]{1,0:T(8,128)(2,1)S(1)}, u32[]{:S(2)}, u32[]{:S(2)}) collective-permute-start(bf16[128,512]{1,0:T(8,128)(2,1)S(1)} %get-tuple-element.157), channel_id=1, source_target_pairs={{0,8},{1,9},{2,10},{3,11},{4,12},{5,13},{6,14},{7,15},{8,0},{9,1},... | collective-permute-start | bytes 393224 | tf_op jit(solution)/shard_map/ppermute | solution.py:550
  217.6 30.0 %collective-permute-start.14 = (bf16[128,512]{1,0:T(8,128)(2,1)S(1)}, bf16[128,512]{1,0:T(8,128)(2,1)S(1)}, u32[]{:S(2)}, u32[]{:S(2)}) collective-permute-start(bf16[128,512]{1,0:T(8,128)(2,1)S(1)} %get-tuple-element.156), channel_id=1, source_target_pairs={{0,12},{1,13},{2,14},{3,15},{4,8},{5,9},{6,10},{7,11},{8,4},{9,5},... | collective-permute-start | bytes 393224 | tf_op jit(solution)/shard_map/ppermute | solution.py:550
  217.6 20.9 %copy-start.7 = (bf16[2,2048,128]{2,1,0:T(8,128)(2,1)S(1)}, bf16[2,2048,128]{2,1,0:T(8,128)(2,1)}, u32[]{:S(2)}) copy-start(bf16[2,2048,128]{2,1,0:T(8,128)(2,1)} %get-tuple-element.109) | copy-start | bytes 3145732
  217.6 26.1 %copy-start.13 = (bf16[1,4,2,128]{3,1,2,0:T(4,128)(2,1)S(1)}, bf16[1,4,2,128]{3,1,2,0:T(4,128)(2,1)}, u32[]{:S(2)}) copy-start(bf16[1,4,2,128]{3,1,2,0:T(4,128)(2,1)} %copy.38) | copy-start | bytes 6148
  237.9 6.0 %collective-permute-start.18 = (bf16[256,128]{1,0:T(8,128)(2,1)S(1)}, bf16[256,128]{1,0:T(8,128)(2,1)S(1)}, u32[]{:S(2)}, u32[]{:S(2)}) collective-permute-start(bf16[256,128]{1,0:T(8,128)(2,1)S(1)} %pad_bitcast_fusion), channel_id=1, source_target_pairs={{0,16},{16,0},{1,17},{17,1},{2,18},{18,2},{3,19},{19,3},{4,20},{20... | collective-permute-start | bytes 196616 | tf_op jit(solution)/shard_map/ppermute | solution.py:520
  238.0 88.7 %collective-permute-start.15 = (bf16[4096,512]{1,0:T(8,128)(2,1)}, bf16[4096,512]{1,0:T(8,128)(2,1)}, u32[]{:S(2)}, u32[]{:S(2)}) collective-permute-start(bf16[4096,512]{1,0:T(8,128)(2,1)} %get-tuple-element.107), channel_id=1, source_target_pairs={{0,16},{16,0},{1,17},{17,1},{2,18},{18,2},{3,19},{19,3},{4,20},{20... | collective-permute-start | bytes 12582920 | tf_op jit(solution)/shard_map/ppermute | solution.py:520
  244.0 11.1 %collective-permute-start.19 = (bf16[1088,128]{1,0:T(8,128)(2,1)S(1)}, bf16[1088,128]{1,0:T(8,128)(2,1)S(1)}, u32[]{:S(2)}, u32[]{:S(2)}) collective-permute-start(bf16[1088,128]{1,0:T(8,128)(2,1)S(1)} %get-tuple-element.153), channel_id=1, source_target_pairs={{0,1},{1,0},{2,3},{3,2},{4,5},{5,4},{6,7},{7,6},{8,9},{9,8},{10,11... | collective-permute-start | bytes 835592 | tf_op jit(solution)/shard_map/ppermute | solution.py:550
  245.8 14.3 %collective-permute-start.20 = (bf16[1088,128]{1,0:T(8,128)(2,1)S(1)}, bf16[1088,128]{1,0:T(8,128)(2,1)S(1)}, u32[]{:S(2)}, u32[]{:S(2)}) collective-permute-start(bf16[1088,128]{1,0:T(8,128)(2,1)S(1)} %get-tuple-element.155), channel_id=1, source_target_pairs={{0,2},{1,3},{2,0},{3,1},{4,6},{5,7},{6,4},{7,5},{8,10},{9,11},{10,... | collective-permute-start | bytes 835592 | tf_op jit(solution)/shard_map/ppermute | solution.py:550
  247.3 12.8 %collective-permute-start.21 = (bf16[1088,128]{1,0:T(8,128)(2,1)S(1)}, bf16[1088,128]{1,0:T(8,128)(2,1)S(1)}, u32[]{:S(2)}, u32[]{:S(2)}) collective-permute-start(bf16[1088,128]{1,0:T(8,128)(2,1)S(1)} %get-tuple-element.154), channel_id=1, source_target_pairs={{0,3},{1,2},{2,1},{3,0},{4,7},{5,6},{6,5},{7,4},{8,11},{9,10},{10,... | collective-permute-start | bytes 835592 | tf_op jit(solution)/shard_map/ppermute | solution.py:550
  247.7 5.0 %collective-permute-start.31 = (bf16[128,512]{1,0:T(8,128)(2,1)S(1)}, bf16[128,512]{1,0:T(8,128)(2,1)S(1)}, u32[]{:S(2)}, u32[]{:S(2)}) collective-permute-start(bf16[128,512]{1,0:T(8,128)(2,1)S(1)} %get-tuple-element.119), channel_id=1, source_target_pairs={{0,4},{1,5},{2,6},{3,7},{4,0},{5,1},{6,2},{7,3},{8,12},{9,13},{10,... | collective-permute-start | bytes 393224 | tf_op jit(solution)/shard_map/ppermute | solution.py:550
  248.7 2.2 copy-start.2
  252.8 11.8 %collective-permute-start.32 = (bf16[128,512]{1,0:T(8,128)(2,1)S(1)}, bf16[128,512]{1,0:T(8,128)(2,1)S(1)}, u32[]{:S(2)}, u32[]{:S(2)}) collective-permute-start(bf16[128,512]{1,0:T(8,128)(2,1)S(1)} %get-tuple-element.119), channel_id=1, source_target_pairs={{0,8},{1,9},{2,10},{3,11},{4,12},{5,13},{6,14},{7,15},{8,0},{9,1},... | collective-permute-start | bytes 393224 | tf_op jit(solution)/shard_map/ppermute | solution.py:550
  255.2 17.8 %collective-permute-start.33 = (bf16[128,512]{1,0:T(8,128)(2,1)S(1)}, bf16[128,512]{1,0:T(8,128)(2,1)S(1)}, u32[]{:S(2)}, u32[]{:S(2)}) collective-permute-start(bf16[128,512]{1,0:T(8,128)(2,1)S(1)} %get-tuple-element.119), channel_id=1, source_target_pairs={{0,12},{1,13},{2,14},{3,15},{4,8},{5,9},{6,10},{7,11},{8,4},{9,5},... | collective-permute-start | bytes 393224 | tf_op jit(solution)/shard_map/ppermute | solution.py:550
  260.3 7.0 %collective-permute-start.22 = (bf16[272,128]{1,0:T(8,128)(2,1)S(1)}, bf16[272,128]{1,0:T(8,128)(2,1)S(1)}, u32[]{:S(2)}, u32[]{:S(2)}) collective-permute-start(bf16[272,128]{1,0:T(8,128)(2,1)S(1)} %get-tuple-element.160), channel_id=1, source_target_pairs={{0,4},{1,5},{2,6},{3,7},{4,0},{5,1},{6,2},{7,3},{8,12},{9,13},{10,... | collective-permute-start | bytes 208904 | tf_op jit(solution)/shard_map/ppermute | solution.py:550
  261.1 10.2 %collective-permute-start.23 = (bf16[272,128]{1,0:T(8,128)(2,1)S(1)}, bf16[272,128]{1,0:T(8,128)(2,1)S(1)}, u32[]{:S(2)}, u32[]{:S(2)}) collective-permute-start(bf16[272,128]{1,0:T(8,128)(2,1)S(1)} %get-tuple-element.162), channel_id=1, source_target_pairs={{0,8},{1,9},{2,10},{3,11},{4,12},{5,13},{6,14},{7,15},{8,0},{9,1},... | collective-permute-start | bytes 208904 | tf_op jit(solution)/shard_map/ppermute | solution.py:550
  264.6 6.7 %collective-permute-start.24 = (bf16[272,128]{1,0:T(8,128)(2,1)S(1)}, bf16[272,128]{1,0:T(8,128)(2,1)S(1)}, u32[]{:S(2)}, u32[]{:S(2)}) collective-permute-start(bf16[272,128]{1,0:T(8,128)(2,1)S(1)} %get-tuple-element.161), channel_id=1, source_target_pairs={{0,12},{1,13},{2,14},{3,15},{4,8},{5,9},{6,10},{7,11},{8,4},{9,5},... | collective-permute-start | bytes 208904 | tf_op jit(solution)/shard_map/ppermute | solution.py:550
  271.4 5.1 %collective-permute-start.25 = (bf16[272,128]{1,0:T(8,128)(2,1)S(1)}, bf16[272,128]{1,0:T(8,128)(2,1)S(1)}, u32[]{:S(2)}, u32[]{:S(2)}) collective-permute-start(bf16[272,128]{1,0:T(8,128)(2,1)S(1)} %get-tuple-element.121), channel_id=1, source_target_pairs={{0,4},{1,5},{2,6},{3,7},{4,0},{5,1},{6,2},{7,3},{8,12},{9,13},{10,... | collective-permute-start | bytes 208904 | tf_op jit(solution)/shard_map/ppermute | solution.py:550
  272.9 49.8 %collective-permute-start.34 = (bf16[512,512]{1,0:T(8,128)(2,1)S(1)}, bf16[512,512]{1,0:T(8,128)(2,1)S(1)}, u32[]{:S(2)}, u32[]{:S(2)}) collective-permute-start(bf16[512,512]{1,0:T(8,128)(2,1)S(1)} %bitcast.164), channel_id=1, source_target_pairs={{0,1},{1,0},{2,3},{3,2},{4,5},{5,4},{6,7},{7,6},{8,9},{9,8},{10,11... | collective-permute-start | bytes 1572872 | tf_op jit(solution)/shard_map/ppermute | solution.py:550
  274.5 48.3 %collective-permute-start.35 = (bf16[512,512]{1,0:T(8,128)(2,1)S(1)}, bf16[512,512]{1,0:T(8,128)(2,1)S(1)}, u32[]{:S(2)}, u32[]{:S(2)}) collective-permute-start(bf16[512,512]{1,0:T(8,128)(2,1)S(1)} %bitcast.165), channel_id=1, source_target_pairs={{0,2},{1,3},{2,0},{3,1},{4,6},{5,7},{6,4},{7,5},{8,10},{9,11},{10,... | collective-permute-start | bytes 1572872 | tf_op jit(solution)/shard_map/ppermute | solution.py:550
  276.0 46.8 %collective-permute-start.36 = (bf16[512,512]{1,0:T(8,128)(2,1)S(1)}, bf16[512,512]{1,0:T(8,128)(2,1)S(1)}, u32[]{:S(2)}, u32[]{:S(2)}) collective-permute-start(bf16[512,512]{1,0:T(8,128)(2,1)S(1)} %bitcast.166), channel_id=1, source_target_pairs={{0,3},{1,2},{2,1},{3,0},{4,7},{5,6},{6,5},{7,4},{8,11},{9,10},{10,... | collective-permute-start | bytes 1572872 | tf_op jit(solution)/shard_map/ppermute | solution.py:550
  276.5 6.0 %collective-permute-start.26 = (bf16[272,128]{1,0:T(8,128)(2,1)S(1)}, bf16[272,128]{1,0:T(8,128)(2,1)S(1)}, u32[]{:S(2)}, u32[]{:S(2)}) collective-permute-start(bf16[272,128]{1,0:T(8,128)(2,1)S(1)} %get-tuple-element.121), channel_id=1, source_target_pairs={{0,8},{1,9},{2,10},{3,11},{4,12},{5,13},{6,14},{7,15},{8,0},{9,1},... | collective-permute-start | bytes 208904 | tf_op jit(solution)/shard_map/ppermute | solution.py:550
  282.4 6.1 %collective-permute-start.27 = (bf16[272,128]{1,0:T(8,128)(2,1)S(1)}, bf16[272,128]{1,0:T(8,128)(2,1)S(1)}, u32[]{:S(2)}, u32[]{:S(2)}) collective-permute-start(bf16[272,128]{1,0:T(8,128)(2,1)S(1)} %get-tuple-element.121), channel_id=1, source_target_pairs={{0,12},{1,13},{2,14},{3,15},{4,8},{5,9},{6,10},{7,11},{8,4},{9,5},... | collective-permute-start | bytes 208904 | tf_op jit(solution)/shard_map/ppermute | solution.py:550
  288.6 14.8 %collective-permute-start.28 = (bf16[1088,128]{1,0:T(8,128)(2,1)S(1)}, bf16[1088,128]{1,0:T(8,128)(2,1)S(1)}, u32[]{:S(2)}, u32[]{:S(2)}) collective-permute-start(bf16[1088,128]{1,0:T(8,128)(2,1)S(1)} %bitcast.170), channel_id=1, source_target_pairs={{0,1},{1,0},{2,3},{3,2},{4,5},{5,4},{6,7},{7,6},{8,9},{9,8},{10,11... | collective-permute-start | bytes 835592 | tf_op jit(solution)/shard_map/ppermute | solution.py:550
  303.4 7.0 %collective-permute-start.29 = (bf16[1088,128]{1,0:T(8,128)(2,1)S(1)}, bf16[1088,128]{1,0:T(8,128)(2,1)S(1)}, u32[]{:S(2)}, u32[]{:S(2)}) collective-permute-start(bf16[1088,128]{1,0:T(8,128)(2,1)S(1)} %bitcast.172), channel_id=1, source_target_pairs={{0,2},{1,3},{2,0},{3,1},{4,6},{5,7},{6,4},{7,5},{8,10},{9,11},{10,... | collective-permute-start | bytes 835592 | tf_op jit(solution)/shard_map/ppermute | solution.py:550
  310.4 7.4 %collective-permute-start.30 = (bf16[1088,128]{1,0:T(8,128)(2,1)S(1)}, bf16[1088,128]{1,0:T(8,128)(2,1)S(1)}, u32[]{:S(2)}, u32[]{:S(2)}) collective-permute-start(bf16[1088,128]{1,0:T(8,128)(2,1)S(1)} %bitcast.173), channel_id=1, source_target_pairs={{0,3},{1,2},{2,1},{3,0},{4,7},{5,6},{6,5},{7,4},{8,11},{9,10},{10,... | collective-permute-start | bytes 835592 | tf_op jit(solution)/shard_map/ppermute | solution.py:550
  329.4 3.4 %copy-start = (bf16[8192,512]{1,0:T(8,128)(2,1)}, bf16[8192,512]{1,0:T(8,128)(2,1)S(1)}, u32[]{:S(2)}) copy-start(bf16[8192,512]{1,0:T(8,128)(2,1)S(1)} %constant_dynamic-update-slice_fusion) | copy-start | bytes 25165828

commit v3 on v2

--- a/solution.py
+++ b/solution.py
@@ -38,6 +38,10 @@
     for start in range(LANES, rows.shape[1], LANES):
         total = total + rows[:, start : start + LANES]
     return total
+
+
+def as_column(row):
+    return jnp.broadcast_to(row, (LANES, row.shape[1])).T
 
 
 def as_row(sums):
@@ -102,9 +106,10 @@
 
 
 def attn_kernel(seqs, place, *refs):
-    (tok, wq0, wq1, wk0, wk1, wv0, wv1, wo0, wo1, vec) = refs[:10]
-    (query_o, keys_o, values_o, mixed_o, signed_o, slope_o, first_o, hidden_o) = refs[10:18]
-    wqkv_t, wo_t = refs[18:20]
+    (tok, wq0, wq1, wk0, wk1, wv0, wv1, wo0, wo1) = refs[:9]
+    gain1, shift1, bout, small0, small1 = refs[9:14]
+    (query_o, keys_o, values_o, mixed_o, signed_o, slope_o, first_o, hidden_o) = refs[14:22]
+    wqkv_t, wo_t, vec = refs[22:25]
     dim = tok.shape[1]
     lanes = seqs * SEQ
 
@@ -115,6 +120,12 @@
             wqkv_t[index * part : (index + 1) * part, :] = turned(ref[...])
         wo_t[:, :part] = turned(wo0[...])
         wo_t[:, part:] = turned(wo1[...])
+        for index, ref in ((0, gain1), (1, shift1), (5, bout)):
+            vec[index * dim : (index + 1) * dim, :] = as_column(ref[...])
+        for index in range(3):
+            for c, ref in enumerate((small0, small1)):
+                start = (2 + index) * dim + c * part
+                vec[start : start + part, :] = as_column(ref[:, index * part : (index + 1) * part])
 
     half = lax.broadcasted_iota(jnp.int32, (HALF, SEQ), 1)
     mask = lax.broadcasted_iota(jnp.int32, (HALF, SEQ), 0) <= jnp.where(half < HALF, half, half - HALF)
@@ -167,9 +178,9 @@
 
 
 def mlp_kernel(seqs, block, place, *refs):
-    (hid, cot, wu0, wu1, wd0, wd1, vec, bup) = refs[:8]
-    (out_o, low_o, grad_o, gvec_o) = refs[8:12]
-    wu_t, wd_t, gup, gdown, gvec, gbup = refs[12:18]
+    (hid, cot, wu0, wu1, wd0, wd1, gain2, shift2, small0, small1) = refs[:10]
+    (act_o, low_o, own_o, other_o, gvec_o) = refs[10:15]
+    wu_t, gup, gdown, gvec, gbup, vec, bup = refs[15:22]
     dim = hid.shape[1]
     units = wu0.shape[1]
     lanes = seqs * SEQ
@@ -177,9 +188,12 @@
 
     @pl.when(step == 0)
     def _():
-        for index, (up, down) in enumerate(((wu0, wd0), (wu1, wd1))):
-            wu_t[index * units : (index + 1) * units, :] = turned(up[...])
-            wd_t[:, index * units : (index + 1) * units] = turned(down[...])
+        for index, (up, small) in enumerate(((wu0, small0), (wu1, small1))):
+            rows = slice(index * units, (index + 1) * units)
+            wu_t[rows, :] = turned(up[...])
+            bup[rows, :] = as_column(small[:, small.shape[1] - units :])
+        for index, ref in enumerate((gain2, shift2)):
+            vec[index * dim : (index + 1) * dim, :] = as_column(ref[...])
         gup[...] = jnp.zeros_like(gup)
         gdown[...] = jnp.zeros_like(gdown)
         gvec[...] = jnp.zeros_like(gvec)
@@ -191,7 +205,6 @@
     gain = wide(vec[0:dim, :], lanes)
     plain, factor = norm_plain(hidden)
     second = (plain * gain + wide(vec[dim : 2 * dim, :], lanes)).astype(BF)
-    ffout = None
     dnorm = None
     for start in range(0, 2 * units, block):
         span = slice(start, start + block)
@@ -203,17 +216,14 @@
         cdf = 0.5 * lax.erf(upper * (1.0 / math.sqrt(2.0))) + 0.5
         density = jnp.exp(-0.5 * (upper * upper)) * (1.0 / math.sqrt(2.0 * math.pi))
         act = (upper * cdf).astype(BF)
-        dup_wide = dact * (cdf + upper * density)
-        dup = dup_wide.astype(BF)
+        dup = (dact * (cdf + upper * density)).astype(BF)
+        for s in range(seqs):
+            act_o[s, span, :] = act[:, s * SEQ : (s + 1) * SEQ]
         gbup[span, :] += lane_fold(dup.astype(F32))
-        out_part = dot(wd_t[:, span], act)
         dn_part = dot(up_ref[:, inner], dup)
-        ffout = out_part if ffout is None else ffout + out_part
         dnorm = dn_part if dnorm is None else dnorm + dn_part
         gup[:, span] += tail_dot(second, dup)
         gdown[span, :] += tail_dot(act, grad_low)
-    out = hidden + ffout + wide(vec[2 * dim : 3 * dim, :], lanes)
-    out_o[...] = out.T.astype(BF)
     gvec[0:dim, :] += lane_fold(dnorm * plain)
     gvec[dim : 2 * dim, :] += lane_fold(dnorm)
     gvec[2 * dim : 3 * dim, :] += lane_fold(grad_out)
@@ -224,22 +234,73 @@
 
     @pl.when(step == pl.num_programs(0) - 1)
     def _():
-        for half in range(2):
+        for half, grad_o in enumerate((own_o, other_o)):
             for index in range(units // dim):
                 start = half * units + index * dim
-                grad_o[half, index * dim : (index + 1) * dim, :] = gup[:, start : start + dim].astype(BF)
-            grad_o[half, units:, :] = gdown[half * units : (half + 1) * units, :].astype(BF)
+                grad_o[index * dim : (index + 1) * dim, :] = gup[:, start : start + dim].astype(BF)
+            grad_o[units:, :] = gdown[half * units : (half + 1) * units, :].astype(BF)
         for index in range(4):
             gvec_o[index : index + 1, :] = as_row(gvec[index * dim : (index + 1) * dim, :])
         for index in range(2 * units // dim):
             gvec_o[4 + index : 5 + index, :] = as_row(gbup[index * dim : (index + 1) * dim, :])
 
 
+def out_kernel(seqs, place, hid, act, wd0, wd1, bdown, out_o, whole_o, wd_t, vec):
+    units = wd0.shape[0]
+
+    @pl.when(pl.program_id(0) == 0)
+    def _():
+        wd_t[:, :units] = turned(wd0[...])
+        wd_t[:, units:] = turned(wd1[...])
+        vec[...] = as_column(bdown[...])
+
+    for s in range(seqs):
+        rows = slice(s * SEQ, (s + 1) * SEQ)
+        out = hid[s] + dot(wd_t[...], act[s]) + wide(vec[...], SEQ)
+        made = out.T.astype(BF)
+        out_o[rows, :] = made
+        whole_o[rows, :] = made
+
+
+def ff_unpack_kernel(total, up_o, down_o):
+    dim, units = up_o.shape
+    for start in range(0, units, dim):
+        up_o[:, start : start + dim] = total[start : start + dim, :].astype(F32)
+    down_o[...] = total[units:, :].astype(F32)
+
+
+def at_unpack_kernel(here, b0, b1, b2, b3, *refs):
+    outs, hold = refs[:-1], refs[-1]
+    size = b0.shape[0]
+    for m, block in enumerate((b0, b1, b2, b3)):
+        hold[here[m]] = block[...]
+    rows = lambda start, count: [
+        hold[k, max(start - k * size, 0) : min(start + count - k * size, size), :].astype(F32)
+        for k in range(4)
+        if start < (k + 1) * size and start + count > k * size
+    ]
+    get = lambda start, count: jnp.concatenate(rows(start, count), axis=0)
+    dim = outs[0].shape[0]
+    for g in range(2):
+        base = g * 4 * dim
+        for index in range(3):
+            outs[index][:, g * LANES : (g + 1) * LANES] = get(base + index * dim, dim)
+        for index in range(dim // LANES):
+            outs[3][g * LANES : (g + 1) * LANES, index * LANES : (index + 1) * LANES] = get(
+                base + 3 * dim + index * LANES, LANES
+            )
+    at = 8 * dim
+    for out in outs[4:]:
+        for start in range(0, out.shape[1], LANES):
+            out[:, start : start + LANES] = get(at // 16 * 16, 16)[at % 16 : at % 16 + 1]
+            at += 1
+
+
 def grad_kernel(seqs, group, *refs):
     (low_i, first_i, query_i, keys_i, values_i, mixed_i, signed_i, slope_i) = refs[:8]
     wo0, wo1 = refs[8:10]
-    (dq_o, dk_o, dv_o, grad_o, gvec_o) = refs[10:15]
-    gqkv, gout, gb = refs[15:18]
+    (dq_o, dk_o, dv_o, own_o, other_o, gvec_o) = refs[10:16]
+    gqkv, gout, gb = refs[16:19]
     dim = low_i.shape[1]
     part = 2 * LANES
     step = pl.program_id(0)
@@ -315,13 +376,13 @@
 
     @pl.when(step == pl.num_programs(0) - 1)
     def _():
-        for c in range(2):
+        for c, grad_o in enumerate((own_o, other_o)):
             for index in range(3):
                 start = index * part + c * LANES
-                grad_o[c, index * dim : (index + 1) * dim, :] = gqkv[:, start : start + LANES].astype(BF)
+                grad_o[index * dim : (index + 1) * dim, :] = gqkv[:, start : start + LANES].astype(BF)
             for index in range(dim // LANES):
                 start = 3 * dim + index * LANES
-                grad_o[c, start : start + LANES, :] = gout[
+                grad_o[start : start + LANES, :] = gout[
                     c * LANES : (c + 1) * LANES, index * LANES : (index + 1) * LANES
                 ].astype(BF)
             gvec_o[c : c + 1, :] = as_row(gb[c * LANES : (c + 1) * LANES, :])
@@ -332,16 +393,17 @@
 
 def input_kernel(seqs, place, *refs):
     tok, dhid, dq0, dk0, dv0, dq1, dk1, dv1 = refs[:8]
-    wq0, wq1, wk0, wk1, wv0, wv1, vec = refs[8:15]
-    tgrad_o, gvec_o = refs[15:17]
-    gvec = refs[17]
+    wq0, wq1, wk0, wk1, wv0, wv1, gain1 = refs[8:15]
+    tgrad_o, whole_o, gvec_o = refs[15:18]
+    gvec, vec = refs[18:20]
     dim = tok.shape[1]
 
     @pl.when(pl.program_id(0) == 0)
     def _():
         gvec[...] = jnp.zeros_like(gvec)
-
-    gain = wide(vec[0:dim, :], SEQ)
+        vec[...] = as_column(gain1[...])
+
+    gain = wide(vec[...], SEQ)
     for s in range(seqs):
         rows = slice(s * SEQ, (s + 1) * SEQ)
         dnorm = None
@@ -356,7 +418,9 @@
         gvec[0:dim, :] += lane_fold(dnorm * plain)
         gvec[dim : 2 * dim, :] += lane_fold(dnorm)
         tgrad = dhid[s].astype(F32) + norm_back(dnorm, plain, factor, gain)
-        tgrad_o[rows, :] = tgrad.T.astype(BF)
+        made = tgrad.T.astype(BF)
+        tgrad_o[rows, :] = made
+        whole_o[rows, :] = made
 
     @pl.when(pl.program_id(0) == pl.num_programs(0) - 1)
     def _():
@@ -392,7 +456,7 @@
     return pl.BlockSpec((seqs,) + dims, lambda i, place: (i,) + (0,) * len(dims))
 
 
-def attn_call(place, tokens, own, weights, vec, seqs):
+def attn_call(place, tokens, own, weights, vectors, seqs):
     dim = tokens.shape[1]
     count = own // SEQ
     steps = count // seqs
@@ -403,18 +467,23 @@
         functools.partial(attn_kernel, seqs),
         grid_spec=prefetch(
             (steps,),
-            [row_block(seqs, dim, steps)] + [whole_vmem()] * 9,
+            [row_block(seqs, dim, steps)] + [whole_vmem()] * 13,
             [placed_seq_block(seqs, *feat)] * 4
             + [placed_seq_block(seqs, *wide_block)] * 2
             + [placed_seq_block(seqs, dim, SEQ)] * 2,
-            [pltpu.VMEM((3 * dim, dim), BF), pltpu.VMEM((dim, dim), BF)],
+            [
+                pltpu.VMEM((3 * dim, dim), BF),
+                pltpu.VMEM((dim, dim), BF),
+                pltpu.VMEM((6 * dim, LANES), F32),
+            ],
         ),
         out_shape=[shape((count,) + feat, BF)] * 4
         + [shape((count,) + wide_block, BF)] * 2
         + [shape((count, dim, SEQ), BF), shape((count, dim, SEQ), F32)],
         compiler_params=params(),
+        cost_estimate=pl.CostEstimate(flops=1, bytes_accessed=1, transcendentals=0),
         name="attn_forward",
-    )(place, tokens, *weights, vec)
+    )(place, tokens, *weights, *vectors)
 
 
 def grad_call(group, low, first, saved, weights, seqs):
@@ -431,12 +500,13 @@
         + [one(HALF + SEQ, SEQ)] * 2
         + [whole_vmem()] * 2,
         out_specs=[seq_block(seqs, part, SEQ), seq_block(seqs, SEQ, part), seq_block(seqs, SEQ, part)]
-        + [whole_vmem()] * 2,
+        + [whole_vmem()] * 3,
         out_shape=[
             shape((count, part, SEQ), BF),
             shape((count, SEQ, part), BF),
             shape((count, SEQ, part), BF),
-            shape((2, 4 * dim, LANES), BF),
+            shape((4 * dim, LANES), BF),
+            shape((4 * dim, LANES), BF),
             shape((8, LANES), F32),
         ],
         scratch_shapes=[
@@ -445,11 +515,12 @@
             pltpu.VMEM((4 * LANES, LANES), F32),
         ],
         compiler_params=params(),
+        cost_estimate=pl.CostEstimate(flops=1, bytes_accessed=1, transcendentals=0),
         name="attn_backward",
     )(low, first, *saved, *weights)
 
 
-def input_call(place, tokens, dhidden, pieces, weights, vec, seqs):
+def input_call(place, tokens, dhidden, pieces, weights, gain1, seqs):
     dim = tokens.shape[1]
     count = dhidden.shape[0]
     steps = count // seqs
@@ -468,20 +539,23 @@
             + [whole_vmem()] * 7,
             [
                 pl.BlockSpec((seqs * SEQ, dim), lambda i, place: (i, 0)),
+                row_block(seqs, dim, steps),
                 whole_vmem(),
             ],
-            [pltpu.VMEM((2 * dim, LANES), F32)],
+            [pltpu.VMEM((2 * dim, LANES), F32), pltpu.VMEM((dim, LANES), F32)],
         ),
         out_shape=[
             jax.ShapeDtypeStruct((count * SEQ, dim), BF),
+            jax.ShapeDtypeStruct(tokens.shape, BF),
             jax.ShapeDtypeStruct((8, dim), F32),
         ],
         compiler_params=params(),
+        cost_estimate=pl.CostEstimate(flops=1, bytes_accessed=1, transcendentals=0),
         name="input_grad",
-    )(place, tokens, dhidden, *pieces, *weights, vec)
-
-
-def mlp_call(place, hidden, cotangent, weights, vec, bup, seqs, block):
+    )(place, tokens, dhidden, *pieces, *weights, gain1)
+
+
+def mlp_call(place, hidden, cotangent, weights, vectors, seqs, block):
     count, dim = hidden.shape[:2]
     steps = count // seqs
     units = weights[0].shape[1]
@@ -490,30 +564,85 @@
         functools.partial(mlp_kernel, seqs, block),
         grid_spec=prefetch(
             (steps,),
-            [placed_seq_block(seqs, dim, SEQ), row_block(seqs, dim, steps)] + [whole_vmem()] * 6,
-            [
-                pl.BlockSpec((seqs * SEQ, dim), lambda i, place: (i, 0)),
-                placed_seq_block(seqs, dim, SEQ),
-            ]
-            + [whole_vmem()] * 2,
+            [placed_seq_block(seqs, dim, SEQ), row_block(seqs, dim, steps)] + [whole_vmem()] * 8,
+            [placed_seq_block(seqs, 2 * units, SEQ), placed_seq_block(seqs, dim, SEQ)]
+            + [whole_vmem()] * 3,
             [
                 pltpu.VMEM((2 * units, dim), BF),
-                pltpu.VMEM((dim, 2 * units), BF),
                 pltpu.VMEM((dim, 2 * units), F32),
                 pltpu.VMEM((2 * units, dim), F32),
                 pltpu.VMEM((4 * dim, LANES), F32),
                 pltpu.VMEM((2 * units, LANES), F32),
+                pltpu.VMEM((2 * dim, LANES), F32),
+                pltpu.VMEM((2 * units, LANES), F32),
             ],
         ),
         out_shape=[
-            shape((count * SEQ, dim), BF),
+            shape((count, 2 * units, SEQ), BF),
             shape((count, dim, SEQ), BF),
-            shape((2, 2 * units, dim), BF),
+            shape((2 * units, dim), BF),
+            shape((2 * units, dim), BF),
             shape((8, dim), F32),
         ],
         compiler_params=params(),
+        cost_estimate=pl.CostEstimate(flops=1, bytes_accessed=1, transcendentals=0),
         name="feed_forward",
-    )(place, hidden, cotangent, *weights, vec, bup)
+    )(place, hidden, cotangent, *weights, *vectors)
+
+
+def out_call(place, hidden, act, weights, bdown, rows, seqs):
+    count, dim = hidden.shape[:2]
+    units = act.shape[1]
+    steps = count // seqs
+    return pl.pallas_call(
+        functools.partial(out_kernel, seqs),
+        grid_spec=prefetch(
+            (steps,),
+            [placed_seq_block(seqs, dim, SEQ), placed_seq_block(seqs, units, SEQ)] + [whole_vmem()] * 3,
+            [
+                pl.BlockSpec((seqs * SEQ, dim), lambda i, place: (i, 0)),
+                row_block(seqs, dim, steps),
+            ],
+            [pltpu.VMEM((dim, units), BF), pltpu.VMEM((dim, LANES), F32)],
+        ),
+        out_shape=[
+            jax.ShapeDtypeStruct((count * SEQ, dim), BF),
+            jax.ShapeDtypeStruct((rows, dim), BF),
+        ],
+        compiler_params=params(),
+        cost_estimate=pl.CostEstimate(flops=1, bytes_accessed=1, transcendentals=0),
+        name="layer_out",
+    )(place, hidden, act, *weights, bdown)
+
+
+def ff_unpack_call(total, units):
+    dim = total.shape[1]
+    return pl.pallas_call(
+        ff_unpack_kernel,
+        in_specs=[whole_vmem()],
+        out_specs=[whole_vmem()] * 2,
+        out_shape=[
+            jax.ShapeDtypeStruct((dim, units), F32),
+            jax.ShapeDtypeStruct((units, dim), F32),
+        ],
+        compiler_params=pltpu.CompilerParams(vmem_limit_bytes=VMEM_LIMIT),
+        name="ff_unpack",
+    )(total)
+
+
+def at_unpack_call(here, blocks, dim, local, sizes):
+    shape = jax.ShapeDtypeStruct
+    outs = [shape((dim, local), F32)] * 3 + [shape((local, dim), F32)]
+    outs += [shape((1, n), F32) for n in sizes]
+    return pl.pallas_call(
+        at_unpack_kernel,
+        in_specs=[pl.BlockSpec(memory_space=pltpu.SMEM)] + [whole_vmem()] * 4,
+        out_specs=[whole_vmem()] * len(outs),
+        out_shape=outs,
+        scratch_shapes=[pltpu.VMEM((4,) + blocks[0].shape, BF)],
+        compiler_params=pltpu.CompilerParams(vmem_limit_bytes=VMEM_LIMIT),
+        name="at_unpack",
+    )(here, *blocks)
 
 
 def shifted(value, axis, count, shift):
@@ -589,22 +718,28 @@
     for w in (wq, wk, wv):
         weights += gathered(w, mp, 1)
     weights += gathered(wo, mp, 0)
-    small = jnp.concatenate([bq, bk, bv, bu])
-    blocks = [small] + [shifted(small, "mp", mp, -r) for r in range(1, mp)]
+    small = jnp.concatenate([bq, bk, bv, bu]).reshape(1, -1)
+    smalls = [small] + [shifted(small, "mp", mp, -r) for r in range(1, mp)]
+    if per > 1:
+        cuts = [0, local, 2 * local, 3 * local, 3 * local + units]
+        smalls = [
+            jnp.concatenate(
+                [
+                    block[:, lo:hi]
+                    for lo, hi in zip(cuts, cuts[1:])
+                    for block in smalls[c * per : (c + 1) * per]
+                ],
+                axis=1,
+            )
+            for c in range(2)
+        ]
     mlp_weights = gathered(wu, mp, 1) + gathered(wd, mp, 0)
-    spread = lambda lo, hi: jnp.concatenate([b[lo:hi] for b in blocks])
-    over = lambda vector: jnp.broadcast_to(vector[:, None], (vector.shape[0], LANES))
-    vec1 = over(
-        jnp.concatenate(
-            [gain1, shift1] + [spread(i * local, (i + 1) * local) for i in range(3)] + [bo]
-        )
-    )
-    vec2 = over(jnp.concatenate([gain2, shift2, bd]))
-    bup = over(spread(3 * local, 3 * local + units))
-
-    def whole(part, others):
-        full = jnp.zeros((rows, dim), BF)
-        for r, block in enumerate([part] + others):
+    gain1, shift1, bo, gain2, shift2, bd = (
+        v.reshape(1, -1) for v in (gain1, shift1, bo, gain2, shift2, bd)
+    )
+
+    def filled(full, others):
+        for r, block in enumerate(others, 1):
             full = lax.dynamic_update_slice_in_dim(full, block, ((me - r) % mp) * own, 0)
         return full
 
@@ -615,9 +750,9 @@
         g, j = divmod(r, per)
         if per == 1:
             return grad[g]
-        up = grad[g, : per * units].reshape(-1, dim, dim)
+        up = grad[g][: per * units].reshape(-1, dim, dim)
         up = jnp.concatenate(list(up), axis=1)[:, j * units : (j + 1) * units]
-        down = grad[g, per * units + j * units : per * units + (j + 1) * units]
+        down = grad[g][per * units + j * units : per * units + (j + 1) * units]
         return jnp.concatenate([up.reshape(-1, dim), down], axis=0)
 
     def at_piece(grads, r):
@@ -626,10 +761,10 @@
             return jnp.concatenate([grad[g] for grad in grads], axis=0)
         parts = []
         for index in range(3):
-            block = [grad[g, index * dim : (index + 1) * dim] for grad in grads]
+            block = [grad[g][index * dim : (index + 1) * dim] for grad in grads]
             block = jnp.concatenate(block, axis=1)[:, j * local : (j + 1) * local]
             parts.append(block.reshape(-1, LANES))
-        block = [grad[g, 3 * dim :].reshape(-1, LANES, LANES) for grad in grads]
+        block = [grad[g][3 * dim :].reshape(-1, LANES, LANES) for grad in grads]
         block = jnp.concatenate([jnp.concatenate(list(b), axis=1) for b in block], axis=0)
         parts.append(block[j * local : (j + 1) * local].reshape(-1, LANES))
         return jnp.concatenate(parts, axis=0)
@@ -637,94 +772,118 @@
     def mp_send(piece):
         return [piece(0)] + [shifted(piece(r), "mp", mp, r) for r in range(1, mp)]
 
-    *saved, first, hidden = attn_call(place, tokens, own, weights, vec1, 2)
+    *saved, first, hidden = attn_call(
+        place, tokens, own, weights, [gain1, shift1, bo] + smalls, 2
+    )
     hidden, mlp_weights = tie((hidden, mlp_weights))
-    out, low, grad_ff, vec_ff = mlp_call(place, hidden, cotangent, mlp_weights, vec2, bup, 2, 512)
-
-    ff = mp_send(lambda r: ff_piece(grad_ff, r))
-    outs = spread_out(out)
-    low, ff[0], out = tie((low, ff[0], out))
-    dq0, dk0, dv0, grad0, vec_at0 = grad_call(0, low, first, saved, weights[6:], 2)
-    ff, outs, dq0 = tie((ff, outs, dq0))
-    ff = dp_sum.scatter(total_of(ff), 0)
-    out_full = whole(out, outs)
+    act, low, *grad_ff, vec_ff = mlp_call(
+        place, hidden, cotangent, mlp_weights, [gain2, shift2] + smalls, 2, 512
+    )
+    ff = total_of(mp_send(lambda r: ff_piece(grad_ff, r)))
+    low, ff = tie((low, ff))
+    ff = lax.psum(ff, "dp")
+    dq0, dk0, dv0, *grad0, vec_at0 = grad_call(0, low, first, saved, weights[6:], 2)
+    at0 = mp_send(lambda r: at_piece([grad0], r)) if per == 1 else []
+    low, at0 = tie((low, at0))
+    dq1, dk1, dv1, *grad1, vec_at1 = grad_call(1, low, first, saved, weights[6:], 2)
+    at0, dq1 = tie((at0, dq1))
+    def finish(low, dq1, at0, act):
+        at1 = mp_send(lambda r: at_piece([grad1], r)) if per == 1 else []
+        low, at1, dq1 = tie((low, at1, dq1))
+        pieces = [dq0, dk0, dv0, dq1, dk1, dv1]
+        tgrad, tgrad_full, vec_in = input_call(place, tokens, low, pieces, weights[:6], gain1, 2)
+        at1, tgrad = tie((at1, tgrad))
+
+        vecs = [vec_ff[:4].reshape(-1, LANES), vec_in[:2].reshape(-1, LANES)]
+        if per == 1:
+            grow = -(-(6 * dim + 3 * local + units) // (16 * dp * LANES)) * 16 * dp
+
+            def vec_piece(r):
+                gb = vec_ff[4 + r * units // dim : 4 + (r + 1) * units // dim].reshape(-1, LANES)
+                bias = [v[2 * i + r : 2 * i + r + 1] for i in range(3) for v in (vec_at0, vec_at1)]
+                made = jnp.concatenate(vecs + bias + [gb], axis=0)
+                return jnp.pad(made, ((0, grow - made.shape[0]), (0, 0))).astype(BF)
+
+            at = jnp.concatenate(
+                [total_of(at0), total_of(at1), total_of(mp_send(vec_piece))], axis=0
+            )
+        else:
+            same = jnp.concatenate([v.reshape(-1) for v in vecs])
+            gbup = vec_ff[4:].reshape(-1)
+            bias = [
+                jnp.concatenate([v[2 * i + c] for c in range(2) for v in (vec_at0, vec_at1)])
+                for i in range(3)
+            ]
+
+            def all_piece(r):
+                vector = jnp.concatenate(
+                    [same]
+                    + [b[r * local : (r + 1) * local] for b in bias]
+                    + [gbup[r * units : (r + 1) * units]]
+                )
+                size = -(-vector.shape[0] // (16 * dp * LANES)) * (16 * dp * LANES)
+                vector = jnp.pad(vector, (0, size - vector.shape[0])).reshape(-1, LANES).astype(BF)
+                return jnp.concatenate([at_piece([grad0, grad1], r), vector], axis=0)
+
+            at = total_of(mp_send(all_piece))
+        at = dp_sum.scatter(at, 0)
+        tgrads = spread_out(tgrad)
+        act, at[0], tgrad = tie((act, at[0], tgrad))
+        out, out_full = out_call(place, hidden, act, mlp_weights[2:], bd, rows, 2)
+        at, out, tgrads = tie((at, out, tgrads))
+        at = total_of(at)
+        stages = len(dp_sum.groups)
+        for stage in range(1, stages):
+            at = total_of(dp_sum.scatter(at, stage))
+        outs = spread_out(out)
+        tgrad_full = filled(tgrad_full, tgrads)
+        for stage in reversed(range(1, stages)):
+            at = dp_sum.join(dp_sum.gather(at, stage), stage)
+        at = dp_sum.gather(at, 0)
+
+        sizes = [dim] * 6 + [local] * 3 + [units]
+        if per == 1 and len(at) == 4:
+            here = dp_sum.place(*dp_sum.groups[0]).astype(jnp.int32) ^ jnp.arange(4, dtype=jnp.int32)
+            *g_at, g0, g1, g2, g3, g4, g5, q0, q1, q2, g_bup = at_unpack_call(
+                here, at, dim, local, sizes
+            )
+            g_qkv, g_out = g_at[:3], g_at[3]
+            g_same = [v.reshape(-1) for v in (g0, g1, g2, g3, g4, g5)]
+            g_bias = [v.reshape(-1) for v in (q0, q1, q2)]
+            g_bup = g_bup.reshape(-1)
+        else:
+            at = dp_sum.join(at, 0).astype(F32)
+            each = dim * local // LANES
+            g_qkv = [at[i * each : (i + 1) * each].reshape(dim, local) for i in range(3)]
+            g_out = at[3 * each : 4 * each].reshape(local, dim)
+            vector = at[4 * each :].reshape(-1)
+            parts = []
+            for size in sizes:
+                parts.append(vector[:size])
+                vector = vector[size:]
+            g_same, g_bias, g_bup = parts[:6], parts[6:9], parts[9]
+        out_full = filled(out_full, outs)
+        return (out_full, tgrad_full, list(g_same), list(g_qkv), list(g_bias), g_out, g_bup)
+
+    blank = jax.eval_shape(finish, low, dq1, at0, act)
+    out_full, tgrad_full, g_same, g_qkv, g_bias, g_out, g_bup = lax.cond(
+        lax.axis_index("dp") != dp,
+        finish,
+        lambda *_: jax.tree.map(lambda v: jnp.zeros(v.shape, v.dtype), blank),
+        low,
+        dq1,
+        at0,
+        act,
+    )
     if per == 1:
-        at0 = mp_send(lambda r: at_piece([grad0], r))
-    low, ff[0] = tie((low, ff[0]))
-    dq1, dk1, dv1, grad1, vec_at1 = grad_call(1, low, first, saved, weights[6:], 2)
-    ff, dq1 = tie((ff, dq1))
-    ff = dp_sum.scatter(total_of(ff), 1)
-    if per == 1:
-        at1 = mp_send(lambda r: at_piece([grad1], r))
-    low, ff[0] = tie((low, ff[0]))
-    tgrad, vec_in = input_call(
-        place, tokens, low, [dq0, dk0, dv0, dq1, dk1, dv1], weights[:6], vec1, 2
-    )
-    tgrads = spread_out(tgrad)
-
-    same = jnp.concatenate([vec_ff[:4].reshape(-1), vec_in[:2].reshape(-1)])
-    gbup = vec_ff[4:].reshape(-1)
-    bias = []
-    for index in range(3):
-        chunks = [v[2 * index + c] for c in range(2) for v in (vec_at0, vec_at1)]
-        bias.append(jnp.concatenate(chunks))
-
-    def vec_piece(r):
-        vector = jnp.concatenate(
-            [same] + [b[r * local : (r + 1) * local] for b in bias] + [gbup[r * units : (r + 1) * units]]
-        )
-        size = -(-vector.shape[0] // (16 * dp * LANES)) * (16 * dp * LANES)
-        return jnp.pad(vector, (0, size - vector.shape[0])).reshape(-1, LANES).astype(BF)
-
-    ff, tgrad = tie((ff, tgrad))
-    if per == 1:
-        vecs = mp_send(vec_piece)
-        at = jnp.concatenate([total_of(at0), total_of(at1), total_of(vecs)], axis=0)
+        g_up, g_down = ff_unpack_call(ff, units)
     else:
-        at = total_of(
-            mp_send(lambda r: jnp.concatenate([at_piece([grad0, grad1], r), vec_piece(r)], axis=0))
-        )
-    stages = len(dp_sum.groups)
-    for stage in range(2, stages):
-        ff = dp_sum.scatter(total_of(ff), stage)
-    ff = total_of(ff)
-    for stage in range(stages):
-        at = total_of(dp_sum.scatter(at, stage))
-    for stage in reversed(range(stages)):
-        ff = dp_sum.join(dp_sum.gather(ff, stage), stage)
-        at = dp_sum.join(dp_sum.gather(at, stage), stage)
-    ff, at = ff.astype(F32), at.astype(F32)
-
-    if per == 1:
-        g_up = jnp.concatenate(list(ff[:units].reshape(-1, dim, dim)), axis=1)
-        tall = 4 * dim
-        halves = [at[:tall], at[tall : 2 * tall]]
-        g_qkv = [
-            jnp.concatenate([h[i * dim : (i + 1) * dim] for h in halves], axis=1) for i in range(3)
-        ]
-        g_out = jnp.concatenate(
-            [
-                jnp.concatenate(list(h[3 * dim :].reshape(-1, LANES, LANES)), axis=1)
-                for h in halves
-            ],
-            axis=0,
-        )
-        used = 2 * tall
-    else:
+        ff = ff.astype(F32)
         g_up = ff[:units].reshape(dim, units)
-        each = dim * local // LANES
-        g_qkv = [at[i * each : (i + 1) * each].reshape(dim, local) for i in range(3)]
-        g_out = at[3 * each : 4 * each].reshape(local, dim)
-        used = 4 * each
-    g_down = ff[units:]
-    vector = at[used:].reshape(-1)
-    g_same = [vector[i * dim : (i + 1) * dim] for i in range(6)]
-    base = 6 * dim
-    g_bias = [vector[base + i * local : base + (i + 1) * local] for i in range(3)]
-    g_bup = vector[base + 3 * local : base + 3 * local + units]
+        g_down = ff[units:]
     return (
         out_full,
-        whole(tgrad, tgrads),
+        tgrad_full,
         g_same[4],
         g_same[5],
         g_qkv[0],

time: 340 us -> 301 us (0.89)
  local copies, waits for them, and re-layouts: 48 us -> 12.5 us
  starting transfers between devices: 45.6 us -> 21.5 us
  Pallas kernels: 188 us -> 207 us
  between operations: 1.56 us -> 14.3 us
  other arithmetic: 13.2 us -> 7.78 us
  waiting for transfers between devices: 36.9 us -> 32.5 us
    ppermute x24 -> x12, starting transfers between devices: 42 us -> 17.5 us  [swap(): lax.ppermute(value, 'dp', [(i, i ^ distance) for i in range(self.count)])]
    pallas_call x0 -> x3, Pallas kernels: none -> 24.4 us  [the longest x1 18 us: out_call(): pl.pallas_call(functools.partial(out_kernel, seqs), grid_spec=prefetch((s...]
    ppermute x24 -> x12, waiting for transfers between devices: 36.8 us -> 18.1 us  [swap(): lax.ppermute(value, 'dp', [(i, i ^ distance) for i in range(self.count)])]
    unnamed x58 -> x32, local copies, waits for them, and re-layouts: 18.5 us -> 0.77 us
    ppermute x13, waiting for transfers between devices: 0.03 us -> 14.4 us  [shifted(): lax.ppermute(value, axis, [(i, (i + shift) % count) for i in range(count)])]
    squeeze x5 -> x0, local copies, waits for them, and re-layouts: 7.8 us -> none  [the longest x1 3.81 us: ff_piece(): return grad[g]]
    concatenate x8 -> x2, other arithmetic: 6.37 us -> 0.81 us  [the longest x1 0.74 us: body(): small = jnp.concatenate([bq, bk, bv, bu]).reshape(1, -1)]
    pallas_call x1, Pallas kernels: 73.6 us -> 68.5 us  [mlp_call(): pl.pallas_call(functools.partial(mlp_kernel, seqs, block), grid_spec=pref...]
  transfers between devices with their start and end apart: 37 -> 26, of which waited for: 8 -> 12; matrix products, arithmetic and copies ran while one was open for 13% -> 5% of each run, Pallas kernels for 34% -> 46%
where the time goes in v3:
time: 301 us; the launch traced here: 296 us
  Pallas kernels  207 us (69%)
  waiting for transfers between devices  32.5 us (11%)
  starting transfers between devices  21.5 us (7%)
  between operations  14.3 us (5%)
  local copies, waits for them, and re-layouts  12.5 us (4%)
  other arithmetic  7.78 us (3%)
    pallas_call x1, Pallas kernels, mlp_call(): pl.pallas_call(functools.partial(mlp_kernel, seqs, block), grid_spec=pref...  68.5 us
    pallas_call x2, Pallas kernels, grad_call(): pl.pallas_call(functools.partial(grad_kernel, seqs, group), grid=(steps,)...  49.5 us
    pallas_call x1, Pallas kernels, attn_call(): pl.pallas_call(functools.partial(attn_kernel, seqs), grid_spec=prefetch((...  47.4 us
    ppermute x12, waiting for transfers between devices, swap(): lax.ppermute(value, 'dp', [(i, i ^ distance) for i in range(self.count)])  18.1 us
    pallas_call x1, Pallas kernels, out_call(): pl.pallas_call(functools.partial(out_kernel, seqs), grid_spec=prefetch((s...  18 us
    pallas_call x1, Pallas kernels, input_call(): pl.pallas_call(functools.partial(input_kernel, seqs), grid_spec=prefetch(...  17.5 us
    ppermute x12, starting transfers between devices, swap(): lax.ppermute(value, 'dp', [(i, i ^ distance) for i in range(self.count)])  17.5 us
    ppermute x13, waiting for transfers between devices, shifted(): lax.ppermute(value, axis, [(i, (i + shift) % count) for i in range(count)])  14.4 us
  transfers between devices with their start and end apart: 26, of which 12 were waited for; matrix products, arithmetic and copies ran while one was open for 5% of the time, Pallas kernels for 46%

profile of v3, /device:TPU:0, one launch (start us, length us, event | category | flops | bytes accessed | tf_op | source)
XLA Modules:
  0.0 296.2 jit_solution(14773086427294591292)
XLA Ops:
  7.2 0.0 all-reduce.4.cloned.1.call-start
  7.2 0.5 collective-permute-start.21
  7.8 0.1 collective-permute-start.22
  7.8 0.4 collective-permute-start.16
  8.3 0.7 pad_maximum_fusion.1
  9.0 0.1 collective-permute-start.20
  9.2 0.4 collective-permute-start.17
  9.6 1.9 collective-permute-done.20.refs_13_.refs_9_
  11.5 0.1 collective-permute-start.18
  11.6 0.5 collective-permute-done.16.refs_2_
  12.1 0.4 collective-permute-start.19
  12.5 0.7 collective-permute-done.18.refs_6_
  13.2 0.7 collective-permute-done.19.refs_8_.refs_9_
  13.9 0.7 copy-done.1
  14.6 47.4 %attn_forward.1 = (bf16[16,2,2,128,256]{4,3,2,1,0:T(8,128)(2,1)}, bf16[16,2,2,128,256]{4,3,2,1,0:T(8,128)(2,1)}, bf16[16,2,2,128,256]{4,3,2,1,0:T(8,128)(2,1)}, ...) custom-call(s32[1]{0:T(128)} %bitcast.27.place, ...), custom_call_target="tpu_custom_call" | custom-call | flops 1 | bytes 1 | tf_op jit(solution)/shard_map/attn_forward/pallas_call | solution.py:466
  62.0 68.5 %feed_forward.1 = (bf16[16,2048,256]{2,1,0:T(8,128)(2,1)}, bf16[16,512,256]{2,1,0:T(8,128)(2,1)}, bf16[2048,512]{1,0:T(8,128)(2,1)}, bf16[2048,512]{1,0:T(8,128)(2,1)}, f32[8,512]{1,0:T(8,128)S(1)}) custom-call(s32[1]{0:T(128)} %bitcast.27.place, f32[16,512,256]{2,1,0:T(8,128)} %get-tuple-element.197.refs_0_, bf16[8192,512]{1,0:T(8,128)(2,1)} %refs_1_.3, ...), custom_call_target="tpu_custom_call" | custom-call | flops 1 | bytes 1 | tf_op jit(solution)/shard_map/feed_forward/pallas_call | solution.py:563
  130.5 0.4 collective-permute-start.23
  131.0 4.0 %collective-permute-done.23 = bf16[2048,512]{1,0:T(8,128)(2,1)S(1)} collective-permute-done((bf16[2048,512]{1,0:T(8,128)(2,1)}, bf16[2048,512]{1,0:T(8,128)(2,1)S(1)}, u32[]{:S(2)}, u32[]{:S(2)}) %collective-permute-start.23) | collective-permute-done | bytes 2097184 | tf_op jit(solution)/shard_map/ppermute | solution.py:649
  135.0 3.5 %add_convert_fusion.4 = bf16[2048,512]{1,0:T(8,128)(2,1)} fusion(bf16[2048,512]{1,0:T(8,128)(2,1)S(1)} %collective-permute-done.23, bf16[2048,512]{1,0:T(8,128)(2,1)} %get-tuple-element.203), kind=kLoop, calls=%fused_computation.25 | loop fusion | flops 4194304 | bytes 6291456 | tf_op jit(solution)/shard_map/convert_element_type | solution.py:665
  138.5 24.8 %attn_backward.2 = (bf16[16,256,256]{2,1,0:T(8,128)(2,1)}, bf16[16,256,256]{2,1,0:T(8,128)(2,1)}, bf16[16,256,256]{2,1,0:T(8,128)(2,1)}, bf16[2048,128]{1,0:T(8,...) custom-call(bf16[16,512,256]{2,1,0:T(8,128)(2,1)} %get-tuple-element.217.refs_0_, ...), custom_call_target="tpu_custom_call" | custom-call | flops 1 | bytes 1 | tf_op jit(solution)/shard_map/attn_backward/pallas_call | solution.py:495
  163.3 0.4 collective-permute-start.24
  163.8 1.9 collective-permute-done.24
  165.7 24.7 %attn_backward.3 = (bf16[16,256,256]{2,1,0:T(8,128)(2,1)}, bf16[16,256,256]{2,1,0:T(8,128)(2,1)}, bf16[16,256,256]{2,1,0:T(8,128)(2,1)}, bf16[2048,128]{1,0:T(8,...) custom-call(bf16[16,512,256]{2,1,0:T(8,128)(2,1)} %get-tuple-element.217.refs_0_, ...), custom_call_target="tpu_custom_call" | custom-call | flops 1 | bytes 1 | tf_op jit(solution)/shard_map/attn_backward/pallas_call | solution.py:495
  190.5 95.0 %conditional.1 = (bf16[8192,512]{1,0:T(8,128)(2,1)}, bf16[8192,512]{1,0:T(8,128)(2,1)}, f32[512]{0:T(512)S(1)}, f32[512]{0:T(512)S(1)}, f32[512]{0:T(512)S(1)}, ...) conditional(s32[]{:T(128)} %convert_element_type.77, () %tuple.24, ...), branch_computations={%region_0.0_spmd, %region_1.0_spmd} | conditional | flops 6969428 | bytes 76370632 | solution.py:869
  190.5 0.4 collective-permute-start
  190.9 1.9 collective-permute-done
  192.8 17.5 %input_grad.1 = (bf16[4096,512]{1,0:T(8,128)(2,1)}, bf16[8192,512]{1,0:T(8,128)(2,1)}, f32[8,512]{1,0:T(8,128)}) custom-call(s32[1]{0:T(128)} %get-tuple-element.59.place, bf16[8192,512]{1,0:T(8,128)(2,1)} %get-tuple-element.70.refs_0_, bf16[16,512,256]{2,1,0:T(8,128)(2,1)} %get-tuple-element.71.refs_1_, bf16[16,256,256]{2,1,0:T(8,128)(2,1)} %get-tuple-element.72.refs_2_, ...), custom_call_target="tpu_custom_call" | custom-call | flops 1 | bytes 1 | tf_op jit(solution)/shard_map/cond/branch_1_fun/input_grad/pallas_call | solution.py:533
  210.3 0.4 collective-permute-start.5
  210.8 1.3 add_convert_fusion.1
  212.1 0.7 slice.67
  212.8 0.1 concatenate.11
  213.0 0.3 collective-permute-start.1
  213.3 1.3 add_convert_fusion
  214.6 0.1 concatenate.10
  214.8 2.8 collective-permute-done.1
  217.6 0.1 pad_maximum_fusion
  217.7 0.1 dynamic-slice_bitcast_fusion
  217.8 2.8 collective-permute-start.2
  220.6 1.5 collective-permute-start.3
  222.1 0.0 collective-permute-start.4
  222.2 18.0 %layer_out.1 = (bf16[4096,512]{1,0:T(8,128)(2,1)}, bf16[8192,512]{1,0:T(8,128)(2,1)}) custom-call(s32[1]{0:T(128)} %get-tuple-element.59.place, f32[16,512,256]{2,1,0:T(8,128)} %get-tuple-element.60.hid, bf16[16,2048,256]{2,1,0:T(8,128)(2,1)} %get-tuple-element.93.act, bf16[1024,512]{1,0:T(8,128)(2,1)S(1)} %get-tuple-element.94.wd0, ...), custom_call_target="tpu_custom_call" | custom-call | flops 1 | bytes 1 | tf_op jit(solution)/shard_map/cond/branch_1_fun/layer_out/pallas_call | solution.py:597
  240.2 0.1 collective-permute-start.6
  240.3 0.1 add_convert_fusion.2
  240.5 4.2 %collective-permute-start.9 = (bf16[272,128]{1,0:T(8,128)(2,1)S(1)}, bf16[272,128]{1,0:T(8,128)(2,1)S(1)}, u32[]{:S(2)}, u32[]{:S(2)}) collective-permute-start(bf16[272,128]{1,0:T(8,128)(2,1)S(1)} %get-tuple-element.261), channel_id=1, source_target_pairs={{0,12},{1,13},{2,14},{3,15},{4,8},{5,9},{6,10},{7,11},{8,4},{9,5},... | collective-permute-start | bytes 208904 | tf_op jit(solution)/shard_map/cond/branch_1_fun/ppermute | solution.py:679
  244.7 0.6 collective-permute-start.7
  245.3 2.3 collective-permute-done.9
  247.7 3.6 %collective-permute-done.8 = bf16[272,128]{1,0:T(8,128)(2,1)S(1)} collective-permute-done((bf16[272,128]{1,0:T(8,128)(2,1)S(1)}, bf16[272,128]{1,0:T(8,128)(2,1)S(1)}, u32[]{:S(2)}, u32[]{:S(2)}) %collective-permute-start.8) | collective-permute-done | bytes 69664 | tf_op jit(solution)/shard_map/cond/branch_1_fun/ppermute | solution.py:679
  251.3 0.1 bitcast_dynamic-update-slice_fusion.3
  251.4 1.1 collective-permute-start.10
  252.4 0.5 iota_xor_fusion.here
  252.9 1.9 collective-permute-start.11
  254.9 1.4 collective-permute-start.12
  256.3 8.1 %collective-permute-done.11 = bf16[272,128]{1,0:T(8,128)(2,1)S(1)} collective-permute-done((bf16[272,128]{1,0:T(8,128)(2,1)S(1)}, bf16[272,128]{1,0:T(8,128)(2,1)S(1)}, u32[]{:S(2)}, u32[]{:S(2)}) %collective-permute-start.11) | collective-permute-done | bytes 69664 | tf_op jit(solution)/shard_map/cond/branch_1_fun/ppermute | solution.py:679
  264.5 2.1 collective-permute-start.13
  266.6 1.5 collective-permute-start.14
  268.1 0.2 collective-permute-start.15
  268.4 4.5 %constant_dynamic-update-slice_fusion = bf16[8192,512]{1,0:T(8,128)(2,1)} fusion(bf16[8192,512]{1,0:T(8,128)(2,1)} %get-tuple-element.102, bf16[4096,512]{1,0:T(8,128)(2,1)} %collective-permute-done.5, s32[]{:T(128)S(6)} %select_n.56), kind=kLoop, calls=%fused_computation.22 | loop fusion | bytes 8388612 | tf_op jit(solution)/shard_map/cond/branch_1_fun/dynamic_update_slice | solution.py:743
  272.9 4.0 %collective-permute-done.14.b2 = bf16[1088,128]{1,0:T(8,128)(2,1)S(1)} collective-permute-done((bf16[1088,128]{1,0:T(8,128)(2,1)S(1)}, bf16[1088,128]{1,0:T(8,128)(2,1)S(1)}, u32[]{:S(2)}, u32[]{:S(2)}) %collective-permute-start.14) | collective-permute-done | bytes 278560 | tf_op jit(solution)/shard_map/cond/branch_1_fun/ppermute | solution.py:679
  276.9 0.7 copy-done.7
  277.6 0.7 copy-done.8
  278.3 2.7 at_unpack.1
  281.0 4.5 %constant_dynamic-update-slice_fusion.1 = bf16[8192,512]{1,0:T(8,128)(2,1)} fusion(bf16[8192,512]{1,0:T(8,128)(2,1)} %get-tuple-element.97, bf16[4096,512]{1,0:T(8,128)(2,1)} %collective-permute-done.6, s32[]{:T(128)S(6)} %select_n.56), kind=kLoop, calls=%fused_computation.23 | loop fusion | bytes 8388612 | tf_op jit(solution)/shard_map/cond/branch_1_fun/dynamic_update_slice | solution.py:743
  285.5 0.0 all-reduce.4.cloned.1.call-done.total
  285.5 3.7 %ff_unpack.1 = (f32[512,1024]{1,0:T(8,128)}, f32[1024,512]{1,0:T(8,128)}) custom-call(bf16[2048,512]{1,0:T(8,128)(2,1)} %all-reduce.4.cloned.1.call-done.total), custom_call_target="tpu_custom_call" | custom-call | tf_op jit(solution)/shard_map/ff_unpack/pallas_call | solution.py:620
  (70 shorter events, 0.4 us)
Async XLA Ops:
  7.2 278.3 %all-reduce.4.cloned.1.call-start = ((), (), s32[]{:S(2)}) async-start(), calls=%async_computation | async-start | bytes 4194304 | tf_op jit(solution)/shard_map/psum | solution.py:784
  7.2 54.8 %collective-permute-start.21 = (bf16[512,1024]{1,0:T(8,128)(2,1)}, bf16[512,1024]{1,0:T(8,128)(2,1)}, u32[]{:S(2)}, u32[]{:S(2)}) collective-permute-start(bf16[512,1024]{1,0:T(8,128)(2,1)} %refs_2_), channel_id=1, source_target_pairs={{0,16},{16,0},{1,17},{17,1},{2,18},{18,2},{3,19},{19,3},{4,20},{20... | collective-permute-start | bytes 3145736 | tf_op jit(solution)/shard_map/ppermute | solution.py:649
  7.8 54.3 %collective-permute-start.22 = (bf16[1024,512]{1,0:T(8,128)(2,1)}, bf16[1024,512]{1,0:T(8,128)(2,1)S(1)}, u32[]{:S(2)}, u32[]{:S(2)}) collective-permute-start(bf16[1024,512]{1,0:T(8,128)(2,1)} %refs_4_), channel_id=1, source_target_pairs={{0,16},{16,0},{1,17},{17,1},{2,18},{18,2},{3,19},{19,3},{4,20},{20... | collective-permute-start | bytes 3145736 | tf_op jit(solution)/shard_map/ppermute | solution.py:649
  7.8 4.3 %collective-permute-start.16 = (bf16[512,256]{1,0:T(8,128)(2,1)}, bf16[512,256]{1,0:T(8,128)(2,1)S(1)}, u32[]{:S(2)}, u32[]{:S(2)}) collective-permute-start(bf16[512,256]{1,0:T(8,128)(2,1)} %refs_1_.2), channel_id=1, source_target_pairs={{0,16},{16,0},{1,17},{17,1},{2,18},{18,2},{3,19},{19,3},{4,20},{20... | collective-permute-start | bytes 786440 | tf_op jit(solution)/shard_map/ppermute | solution.py:649
  9.0 4.9 %copy-start.9 = (f32[1,1792]{1,0:T(1,128)}, f32[1,1792]{1,0:T(1,128)S(1)}, u32[]{:S(2)}) copy-start(f32[1,1792]{1,0:T(1,128)S(1)} %reshape.120.refs_12_.refs_8_) | copy-start | bytes 21508
  9.0 2.5 collective-permute-start.20
  9.2 3.3 %collective-permute-start.17 = (bf16[512,256]{1,0:T(8,128)(2,1)}, bf16[512,256]{1,0:T(8,128)(2,1)S(1)}, u32[]{:S(2)}, u32[]{:S(2)}) collective-permute-start(bf16[512,256]{1,0:T(8,128)(2,1)} %refs_3_.1), channel_id=1, source_target_pairs={{0,16},{16,0},{1,17},{17,1},{2,18},{18,2},{3,19},{19,3},{4,20},{20... | collective-permute-start | bytes 786440 | tf_op jit(solution)/shard_map/ppermute | solution.py:649
  11.5 2.4 copy-start.10
  11.5 1.7 collective-permute-start.18
  12.1 1.7 collective-permute-start.19
  13.9 0.7 copy-start.1
  14.6 47.4 %copy-start = (bf16[1024,512]{1,0:T(8,128)(2,1)S(1)}, bf16[1024,512]{1,0:T(8,128)(2,1)}, u32[]{:S(2)}) copy-start(bf16[1024,512]{1,0:T(8,128)(2,1)} %refs_4_) | copy-start | bytes 3145732
  130.5 4.4 %collective-permute-start.23 = (bf16[2048,512]{1,0:T(8,128)(2,1)}, bf16[2048,512]{1,0:T(8,128)(2,1)S(1)}, u32[]{:S(2)}, u32[]{:S(2)}) collective-permute-start(bf16[2048,512]{1,0:T(8,128)(2,1)} %get-tuple-element.204), channel_id=1, source_target_pairs={{0,16},{16,0},{1,17},{17,1},{2,18},{18,2},{3,19},{19,3},{4,20},{20... | collective-permute-start | bytes 6291464 | tf_op jit(solution)/shard_map/ppermute | solution.py:649
  163.3 2.3 collective-permute-start.24
  165.7 24.8 %copy-start.3 = (bf16[512,256]{1,0:T(8,128)(2,1)S(1)}, bf16[512,256]{1,0:T(8,128)(2,1)}, u32[]{:S(2)}) copy-start(bf16[512,256]{1,0:T(8,128)(2,1)} %refs_1_.2) | copy-start | bytes 786436
  165.7 24.8 %copy-start.4 = (bf16[512,256]{1,0:T(8,128)(2,1)S(1)}, bf16[512,256]{1,0:T(8,128)(2,1)}, u32[]{:S(2)}) copy-start(bf16[512,256]{1,0:T(8,128)(2,1)} %refs_3_.1) | copy-start | bytes 786436
  165.7 24.8 %copy-start.5 = (bf16[512,256]{1,0:T(8,128)(2,1)S(1)}, bf16[512,256]{1,0:T(8,128)(2,1)}, u32[]{:S(2)}) copy-start(bf16[512,256]{1,0:T(8,128)(2,1)} %refs_5_.1) | copy-start | bytes 786436
  165.7 24.8 %copy-start.11 = (f32[512]{0:T(512)S(1)}, f32[512]{0:T(512)}, u32[]{:S(2)}) copy-start(f32[512]{0:T(512)} %param.21) | copy-start | bytes 6148
  165.7 24.8 %copy-start.12 = (f32[512]{0:T(512)S(1)}, f32[512]{0:T(512)}, u32[]{:S(2)}) copy-start(f32[512]{0:T(512)} %param.36) | copy-start | bytes 6148
  190.5 2.3 collective-permute-start
  210.3 29.9 %collective-permute-start.5 = (bf16[4096,512]{1,0:T(8,128)(2,1)}, bf16[4096,512]{1,0:T(8,128)(2,1)}, u32[]{:S(2)}, u32[]{:S(2)}) collective-permute-start(bf16[4096,512]{1,0:T(8,128)(2,1)} %get-tuple-element.92), channel_id=1, source_target_pairs={{0,16},{16,0},{1,17},{17,1},{2,18},{18,2},{3,19},{19,3},{4,20},{20... | collective-permute-start | bytes 12582920 | tf_op jit(solution)/shard_map/cond/branch_1_fun/ppermute | solution.py:649
  213.0 4.6 %collective-permute-start.1 = (bf16[256,128]{1,0:T(8,128)(2,1)S(1)}, bf16[256,128]{1,0:T(8,128)(2,1)S(1)}, u32[]{:S(2)}, u32[]{:S(2)}) collective-permute-start(bf16[256,128]{1,0:T(8,128)(2,1)S(1)} %pad.8), channel_id=1, source_target_pairs={{0,16},{16,0},{1,17},{17,1},{2,18},{18,2},{3,19},{19,3},{4,20},{20... | collective-permute-start | bytes 196616 | tf_op jit(solution)/shard_map/cond/branch_1_fun/ppermute | solution.py:649
  217.8 22.4 %collective-permute-start.2 = (bf16[1088,128]{1,0:T(8,128)(2,1)S(1)}, bf16[1088,128]{1,0:T(8,128)(2,1)S(1)}, u32[]{:S(2)}, u32[]{:S(2)}) collective-permute-start(bf16[1088,128]{1,0:T(8,128)(2,1)S(1)} %get-tuple-element.258), channel_id=1, source_target_pairs={{0,1},{1,0},{2,3},{3,2},{4,5},{5,4},{6,7},{7,6},{8,9},{9,8},{10,11... | collective-permute-start | bytes 835592 | tf_op jit(solution)/shard_map/cond/branch_1_fun/ppermute | solution.py:679
  220.6 19.6 %collective-permute-start.3 = (bf16[1088,128]{1,0:T(8,128)(2,1)S(1)}, bf16[1088,128]{1,0:T(8,128)(2,1)S(1)}, u32[]{:S(2)}, u32[]{:S(2)}) collective-permute-start(bf16[1088,128]{1,0:T(8,128)(2,1)S(1)} %get-tuple-element.257), channel_id=1, source_target_pairs={{0,2},{1,3},{2,0},{3,1},{4,6},{5,7},{6,4},{7,5},{8,10},{9,11},{10,... | collective-permute-start | bytes 835592 | tf_op jit(solution)/shard_map/cond/branch_1_fun/ppermute | solution.py:679
  222.1 18.1 %collective-permute-start.4 = (bf16[1088,128]{1,0:T(8,128)(2,1)S(1)}, bf16[1088,128]{1,0:T(8,128)(2,1)S(1)}, u32[]{:S(2)}, u32[]{:S(2)}) collective-permute-start(bf16[1088,128]{1,0:T(8,128)(2,1)S(1)} %get-tuple-element.256), channel_id=1, source_target_pairs={{0,3},{1,2},{2,1},{3,0},{4,7},{5,6},{6,5},{7,4},{8,11},{9,10},{10,... | collective-permute-start | bytes 835592 | tf_op jit(solution)/shard_map/cond/branch_1_fun/ppermute | solution.py:679
  240.2 40.7 %collective-permute-start.6 = (bf16[4096,512]{1,0:T(8,128)(2,1)}, bf16[4096,512]{1,0:T(8,128)(2,1)}, u32[]{:S(2)}, u32[]{:S(2)}) collective-permute-start(bf16[4096,512]{1,0:T(8,128)(2,1)} %get-tuple-element.100), channel_id=1, source_target_pairs={{0,16},{16,0},{1,17},{17,1},{2,18},{18,2},{3,19},{19,3},{4,20},{20... | collective-permute-start | bytes 12582920 | tf_op jit(solution)/shard_map/cond/branch_1_fun/ppermute | solution.py:649
  240.5 7.2 %collective-permute-start.9 = (bf16[272,128]{1,0:T(8,128)(2,1)S(1)}, bf16[272,128]{1,0:T(8,128)(2,1)S(1)}, u32[]{:S(2)}, u32[]{:S(2)}) collective-permute-start(bf16[272,128]{1,0:T(8,128)(2,1)S(1)} %get-tuple-element.261), channel_id=1, source_target_pairs={{0,12},{1,13},{2,14},{3,15},{4,8},{5,9},{6,10},{7,11},{8,4},{9,5},... | collective-permute-start | bytes 208904 | tf_op jit(solution)/shard_map/cond/branch_1_fun/ppermute | solution.py:679
  244.7 6.5 %collective-permute-start.8 = (bf16[272,128]{1,0:T(8,128)(2,1)S(1)}, bf16[272,128]{1,0:T(8,128)(2,1)S(1)}, u32[]{:S(2)}, u32[]{:S(2)}) collective-permute-start(bf16[272,128]{1,0:T(8,128)(2,1)S(1)} %get-tuple-element.262), channel_id=1, source_target_pairs={{0,8},{1,9},{2,10},{3,11},{4,12},{5,13},{6,14},{7,15},{8,0},{9,1},... | collective-permute-start | bytes 208904 | tf_op jit(solution)/shard_map/cond/branch_1_fun/ppermute | solution.py:679
  244.7 6.5 %collective-permute-start.7 = (bf16[272,128]{1,0:T(8,128)(2,1)S(1)}, bf16[272,128]{1,0:T(8,128)(2,1)S(1)}, u32[]{:S(2)}, u32[]{:S(2)}) collective-permute-start(bf16[272,128]{1,0:T(8,128)(2,1)S(1)} %get-tuple-element.260), channel_id=1, source_target_pairs={{0,4},{1,5},{2,6},{3,7},{4,0},{5,1},{6,2},{7,3},{8,12},{9,13},{10,... | collective-permute-start | bytes 208904 | tf_op jit(solution)/shard_map/cond/branch_1_fun/ppermute | solution.py:679
  251.4 5.0 %collective-permute-start.10 = (bf16[272,128]{1,0:T(8,128)(2,1)S(1)}, bf16[272,128]{1,0:T(8,128)(2,1)S(1)}, u32[]{:S(2)}, u32[]{:S(2)}) collective-permute-start(bf16[272,128]{1,0:T(8,128)(2,1)S(1)} %get-tuple-element.255), channel_id=1, source_target_pairs={{0,4},{1,5},{2,6},{3,7},{4,0},{5,1},{6,2},{7,3},{8,12},{9,13},{10,... | collective-permute-start | bytes 208904 | tf_op jit(solution)/shard_map/cond/branch_1_fun/ppermute | solution.py:679
  252.9 11.5 %collective-permute-start.11 = (bf16[272,128]{1,0:T(8,128)(2,1)S(1)}, bf16[272,128]{1,0:T(8,128)(2,1)S(1)}, u32[]{:S(2)}, u32[]{:S(2)}) collective-permute-start(bf16[272,128]{1,0:T(8,128)(2,1)S(1)} %get-tuple-element.255), channel_id=1, source_target_pairs={{0,8},{1,9},{2,10},{3,11},{4,12},{5,13},{6,14},{7,15},{8,0},{9,1},... | collective-permute-start | bytes 208904 | tf_op jit(solution)/shard_map/cond/branch_1_fun/ppermute | solution.py:679
  254.9 9.6 %collective-permute-start.12 = (bf16[272,128]{1,0:T(8,128)(2,1)S(1)}, bf16[272,128]{1,0:T(8,128)(2,1)S(1)}, u32[]{:S(2)}, u32[]{:S(2)}) collective-permute-start(bf16[272,128]{1,0:T(8,128)(2,1)S(1)} %get-tuple-element.255), channel_id=1, source_target_pairs={{0,12},{1,13},{2,14},{3,15},{4,8},{5,9},{6,10},{7,11},{8,4},{9,5},... | collective-permute-start | bytes 208904 | tf_op jit(solution)/shard_map/cond/branch_1_fun/ppermute | solution.py:679
  264.5 8.3 %copy-start.2 = (bf16[4,272,128]{2,1,0:T(8,128)(2,1)}, bf16[4,272,128]{2,1,0:T(8,128)(2,1)S(1)}, u32[]{:S(2)}) copy-start(bf16[4,272,128]{2,1,0:T(8,128)(2,1)S(1)} %bitcast_dynamic-update-slice_fusion) | copy-start | bytes 835588 | tf_op jit(solution)/shard_map/cond
  264.5 8.3 %collective-permute-start.13 = (bf16[1088,128]{1,0:T(8,128)(2,1)S(1)}, bf16[1088,128]{1,0:T(8,128)(2,1)S(1)}, u32[]{:S(2)}, u32[]{:S(2)}) collective-permute-start(bf16[1088,128]{1,0:T(8,128)(2,1)S(1)} %bitcast.49), channel_id=1, source_target_pairs={{0,1},{1,0},{2,3},{3,2},{4,5},{5,4},{6,7},{7,6},{8,9},{9,8},{10,11... | collective-permute-start | bytes 835592 | tf_op jit(solution)/shard_map/cond/branch_1_fun/ppermute | solution.py:679
  266.6 10.2 %collective-permute-start.14 = (bf16[1088,128]{1,0:T(8,128)(2,1)S(1)}, bf16[1088,128]{1,0:T(8,128)(2,1)S(1)}, u32[]{:S(2)}, u32[]{:S(2)}) collective-permute-start(bf16[1088,128]{1,0:T(8,128)(2,1)S(1)} %bitcast.50), channel_id=1, source_target_pairs={{0,2},{1,3},{2,0},{3,1},{4,6},{5,7},{6,4},{7,5},{8,10},{9,11},{10,... | collective-permute-start | bytes 835592 | tf_op jit(solution)/shard_map/cond/branch_1_fun/ppermute | solution.py:679
  268.1 8.7 %collective-permute-start.15 = (bf16[1088,128]{1,0:T(8,128)(2,1)S(1)}, bf16[1088,128]{1,0:T(8,128)(2,1)S(1)}, u32[]{:S(2)}, u32[]{:S(2)}) collective-permute-start(bf16[1088,128]{1,0:T(8,128)(2,1)S(1)} %bitcast.51), channel_id=1, source_target_pairs={{0,3},{1,2},{2,1},{3,0},{4,7},{5,6},{6,5},{7,4},{8,11},{9,10},{10,... | collective-permute-start | bytes 835592 | tf_op jit(solution)/shard_map/cond/branch_1_fun/ppermute | solution.py:679
  272.9 4.0 %copy-start.6 = (bf16[1088,128]{1,0:T(8,128)(2,1)}, bf16[1088,128]{1,0:T(8,128)(2,1)S(1)}, u32[]{:S(2)}) copy-start(bf16[1088,128]{1,0:T(8,128)(2,1)S(1)} %collective-permute-done.13.b1) | copy-start | bytes 835588 | tf_op jit(solution)/shard_map/cond
  276.9 0.7 copy-start.7
  277.6 0.7 copy-start.8
  285.4 3.8 %copy-start.13 = (f32[512]{0:T(512)}, f32[512]{0:T(512)S(1)}, u32[]{:S(2)}) copy-start(f32[512]{0:T(512)S(1)} %get-tuple-element.190) | copy-start | bytes 6148
  285.4 3.8 %copy-start.14 = (f32[512]{0:T(512)}, f32[512]{0:T(512)S(1)}, u32[]{:S(2)}) copy-start(f32[512]{0:T(512)S(1)} %get-tuple-element.191) | copy-start | bytes 6148
  285.4 3.8 %copy-start.15 = (f32[512]{0:T(512)}, f32[512]{0:T(512)S(1)}, u32[]{:S(2)}) copy-start(f32[512]{0:T(512)S(1)} %get-tuple-element.195) | copy-start | bytes 6148
  285.4 3.8 %copy-start.16 = (f32[512]{0:T(512)}, f32[512]{0:T(512)S(1)}, u32[]{:S(2)}) copy-start(f32[512]{0:T(512)S(1)} %get-tuple-element.189) | copy-start | bytes 6148
  285.4 3.8 %copy-start.17 = (f32[512]{0:T(512)}, f32[512]{0:T(512)S(1)}, u32[]{:S(2)}) copy-start(f32[512]{0:T(512)S(1)} %get-tuple-element.180) | copy-start | bytes 6148
  285.5 3.8 %copy-start.18 = (f32[512]{0:T(512)}, f32[512]{0:T(512)S(1)}, u32[]{:S(2)}) copy-start(f32[512]{0:T(512)S(1)} %get-tuple-element.181) | copy-start | bytes 6148
  285.5 3.8 %copy-start.19 = (f32[256]{0:T(256)}, f32[256]{0:T(256)S(1)}, u32[]{:S(2)}) copy-start(f32[256]{0:T(256)S(1)} %get-tuple-element.183) | copy-start | bytes 3076
Sparse Core Ops, SparseCore 0:
  138.7 140.5 all-reduce.3

commit v4 on v3

--- a/solution.py
+++ b/solution.py
@@ -15,6 +15,7 @@
 BF = jnp.bfloat16
 F32 = jnp.float32
 VMEM_LIMIT = 60 * 1024 * 1024
+SEQS = {"attn": 4, "mlp": 2, "grad": 2, "input": 4, "out": 4}
 
 
 def dot(left, right):
@@ -99,17 +100,16 @@
         magnitude = jnp.where(mask, root, -1e30)
     top = jnp.max(magnitude, axis=0, keepdims=True)
     expo = jnp.exp(magnitude - top)
-    probs = expo * (1.0 / jnp.sum(expo, axis=0, keepdims=True))
-    sign = scores * inverse
-    slope = inverse * inverse * inverse + sign * sign
-    return (sign * probs).astype(BF), (probs * slope).astype(BF)
+    norm = 1.0 / jnp.sum(expo, axis=0, keepdims=True)
+    low_expo, sign, low = expo.astype(BF), (scores * inverse).astype(BF), inverse.astype(BF)
+    return sign * low_expo, (low * low * low + sign * sign) * low_expo, norm
 
 
 def attn_kernel(seqs, place, *refs):
     (tok, wq0, wq1, wk0, wk1, wv0, wv1, wo0, wo1) = refs[:9]
     gain1, shift1, bout, small0, small1 = refs[9:14]
-    (query_o, keys_o, values_o, mixed_o, signed_o, slope_o, first_o, hidden_o) = refs[14:22]
-    wqkv_t, wo_t, vec = refs[22:25]
+    (query_o, keys_o, values_o, mixed_o, signed_o, slope_o, norm_o, first_o, hidden_o) = refs[14:23]
+    wqkv_t, wo_t, vec = refs[23:26]
     dim = tok.shape[1]
     lanes = seqs * SEQ
 
@@ -130,57 +130,79 @@
     half = lax.broadcasted_iota(jnp.int32, (HALF, SEQ), 1)
     mask = lax.broadcasted_iota(jnp.int32, (HALF, SEQ), 0) <= jnp.where(half < HALF, half, half - HALF)
     pairs = dim // LANES
-    x = tok[...].astype(F32).T
-    plain, _ = norm_plain(x)
-    first = (plain * wide(vec[0:dim, :], lanes) + wide(vec[dim : 2 * dim, :], lanes)).astype(BF)
-    outs = []
-    for index in range(3):
-        made = dot(wqkv_t[index * dim : (index + 1) * dim, :], first)
-        made = made + wide(vec[(2 + index) * dim : (3 + index) * dim, :], lanes)
-        made = made.astype(BF)
-        if index == 0:
-            made = made * jnp.asarray(1.0 / math.sqrt(HEAD_DIM), BF)
-        outs.append(made)
-    query, keys, values = outs
-    mixed_all = []
+    scale = jnp.asarray(1.0 / math.sqrt(HEAD_DIM), BF)
+
+    def prepare(s):
+        x = tok[s * SEQ : (s + 1) * SEQ, :].astype(F32).T
+        plain, _ = norm_plain(x)
+        first = (plain * wide(vec[0:dim, :], SEQ) + wide(vec[dim : 2 * dim, :], SEQ)).astype(BF)
+        first_o[s] = first
+        return first
+
+    def project(s, p, first):
+        c, g = divmod(p, 2)
+        made = []
+        for index in range(3):
+            rows = slice(index * dim + p * LANES, index * dim + (p + 1) * LANES)
+            bias = slice(2 * dim + rows.start, 2 * dim + rows.stop)
+            made.append((dot(wqkv_t[rows, :], first) + wide(vec[bias, :], SEQ)).astype(BF))
+        query, keys, values = made[0] * scale, made[1], made[2]
+        query_o[s, c, g], keys_o[s, c, g], values_o[s, c, g] = query, keys, values
+        near_q, far_q = pair_near_far(query)
+        kp = turned(keys)
+        return dot(kp[:HALF], near_q), dot(kp, far_q), values
+
+    def mix(s, p, near_s, far_s, values):
+        c, g = divmod(p, 2)
+        near, near_g, near_n = attend(near_s, mask)
+        far, far_g, far_n = attend(far_s, mask)
+        norms = [
+            jnp.concatenate([near_n[:, lanes], far_n[:, lanes]], axis=1)
+            for lanes in (slice(0, HALF), slice(HALF, SEQ))
+        ]
+        signed_o[s, c, g, :HALF], signed_o[s, c, g, HALF:] = near, far
+        slope_o[s, c, g, :HALF], slope_o[s, c, g, HALF:] = near_g, far_g
+        near_m, far_m = dot(values[:, :HALF], near), dot(values, far)
+        made = jnp.concatenate(
+            [
+                jnp.concatenate([near_m[:HEAD_DIM, :HALF], far_m[:HEAD_DIM, :HALF]], axis=1) * norms[0],
+                jnp.concatenate([near_m[HEAD_DIM:, HALF:], far_m[HEAD_DIM:, HALF:]], axis=1) * norms[1],
+            ],
+            axis=0,
+        ).astype(BF)
+        mixed_o[s, c, g] = made
+        for e in range(2):
+            norm_o[s, c, g, e : e + 1, :] = norms[e]
+        return made
+
+    def finish(s, mixed):
+        x = tok[s * SEQ : (s + 1) * SEQ, :].astype(F32).T
+        hidden_o[s] = x + dot(wo_t[...], jnp.concatenate(mixed, axis=0)) + wide(vec[5 * dim : 6 * dim, :], SEQ)
+
+    first = prepare(0)
+    ready = project(0, 0, first)
+    mixed = []
     for s in range(seqs):
-        span = slice(s * SEQ, (s + 1) * SEQ)
-        first_o[s] = first[:, span]
-        k_nat = turned(keys[:, span])
-        parts = []
+        done, mixed = mixed, []
         for p in range(pairs):
-            rows = slice(p * LANES, (p + 1) * LANES)
-            c, g = divmod(p, 2)
-            query_o[s, c, g], keys_o[s, c, g] = query[rows, span], keys[rows, span]
-            values_o[s, c, g] = values[rows, span]
-            near_q, far_q = pair_near_far(query[rows, span])
-            kp = k_nat[:, rows]
-            near, near_g = attend(dot(kp[:HALF], near_q), mask)
-            far, far_g = attend(dot(kp, far_q), mask)
-            signed_o[s, c, g, :HALF], signed_o[s, c, g, HALF:] = near, far
-            slope_o[s, c, g, :HALF], slope_o[s, c, g, HALF:] = near_g, far_g
-            v = values[rows, span]
-            near_m, far_m = dot(v[:, :HALF], near), dot(v, far)
-            made = jnp.concatenate(
-                [
-                    jnp.concatenate([near_m[:HEAD_DIM, :HALF], far_m[:HEAD_DIM, :HALF]], axis=1),
-                    jnp.concatenate([near_m[HEAD_DIM:, HALF:], far_m[HEAD_DIM:, HALF:]], axis=1),
-                ],
-                axis=0,
-            ).astype(BF)
-            mixed_o[s, c, g] = made
-            parts.append(made)
-        mixed_all.append(jnp.concatenate(parts, axis=0))
-    mixed = jnp.concatenate(mixed_all, axis=1)
-    hidden = x + dot(wo_t[...], mixed) + wide(vec[5 * dim : 6 * dim, :], lanes)
-    for s in range(seqs):
-        hidden_o[s] = hidden[:, s * SEQ : (s + 1) * SEQ]
+            current = ready
+            if p == pairs // 2 and s + 1 < seqs:
+                following = prepare(s + 1)
+            if p + 1 < pairs:
+                ready = project(s, p + 1, first)
+            elif s + 1 < seqs:
+                first = following
+                ready = project(s + 1, 0, first)
+            mixed.append(mix(s, p, *current))
+            if p == 0 and s > 0:
+                finish(s - 1, done)
+    finish(seqs - 1, mixed)
 
 
 def mlp_kernel(seqs, block, place, *refs):
     (hid, cot, wu0, wu1, wd0, wd1, gain2, shift2, small0, small1) = refs[:10]
     (act_o, low_o, own_o, other_o, gvec_o) = refs[10:15]
-    wu_t, gup, gdown, gvec, gbup, vec, bup = refs[15:22]
+    wu_t, gup, gdown, gvec, vec, bup = refs[15:21]
     dim = hid.shape[1]
     units = wu0.shape[1]
     lanes = seqs * SEQ
@@ -197,7 +219,6 @@
         gup[...] = jnp.zeros_like(gup)
         gdown[...] = jnp.zeros_like(gdown)
         gvec[...] = jnp.zeros_like(gvec)
-        gbup[...] = jnp.zeros_like(gbup)
 
     hidden = jnp.concatenate([hid[s] for s in range(seqs)], axis=1)
     grad_out = cot[...].astype(F32).T
@@ -205,6 +226,8 @@
     gain = wide(vec[0:dim, :], lanes)
     plain, factor = norm_plain(hidden)
     second = (plain * gain + wide(vec[dim : 2 * dim, :], lanes)).astype(BF)
+    ones = jnp.ones((16, lanes), BF)
+    second_ones = jnp.concatenate([second, ones], axis=0)
     dnorm = None
     for start in range(0, 2 * units, block):
         span = slice(start, start + block)
@@ -213,22 +236,25 @@
         inner = slice(inner, inner + block)
         upper = dot(wu_t[span, :], second) + wide(bup[span, :], lanes)
         dact = dot(down_ref[inner, :], grad_low)
-        cdf = 0.5 * lax.erf(upper * (1.0 / math.sqrt(2.0))) + 0.5
-        density = jnp.exp(-0.5 * (upper * upper)) * (1.0 / math.sqrt(2.0 * math.pi))
+        part = upper * (1.0 / math.sqrt(2.0))
+        cdf = 0.5 * lax.erf(part) + 0.5
+        density = jnp.exp2((part * part) * (-1.0 / math.log(2.0)))
         act = (upper * cdf).astype(BF)
-        dup = (dact * (cdf + upper * density)).astype(BF)
+        dup = (dact * (cdf + part * density * (1.0 / math.sqrt(math.pi)))).astype(BF)
         for s in range(seqs):
             act_o[s, span, :] = act[:, s * SEQ : (s + 1) * SEQ]
-        gbup[span, :] += lane_fold(dup.astype(F32))
         dn_part = dot(up_ref[:, inner], dup)
         dnorm = dn_part if dnorm is None else dnorm + dn_part
-        gup[:, span] += tail_dot(second, dup)
-        gdown[span, :] += tail_dot(act, grad_low)
+        gup[:, span] += tail_dot(second_ones, dup)
+        if start == 0:
+            act = jnp.concatenate([ones, act], axis=0)
+            gdown[: 16 + block, :] += tail_dot(act, grad_low)
+        else:
+            gdown[16 + start : 16 + start + block, :] += tail_dot(act, grad_low)
     gvec[0:dim, :] += lane_fold(dnorm * plain)
     gvec[dim : 2 * dim, :] += lane_fold(dnorm)
-    gvec[2 * dim : 3 * dim, :] += lane_fold(grad_out)
     dhidden = grad_out + norm_back(dnorm, plain, factor, gain)
-    gvec[3 * dim :, :] += lane_fold(dhidden)
+    gvec[2 * dim :, :] += lane_fold(dhidden)
     for s in range(seqs):
         low_o[s] = dhidden[:, s * SEQ : (s + 1) * SEQ].astype(BF)
 
@@ -237,12 +263,13 @@
         for half, grad_o in enumerate((own_o, other_o)):
             for index in range(units // dim):
                 start = half * units + index * dim
-                grad_o[index * dim : (index + 1) * dim, :] = gup[:, start : start + dim].astype(BF)
-            grad_o[units:, :] = gdown[half * units : (half + 1) * units, :].astype(BF)
-        for index in range(4):
-            gvec_o[index : index + 1, :] = as_row(gvec[index * dim : (index + 1) * dim, :])
+                grad_o[index * dim : (index + 1) * dim, :] = gup[:dim, start : start + dim].astype(BF)
+            grad_o[units:, :] = gdown[16 + half * units : 16 + (half + 1) * units, :].astype(BF)
+        for index, row in ((0, 0), (1, 1), (2, 3)):
+            gvec_o[row : row + 1, :] = as_row(gvec[index * dim : (index + 1) * dim, :])
+        gvec_o[2:3, :] = gdown[:1, :]
         for index in range(2 * units // dim):
-            gvec_o[4 + index : 5 + index, :] = as_row(gbup[index * dim : (index + 1) * dim, :])
+            gvec_o[4 + index : 5 + index, :] = gup[dim : dim + 1, index * dim : (index + 1) * dim]
 
 
 def out_kernel(seqs, place, hid, act, wd0, wd1, bdown, out_o, whole_o, wd_t, vec):
@@ -296,11 +323,12 @@
             at += 1
 
 
-def grad_kernel(seqs, group, *refs):
-    (low_i, first_i, query_i, keys_i, values_i, mixed_i, signed_i, slope_i) = refs[:8]
-    wo0, wo1 = refs[8:10]
-    (dq_o, dk_o, dv_o, own_o, other_o, gvec_o) = refs[10:16]
-    gqkv, gout, gb = refs[16:19]
+def grad_kernel(seqs, *refs):
+    (low_i, first_i, query_i, keys_i, values_i, mixed_i, signed_i, slope_i, norm_i) = refs[:9]
+    wo0, wo1 = refs[9:11]
+    outs = refs[11:17]
+    own_o, other_o, gvec_o = refs[17:20]
+    gqkv, gout, gb = refs[20:23]
     dim = low_i.shape[1]
     part = 2 * LANES
     step = pl.program_id(0)
@@ -312,90 +340,120 @@
         gout[...] = jnp.zeros_like(gout)
         gb[...] = jnp.zeros_like(gb)
 
-    place = slice(group * LANES, (group + 1) * LANES)
     first = jnp.concatenate([first_i[s] for s in range(seqs)], axis=1)
     low = jnp.concatenate([low_i[s] for s in range(seqs)], axis=1)
-    dmixed = jnp.concatenate([dot(wo0[place, :], low), dot(wo1[place, :], low)], axis=0).astype(BF)
-    mixed = jnp.concatenate(
-        [
-            jnp.concatenate([mixed_i[s, 0, 0], mixed_i[s, 1, 0]], axis=0)
-            for s in range(seqs)
-        ],
-        axis=1,
-    )
-    dq_all, dk_all, dv_all = [], [], []
-    for s in range(seqs):
-        span = slice(s * SEQ, (s + 1) * SEQ)
-        dq, dk, dv = [], [], []
-        for c in range(2):
-            rows = slice(c * LANES, (c + 1) * LANES)
-            q, k = query_i[s, c, 0], keys_i[s, c, 0]
-            dm = dmixed[rows, span]
-            v_nat = turned(values_i[s, c, 0])
-            near_q, far_q = pair_near_far(q)
-            near_m, far_m = pair_near_far(dm)
-            low_pair = []
-            for index in range(2):
-                keys = slice(0, HALF) if index == 0 else slice(0, SEQ)
-                block = slice(0, HALF) if index == 0 else slice(HALF, HALF + SEQ)
-                dsigned = dot(v_nat[keys], (near_m, far_m)[index])
-                signed = signed_i[s, c, 0, block].astype(F32)
-                row_dot = jnp.sum(signed * dsigned, axis=0, keepdims=True)
-                dscores = slope_i[s, c, 0, block].astype(F32) * dsigned - signed * row_dot
-                low_pair.append(dscores.astype(BF))
-            near, far = low_pair
-            near_p, far_p = dot(k[:, :HALF], near), dot(k, far)
-            dq.append(
-                jnp.concatenate(
-                    [
-                        jnp.concatenate([near_p[:HEAD_DIM, :HALF], far_p[:HEAD_DIM, :HALF]], axis=1),
-                        jnp.concatenate([near_p[HEAD_DIM:, HALF:], far_p[HEAD_DIM:, HALF:]], axis=1),
-                    ],
-                    axis=0,
-                )
+
+    def pair(s, c, g, dm):
+        q, k = query_i[s, c, g], keys_i[s, c, g]
+        v_nat = turned(values_i[s, c, g])
+        near_q, far_q = pair_near_far(q)
+        near_m, far_m = pair_near_far(dm)
+        low_pair = []
+        for index in range(2):
+            keys = slice(0, HALF) if index == 0 else slice(0, SEQ)
+            block = slice(0, HALF) if index == 0 else slice(HALF, HALF + SEQ)
+            lanes = slice(index * HALF, (index + 1) * HALF)
+            dsigned = dot(v_nat[keys], (near_m, far_m)[index])
+            signed = signed_i[s, c, g, block].astype(F32)
+            row_dot = jnp.sum(signed * dsigned, axis=0, keepdims=True)
+            row_dot = row_dot * jnp.concatenate(
+                [norm_i[s, c, g, e : e + 1, lanes] for e in range(2)], axis=1
             )
-            near_p, far_p = tail_dot(near, near_q), tail_dot(far, far_q)
-            dk.append(jnp.concatenate([far_p[:HALF] + near_p, far_p[HALF:]], axis=0))
-            near_p = tail_dot(signed_i[s, c, 0, :HALF], near_m)
-            far_p = tail_dot(signed_i[s, c, 0, HALF:], far_m)
-            dv.append(jnp.concatenate([far_p[:HALF] + near_p, far_p[HALF:]], axis=0))
-        dq_all.append((jnp.concatenate(dq, axis=0) * scale).astype(BF))
-        dk_all.append(jnp.concatenate(dk, axis=1).astype(BF))
-        dv_all.append(jnp.concatenate(dv, axis=1).astype(BF))
-        dq_o[s], dk_o[s], dv_o[s] = dq_all[s], dk_all[s], dv_all[s]
-    gout[...] += tail_dot(mixed, low)
-    dq, dk, dv = jnp.concatenate(dq_all, axis=1), jnp.concatenate(dk_all, axis=0), jnp.concatenate(dv_all, axis=0)
-    gqkv[:, :part] += tail_dot(first, dq)
-    gqkv[:, part : 2 * part] += dot(first, dk)
-    gqkv[:, 2 * part :] += dot(first, dv)
-    gb[:part, :] += lane_fold(dq.astype(F32))
-    for index, block in ((2, dk), (3, dv)):
-        total = jnp.sum(block.astype(F32).reshape(-1, 8, part), axis=0)
-        gb[index * LANES : index * LANES + 8, :] += total[:, :LANES]
-        gb[index * LANES + 8 : index * LANES + 16, :] += total[:, LANES:]
+            dscores = slope_i[s, c, g, block].astype(F32) * dsigned - signed * row_dot
+            low_pair.append(dscores.astype(BF))
+        near, far = low_pair
+        near_p, far_p = dot(k[:, :HALF], near), dot(k, far)
+        dq = jnp.concatenate(
+            [
+                jnp.concatenate([near_p[:HEAD_DIM, :HALF], far_p[:HEAD_DIM, :HALF]], axis=1),
+                jnp.concatenate([near_p[HEAD_DIM:, HALF:], far_p[HEAD_DIM:, HALF:]], axis=1),
+            ],
+            axis=0,
+        )
+        near_p, far_p = tail_dot(near, near_q), tail_dot(far, far_q)
+        dk = jnp.concatenate([far_p[:HALF] + near_p, far_p[HALF:]], axis=0)
+        near_p = tail_dot(signed_i[s, c, g, :HALF], near_m)
+        far_p = tail_dot(signed_i[s, c, g, HALF:], far_m)
+        dv = jnp.concatenate([far_p[:HALF] + near_p, far_p[HALF:]], axis=0)
+        return dq, dk, dv
+
+    for g in range(2):
+        place = slice(g * LANES, (g + 1) * LANES)
+        spread = lambda s, c, e: jnp.broadcast_to(norm_i[s, c, g, e : e + 1, :], (HEAD_DIM, SEQ))
+        norms = jnp.concatenate(
+            [
+                jnp.concatenate([spread(s, c, e) for c in range(2) for e in range(2)], axis=0)
+                for s in range(seqs)
+            ],
+            axis=1,
+        )
+        dmixed = jnp.concatenate([dot(wo0[place, :], low), dot(wo1[place, :], low)], axis=0)
+        dmixed = (dmixed * norms).astype(BF)
+        mixed = jnp.concatenate(
+            [
+                jnp.concatenate([mixed_i[s, 0, g], mixed_i[s, 1, g]], axis=0)
+                for s in range(seqs)
+            ],
+            axis=1,
+        )
+        dq_o, dk_o, dv_o = outs[3 * g : 3 * g + 3]
+        dq_all, dk_all, dv_all = [], [], []
+        for s in range(seqs):
+            span = slice(s * SEQ, (s + 1) * SEQ)
+            dq, dk, dv = zip(
+                *[pair(s, c, g, dmixed[c * LANES : (c + 1) * LANES, span]) for c in range(2)]
+            )
+            dq_all.append((jnp.concatenate(dq, axis=0) * scale).astype(BF))
+            dk_all.append(jnp.concatenate(dk, axis=1).astype(BF))
+            dv_all.append(jnp.concatenate(dv, axis=1).astype(BF))
+            dq_o[s], dk_o[s], dv_o[s] = dq_all[s], dk_all[s], dv_all[s]
+        gout[g * part : (g + 1) * part, :] += tail_dot(mixed, low)
+        dq = jnp.concatenate(dq_all, axis=1)
+        dk, dv = jnp.concatenate(dk_all, axis=0), jnp.concatenate(dv_all, axis=0)
+        at = 3 * g * part
+        gqkv[:, at : at + part] += tail_dot(first, dq)
+        gqkv[:, at + part : at + 2 * part] += dot(first, dk)
+        gqkv[:, at + 2 * part : at + 3 * part] += dot(first, dv)
+        base = g * 4 * LANES
+        gb[base : base + part, :] += lane_fold(dq.astype(F32))
+        for index, block in ((2, dk), (3, dv)):
+            total = jnp.sum(block.astype(F32).reshape(-1, 8, part), axis=0)
+            rows = base + index * LANES
+            gb[rows : rows + 8, :] += total[:, :LANES]
+            gb[rows + 8 : rows + 16, :] += total[:, LANES:]
 
     @pl.when(step == pl.num_programs(0) - 1)
     def _():
-        for c, grad_o in enumerate((own_o, other_o)):
-            for index in range(3):
-                start = index * part + c * LANES
-                grad_o[index * dim : (index + 1) * dim, :] = gqkv[:, start : start + LANES].astype(BF)
-            for index in range(dim // LANES):
-                start = 3 * dim + index * LANES
-                grad_o[start : start + LANES, :] = gout[
-                    c * LANES : (c + 1) * LANES, index * LANES : (index + 1) * LANES
-                ].astype(BF)
-            gvec_o[c : c + 1, :] = as_row(gb[c * LANES : (c + 1) * LANES, :])
-            for index in (2, 3):
-                rows = slice(index * LANES + 8 * c, index * LANES + 8 * c + 8)
-                gvec_o[2 * index - 2 + c : 2 * index - 1 + c, :] = jnp.sum(gb[rows, :], axis=0, keepdims=True)
+        for g in range(2):
+            base = g * 4 * LANES
+            tall = g * 4 * dim
+            for c, grad_o in enumerate((own_o, other_o)):
+                for index in range(3):
+                    start = 3 * g * part + index * part + c * LANES
+                    grad_o[tall + index * dim : tall + (index + 1) * dim, :] = gqkv[
+                        :, start : start + LANES
+                    ].astype(BF)
+                for index in range(dim // LANES):
+                    start = tall + 3 * dim + index * LANES
+                    grad_o[start : start + LANES, :] = gout[
+                        g * part + c * LANES : g * part + (c + 1) * LANES,
+                        index * LANES : (index + 1) * LANES,
+                    ].astype(BF)
+                gvec_o[8 * g + c : 8 * g + c + 1, :] = as_row(
+                    gb[base + c * LANES : base + (c + 1) * LANES, :]
+                )
+                for index in (2, 3):
+                    rows = slice(base + index * LANES + 8 * c, base + index * LANES + 8 * c + 8)
+                    at = 8 * g + 2 * index - 2 + c
+                    gvec_o[at : at + 1, :] = jnp.sum(gb[rows, :], axis=0, keepdims=True)
 
 
 def input_kernel(seqs, place, *refs):
     tok, dhid, dq0, dk0, dv0, dq1, dk1, dv1 = refs[:8]
     wq0, wq1, wk0, wk1, wv0, wv1, gain1 = refs[8:15]
-    tgrad_o, whole_o, gvec_o = refs[15:18]
-    gvec, vec = refs[18:20]
+    vec_ff, vec_at = refs[15:17]
+    tgrad_o, whole_o, gvec_o, own_o, other_o = refs[17:22]
+    gvec, vec, pack = refs[22:25]
     dim = tok.shape[1]
 
     @pl.when(pl.program_id(0) == 0)
@@ -426,6 +484,20 @@
     def _():
         for index in range(2):
             gvec_o[index : index + 1, :] = as_row(gvec[index * dim : (index + 1) * dim, :])
+        same = [(vec_ff, r) for r in range(4)] + [(gvec_o, 0), (gvec_o, 1)]
+        units = 2 * dim
+        pack[...] = jnp.zeros_like(pack)
+        for c, out in enumerate((own_o, other_o)):
+            rows = [ref[r : r + 1, k : k + LANES] for ref, r in same for k in range(0, dim, LANES)]
+            rows += [vec_at[r : r + 1, :] for i in range(3) for r in (2 * i + c, 8 + 2 * i + c)]
+            rows += [
+                vec_ff[4 + r : 5 + r, k : k + LANES]
+                for r in range(c * units // dim, (c + 1) * units // dim)
+                for k in range(0, dim, LANES)
+            ]
+            for index, row in enumerate(rows):
+                pack[index : index + 1, :] = row
+            out[...] = pack[...].astype(BF)
 
 
 def whole_vmem():
@@ -470,6 +542,7 @@
             [row_block(seqs, dim, steps)] + [whole_vmem()] * 13,
             [placed_seq_block(seqs, *feat)] * 4
             + [placed_seq_block(seqs, *wide_block)] * 2
+            + [placed_seq_block(seqs, 2, 2, 8, SEQ)]
             + [placed_seq_block(seqs, dim, SEQ)] * 2,
             [
                 pltpu.VMEM((3 * dim, dim), BF),
@@ -479,6 +552,7 @@
         ),
         out_shape=[shape((count,) + feat, BF)] * 4
         + [shape((count,) + wide_block, BF)] * 2
+        + [shape((count, 2, 2, 8, SEQ), F32)]
         + [shape((count, dim, SEQ), BF), shape((count, dim, SEQ), F32)],
         compiler_params=params(),
         cost_estimate=pl.CostEstimate(flops=1, bytes_accessed=1, transcendentals=0),
@@ -486,33 +560,37 @@
     )(place, tokens, *weights, *vectors)
 
 
-def grad_call(group, low, first, saved, weights, seqs):
+def grad_call(low, first, saved, weights, seqs):
     count, dim = low.shape[:2]
     steps = count // seqs
-    one = lambda *dims: pl.BlockSpec((seqs, 2, 1) + dims, lambda i: (i, 0, group, 0, 0))
+    every = lambda *dims: seq_block(seqs, 2, 2, *dims)
     shape = jax.ShapeDtypeStruct
     part = 2 * LANES
+    trio = [seq_block(seqs, part, SEQ), seq_block(seqs, SEQ, part), seq_block(seqs, SEQ, part)]
     return pl.pallas_call(
-        functools.partial(grad_kernel, seqs, group),
+        functools.partial(grad_kernel, seqs),
         grid=(steps,),
         in_specs=[seq_block(seqs, dim, SEQ)] * 2
-        + [one(LANES, SEQ)] * 4
-        + [one(HALF + SEQ, SEQ)] * 2
+        + [every(LANES, SEQ)] * 4
+        + [every(HALF + SEQ, SEQ)] * 2
+        + [every(8, SEQ)]
         + [whole_vmem()] * 2,
-        out_specs=[seq_block(seqs, part, SEQ), seq_block(seqs, SEQ, part), seq_block(seqs, SEQ, part)]
-        + [whole_vmem()] * 3,
+        out_specs=trio * 2 + [whole_vmem()] * 3,
         out_shape=[
             shape((count, part, SEQ), BF),
             shape((count, SEQ, part), BF),
             shape((count, SEQ, part), BF),
-            shape((4 * dim, LANES), BF),
-            shape((4 * dim, LANES), BF),
-            shape((8, LANES), F32),
+        ]
+        * 2
+        + [
+            shape((8 * dim, LANES), BF),
+            shape((8 * dim, LANES), BF),
+            shape((16, LANES), F32),
         ],
         scratch_shapes=[
-            pltpu.VMEM((dim, 3 * part), F32),
-            pltpu.VMEM((part, dim), F32),
-            pltpu.VMEM((4 * LANES, LANES), F32),
+            pltpu.VMEM((dim, 6 * part), F32),
+            pltpu.VMEM((2 * part, dim), F32),
+            pltpu.VMEM((8 * LANES, LANES), F32),
         ],
         compiler_params=params(),
         cost_estimate=pl.CostEstimate(flops=1, bytes_accessed=1, transcendentals=0),
@@ -520,7 +598,7 @@
     )(low, first, *saved, *weights)
 
 
-def input_call(place, tokens, dhidden, pieces, weights, gain1, seqs):
+def input_call(place, tokens, dhidden, pieces, weights, gain1, vectors, grow, seqs):
     dim = tokens.shape[1]
     count = dhidden.shape[0]
     steps = count // seqs
@@ -536,23 +614,29 @@
             (steps,),
             [row_block(seqs, dim, steps), placed_seq_block(seqs, dim, SEQ)]
             + trio * 2
-            + [whole_vmem()] * 7,
+            + [whole_vmem()] * 9,
             [
                 pl.BlockSpec((seqs * SEQ, dim), lambda i, place: (i, 0)),
                 row_block(seqs, dim, steps),
-                whole_vmem(),
+            ]
+            + [whole_vmem()] * 3,
+            [
+                pltpu.VMEM((2 * dim, LANES), F32),
+                pltpu.VMEM((dim, LANES), F32),
+                pltpu.VMEM((grow, LANES), F32),
             ],
-            [pltpu.VMEM((2 * dim, LANES), F32), pltpu.VMEM((dim, LANES), F32)],
         ),
         out_shape=[
             jax.ShapeDtypeStruct((count * SEQ, dim), BF),
             jax.ShapeDtypeStruct(tokens.shape, BF),
             jax.ShapeDtypeStruct((8, dim), F32),
+            jax.ShapeDtypeStruct((grow, LANES), BF),
+            jax.ShapeDtypeStruct((grow, LANES), BF),
         ],
         compiler_params=params(),
         cost_estimate=pl.CostEstimate(flops=1, bytes_accessed=1, transcendentals=0),
         name="input_grad",
-    )(place, tokens, dhidden, *pieces, *weights, gain1)
+    )(place, tokens, dhidden, *pieces, *weights, gain1, *vectors)
 
 
 def mlp_call(place, hidden, cotangent, weights, vectors, seqs, block):
@@ -569,10 +653,9 @@
             + [whole_vmem()] * 3,
             [
                 pltpu.VMEM((2 * units, dim), BF),
-                pltpu.VMEM((dim, 2 * units), F32),
-                pltpu.VMEM((2 * units, dim), F32),
-                pltpu.VMEM((4 * dim, LANES), F32),
-                pltpu.VMEM((2 * units, LANES), F32),
+                pltpu.VMEM((dim + 16, 2 * units), F32),
+                pltpu.VMEM((2 * units + 16, dim), F32),
+                pltpu.VMEM((3 * dim, LANES), F32),
                 pltpu.VMEM((2 * dim, LANES), F32),
                 pltpu.VMEM((2 * units, LANES), F32),
             ],
@@ -773,42 +856,41 @@
         return [piece(0)] + [shifted(piece(r), "mp", mp, r) for r in range(1, mp)]
 
     *saved, first, hidden = attn_call(
-        place, tokens, own, weights, [gain1, shift1, bo] + smalls, 2
+        place, tokens, own, weights, [gain1, shift1, bo] + smalls, SEQS["attn"]
     )
     hidden, mlp_weights = tie((hidden, mlp_weights))
     act, low, *grad_ff, vec_ff = mlp_call(
-        place, hidden, cotangent, mlp_weights, [gain2, shift2] + smalls, 2, 512
+        place, hidden, cotangent, mlp_weights, [gain2, shift2] + smalls, SEQS["mlp"], 512
     )
     ff = total_of(mp_send(lambda r: ff_piece(grad_ff, r)))
     low, ff = tie((low, ff))
     ff = lax.psum(ff, "dp")
-    dq0, dk0, dv0, *grad0, vec_at0 = grad_call(0, low, first, saved, weights[6:], 2)
-    at0 = mp_send(lambda r: at_piece([grad0], r)) if per == 1 else []
-    low, at0 = tie((low, at0))
-    dq1, dk1, dv1, *grad1, vec_at1 = grad_call(1, low, first, saved, weights[6:], 2)
-    at0, dq1 = tie((at0, dq1))
-    def finish(low, dq1, at0, act):
-        at1 = mp_send(lambda r: at_piece([grad1], r)) if per == 1 else []
-        low, at1, dq1 = tie((low, at1, dq1))
-        pieces = [dq0, dk0, dv0, dq1, dk1, dv1]
-        tgrad, tgrad_full, vec_in = input_call(place, tokens, low, pieces, weights[:6], gain1, 2)
-        at1, tgrad = tie((at1, tgrad))
-
-        vecs = [vec_ff[:4].reshape(-1, LANES), vec_in[:2].reshape(-1, LANES)]
+    *pieces, grad_own, grad_other, vec_at = grad_call(low, first, saved, weights[6:], SEQS["grad"])
+    grad_at = [grad_own, grad_other]
+
+    def finish(low, act, grad_at):
+        at = mp_send(lambda r: grad_at[r]) if per == 1 else []
+        low, at = tie((low, at))
+        grow = -(-(6 * dim + 3 * local + units) // (16 * dp * LANES)) * 16 * dp
+        tgrad, tgrad_full, vec_in, *vec_low = input_call(
+            place,
+            tokens,
+            low,
+            pieces,
+            weights[:6],
+            gain1,
+            [vec_ff, vec_at],
+            max(grow, -(-(6 * dim + 6 * LANES + 2 * dim) // LANES)),
+            SEQS["input"],
+        )
+        at, tgrad = tie((at, tgrad))
+
         if per == 1:
-            grow = -(-(6 * dim + 3 * local + units) // (16 * dp * LANES)) * 16 * dp
-
-            def vec_piece(r):
-                gb = vec_ff[4 + r * units // dim : 4 + (r + 1) * units // dim].reshape(-1, LANES)
-                bias = [v[2 * i + r : 2 * i + r + 1] for i in range(3) for v in (vec_at0, vec_at1)]
-                made = jnp.concatenate(vecs + bias + [gb], axis=0)
-                return jnp.pad(made, ((0, grow - made.shape[0]), (0, 0))).astype(BF)
-
-            at = jnp.concatenate(
-                [total_of(at0), total_of(at1), total_of(mp_send(vec_piece))], axis=0
-            )
+            at = jnp.concatenate([total_of(at), total_of(mp_send(lambda r: vec_low[r]))], axis=0)
         else:
-            same = jnp.concatenate([v.reshape(-1) for v in vecs])
+            same = jnp.concatenate([vec_ff[:4].reshape(-1), vec_in[:2].reshape(-1)])
+            vec_at0, vec_at1 = vec_at[:8], vec_at[8:]
+            grads = [[v[: 4 * dim] for v in grad_at], [v[4 * dim :] for v in grad_at]]
             gbup = vec_ff[4:].reshape(-1)
             bias = [
                 jnp.concatenate([v[2 * i + c] for c in range(2) for v in (vec_at0, vec_at1)])
@@ -823,13 +905,15 @@
                 )
                 size = -(-vector.shape[0] // (16 * dp * LANES)) * (16 * dp * LANES)
                 vector = jnp.pad(vector, (0, size - vector.shape[0])).reshape(-1, LANES).astype(BF)
-                return jnp.concatenate([at_piece([grad0, grad1], r), vector], axis=0)
+                return jnp.concatenate([at_piece(grads, r), vector], axis=0)
 
             at = total_of(mp_send(all_piece))
         at = dp_sum.scatter(at, 0)
         tgrads = spread_out(tgrad)
         act, at[0], tgrad = tie((act, at[0], tgrad))
-        out, out_full = out_call(place, hidden, act, mlp_weights[2:], bd, rows, 2)
+        out, out_full = out_call(
+            place, hidden, act, mlp_weights[2:], bd, rows, SEQS["out"]
+        )
         at, out, tgrads = tie((at, out, tgrads))
         at = total_of(at)
         stages = len(dp_sum.groups)
@@ -837,9 +921,12 @@
             at = total_of(dp_sum.scatter(at, stage))
         outs = spread_out(out)
         tgrad_full = filled(tgrad_full, tgrads)
+        at, tgrad_full = tie((at, tgrad_full))
         for stage in reversed(range(1, stages)):
             at = dp_sum.join(dp_sum.gather(at, stage), stage)
         at = dp_sum.gather(at, 0)
+        out_full = filled(out_full, outs)
+        at, out_full = tie((at, out_full))
 
         sizes = [dim] * 6 + [local] * 3 + [units]
         if per == 1 and len(at) == 4:
@@ -862,18 +949,16 @@
                 parts.append(vector[:size])
                 vector = vector[size:]
             g_same, g_bias, g_bup = parts[:6], parts[6:9], parts[9]
-        out_full = filled(out_full, outs)
         return (out_full, tgrad_full, list(g_same), list(g_qkv), list(g_bias), g_out, g_bup)
 
-    blank = jax.eval_shape(finish, low, dq1, at0, act)
+    blank = jax.eval_shape(finish, low, act, grad_at)
     out_full, tgrad_full, g_same, g_qkv, g_bias, g_out, g_bup = lax.cond(
         lax.axis_index("dp") != dp,
         finish,
         lambda *_: jax.tree.map(lambda v: jnp.zeros(v.shape, v.dtype), blank),
         low,
-        dq1,
-        at0,
         act,
+        grad_at,
     )
     if per == 1:
         g_up, g_down = ff_unpack_call(ff, units)

time: 301 us -> 281 us (0.934); the launches traced: 296 us -> 281 us
  Pallas kernels: 207 us -> 196 us
    pallas_call x1, Pallas kernels: 47.4 us -> 42.5 us  [attn_call(): pl.pallas_call(functools.partial(attn_kernel, seqs), grid_spec=prefetch((...]
    pallas_call x2 -> x1, Pallas kernels: 49.5 us -> 46.9 us  [grad_call(): pl.pallas_call(functools.partial(grad_kernel, seqs), grid=(steps,), in_sp...]
    ppermute x13 -> x12, waiting for transfers between devices: 14.4 us -> 13.1 us  [shifted(): lax.ppermute(value, axis, [(i, (i + shift) % count) for i in range(count)])]
  transfers between devices with their start and end apart: 26 -> 25, of which waited for: 12 -> 13; matrix products, arithmetic and copies ran while one was open for 5% -> 5% of each run, Pallas kernels for 46% -> 44%
where the time goes in v4:
time: 281 us
  Pallas kernels  196 us (70%)
  waiting for transfers between devices  29.6 us (11%)
  starting transfers between devices  21.1 us (8%)
  between operations  14.3 us (5%)
  local copies, waits for them, and re-layouts  11.4 us (4%)
  other arithmetic  7.79 us (3%)
    pallas_call x1, Pallas kernels, mlp_call(): pl.pallas_call(functools.partial(mlp_kernel, seqs, block), grid_spec=pref...  67.8 us
    pallas_call x1, Pallas kernels, grad_call(): pl.pallas_call(functools.partial(grad_kernel, seqs), grid=(steps,), in_sp...  46.9 us
    pallas_call x1, Pallas kernels, attn_call(): pl.pallas_call(functools.partial(attn_kernel, seqs), grid_spec=prefetch((...  42.5 us
    ppermute x12, starting transfers between devices, swap(): lax.ppermute(value, 'dp', [(i, i ^ distance) for i in range(self.count)])  17.4 us
    pallas_call x1, Pallas kernels, input_call(): pl.pallas_call(functools.partial(input_kernel, seqs), grid_spec=prefetch(...  16.6 us
    ppermute x12, waiting for transfers between devices, swap(): lax.ppermute(value, 'dp', [(i, i ^ distance) for i in range(self.count)])  16.5 us
    pallas_call x1, Pallas kernels, out_call(): pl.pallas_call(functools.partial(out_kernel, seqs), grid_spec=prefetch((s...  16.3 us
    ppermute x12, waiting for transfers between devices, shifted(): lax.ppermute(value, axis, [(i, (i + shift) % count) for i in range(count)])  13.1 us
  transfers between devices with their start and end apart: 25, of which 13 were waited for; matrix products, arithmetic and copies ran while one was open for 5% of the time, Pallas kernels for 44%

profile of v4, /device:TPU:0, one launch (start us, length us, event | category | flops | bytes accessed | tf_op | source)
XLA Modules:
  0.0 280.8 jit_solution(9320116429413494516)
XLA Ops:
  7.2 0.0 all-reduce.2.cloned.1.call-start
  7.2 0.5 collective-permute-start.21
  7.8 0.1 collective-permute-start.22
  7.8 0.4 collective-permute-start.16
  8.3 0.7 pad_maximum_fusion.1
  9.0 0.1 collective-permute-start.20
  9.2 0.4 collective-permute-start.17
  9.6 1.9 collective-permute-done.20.refs_13_.refs_9_
  11.5 0.1 collective-permute-start.18
  11.6 0.5 collective-permute-done.16.refs_2_
  12.1 0.4 collective-permute-start.19
  12.5 0.7 collective-permute-done.18.refs_6_
  13.2 0.7 collective-permute-done.19.refs_8_.refs_10_
  13.9 0.7 copy-done.7
  14.6 42.5 %attn_forward.1 = (bf16[16,2,2,128,256]{4,3,2,1,0:T(8,128)(2,1)}, bf16[16,2,2,128,256]{4,3,2,1,0:T(8,128)(2,1)}, bf16[16,2,2,128,256]{4,3,2,1,0:T(8,128)(2,1)}, ...) custom-call(s32[1]{0:T(128)} %bitcast.27.place, ...), custom_call_target="tpu_custom_call" | custom-call | flops 1 | bytes 1 | tf_op jit(solution)/shard_map/attn_forward/pallas_call | solution.py:538
  57.1 67.8 %feed_forward.1 = (bf16[16,2048,256]{2,1,0:T(8,128)(2,1)}, bf16[16,512,256]{2,1,0:T(8,128)(2,1)}, bf16[2048,512]{1,0:T(8,128)(2,1)}, bf16[2048,512]{1,0:T(8,128)(2,1)}, f32[8,512]{1,0:T(8,128)S(1)}) custom-call(s32[1]{0:T(128)} %bitcast.27.place, f32[16,512,256]{2,1,0:T(8,128)} %get-tuple-element.187.refs_0_, bf16[8192,512]{1,0:T(8,128)(2,1)} %refs_1_.3, ...), custom_call_target="tpu_custom_call" | custom-call | flops 1 | bytes 1 | tf_op jit(solution)/shard_map/feed_forward/pallas_call | solution.py:647
  124.9 0.5 collective-permute-start.23
  125.3 4.0 %collective-permute-done.23 = bf16[2048,512]{1,0:T(8,128)(2,1)S(1)} collective-permute-done((bf16[2048,512]{1,0:T(8,128)(2,1)}, bf16[2048,512]{1,0:T(8,128)(2,1)S(1)}, u32[]{:S(2)}, u32[]{:S(2)}) %collective-permute-start.23) | collective-permute-done | bytes 2097184 | tf_op jit(solution)/shard_map/ppermute | solution.py:732
  129.3 3.5 %add_convert_fusion.3 = bf16[2048,512]{1,0:T(8,128)(2,1)} fusion(bf16[2048,512]{1,0:T(8,128)(2,1)S(1)} %collective-permute-done.23, bf16[2048,512]{1,0:T(8,128)(2,1)} %get-tuple-element.193), kind=kLoop, calls=%fused_computation.22 | loop fusion | flops 4194304 | bytes 6291456 | tf_op jit(solution)/shard_map/convert_element_type | solution.py:748
  132.9 0.0 all-reduce.2.cloned.1.call-update
  132.9 0.0 copy-start.2
  132.9 0.0 copy-start.6
  133.0 46.9 %attn_backward.1 = (bf16[16,256,256]{2,1,0:T(8,128)(2,1)}, bf16[16,256,256]{2,1,0:T(8,128)(2,1)}, bf16[16,256,256]{2,1,0:T(8,128)(2,1)}, bf16[16,256,256]{2,1,0:...) custom-call(bf16[16,512,256]{2,1,0:T(8,128)(2,1)} %get-tuple-element, ...), custom_call_target="tpu_custom_call" | custom-call | flops 1 | bytes 1 | tf_op jit(solution)/shard_map/attn_backward/pallas_call | solution.py:570
  179.9 90.2 %conditional.1 = (bf16[8192,512]{1,0:T(8,128)(2,1)}, bf16[8192,512]{1,0:T(8,128)(2,1)}, f32[512]{0:T(512)S(1)}, f32[512]{0:T(512)S(1)}, f32[512]{0:T(512)}, /*in...) conditional(s32[]{:T(128)} %convert_element_type.63, () %tuple.24, ...), branch_computations={%region_0.0_spmd, %region_1.0_spmd} | conditional | flops 5849172 | bytes 78395096 | solution.py:955
  179.9 0.4 collective-permute-start
  180.4 2.6 collective-permute-done
  183.0 16.6 %input_grad.1 = (bf16[4096,512]{1,0:T(8,128)(2,1)}, bf16[8192,512]{1,0:T(8,128)(2,1)}, f32[8,512]{1,0:T(8,128)}, bf16[256,128]{1,0:T(8,128)(2,1)}, bf16[256,128]{1,0:T(8,128)(2,1)}) custom-call(s32[1]{0:T(128)} %get-tuple-element.59.place, bf16[8192,512]{1,0:T(8,128)(2,1)} %get-tuple-element.60.refs_0_, bf16[16,512,256]{2,1,0:T(8,128)(2,1)} %get-tuple-element.61.refs_1_, ...), custom_call_target="tpu_custom_call" | custom-call | flops 1 | bytes 1 | tf_op jit(solution)/shard_map/cond/branch_1_fun/input_grad/pallas_call | solution.py:611
  199.6 0.4 collective-permute-start.5
  200.0 0.2 collective-permute-start.1
  200.2 1.8 add_convert_fusion
  202.0 2.6 collective-permute-done.1
  204.6 0.9 add_convert_fusion.2
  205.5 0.1 pad_maximum_fusion
  205.6 0.1 dynamic-slice_bitcast_fusion
  205.7 3.7 %collective-permute-start.4 = (bf16[1088,128]{1,0:T(8,128)(2,1)S(1)}, bf16[1088,128]{1,0:T(8,128)(2,1)S(1)}, u32[]{:S(2)}, u32[]{:S(2)}) collective-permute-start(bf16[1088,128]{1,0:T(8,128)(2,1)S(1)} %get-tuple-element.236), channel_id=1, source_target_pairs={{0,3},{1,2},{2,1},{3,0},{4,7},{5,6},{6,5},{7,4},{8,11},{9,10},{10,... | collective-permute-start | bytes 835592 | tf_op jit(solution)/shard_map/cond/branch_1_fun/ppermute | solution.py:762
  209.4 0.6 collective-permute-start.3
  209.9 0.1 collective-permute-start.2
  210.0 16.3 %layer_out.1 = (bf16[4096,512]{1,0:T(8,128)(2,1)}, bf16[8192,512]{1,0:T(8,128)(2,1)}) custom-call(s32[1]{0:T(128)} %get-tuple-element.59.place, f32[16,512,256]{2,1,0:T(8,128)} %get-tuple-element.84.hid, bf16[16,2048,256]{2,1,0:T(8,128)(2,1)} %get-tuple-element.85.act, bf16[1024,512]{1,0:T(8,128)(2,1)S(1)} %get-tuple-element.86.wd0, ...), custom_call_target="tpu_custom_call" | custom-call | flops 1 | bytes 1 | tf_op jit(solution)/shard_map/cond/branch_1_fun/layer_out/pallas_call | solution.py:680
  226.3 0.1 collective-permute-start.15
  226.5 0.6 iota_xor_fusion.here
  227.0 0.1 add_convert_fusion.1
  227.2 2.0 collective-permute-start.6
  229.2 2.6 collective-permute-start.8
  231.8 0.5 collective-permute-start.7
  232.3 4.5 %constant_dynamic-update-slice_fusion.1 = bf16[8192,512]{1,0:T(8,128)(2,1)} fusion(bf16[8192,512]{1,0:T(8,128)(2,1)} %get-tuple-element.94, bf16[4096,512]{1,0:T(8,128)(2,1)} %collective-permute-done.5, s32[]{:T(128)S(6)} %select_n.62), kind=kLoop, calls=%fused_computation.20 | loop fusion | bytes 8388612 | tf_op jit(solution)/shard_map/cond/branch_1_fun/dynamic_update_slice | solution.py:826
  236.8 0.2 collective-permute-done.8
  237.0 3.0 %collective-permute-done.7 = bf16[272,128]{1,0:T(8,128)(2,1)S(1)} collective-permute-done((bf16[272,128]{1,0:T(8,128)(2,1)S(1)}, bf16[272,128]{1,0:T(8,128)(2,1)S(1)}, u32[]{:S(2)}, u32[]{:S(2)}) %collective-permute-start.7) | collective-permute-done | bytes 69664 | tf_op jit(solution)/shard_map/cond/branch_1_fun/ppermute | solution.py:762
  240.0 2.4 collective-permute-start.11
  242.4 2.0 collective-permute-start.9
  244.5 6.6 %collective-permute-done.9 = bf16[272,128]{1,0:T(8,128)(2,1)S(1)} collective-permute-done((bf16[272,128]{1,0:T(8,128)(2,1)S(1)}, bf16[272,128]{1,0:T(8,128)(2,1)S(1)}, u32[]{:S(2)}, u32[]{:S(2)}) %collective-permute-start.9) | collective-permute-done | bytes 69664 | tf_op jit(solution)/shard_map/cond/branch_1_fun/ppermute | solution.py:762
  251.1 0.6 collective-permute-done.10
  251.7 2.2 collective-permute-start.14
  253.9 0.8 collective-permute-start.13
  254.7 0.6 collective-permute-start.12
  255.3 4.5 %constant_dynamic-update-slice_fusion = bf16[8192,512]{1,0:T(8,128)(2,1)} fusion(bf16[8192,512]{1,0:T(8,128)(2,1)} %get-tuple-element.98, bf16[4096,512]{1,0:T(8,128)(2,1)} %collective-permute-done.15, s32[]{:T(128)S(6)} %select_n.62), kind=kLoop, calls=%fused_computation.19 | loop fusion | bytes 8388612 | tf_op jit(solution)/shard_map/cond/branch_1_fun/dynamic_update_slice | solution.py:826
  259.8 2.5 collective-permute-done.14.b3
  262.3 3.7 %collective-permute-done.13.b2 = bf16[1088,128]{1,0:T(8,128)(2,1)S(1)} collective-permute-done((bf16[1088,128]{1,0:T(8,128)(2,1)S(1)}, bf16[1088,128]{1,0:T(8,128)(2,1)S(1)}, u32[]{:S(2)}, u32[]{:S(2)}) %collective-permute-start.13) | collective-permute-done | bytes 278560 | tf_op jit(solution)/shard_map/cond/branch_1_fun/ppermute | solution.py:762
  266.0 0.7 copy-done.9
  266.7 0.7 copy-done.10
  267.4 2.7 at_unpack.1
  270.1 0.0 copy-start.15
  270.1 0.0 copy-start.16
  270.1 0.0 all-reduce.2.cloned.1.call-done.total
  270.2 3.7 %ff_unpack.1 = (f32[512,1024]{1,0:T(8,128)}, f32[1024,512]{1,0:T(8,128)}) custom-call(bf16[2048,512]{1,0:T(8,128)(2,1)} %all-reduce.2.cloned.1.call-done.total), custom_call_target="tpu_custom_call" | custom-call | tf_op jit(solution)/shard_map/ff_unpack/pallas_call | solution.py:703
  (47 shorter events, 0.3 us)
Async XLA Ops:
  7.2 263.0 %all-reduce.2.cloned.1.call-start = ((), (), s32[]{:S(2)}) async-start(), calls=%async_computation | async-start | bytes 4194304 | tf_op jit(solution)/shard_map/psum | solution.py:867
  7.2 49.9 %collective-permute-start.21 = (bf16[512,1024]{1,0:T(8,128)(2,1)}, bf16[512,1024]{1,0:T(8,128)(2,1)}, u32[]{:S(2)}, u32[]{:S(2)}) collective-permute-start(bf16[512,1024]{1,0:T(8,128)(2,1)} %refs_2_), channel_id=1, source_target_pairs={{0,16},{16,0},{1,17},{17,1},{2,18},{18,2},{3,19},{19,3},{4,20},{20... | collective-permute-start | bytes 3145736 | tf_op jit(solution)/shard_map/ppermute | solution.py:732
  7.8 49.3 %collective-permute-start.22 = (bf16[1024,512]{1,0:T(8,128)(2,1)}, bf16[1024,512]{1,0:T(8,128)(2,1)S(1)}, u32[]{:S(2)}, u32[]{:S(2)}) collective-permute-start(bf16[1024,512]{1,0:T(8,128)(2,1)} %refs_4_), channel_id=1, source_target_pairs={{0,16},{16,0},{1,17},{17,1},{2,18},{18,2},{3,19},{19,3},{4,20},{20... | collective-permute-start | bytes 3145736 | tf_op jit(solution)/shard_map/ppermute | solution.py:732
  7.8 4.3 %collective-permute-start.16 = (bf16[512,256]{1,0:T(8,128)(2,1)}, bf16[512,256]{1,0:T(8,128)(2,1)S(1)}, u32[]{:S(2)}, u32[]{:S(2)}) collective-permute-start(bf16[512,256]{1,0:T(8,128)(2,1)} %refs_1_.2), channel_id=1, source_target_pairs={{0,16},{16,0},{1,17},{17,1},{2,18},{18,2},{3,19},{19,3},{4,20},{20... | collective-permute-start | bytes 786440 | tf_op jit(solution)/shard_map/ppermute | solution.py:732
  9.0 4.9 %copy-start.11 = (f32[1,1792]{1,0:T(1,128)}, f32[1,1792]{1,0:T(1,128)S(1)}, u32[]{:S(2)}) copy-start(f32[1,1792]{1,0:T(1,128)S(1)} %reshape.106.refs_12_.refs_8_) | copy-start | bytes 21508
  9.0 2.5 collective-permute-start.20
  9.2 3.3 %collective-permute-start.17 = (bf16[512,256]{1,0:T(8,128)(2,1)}, bf16[512,256]{1,0:T(8,128)(2,1)S(1)}, u32[]{:S(2)}, u32[]{:S(2)}) collective-permute-start(bf16[512,256]{1,0:T(8,128)(2,1)} %refs_3_.1), channel_id=1, source_target_pairs={{0,16},{16,0},{1,17},{17,1},{2,18},{18,2},{3,19},{19,3},{4,20},{20... | collective-permute-start | bytes 786440 | tf_op jit(solution)/shard_map/ppermute | solution.py:732
  11.5 2.4 copy-start.12
  11.5 1.7 collective-permute-start.18
  12.1 1.7 collective-permute-start.19
  13.2 43.9 %copy-start.5 = (bf16[512,256]{1,0:T(8,128)(2,1)}, bf16[512,256]{1,0:T(8,128)(2,1)S(1)}, u32[]{:S(2)}) copy-start(bf16[512,256]{1,0:T(8,128)(2,1)S(1)} %collective-permute-done.18.refs_6_) | copy-start | bytes 786436
  13.9 0.7 copy-start.7
  14.6 42.5 %copy-start = (bf16[1024,512]{1,0:T(8,128)(2,1)S(1)}, bf16[1024,512]{1,0:T(8,128)(2,1)}, u32[]{:S(2)}) copy-start(bf16[1024,512]{1,0:T(8,128)(2,1)} %refs_4_) | copy-start | bytes 3145732
  124.9 4.5 %collective-permute-start.23 = (bf16[2048,512]{1,0:T(8,128)(2,1)}, bf16[2048,512]{1,0:T(8,128)(2,1)S(1)}, u32[]{:S(2)}, u32[]{:S(2)}) collective-permute-start(bf16[2048,512]{1,0:T(8,128)(2,1)} %get-tuple-element.194), channel_id=1, source_target_pairs={{0,16},{16,0},{1,17},{17,1},{2,18},{18,2},{3,19},{19,3},{4,20},{20... | collective-permute-start | bytes 6291464 | tf_op jit(solution)/shard_map/ppermute | solution.py:732
  132.9 47.0 %copy-start.2 = (bf16[512,256]{1,0:T(8,128)(2,1)S(1)}, bf16[512,256]{1,0:T(8,128)(2,1)}, u32[]{:S(2)}) copy-start(bf16[512,256]{1,0:T(8,128)(2,1)} %refs_1_.2) | copy-start | bytes 786436
  132.9 47.0 %copy-start.3 = (bf16[512,256]{1,0:T(8,128)(2,1)S(1)}, bf16[512,256]{1,0:T(8,128)(2,1)}, u32[]{:S(2)}) copy-start(bf16[512,256]{1,0:T(8,128)(2,1)} %refs_3_.1) | copy-start | bytes 786436
  132.9 47.0 %copy-start.4 = (bf16[512,256]{1,0:T(8,128)(2,1)S(1)}, bf16[512,256]{1,0:T(8,128)(2,1)}, u32[]{:S(2)}) copy-start(bf16[512,256]{1,0:T(8,128)(2,1)} %refs_5_.1) | copy-start | bytes 786436
  132.9 47.0 %copy-start.6 = (bf16[512,256]{1,0:T(8,128)(2,1)S(1)}, bf16[512,256]{1,0:T(8,128)(2,1)}, u32[]{:S(2)}) copy-start(bf16[512,256]{1,0:T(8,128)(2,1)} %copy-done.5) | copy-start | bytes 786436
  132.9 47.0 %copy-start.13 = (f32[512]{0:T(512)S(1)}, f32[512]{0:T(512)}, u32[]{:S(2)}) copy-start(f32[512]{0:T(512)} %param.21) | copy-start | bytes 6148
  133.0 46.9 %copy-start.14 = (f32[512]{0:T(512)S(1)}, f32[512]{0:T(512)}, u32[]{:S(2)}) copy-start(f32[512]{0:T(512)} %param.36) | copy-start | bytes 6148
  179.9 3.1 %collective-permute-start = (bf16[4096,128]{1,0:T(8,128)(2,1)}, bf16[4096,128]{1,0:T(8,128)(2,1)}, u32[]{:S(2)}, u32[]{:S(2)}) collective-permute-start(bf16[4096,128]{1,0:T(8,128)(2,1)} %get-tuple-element.56), channel_id=1, source_target_pairs={{0,16},{16,0},{1,17},{17,1},{2,18},{18,2},{3,19},{19,3},{4,20},{20... | collective-permute-start | bytes 3145736 | tf_op jit(solution)/shard_map/cond/branch_1_fun/ppermute | solution.py:732
  199.6 26.7 %collective-permute-start.5 = (bf16[4096,512]{1,0:T(8,128)(2,1)}, bf16[4096,512]{1,0:T(8,128)(2,1)}, u32[]{:S(2)}, u32[]{:S(2)}) collective-permute-start(bf16[4096,512]{1,0:T(8,128)(2,1)} %get-tuple-element.82), channel_id=1, source_target_pairs={{0,16},{16,0},{1,17},{17,1},{2,18},{18,2},{3,19},{19,3},{4,20},{20... | collective-permute-start | bytes 12582920 | tf_op jit(solution)/shard_map/cond/branch_1_fun/ppermute | solution.py:732
  200.0 4.6 %collective-permute-start.1 = (bf16[256,128]{1,0:T(8,128)(2,1)}, bf16[256,128]{1,0:T(8,128)(2,1)S(1)}, u32[]{:S(2)}, u32[]{:S(2)}) collective-permute-start(bf16[256,128]{1,0:T(8,128)(2,1)} %get-tuple-element.81), channel_id=1, source_target_pairs={{0,16},{16,0},{1,17},{17,1},{2,18},{18,2},{3,19},{19,3},{4,20},{20... | collective-permute-start | bytes 196616 | tf_op jit(solution)/shard_map/cond/branch_1_fun/ppermute | solution.py:732
  205.7 20.6 %collective-permute-start.4 = (bf16[1088,128]{1,0:T(8,128)(2,1)S(1)}, bf16[1088,128]{1,0:T(8,128)(2,1)S(1)}, u32[]{:S(2)}, u32[]{:S(2)}) collective-permute-start(bf16[1088,128]{1,0:T(8,128)(2,1)S(1)} %get-tuple-element.236), channel_id=1, source_target_pairs={{0,3},{1,2},{2,1},{3,0},{4,7},{5,6},{6,5},{7,4},{8,11},{9,10},{10,... | collective-permute-start | bytes 835592 | tf_op jit(solution)/shard_map/cond/branch_1_fun/ppermute | solution.py:762
  209.4 16.9 %collective-permute-start.3 = (bf16[1088,128]{1,0:T(8,128)(2,1)S(1)}, bf16[1088,128]{1,0:T(8,128)(2,1)S(1)}, u32[]{:S(2)}, u32[]{:S(2)}) collective-permute-start(bf16[1088,128]{1,0:T(8,128)(2,1)S(1)} %get-tuple-element.237), channel_id=1, source_target_pairs={{0,2},{1,3},{2,0},{3,1},{4,6},{5,7},{6,4},{7,5},{8,10},{9,11},{10,... | collective-permute-start | bytes 835592 | tf_op jit(solution)/shard_map/cond/branch_1_fun/ppermute | solution.py:762
  209.9 16.4 %collective-permute-start.2 = (bf16[1088,128]{1,0:T(8,128)(2,1)S(1)}, bf16[1088,128]{1,0:T(8,128)(2,1)S(1)}, u32[]{:S(2)}, u32[]{:S(2)}) collective-permute-start(bf16[1088,128]{1,0:T(8,128)(2,1)S(1)} %get-tuple-element.238), channel_id=1, source_target_pairs={{0,1},{1,0},{2,3},{3,2},{4,5},{5,4},{6,7},{7,6},{8,9},{9,8},{10,11... | collective-permute-start | bytes 835592 | tf_op jit(solution)/shard_map/cond/branch_1_fun/ppermute | solution.py:762
  226.3 29.0 %collective-permute-start.15 = (bf16[4096,512]{1,0:T(8,128)(2,1)}, bf16[4096,512]{1,0:T(8,128)(2,1)}, u32[]{:S(2)}, u32[]{:S(2)}) collective-permute-start(bf16[4096,512]{1,0:T(8,128)(2,1)} %get-tuple-element.99), channel_id=1, source_target_pairs={{0,16},{16,0},{1,17},{17,1},{2,18},{18,2},{3,19},{19,3},{4,20},{20... | collective-permute-start | bytes 12582920 | tf_op jit(solution)/shard_map/cond/branch_1_fun/ppermute | solution.py:732
  227.2 9.6 %collective-permute-start.6 = (bf16[272,128]{1,0:T(8,128)(2,1)S(1)}, bf16[272,128]{1,0:T(8,128)(2,1)S(1)}, u32[]{:S(2)}, u32[]{:S(2)}) collective-permute-start(bf16[272,128]{1,0:T(8,128)(2,1)S(1)} %get-tuple-element.240), channel_id=1, source_target_pairs={{0,4},{1,5},{2,6},{3,7},{4,0},{5,1},{6,2},{7,3},{8,12},{9,13},{10,... | collective-permute-start | bytes 208904 | tf_op jit(solution)/shard_map/cond/branch_1_fun/ppermute | solution.py:762
  229.2 7.7 %collective-permute-start.8 = (bf16[272,128]{1,0:T(8,128)(2,1)S(1)}, bf16[272,128]{1,0:T(8,128)(2,1)S(1)}, u32[]{:S(2)}, u32[]{:S(2)}) collective-permute-start(bf16[272,128]{1,0:T(8,128)(2,1)S(1)} %get-tuple-element.241), channel_id=1, source_target_pairs={{0,12},{1,13},{2,14},{3,15},{4,8},{5,9},{6,10},{7,11},{8,4},{9,5},... | collective-permute-start | bytes 208904 | tf_op jit(solution)/shard_map/cond/branch_1_fun/ppermute | solution.py:762
  231.8 8.1 %collective-permute-start.7 = (bf16[272,128]{1,0:T(8,128)(2,1)S(1)}, bf16[272,128]{1,0:T(8,128)(2,1)S(1)}, u32[]{:S(2)}, u32[]{:S(2)}) collective-permute-start(bf16[272,128]{1,0:T(8,128)(2,1)S(1)} %get-tuple-element.242), channel_id=1, source_target_pairs={{0,8},{1,9},{2,10},{3,11},{4,12},{5,13},{6,14},{7,15},{8,0},{9,1},... | collective-permute-start | bytes 208904 | tf_op jit(solution)/shard_map/cond/branch_1_fun/ppermute | solution.py:762
  240.0 11.7 %collective-permute-start.11 = (bf16[272,128]{1,0:T(8,128)(2,1)S(1)}, bf16[272,128]{1,0:T(8,128)(2,1)S(1)}, u32[]{:S(2)}, u32[]{:S(2)}) collective-permute-start(bf16[272,128]{1,0:T(8,128)(2,1)S(1)} %fusion.2), channel_id=1, source_target_pairs={{0,12},{1,13},{2,14},{3,15},{4,8},{5,9},{6,10},{7,11},{8,4},{9,5},... | collective-permute-start | bytes 208904 | tf_op jit(solution)/shard_map/cond/branch_1_fun/ppermute | solution.py:762
  242.4 9.3 %collective-permute-start.10 = (bf16[272,128]{1,0:T(8,128)(2,1)S(1)}, bf16[272,128]{1,0:T(8,128)(2,1)S(1)}, u32[]{:S(2)}, u32[]{:S(2)}) collective-permute-start(bf16[272,128]{1,0:T(8,128)(2,1)S(1)} %fusion.2), channel_id=1, source_target_pairs={{0,8},{1,9},{2,10},{3,11},{4,12},{5,13},{6,14},{7,15},{8,0},{9,1},... | collective-permute-start | bytes 208904 | tf_op jit(solution)/shard_map/cond/branch_1_fun/ppermute | solution.py:762
  242.4 8.7 %collective-permute-start.9 = (bf16[272,128]{1,0:T(8,128)(2,1)S(1)}, bf16[272,128]{1,0:T(8,128)(2,1)S(1)}, u32[]{:S(2)}, u32[]{:S(2)}) collective-permute-start(bf16[272,128]{1,0:T(8,128)(2,1)S(1)} %fusion.2), channel_id=1, source_target_pairs={{0,4},{1,5},{2,6},{3,7},{4,0},{5,1},{6,2},{7,3},{8,12},{9,13},{10,... | collective-permute-start | bytes 208904 | tf_op jit(solution)/shard_map/cond/branch_1_fun/ppermute | solution.py:762
  251.7 8.1 %copy-start.1 = (bf16[4,272,128]{2,1,0:T(8,128)(2,1)}, bf16[4,272,128]{2,1,0:T(8,128)(2,1)S(1)}, u32[]{:S(2)}) copy-start(bf16[4,272,128]{2,1,0:T(8,128)(2,1)S(1)} %bitcast_dynamic-update-slice_fusion) | copy-start | bytes 835588 | tf_op jit(solution)/shard_map/cond
  251.7 10.6 %collective-permute-start.14 = (bf16[1088,128]{1,0:T(8,128)(2,1)S(1)}, bf16[1088,128]{1,0:T(8,128)(2,1)S(1)}, u32[]{:S(2)}, u32[]{:S(2)}) collective-permute-start(bf16[1088,128]{1,0:T(8,128)(2,1)S(1)} %bitcast.48), channel_id=1, source_target_pairs={{0,3},{1,2},{2,1},{3,0},{4,7},{5,6},{6,5},{7,4},{8,11},{9,10},{10,... | collective-permute-start | bytes 835592 | tf_op jit(solution)/shard_map/cond/branch_1_fun/ppermute | solution.py:762
  253.9 12.1 %collective-permute-start.13 = (bf16[1088,128]{1,0:T(8,128)(2,1)S(1)}, bf16[1088,128]{1,0:T(8,128)(2,1)S(1)}, u32[]{:S(2)}, u32[]{:S(2)}) collective-permute-start(bf16[1088,128]{1,0:T(8,128)(2,1)S(1)} %bitcast.49), channel_id=1, source_target_pairs={{0,2},{1,3},{2,0},{3,1},{4,6},{5,7},{6,4},{7,5},{8,10},{9,11},{10,... | collective-permute-start | bytes 835592 | tf_op jit(solution)/shard_map/cond/branch_1_fun/ppermute | solution.py:762
  254.7 11.4 %collective-permute-start.12 = (bf16[1088,128]{1,0:T(8,128)(2,1)S(1)}, bf16[1088,128]{1,0:T(8,128)(2,1)S(1)}, u32[]{:S(2)}, u32[]{:S(2)}) collective-permute-start(bf16[1088,128]{1,0:T(8,128)(2,1)S(1)} %bitcast.50), channel_id=1, source_target_pairs={{0,1},{1,0},{2,3},{3,2},{4,5},{5,4},{6,7},{7,6},{8,9},{9,8},{10,11... | collective-permute-start | bytes 835592 | tf_op jit(solution)/shard_map/cond/branch_1_fun/ppermute | solution.py:762
  262.3 3.7 %copy-start.8 = (bf16[1088,128]{1,0:T(8,128)(2,1)}, bf16[1088,128]{1,0:T(8,128)(2,1)S(1)}, u32[]{:S(2)}) copy-start(bf16[1088,128]{1,0:T(8,128)(2,1)S(1)} %collective-permute-done.14.b3) | copy-start | bytes 835588 | tf_op jit(solution)/shard_map/cond
  266.0 0.7 copy-start.9
  266.7 0.7 copy-start.10
  270.1 3.8 %copy-start.15 = (f32[512]{0:T(512)}, f32[512]{0:T(512)S(1)}, u32[]{:S(2)}) copy-start(f32[512]{0:T(512)S(1)} %get-tuple-element.181) | copy-start | bytes 6148
  270.1 3.8 %copy-start.16 = (f32[512]{0:T(512)}, f32[512]{0:T(512)S(1)}, u32[]{:S(2)}) copy-start(f32[512]{0:T(512)S(1)} %get-tuple-element.180) | copy-start | bytes 6148
Sparse Core Ops, SparseCore 0:
  133.0 133.3 all-reduce.1

commit v5 on v4

--- a/solution.py
+++ b/solution.py
@@ -177,7 +177,8 @@
 
     def finish(s, mixed):
         x = tok[s * SEQ : (s + 1) * SEQ, :].astype(F32).T
-        hidden_o[s] = x + dot(wo_t[...], jnp.concatenate(mixed, axis=0)) + wide(vec[5 * dim : 6 * dim, :], SEQ)
+        made = x + dot(wo_t[...], jnp.concatenate(mixed, axis=0)) + wide(vec[5 * dim : 6 * dim, :], SEQ)
+        hidden_o[s] = made.astype(BF)
 
     first = prepare(0)
     ready = project(0, 0, first)
@@ -201,8 +202,8 @@
 
 def mlp_kernel(seqs, block, place, *refs):
     (hid, cot, wu0, wu1, wd0, wd1, gain2, shift2, small0, small1) = refs[:10]
-    (act_o, low_o, own_o, other_o, gvec_o) = refs[10:15]
-    wu_t, gup, gdown, gvec, vec, bup = refs[15:21]
+    (act_o, dup_o, own_o, other_o, gvec_o) = refs[10:15]
+    wu_t, gup, gdown, vec, bup = refs[15:20]
     dim = hid.shape[1]
     units = wu0.shape[1]
     lanes = seqs * SEQ
@@ -218,24 +219,19 @@
             vec[index * dim : (index + 1) * dim, :] = as_column(ref[...])
         gup[...] = jnp.zeros_like(gup)
         gdown[...] = jnp.zeros_like(gdown)
-        gvec[...] = jnp.zeros_like(gvec)
-
-    hidden = jnp.concatenate([hid[s] for s in range(seqs)], axis=1)
-    grad_out = cot[...].astype(F32).T
-    grad_low = grad_out.astype(BF)
-    gain = wide(vec[0:dim, :], lanes)
-    plain, factor = norm_plain(hidden)
-    second = (plain * gain + wide(vec[dim : 2 * dim, :], lanes)).astype(BF)
+
+    hidden = jnp.concatenate([hid[s] for s in range(seqs)], axis=1).astype(F32)
+    grad_low = cot[...].astype(F32).T.astype(BF)
+    plain, _ = norm_plain(hidden)
+    second = plain * wide(vec[0:dim, :], lanes) + wide(vec[dim : 2 * dim, :], lanes)
+    second = second.astype(BF)
     ones = jnp.ones((16, lanes), BF)
     second_ones = jnp.concatenate([second, ones], axis=0)
-    dnorm = None
     for start in range(0, 2 * units, block):
         span = slice(start, start + block)
         half, inner = divmod(start, units)
-        up_ref, down_ref = ((wu0, wd0), (wu1, wd1))[half]
-        inner = slice(inner, inner + block)
         upper = dot(wu_t[span, :], second) + wide(bup[span, :], lanes)
-        dact = dot(down_ref[inner, :], grad_low)
+        dact = dot((wd0, wd1)[half][inner : inner + block, :], grad_low)
         part = upper * (1.0 / math.sqrt(2.0))
         cdf = 0.5 * lax.erf(part) + 0.5
         density = jnp.exp2((part * part) * (-1.0 / math.log(2.0)))
@@ -243,20 +239,13 @@
         dup = (dact * (cdf + part * density * (1.0 / math.sqrt(math.pi)))).astype(BF)
         for s in range(seqs):
             act_o[s, span, :] = act[:, s * SEQ : (s + 1) * SEQ]
-        dn_part = dot(up_ref[:, inner], dup)
-        dnorm = dn_part if dnorm is None else dnorm + dn_part
+            dup_o[s, span, :] = dup[:, s * SEQ : (s + 1) * SEQ]
         gup[:, span] += tail_dot(second_ones, dup)
         if start == 0:
             act = jnp.concatenate([ones, act], axis=0)
             gdown[: 16 + block, :] += tail_dot(act, grad_low)
         else:
             gdown[16 + start : 16 + start + block, :] += tail_dot(act, grad_low)
-    gvec[0:dim, :] += lane_fold(dnorm * plain)
-    gvec[dim : 2 * dim, :] += lane_fold(dnorm)
-    dhidden = grad_out + norm_back(dnorm, plain, factor, gain)
-    gvec[2 * dim :, :] += lane_fold(dhidden)
-    for s in range(seqs):
-        low_o[s] = dhidden[:, s * SEQ : (s + 1) * SEQ].astype(BF)
 
     @pl.when(step == pl.num_programs(0) - 1)
     def _():
@@ -265,9 +254,7 @@
                 start = half * units + index * dim
                 grad_o[index * dim : (index + 1) * dim, :] = gup[:dim, start : start + dim].astype(BF)
             grad_o[units:, :] = gdown[16 + half * units : 16 + (half + 1) * units, :].astype(BF)
-        for index, row in ((0, 0), (1, 1), (2, 3)):
-            gvec_o[row : row + 1, :] = as_row(gvec[index * dim : (index + 1) * dim, :])
-        gvec_o[2:3, :] = gdown[:1, :]
+        gvec_o[0:1, :] = gdown[:1, :]
         for index in range(2 * units // dim):
             gvec_o[4 + index : 5 + index, :] = gup[dim : dim + 1, index * dim : (index + 1) * dim]
 
@@ -283,7 +270,7 @@
 
     for s in range(seqs):
         rows = slice(s * SEQ, (s + 1) * SEQ)
-        out = hid[s] + dot(wd_t[...], act[s]) + wide(vec[...], SEQ)
+        out = hid[s].astype(F32) + dot(wd_t[...], act[s]) + wide(vec[...], SEQ)
         made = out.T.astype(BF)
         out_o[rows, :] = made
         whole_o[rows, :] = made
@@ -296,17 +283,21 @@
     down_o[...] = total[units:, :].astype(F32)
 
 
-def at_unpack_kernel(here, b0, b1, b2, b3, *refs):
+def at_unpack_kernel(here, b0, b1, b2, b3, v0, v1, v2, v3, *refs):
     outs, hold = refs[:-1], refs[-1]
     size = b0.shape[0]
     for m, block in enumerate((b0, b1, b2, b3)):
         hold[here[m]] = block[...]
-    rows = lambda start, count: [
-        hold[k, max(start - k * size, 0) : min(start + count - k * size, size), :].astype(F32)
-        for k in range(4)
-        if start < (k + 1) * size and start + count > k * size
-    ]
-    get = lambda start, count: jnp.concatenate(rows(start, count), axis=0)
+
+    def get(start, count):
+        parts = []
+        while count > 0:
+            k, inner = divmod(start, size)
+            taken = min(count, size - inner)
+            parts.append(hold[k, inner : inner + taken, :].astype(F32))
+            start, count = start + taken, count - taken
+        return parts[0] if len(parts) == 1 else jnp.concatenate(parts, axis=0)
+
     dim = outs[0].shape[0]
     for g in range(2):
         base = g * 4 * dim
@@ -316,20 +307,25 @@
             outs[3][g * LANES : (g + 1) * LANES, index * LANES : (index + 1) * LANES] = get(
                 base + 3 * dim + index * LANES, LANES
             )
-    at = 8 * dim
+    used = sum(out.shape[1] for out in outs[4:]) // LANES
+    used = -(-used // 16) * 16
+    vector = sum(v[:used, :].astype(F32) for v in (v0, v1, v2, v3))
+    at = 0
     for out in outs[4:]:
         for start in range(0, out.shape[1], LANES):
-            out[:, start : start + LANES] = get(at // 16 * 16, 16)[at % 16 : at % 16 + 1]
+            out[:, start : start + LANES] = vector[at : at + 1, :]
             at += 1
 
 
-def grad_kernel(seqs, *refs):
-    (low_i, first_i, query_i, keys_i, values_i, mixed_i, signed_i, slope_i, norm_i) = refs[:9]
-    wo0, wo1 = refs[9:11]
-    outs = refs[11:17]
-    own_o, other_o, gvec_o = refs[17:20]
-    gqkv, gout, gb = refs[20:23]
-    dim = low_i.shape[1]
+def grad_kernel(seqs, place, *refs):
+    (hid, cot, dup, first_i) = refs[:4]
+    (query_i, keys_i, values_i, mixed_i, signed_i, slope_i, norm_i) = refs[4:11]
+    wo0, wo1, wu0, wu1, gain2 = refs[11:16]
+    outs = refs[16:22]
+    low_o, own_o, other_o, gvec_o, hvec_o = refs[22:27]
+    gqkv, gout, gb, hvec, vec = refs[27:32]
+    dim = hid.shape[1]
+    units = wu0.shape[1]
     part = 2 * LANES
     step = pl.program_id(0)
     scale = 1.0 / math.sqrt(HEAD_DIM)
@@ -339,21 +335,42 @@
         gqkv[...] = jnp.zeros_like(gqkv)
         gout[...] = jnp.zeros_like(gout)
         gb[...] = jnp.zeros_like(gb)
-
-    first = jnp.concatenate([first_i[s] for s in range(seqs)], axis=1)
-    low = jnp.concatenate([low_i[s] for s in range(seqs)], axis=1)
-
-    def pair(s, c, g, dm):
+        hvec[...] = jnp.zeros_like(hvec)
+        vec[...] = as_column(gain2[...])
+
+    def hidden_grad(s):
+        dnorm = dot(wu0[...], dup[s, :units, :]) + dot(wu1[...], dup[s, units:, :])
+        plain, factor = norm_plain(hid[s].astype(F32))
+        grad_out = cot[s * SEQ : (s + 1) * SEQ, :].astype(F32).T
+        dhidden = grad_out + norm_back(dnorm, plain, factor, wide(vec[...], SEQ))
+        hvec[0:dim, :] += lane_fold(dnorm * plain)
+        hvec[dim : 2 * dim, :] += lane_fold(dnorm)
+        hvec[2 * dim :, :] += lane_fold(dhidden)
+        low = dhidden.astype(BF)
+        low_o[s] = low
+        dmixed = []
+        for c, wo in enumerate((wo0, wo1)):
+            spread = [
+                jnp.broadcast_to(norm_i[s, c, g, e : e + 1, :], (HEAD_DIM, SEQ))
+                for g in range(2)
+                for e in range(2)
+            ]
+            dmixed.append((dot(wo[...], low) * jnp.concatenate(spread, axis=0)).astype(BF))
+        return low, dmixed
+
+    def inner(s, g, c, dmixed):
+        dm = dmixed[c][g * LANES : (g + 1) * LANES]
+        v_nat = turned(values_i[s, c, g])
+        near_m, far_m = pair_near_far(dm)
+        return dot(v_nat[:HALF], near_m), dot(v_nat, far_m), near_m, far_m
+
+    def outer(s, g, c, near_s, far_s, near_m, far_m):
         q, k = query_i[s, c, g], keys_i[s, c, g]
-        v_nat = turned(values_i[s, c, g])
         near_q, far_q = pair_near_far(q)
-        near_m, far_m = pair_near_far(dm)
         low_pair = []
-        for index in range(2):
-            keys = slice(0, HALF) if index == 0 else slice(0, SEQ)
+        for index, dsigned in enumerate((near_s, far_s)):
             block = slice(0, HALF) if index == 0 else slice(HALF, HALF + SEQ)
             lanes = slice(index * HALF, (index + 1) * HALF)
-            dsigned = dot(v_nat[keys], (near_m, far_m)[index])
             signed = signed_i[s, c, g, block].astype(F32)
             row_dot = jnp.sum(signed * dsigned, axis=0, keepdims=True)
             row_dot = row_dot * jnp.concatenate(
@@ -375,55 +392,47 @@
         near_p = tail_dot(signed_i[s, c, g, :HALF], near_m)
         far_p = tail_dot(signed_i[s, c, g, HALF:], far_m)
         dv = jnp.concatenate([far_p[:HALF] + near_p, far_p[HALF:]], axis=0)
-        return dq, dk, dv
-
-    for g in range(2):
-        place = slice(g * LANES, (g + 1) * LANES)
-        spread = lambda s, c, e: jnp.broadcast_to(norm_i[s, c, g, e : e + 1, :], (HEAD_DIM, SEQ))
-        norms = jnp.concatenate(
-            [
-                jnp.concatenate([spread(s, c, e) for c in range(2) for e in range(2)], axis=0)
-                for s in range(seqs)
-            ],
-            axis=1,
-        )
-        dmixed = jnp.concatenate([dot(wo0[place, :], low), dot(wo1[place, :], low)], axis=0)
-        dmixed = (dmixed * norms).astype(BF)
-        mixed = jnp.concatenate(
-            [
-                jnp.concatenate([mixed_i[s, 0, g], mixed_i[s, 1, g]], axis=0)
-                for s in range(seqs)
-            ],
-            axis=1,
-        )
+        dq, dk, dv = (dq * scale).astype(BF), dk.astype(BF), dv.astype(BF)
         dq_o, dk_o, dv_o = outs[3 * g : 3 * g + 3]
-        dq_all, dk_all, dv_all = [], [], []
-        for s in range(seqs):
-            span = slice(s * SEQ, (s + 1) * SEQ)
-            dq, dk, dv = zip(
-                *[pair(s, c, g, dmixed[c * LANES : (c + 1) * LANES, span]) for c in range(2)]
-            )
-            dq_all.append((jnp.concatenate(dq, axis=0) * scale).astype(BF))
-            dk_all.append(jnp.concatenate(dk, axis=1).astype(BF))
-            dv_all.append(jnp.concatenate(dv, axis=1).astype(BF))
-            dq_o[s], dk_o[s], dv_o[s] = dq_all[s], dk_all[s], dv_all[s]
+        rows = slice(c * LANES, (c + 1) * LANES)
+        dq_o[s, rows, :], dk_o[s, :, rows], dv_o[s, :, rows] = dq, dk, dv
+        base = g * 4 * LANES
+        gb[base + c * LANES : base + (c + 1) * LANES, :] += lane_fold(dq.astype(F32))
+        for index, block in ((2, dk), (3, dv)):
+            at = base + index * LANES + 8 * c
+            gb[at : at + 8, :] += jnp.sum(block.astype(F32).reshape(-1, 8, LANES), axis=0)
+
+    def weight_grads(s, low, g):
+        first = first_i[s]
+        mixed = jnp.concatenate([mixed_i[s, 0, g], mixed_i[s, 1, g]], axis=0)
         gout[g * part : (g + 1) * part, :] += tail_dot(mixed, low)
-        dq = jnp.concatenate(dq_all, axis=1)
-        dk, dv = jnp.concatenate(dk_all, axis=0), jnp.concatenate(dv_all, axis=0)
+        dq_o, dk_o, dv_o = outs[3 * g : 3 * g + 3]
         at = 3 * g * part
-        gqkv[:, at : at + part] += tail_dot(first, dq)
-        gqkv[:, at + part : at + 2 * part] += dot(first, dk)
-        gqkv[:, at + 2 * part : at + 3 * part] += dot(first, dv)
-        base = g * 4 * LANES
-        gb[base : base + part, :] += lane_fold(dq.astype(F32))
-        for index, block in ((2, dk), (3, dv)):
-            total = jnp.sum(block.astype(F32).reshape(-1, 8, part), axis=0)
-            rows = base + index * LANES
-            gb[rows : rows + 8, :] += total[:, :LANES]
-            gb[rows + 8 : rows + 16, :] += total[:, LANES:]
+        gqkv[:, at : at + part] += tail_dot(first, dq_o[s])
+        gqkv[:, at + part : at + 2 * part] += dot(first, dk_o[s])
+        gqkv[:, at + 2 * part : at + 3 * part] += dot(first, dv_o[s])
+
+    order = [(s, g, c) for s in range(seqs) for g in range(2) for c in range(2)]
+    lows, mixes = {}, {}
+    lows[0], mixes[0] = hidden_grad(0)
+    ready = inner(*order[0], mixes[0])
+    for n, (s, g, c) in enumerate(order):
+        current = ready
+        if n + 1 < len(order):
+            following = order[n + 1]
+            ready = inner(*following, mixes[following[0]])
+        outer(s, g, c, *current)
+        if c == 1 and n >= 3:
+            back = order[n - 2]
+            weight_grads(back[0], lows[back[0]], back[1])
+        if (g, c) == (0, 1) and s + 1 < seqs:
+            lows[s + 1], mixes[s + 1] = hidden_grad(s + 1)
+    weight_grads(seqs - 1, lows[seqs - 1], 1)
 
     @pl.when(step == pl.num_programs(0) - 1)
     def _():
+        for index in range(3):
+            hvec_o[index : index + 1, :] = as_row(hvec[index * dim : (index + 1) * dim, :])
         for g in range(2):
             base = g * 4 * LANES
             tall = g * 4 * dim
@@ -451,9 +460,9 @@
 def input_kernel(seqs, place, *refs):
     tok, dhid, dq0, dk0, dv0, dq1, dk1, dv1 = refs[:8]
     wq0, wq1, wk0, wk1, wv0, wv1, gain1 = refs[8:15]
-    vec_ff, vec_at = refs[15:17]
-    tgrad_o, whole_o, gvec_o, own_o, other_o = refs[17:22]
-    gvec, vec, pack = refs[22:25]
+    vec_ff, vec_hid, vec_at = refs[15:18]
+    tgrad_o, whole_o, gvec_o, own_o, other_o = refs[18:23]
+    gvec, vec, pack = refs[23:26]
     dim = tok.shape[1]
 
     @pl.when(pl.program_id(0) == 0)
@@ -484,7 +493,7 @@
     def _():
         for index in range(2):
             gvec_o[index : index + 1, :] = as_row(gvec[index * dim : (index + 1) * dim, :])
-        same = [(vec_ff, r) for r in range(4)] + [(gvec_o, 0), (gvec_o, 1)]
+        same = [(vec_hid, 0), (vec_hid, 1), (vec_ff, 0), (vec_hid, 2), (gvec_o, 0), (gvec_o, 1)]
         units = 2 * dim
         pack[...] = jnp.zeros_like(pack)
         for c, out in enumerate((own_o, other_o)):
@@ -553,29 +562,48 @@
         out_shape=[shape((count,) + feat, BF)] * 4
         + [shape((count,) + wide_block, BF)] * 2
         + [shape((count, 2, 2, 8, SEQ), F32)]
-        + [shape((count, dim, SEQ), BF), shape((count, dim, SEQ), F32)],
+        + [shape((count, dim, SEQ), BF)] * 2,
         compiler_params=params(),
         cost_estimate=pl.CostEstimate(flops=1, bytes_accessed=1, transcendentals=0),
         name="attn_forward",
     )(place, tokens, *weights, *vectors)
 
 
-def grad_call(low, first, saved, weights, seqs):
-    count, dim = low.shape[:2]
+def grad_call(place, hidden, cotangent, dup, first, saved, weights, seqs):
+    count, dim = hidden.shape[:2]
     steps = count // seqs
-    every = lambda *dims: seq_block(seqs, 2, 2, *dims)
+    units = dup.shape[1]
+    every = lambda *dims: placed_seq_block(seqs, 2, 2, *dims)
     shape = jax.ShapeDtypeStruct
     part = 2 * LANES
-    trio = [seq_block(seqs, part, SEQ), seq_block(seqs, SEQ, part), seq_block(seqs, SEQ, part)]
+    trio = [
+        placed_seq_block(seqs, part, SEQ),
+        placed_seq_block(seqs, SEQ, part),
+        placed_seq_block(seqs, SEQ, part),
+    ]
     return pl.pallas_call(
         functools.partial(grad_kernel, seqs),
-        grid=(steps,),
-        in_specs=[seq_block(seqs, dim, SEQ)] * 2
-        + [every(LANES, SEQ)] * 4
-        + [every(HALF + SEQ, SEQ)] * 2
-        + [every(8, SEQ)]
-        + [whole_vmem()] * 2,
-        out_specs=trio * 2 + [whole_vmem()] * 3,
+        grid_spec=prefetch(
+            (steps,),
+            [
+                placed_seq_block(seqs, dim, SEQ),
+                row_block(seqs, dim, steps),
+                placed_seq_block(seqs, units, SEQ),
+                placed_seq_block(seqs, dim, SEQ),
+            ]
+            + [every(LANES, SEQ)] * 4
+            + [every(HALF + SEQ, SEQ)] * 2
+            + [every(8, SEQ)]
+            + [whole_vmem()] * 5,
+            trio * 2 + [placed_seq_block(seqs, dim, SEQ)] + [whole_vmem()] * 4,
+            [
+                pltpu.VMEM((dim, 6 * part), F32),
+                pltpu.VMEM((2 * part, dim), F32),
+                pltpu.VMEM((8 * LANES, LANES), F32),
+                pltpu.VMEM((3 * dim, LANES), F32),
+                pltpu.VMEM((dim, LANES), F32),
+            ],
+        ),
         out_shape=[
             shape((count, part, SEQ), BF),
             shape((count, SEQ, part), BF),
@@ -583,19 +611,16 @@
         ]
         * 2
         + [
+            shape((count, dim, SEQ), BF),
             shape((8 * dim, LANES), BF),
             shape((8 * dim, LANES), BF),
             shape((16, LANES), F32),
-        ],
-        scratch_shapes=[
-            pltpu.VMEM((dim, 6 * part), F32),
-            pltpu.VMEM((2 * part, dim), F32),
-            pltpu.VMEM((8 * LANES, LANES), F32),
+            shape((8, dim), F32),
         ],
         compiler_params=params(),
         cost_estimate=pl.CostEstimate(flops=1, bytes_accessed=1, transcendentals=0),
         name="attn_backward",
-    )(low, first, *saved, *weights)
+    )(place, hidden, cotangent, dup, first, *saved, *weights)
 
 
 def input_call(place, tokens, dhidden, pieces, weights, gain1, vectors, grow, seqs):
@@ -614,7 +639,7 @@
             (steps,),
             [row_block(seqs, dim, steps), placed_seq_block(seqs, dim, SEQ)]
             + trio * 2
-            + [whole_vmem()] * 9,
+            + [whole_vmem()] * 10,
             [
                 pl.BlockSpec((seqs * SEQ, dim), lambda i, place: (i, 0)),
                 row_block(seqs, dim, steps),
@@ -649,20 +674,18 @@
         grid_spec=prefetch(
             (steps,),
             [placed_seq_block(seqs, dim, SEQ), row_block(seqs, dim, steps)] + [whole_vmem()] * 8,
-            [placed_seq_block(seqs, 2 * units, SEQ), placed_seq_block(seqs, dim, SEQ)]
-            + [whole_vmem()] * 3,
+            [placed_seq_block(seqs, 2 * units, SEQ)] * 2 + [whole_vmem()] * 3,
             [
                 pltpu.VMEM((2 * units, dim), BF),
                 pltpu.VMEM((dim + 16, 2 * units), F32),
                 pltpu.VMEM((2 * units + 16, dim), F32),
-                pltpu.VMEM((3 * dim, LANES), F32),
                 pltpu.VMEM((2 * dim, LANES), F32),
                 pltpu.VMEM((2 * units, LANES), F32),
             ],
         ),
         out_shape=[
             shape((count, 2 * units, SEQ), BF),
-            shape((count, dim, SEQ), BF),
+            shape((count, 2 * units, SEQ), BF),
             shape((2 * units, dim), BF),
             shape((2 * units, dim), BF),
             shape((8, dim), F32),
@@ -713,19 +736,19 @@
     )(total)
 
 
-def at_unpack_call(here, blocks, dim, local, sizes):
+def at_unpack_call(here, blocks, vecs, dim, local, sizes):
     shape = jax.ShapeDtypeStruct
     outs = [shape((dim, local), F32)] * 3 + [shape((local, dim), F32)]
     outs += [shape((1, n), F32) for n in sizes]
     return pl.pallas_call(
         at_unpack_kernel,
-        in_specs=[pl.BlockSpec(memory_space=pltpu.SMEM)] + [whole_vmem()] * 4,
+        in_specs=[pl.BlockSpec(memory_space=pltpu.SMEM)] + [whole_vmem()] * 8,
         out_specs=[whole_vmem()] * len(outs),
         out_shape=outs,
         scratch_shapes=[pltpu.VMEM((4,) + blocks[0].shape, BF)],
         compiler_params=pltpu.CompilerParams(vmem_limit_bytes=VMEM_LIMIT),
         name="at_unpack",
-    )(here, *blocks)
+    )(here, *blocks, *vecs)
 
 
 def shifted(value, axis, count, shift):
@@ -816,6 +839,7 @@
             )
             for c in range(2)
         ]
+    weights, smalls, wu, wd = tie((weights, smalls, wu, wd))
     mlp_weights = gathered(wu, mp, 1) + gathered(wd, mp, 0)
     gain1, shift1, bo, gain2, shift2, bd = (
         v.reshape(1, -1) for v in (gain1, shift1, bo, gain2, shift2, bd)
@@ -859,98 +883,127 @@
         place, tokens, own, weights, [gain1, shift1, bo] + smalls, SEQS["attn"]
     )
     hidden, mlp_weights = tie((hidden, mlp_weights))
-    act, low, *grad_ff, vec_ff = mlp_call(
+    act, dup, *grad_ff, vec_ff = mlp_call(
         place, hidden, cotangent, mlp_weights, [gain2, shift2] + smalls, SEQS["mlp"], 512
     )
     ff = total_of(mp_send(lambda r: ff_piece(grad_ff, r)))
-    low, ff = tie((low, ff))
+    dup, ff = tie((dup, ff))
     ff = lax.psum(ff, "dp")
-    *pieces, grad_own, grad_other, vec_at = grad_call(low, first, saved, weights[6:], SEQS["grad"])
+    *pieces, low, grad_own, grad_other, vec_at, vec_hid = grad_call(
+        place,
+        hidden,
+        cotangent,
+        dup,
+        first,
+        saved,
+        weights[6:] + mlp_weights[:2] + [gain2],
+        SEQS["grad"],
+    )
     grad_at = [grad_own, grad_other]
 
-    def finish(low, act, grad_at):
-        at = mp_send(lambda r: grad_at[r]) if per == 1 else []
-        low, at = tie((low, at))
-        grow = -(-(6 * dim + 3 * local + units) // (16 * dp * LANES)) * 16 * dp
-        tgrad, tgrad_full, vec_in, *vec_low = input_call(
+    sizes = [dim] * 6 + [local] * 3 + [units]
+    grow = max(-(-sum(sizes) // (16 * LANES)) * 16, -(-(6 * dim + 6 * LANES + 2 * dim) // (16 * LANES)) * 16)
+
+    def input_grads(low):
+        return input_call(
             place,
             tokens,
             low,
             pieces,
             weights[:6],
             gain1,
-            [vec_ff, vec_at],
-            max(grow, -(-(6 * dim + 6 * LANES + 2 * dim) // LANES)),
+            [vec_ff, vec_hid, vec_at],
+            grow,
             SEQS["input"],
         )
+
+    def layer_outs(act):
+        return out_call(place, hidden, act, mlp_weights[2:], bd, rows, SEQS["out"])
+
+    def finish(low, act, grad_at):
+        at = dp_sum.scatter(total_of(mp_send(lambda r: grad_at[r])), 0)
+        low, at[0] = tie((low, at[0]))
+        tgrad, tgrad_full, _, *vec_low = input_grads(low)
         at, tgrad = tie((at, tgrad))
-
+        at = dp_sum.scatter(total_of(at), 1)
+        vecs = mp_send(lambda r: vec_low[r])
+        tgrads = spread_out(tgrad)
+        act, at[0], vecs[0], tgrad = tie((act, at[0], vecs[0], tgrad))
+        out, out_full = layer_outs(act)
+        at, vecs, out, tgrads = tie((at, vecs, out, tgrads))
+        at = dp_sum.gather(total_of(at), 1)
+        vecs = dp_sum.gather(total_of(vecs), 0)
+        outs = spread_out(out)
+        at = dp_sum.gather(dp_sum.join(at, 1), 0)
+        vecs = dp_sum.gather(total_of(vecs), 1)
+        tgrad_full, tgrads, at[0] = tie((tgrad_full, tgrads, at[0]))
+        tgrad_full = filled(tgrad_full, tgrads)
+        out_full = filled(out_full, outs)
+        at, vecs, out_full, tgrad_full = tie((at, vecs, out_full, tgrad_full))
+        here = dp_sum.place(*dp_sum.groups[0]).astype(jnp.int32) ^ jnp.arange(4, dtype=jnp.int32)
+        made = at_unpack_call(here, at, vecs, dim, local, sizes)
+        flat = [v.reshape(-1) for v in made[4:]]
+        return (out_full, tgrad_full, flat[:6], made[:3], flat[6:9], made[3], flat[9])
+
+    def finish_any(low, act, grad_at):
+        tgrad, tgrad_full, vec_in, *_ = input_grads(low)
+        out, out_full = layer_outs(act)
+        same = [vec_hid[:2], vec_ff[:1], vec_hid[2:3], vec_in[:2]]
+        same = jnp.concatenate([v.reshape(-1) for v in same])
+        vec_at0, vec_at1 = vec_at[:8], vec_at[8:]
+        grads = [[v[: 4 * dim] for v in grad_at], [v[4 * dim :] for v in grad_at]]
+        gbup = vec_ff[4:].reshape(-1)
+        bias = [
+            jnp.concatenate([v[2 * i + c] for c in range(2) for v in (vec_at0, vec_at1)])
+            for i in range(3)
+        ]
+
+        def all_piece(r):
+            vector = jnp.concatenate(
+                [same]
+                + [b[r * local : (r + 1) * local] for b in bias]
+                + [gbup[r * units : (r + 1) * units]]
+            )
+            size = -(-vector.shape[0] // (16 * dp * LANES)) * (16 * dp * LANES)
+            vector = jnp.pad(vector, (0, size - vector.shape[0])).reshape(-1, LANES).astype(BF)
+            return jnp.concatenate([at_piece(grads, r), vector], axis=0)
+
+        at = total_of(mp_send(all_piece))
+        stages = len(dp_sum.groups)
+        for stage in range(stages):
+            at = total_of(dp_sum.scatter(at, stage))
+        for stage in reversed(range(stages)):
+            at = dp_sum.join(dp_sum.gather(at, stage), stage)
+        at = at.astype(F32)
+        each = dim * local // LANES
         if per == 1:
-            at = jnp.concatenate([total_of(at), total_of(mp_send(lambda r: vec_low[r]))], axis=0)
-        else:
-            same = jnp.concatenate([vec_ff[:4].reshape(-1), vec_in[:2].reshape(-1)])
-            vec_at0, vec_at1 = vec_at[:8], vec_at[8:]
-            grads = [[v[: 4 * dim] for v in grad_at], [v[4 * dim :] for v in grad_at]]
-            gbup = vec_ff[4:].reshape(-1)
-            bias = [
-                jnp.concatenate([v[2 * i + c] for c in range(2) for v in (vec_at0, vec_at1)])
+            halves = [at[: 4 * dim], at[4 * dim : 8 * dim]]
+            g_qkv = [
+                jnp.concatenate([h[i * dim : (i + 1) * dim] for h in halves], axis=1)
                 for i in range(3)
             ]
-
-            def all_piece(r):
-                vector = jnp.concatenate(
-                    [same]
-                    + [b[r * local : (r + 1) * local] for b in bias]
-                    + [gbup[r * units : (r + 1) * units]]
-                )
-                size = -(-vector.shape[0] // (16 * dp * LANES)) * (16 * dp * LANES)
-                vector = jnp.pad(vector, (0, size - vector.shape[0])).reshape(-1, LANES).astype(BF)
-                return jnp.concatenate([at_piece(grads, r), vector], axis=0)
-
-            at = total_of(mp_send(all_piece))
-        at = dp_sum.scatter(at, 0)
-        tgrads = spread_out(tgrad)
-        act, at[0], tgrad = tie((act, at[0], tgrad))
-        out, out_full = out_call(
-            place, hidden, act, mlp_weights[2:], bd, rows, SEQS["out"]
-        )
-        at, out, tgrads = tie((at, out, tgrads))
-        at = total_of(at)
-        stages = len(dp_sum.groups)
-        for stage in range(1, stages):
-            at = total_of(dp_sum.scatter(at, stage))
-        outs = spread_out(out)
-        tgrad_full = filled(tgrad_full, tgrads)
-        at, tgrad_full = tie((at, tgrad_full))
-        for stage in reversed(range(1, stages)):
-            at = dp_sum.join(dp_sum.gather(at, stage), stage)
-        at = dp_sum.gather(at, 0)
-        out_full = filled(out_full, outs)
-        at, out_full = tie((at, out_full))
-
-        sizes = [dim] * 6 + [local] * 3 + [units]
-        if per == 1 and len(at) == 4:
-            here = dp_sum.place(*dp_sum.groups[0]).astype(jnp.int32) ^ jnp.arange(4, dtype=jnp.int32)
-            *g_at, g0, g1, g2, g3, g4, g5, q0, q1, q2, g_bup = at_unpack_call(
-                here, at, dim, local, sizes
-            )
-            g_qkv, g_out = g_at[:3], g_at[3]
-            g_same = [v.reshape(-1) for v in (g0, g1, g2, g3, g4, g5)]
-            g_bias = [v.reshape(-1) for v in (q0, q1, q2)]
-            g_bup = g_bup.reshape(-1)
+            g_out = [h[3 * dim :].reshape(-1, LANES, LANES) for h in halves]
+            g_out = jnp.concatenate([jnp.concatenate(list(h), axis=1) for h in g_out], axis=0)
         else:
-            at = dp_sum.join(at, 0).astype(F32)
-            each = dim * local // LANES
             g_qkv = [at[i * each : (i + 1) * each].reshape(dim, local) for i in range(3)]
             g_out = at[3 * each : 4 * each].reshape(local, dim)
-            vector = at[4 * each :].reshape(-1)
-            parts = []
-            for size in sizes:
-                parts.append(vector[:size])
-                vector = vector[size:]
-            g_same, g_bias, g_bup = parts[:6], parts[6:9], parts[9]
-        return (out_full, tgrad_full, list(g_same), list(g_qkv), list(g_bias), g_out, g_bup)
-
+        vector = at[4 * each :].reshape(-1)
+        parts = []
+        for size in sizes:
+            parts.append(vector[:size])
+            vector = vector[size:]
+        return (
+            filled(out_full, spread_out(out)),
+            filled(tgrad_full, spread_out(tgrad)),
+            parts[:6],
+            g_qkv,
+            parts[6:9],
+            g_out,
+            parts[9],
+        )
+
+    if per != 1 or [size for _, size in dp_sum.groups] != [4, 4]:
+        finish = finish_any
     blank = jax.eval_shape(finish, low, act, grad_at)
     out_full, tgrad_full, g_same, g_qkv, g_bias, g_out, g_bup = lax.cond(
         lax.axis_index("dp") != dp,

time: 281 us -> 287 us (1.021); the launches traced: 281 us -> 284 us
  waiting for transfers between devices: 29.6 us -> 8.86 us
  Pallas kernels: 196 us -> 208 us
  starting transfers between devices: 21.1 us -> 30.7 us
    pallas_call x1, Pallas kernels: 46.9 us -> 71.9 us  [grad_call(): pl.pallas_call(functools.partial(grad_kernel, seqs), grid_spec=prefetch((...]
    ppermute x12 -> x18, waiting for transfers between devices: 16.5 us -> 1.33 us  [swap(): lax.ppermute(value, 'dp', [(i, i ^ distance) for i in range(self.count)])]
    pallas_call x1, Pallas kernels: 67.8 us -> 55.2 us  [mlp_call(): pl.pallas_call(functools.partial(mlp_kernel, seqs, block), grid_spec=pref...]
    ppermute x12 -> x18, starting transfers between devices: 17.4 us -> 27.2 us  [swap(): lax.ppermute(value, 'dp', [(i, i ^ distance) for i in range(self.count)])]
    ppermute x12, waiting for transfers between devices: 13.1 us -> 7.49 us  [shifted(): lax.ppermute(value, axis, [(i, (i + shift) % count) for i in range(count)])]
  transfers between devices with their start and end apart: 25 -> 31, of which waited for: 13 -> 5; matrix products, arithmetic and copies ran while one was open for 5% -> 5% of each run, Pallas kernels for 44% -> 53%
where the time goes in v5:
time: 287 us; the launch traced here: 284 us
  Pallas kernels  208 us (72%)
  starting transfers between devices  30.7 us (11%)
  between operations  14.5 us (5%)
  local copies, waits for them, and re-layouts  13 us (5%)
  waiting for transfers between devices  8.86 us (3%)
  other arithmetic  8.02 us (3%)
    pallas_call x1, Pallas kernels, grad_call(): pl.pallas_call(functools.partial(grad_kernel, seqs), grid_spec=prefetch((...  71.9 us
    pallas_call x1, Pallas kernels, mlp_call(): pl.pallas_call(functools.partial(mlp_kernel, seqs, block), grid_spec=pref...  55.2 us
    pallas_call x1, Pallas kernels, attn_call(): pl.pallas_call(functools.partial(attn_kernel, seqs), grid_spec=prefetch((...  42.4 us
    ppermute x18, starting transfers between devices, swap(): lax.ppermute(value, 'dp', [(i, i ^ distance) for i in range(self.count)])  27.2 us
    pallas_call x1, Pallas kernels, input_call(): pl.pallas_call(functools.partial(input_kernel, seqs), grid_spec=prefetch(...  16.6 us
    pallas_call x1, Pallas kernels, out_call(): pl.pallas_call(functools.partial(out_kernel, seqs), grid_spec=prefetch((s...  15.7 us
    dynamic_update_slice x2, local copies, waits for them, and re-layouts, filled(): full = lax.dynamic_update_slice_in_dim(full, block, (me - r) % mp * own, 0)  8.96 us
    ppermute x12, waiting for transfers between devices, shifted(): lax.ppermute(value, axis, [(i, (i + shift) % count) for i in range(count)])  7.49 us
  transfers between devices with their start and end apart: 31, of which 5 were waited for; matrix products, arithmetic and copies ran while one was open for 5% of the time, Pallas kernels for 53%

profile of v5, /device:TPU:0, one launch (start us, length us, event | category | flops | bytes accessed | tf_op | source)
XLA Modules:
  0.0 283.6 jit_solution(824552765624591240)
XLA Ops:
  7.2 0.0 all-reduce.2.cloned.1.call-start
  7.2 0.5 collective-permute-start.22
  7.8 0.1 collective-permute-start.23
  7.8 0.4 collective-permute-start.24
  8.3 0.1 collective-permute-start.25
  8.3 0.7 pad_maximum_fusion
  9.1 0.5 collective-permute-start.26
  9.6 0.8 collective-permute-done.26.refs_13_.refs_9_
  10.5 0.7 copy-done.5
  11.1 0.3 collective-permute-start.27
  11.5 0.2 collective-permute-start.28
  11.7 0.2 copy-done.9
  11.8 42.4 %attn_forward.1 = (bf16[16,2,2,128,256]{4,3,2,1,0:T(8,128)(2,1)}, bf16[16,2,2,128,256]{4,3,2,1,0:T(8,128)(2,1)}, bf16[16,2,2,128,256]{4,3,2,1,0:T(8,128)(2,1)}, ...) custom-call(s32[1]{0:T(128)} %bitcast.26.place, ...), custom_call_target="tpu_custom_call" | custom-call | flops 1 | bytes 1 | tf_op jit(solution)/shard_map/attn_forward/pallas_call | solution.py:547
  54.3 1.0 copy-done
  55.3 55.2 %feed_forward.1 = (bf16[16,2048,256]{2,1,0:T(8,128)(2,1)}, bf16[16,2048,256]{2,1,0:T(8,128)(2,1)}, bf16[2048,512]{1,0:T(8,128)(2,1)}, bf16[2048,512]{1,0:T(8,128)(2,1)}, f32[8,512]{1,0:T(8,128)S(1)}) custom-call(s32[1]{0:T(128)} %bitcast.26.place, bf16[16,512,256]{2,1,0:T(8,128)(2,1)} %get-tuple-element.226.refs_0_, bf16[8192,512]{1,0:T(8,128)(2,1)} %refs_1_.4, ...), custom_call_target="tpu_custom_call" | custom-call | flops 1 | bytes 1 | tf_op jit(solution)/shard_map/feed_forward/pallas_call | solution.py:672
  110.5 0.4 collective-permute-start.29
  110.9 4.0 %collective-permute-done.29 = bf16[2048,512]{1,0:T(8,128)(2,1)S(1)} collective-permute-done((bf16[2048,512]{1,0:T(8,128)(2,1)}, bf16[2048,512]{1,0:T(8,128)(2,1)S(1)}, u32[]{:S(2)}, u32[]{:S(2)}) %collective-permute-start.29) | collective-permute-done | bytes 2097184 | tf_op jit(solution)/shard_map/ppermute | solution.py:755
  114.9 3.5 %add_convert_fusion.5 = bf16[2048,512]{1,0:T(8,128)(2,1)} fusion(bf16[2048,512]{1,0:T(8,128)(2,1)S(1)} %collective-permute-done.29, bf16[2048,512]{1,0:T(8,128)(2,1)} %get-tuple-element.232), kind=kLoop, calls=%fused_computation.20 | loop fusion | flops 4194304 | bytes 6291456 | tf_op jit(solution)/shard_map/convert_element_type | solution.py:771
  118.4 0.0 all-reduce.2.cloned.1.call-update
  118.5 0.0 copy-start.2
  118.5 0.0 copy-start.3
  118.5 0.0 copy-start.4
  118.5 0.0 copy-start.24
  118.5 71.9 %attn_backward.1 = (bf16[16,256,256]{2,1,0:T(8,128)(2,1)}, bf16[16,256,256]{2,1,0:T(8,128)(2,1)}, bf16[16,256,256]{2,1,0:T(8,128)(2,1)}, bf16[16,256,256]{2,1,0:...) custom-call(s32[1]{0:T(128)} %bitcast.26.place, ...), custom_call_target="tpu_custom_call" | custom-call | flops 1 | bytes 1 | tf_op jit(solution)/shard_map/attn_backward/pallas_call | solution.py:584
  190.6 82.2 %conditional.1 = (bf16[8192,512]{1,0:T(8,128)(2,1)}, bf16[8192,512]{1,0:T(8,128)(2,1)}, f32[512]{0:T(512)S(1)}, f32[512]{0:T(512)S(1)}, f32[512]{0:T(512)}, /*in...) conditional(s32[]{:T(128)} %convert_element_type.75, () %tuple.25, ...), branch_computations={%region_0.0_spmd, %region_1.0_spmd} | conditional | flops 3481684 | bytes 76449880 | solution.py:1008
  190.6 0.4 collective-permute-start
  191.0 2.6 collective-permute-done
  193.6 1.8 add_convert_fusion
  195.5 0.9 dynamic-slice_bitcast_fusion
  196.4 3.8 %collective-permute-start.3 = (bf16[1024,128]{1,0:T(8,128)(2,1)}, bf16[1024,128]{1,0:T(8,128)(2,1)}, u32[]{:S(2)}, u32[]{:S(2)}) collective-permute-start(bf16[1024,128]{1,0:T(8,128)(2,1)} %get-tuple-element.279), channel_id=1, source_target_pairs={{0,3},{1,2},{2,1},{3,0},{4,7},{5,6},{6,5},{7,4},{8,11},{9,10},{10,... | collective-permute-start | bytes 786440 | tf_op jit(solution)/shard_map/cond/branch_1_fun/ppermute | solution.py:785
  200.2 0.5 collective-permute-start.2
  200.7 0.0 collective-permute-start.1
  200.8 16.6 %input_grad.1 = (bf16[4096,512]{1,0:T(8,128)(2,1)}, bf16[8192,512]{1,0:T(8,128)(2,1)}, f32[8,512]{1,0:T(8,128)}, bf16[48,128]{1,0:T(8,128)(2,1)}, bf16[48,128]{1,0:T(8,128)(2,1)}) custom-call(s32[1]{0:T(128)} %get-tuple-element.55.place, bf16[8192,512]{1,0:T(8,128)(2,1)} %get-tuple-element.56.refs_0_, bf16[16,512,256]{2,1,0:T(8,128)(2,1)} %get-tuple-element.60.refs_1_, ...), custom_call_target="tpu_custom_call" | custom-call | flops 1 | bytes 1 | tf_op jit(solution)/shard_map/cond/branch_1_fun/input_grad/pallas_call | solution.py:636
  217.3 0.1 collective-permute-start.8
  217.5 1.3 add_convert_fusion.1
  218.8 4.2 %collective-permute-start.6 = (bf16[256,128]{1,0:T(8,128)(2,1)S(1)}, bf16[256,128]{1,0:T(8,128)(2,1)S(1)}, u32[]{:S(2)}, u32[]{:S(2)}) collective-permute-start(bf16[256,128]{1,0:T(8,128)(2,1)S(1)} %get-tuple-element.283), channel_id=1, source_target_pairs={{0,12},{1,13},{2,14},{3,15},{4,8},{5,9},{6,10},{7,11},{8,4},{9,5},... | collective-permute-start | bytes 196616 | tf_op jit(solution)/shard_map/cond/branch_1_fun/ppermute | solution.py:785
  223.0 0.6 collective-permute-start.4
  223.7 15.7 %layer_out.1 = (bf16[4096,512]{1,0:T(8,128)(2,1)}, bf16[8192,512]{1,0:T(8,128)(2,1)}) custom-call(s32[1]{0:T(128)} %get-tuple-element.55.place, bf16[16,512,256]{2,1,0:T(8,128)(2,1)} %get-tuple-element.90.hid, bf16[16,2048,256]{2,1,0:T(8,128)(2,1)} %get-tuple-element.91.act, bf16[1024,512]{1,0:T(8,128)(2,1)S(1)} %get-tuple-element.92.wd0, ...), custom_call_target="tpu_custom_call" | custom-call | flops 1 | bytes 1 | tf_op jit(solution)/shard_map/cond/branch_1_fun/layer_out/pallas_call | solution.py:703
  239.4 0.4 collective-permute-start.21
  239.9 0.5 iota_xor_fusion.here
  240.4 2.7 collective-permute-start.17
  243.1 0.5 collective-permute-start.16
  243.6 0.3 collective-permute-start.15
  244.0 0.1 bitcast_dynamic-update-slice_fusion.3
  244.1 2.6 collective-permute-start.10
  246.7 1.8 collective-permute-start.9
  248.4 1.9 collective-permute-start.11
  250.4 2.0 collective-permute-start.20
  252.4 1.9 collective-permute-start.19
  254.3 0.6 collective-permute-start.18
  255.0 2.4 collective-permute-start.14
  257.3 4.5 %constant_dynamic-update-slice_fusion = bf16[8192,512]{1,0:T(8,128)(2,1)} fusion(bf16[8192,512]{1,0:T(8,128)(2,1)} %get-tuple-element.107, bf16[4096,512]{1,0:T(8,128)(2,1)} %collective-permute-done.8, s32[]{:T(128)S(6)} %select_n.62), kind=kLoop, calls=%fused_computation.17 | loop fusion | bytes 8388612 | tf_op jit(solution)/shard_map/cond/branch_1_fun/dynamic_update_slice | solution.py:850
  261.8 0.6 collective-permute-start.13
  262.5 0.6 collective-permute-start.12
  263.1 4.5 %constant_dynamic-update-slice_fusion.1 = bf16[8192,512]{1,0:T(8,128)(2,1)} fusion(bf16[8192,512]{1,0:T(8,128)(2,1)} %get-tuple-element.104, bf16[4096,512]{1,0:T(8,128)(2,1)} %collective-permute-done.21, s32[]{:T(128)S(6)} %select_n.62), kind=kLoop, calls=%fused_computation.18 | loop fusion | bytes 8388612 | tf_op jit(solution)/shard_map/cond/branch_1_fun/dynamic_update_slice | solution.py:850
  267.6 1.0 collective-permute-done.13.b2
  268.6 0.3 collective-permute-done.12.b1
  268.9 0.4 copy-done.12
  269.3 0.7 copy-done.13
  270.0 2.7 at_unpack.1
  272.7 0.0 copy-start.22
  272.7 0.0 copy-start.23
  272.8 0.0 all-reduce.2.cloned.1.call-done.total
  272.8 3.7 %ff_unpack.1 = (f32[512,1024]{1,0:T(8,128)}, f32[1024,512]{1,0:T(8,128)}) custom-call(bf16[2048,512]{1,0:T(8,128)(2,1)} %all-reduce.2.cloned.1.call-done.total), custom_call_target="tpu_custom_call" | custom-call | tf_op jit(solution)/shard_map/ff_unpack/pallas_call | solution.py:726
  (74 shorter events, 0.3 us)
Async XLA Ops:
  7.2 265.6 %all-reduce.2.cloned.1.call-start = ((), (), s32[]{:S(2)}) async-start(), calls=%async_computation | async-start | bytes 4194304 | tf_op jit(solution)/shard_map/psum | solution.py:891
  7.2 3.2 %collective-permute-start.22 = (bf16[512,256]{1,0:T(8,128)(2,1)}, bf16[512,256]{1,0:T(8,128)(2,1)S(1)}, u32[]{:S(2)}, u32[]{:S(2)}) collective-permute-start(bf16[512,256]{1,0:T(8,128)(2,1)} %refs_1_.2), channel_id=1, source_target_pairs={{0,16},{16,0},{1,17},{17,1},{2,18},{18,2},{3,19},{19,3},{4,20},{20... | collective-permute-start | bytes 786440 | tf_op jit(solution)/shard_map/ppermute | solution.py:755
  7.8 2.7 collective-permute-start.23
  7.8 2.6 collective-permute-start.24
  8.3 2.2 collective-permute-start.25
  9.1 2.8 copy-start.14
  9.1 1.3 collective-permute-start.26
  10.4 1.4 copy-start.16
  10.4 0.7 copy-start.5
  10.5 1.0 copy-start.7
  11.1 0.7 copy-start.9
  11.1 43.1 %collective-permute-start.27 = (bf16[512,1024]{1,0:T(8,128)(2,1)}, bf16[512,1024]{1,0:T(8,128)(2,1)S(1)}, u32[]{:S(2)}, u32[]{:S(2)}) collective-permute-start(bf16[512,1024]{1,0:T(8,128)(2,1)} %refs_13_), channel_id=1, source_target_pairs={{0,16},{16,0},{1,17},{17,1},{2,18},{18,2},{3,19},{19,3},{4,20},{20... | collective-permute-start | bytes 3145736 | tf_op jit(solution)/shard_map/ppermute | solution.py:755
  11.5 42.8 %collective-permute-start.28 = (bf16[1024,512]{1,0:T(8,128)(2,1)}, bf16[1024,512]{1,0:T(8,128)(2,1)S(1)}, u32[]{:S(2)}, u32[]{:S(2)}) collective-permute-start(bf16[1024,512]{1,0:T(8,128)(2,1)} %refs_4_), channel_id=1, source_target_pairs={{0,16},{16,0},{1,17},{17,1},{2,18},{18,2},{3,19},{19,3},{4,20},{20... | collective-permute-start | bytes 3145736 | tf_op jit(solution)/shard_map/ppermute | solution.py:755
  11.8 43.4 %copy-start.1 = (bf16[1024,512]{1,0:T(8,128)(2,1)S(1)}, bf16[1024,512]{1,0:T(8,128)(2,1)}, u32[]{:S(2)}) copy-start(bf16[1024,512]{1,0:T(8,128)(2,1)} %refs_4_) | copy-start | bytes 3145732
  54.3 1.0 copy-start
  110.5 4.4 %collective-permute-start.29 = (bf16[2048,512]{1,0:T(8,128)(2,1)}, bf16[2048,512]{1,0:T(8,128)(2,1)S(1)}, u32[]{:S(2)}, u32[]{:S(2)}) collective-permute-start(bf16[2048,512]{1,0:T(8,128)(2,1)} %get-tuple-element.233), channel_id=1, source_target_pairs={{0,16},{16,0},{1,17},{17,1},{2,18},{18,2},{3,19},{19,3},{4,20},{20... | collective-permute-start | bytes 6291464 | tf_op jit(solution)/shard_map/ppermute | solution.py:755
  118.5 72.0 %copy-start.2 = (bf16[512,256]{1,0:T(8,128)(2,1)S(1)}, bf16[512,256]{1,0:T(8,128)(2,1)}, u32[]{:S(2)}) copy-start(bf16[512,256]{1,0:T(8,128)(2,1)} %refs_1_.2) | copy-start | bytes 786436
  118.5 72.0 %copy-start.3 = (bf16[512,256]{1,0:T(8,128)(2,1)S(1)}, bf16[512,256]{1,0:T(8,128)(2,1)}, u32[]{:S(2)}) copy-start(bf16[512,256]{1,0:T(8,128)(2,1)} %refs_3_) | copy-start | bytes 786436
  118.5 72.0 %copy-start.4 = (bf16[512,256]{1,0:T(8,128)(2,1)S(1)}, bf16[512,256]{1,0:T(8,128)(2,1)}, u32[]{:S(2)}) copy-start(bf16[512,256]{1,0:T(8,128)(2,1)} %refs_5_) | copy-start | bytes 786436
  118.5 72.0 %copy-start.6 = (bf16[512,256]{1,0:T(8,128)(2,1)S(1)}, bf16[512,256]{1,0:T(8,128)(2,1)}, u32[]{:S(2)}) copy-start(bf16[512,256]{1,0:T(8,128)(2,1)} %copy-done.5) | copy-start | bytes 786436
  118.5 72.0 %copy-start.21 = (f32[512]{0:T(512)S(1)}, f32[512]{0:T(512)}, u32[]{:S(2)}) copy-start(f32[512]{0:T(512)} %param.21) | copy-start | bytes 6148
  118.5 72.0 %copy-start.24 = (f32[512]{0:T(512)S(1)}, f32[512]{0:T(512)}, u32[]{:S(2)}) copy-start(f32[512]{0:T(512)} %param.36) | copy-start | bytes 6148
  190.6 3.1 %collective-permute-start = (bf16[4096,128]{1,0:T(8,128)(2,1)}, bf16[4096,128]{1,0:T(8,128)(2,1)}, u32[]{:S(2)}, u32[]{:S(2)}) collective-permute-start(bf16[4096,128]{1,0:T(8,128)(2,1)} %get-tuple-element.59), channel_id=1, source_target_pairs={{0,16},{16,0},{1,17},{17,1},{2,18},{18,2},{3,19},{19,3},{4,20},{20... | collective-permute-start | bytes 3145736 | tf_op jit(solution)/shard_map/cond/branch_1_fun/ppermute | solution.py:755
  191.0 9.8 %copy-start.8 = (bf16[512,256]{1,0:T(8,128)(2,1)S(1)}, bf16[512,256]{1,0:T(8,128)(2,1)}, u32[]{:S(2)}) copy-start(bf16[512,256]{1,0:T(8,128)(2,1)} %get-tuple-element.72.refs_13_) | copy-start | bytes 786436 | tf_op jit(solution)/shard_map/cond
  196.4 20.9 %collective-permute-start.3 = (bf16[1024,128]{1,0:T(8,128)(2,1)}, bf16[1024,128]{1,0:T(8,128)(2,1)}, u32[]{:S(2)}, u32[]{:S(2)}) collective-permute-start(bf16[1024,128]{1,0:T(8,128)(2,1)} %get-tuple-element.279), channel_id=1, source_target_pairs={{0,3},{1,2},{2,1},{3,0},{4,7},{5,6},{6,5},{7,4},{8,11},{9,10},{10,... | collective-permute-start | bytes 786440 | tf_op jit(solution)/shard_map/cond/branch_1_fun/ppermute | solution.py:785
  200.2 17.1 %collective-permute-start.2 = (bf16[1024,128]{1,0:T(8,128)(2,1)}, bf16[1024,128]{1,0:T(8,128)(2,1)}, u32[]{:S(2)}, u32[]{:S(2)}) collective-permute-start(bf16[1024,128]{1,0:T(8,128)(2,1)} %get-tuple-element.280), channel_id=1, source_target_pairs={{0,2},{1,3},{2,0},{3,1},{4,6},{5,7},{6,4},{7,5},{8,10},{9,11},{10,... | collective-permute-start | bytes 786440 | tf_op jit(solution)/shard_map/cond/branch_1_fun/ppermute | solution.py:785
  200.7 16.6 %collective-permute-start.1 = (bf16[1024,128]{1,0:T(8,128)(2,1)S(1)}, bf16[1024,128]{1,0:T(8,128)(2,1)}, u32[]{:S(2)}, u32[]{:S(2)}) collective-permute-start(bf16[1024,128]{1,0:T(8,128)(2,1)S(1)} %get-tuple-element.281), channel_id=1, source_target_pairs={{0,1},{1,0},{2,3},{3,2},{4,5},{5,4},{6,7},{7,6},{8,9},{9,8},{10,11... | collective-permute-start | bytes 786440 | tf_op jit(solution)/shard_map/cond/branch_1_fun/ppermute | solution.py:785
  217.3 22.1 %collective-permute-start.8 = (bf16[4096,512]{1,0:T(8,128)(2,1)}, bf16[4096,512]{1,0:T(8,128)(2,1)}, u32[]{:S(2)}, u32[]{:S(2)}) collective-permute-start(bf16[4096,512]{1,0:T(8,128)(2,1)} %get-tuple-element.86), channel_id=1, source_target_pairs={{0,16},{16,0},{1,17},{17,1},{2,18},{18,2},{3,19},{19,3},{4,20},{20... | collective-permute-start | bytes 12582920 | tf_op jit(solution)/shard_map/cond/branch_1_fun/ppermute | solution.py:755
  218.8 20.5 %collective-permute-start.6 = (bf16[256,128]{1,0:T(8,128)(2,1)S(1)}, bf16[256,128]{1,0:T(8,128)(2,1)S(1)}, u32[]{:S(2)}, u32[]{:S(2)}) collective-permute-start(bf16[256,128]{1,0:T(8,128)(2,1)S(1)} %get-tuple-element.283), channel_id=1, source_target_pairs={{0,12},{1,13},{2,14},{3,15},{4,8},{5,9},{6,10},{7,11},{8,4},{9,5},... | collective-permute-start | bytes 196616 | tf_op jit(solution)/shard_map/cond/branch_1_fun/ppermute | solution.py:785
  223.0 16.4 %collective-permute-start.5 = (bf16[256,128]{1,0:T(8,128)(2,1)S(1)}, bf16[256,128]{1,0:T(8,128)(2,1)S(1)}, u32[]{:S(2)}, u32[]{:S(2)}) collective-permute-start(bf16[256,128]{1,0:T(8,128)(2,1)S(1)} %get-tuple-element.284), channel_id=1, source_target_pairs={{0,8},{1,9},{2,10},{3,11},{4,12},{5,13},{6,14},{7,15},{8,0},{9,1},... | collective-permute-start | bytes 196616 | tf_op jit(solution)/shard_map/cond/branch_1_fun/ppermute | solution.py:785
  223.0 16.4 %collective-permute-start.4 = (bf16[256,128]{1,0:T(8,128)(2,1)S(1)}, bf16[256,128]{1,0:T(8,128)(2,1)S(1)}, u32[]{:S(2)}, u32[]{:S(2)}) collective-permute-start(bf16[256,128]{1,0:T(8,128)(2,1)S(1)} %get-tuple-element.285), channel_id=1, source_target_pairs={{0,4},{1,5},{2,6},{3,7},{4,0},{5,1},{6,2},{7,3},{8,12},{9,13},{10,... | collective-permute-start | bytes 196616 | tf_op jit(solution)/shard_map/cond/branch_1_fun/ppermute | solution.py:785
  223.7 15.7 %collective-permute-start.7 = (bf16[48,128]{1,0:T(8,128)(2,1)}, bf16[48,128]{1,0:T(8,128)(2,1)S(1)}, u32[]{:S(2)}, u32[]{:S(2)}) collective-permute-start(bf16[48,128]{1,0:T(8,128)(2,1)} %get-tuple-element.89), channel_id=1, source_target_pairs={{0,16},{16,0},{1,17},{17,1},{2,18},{18,2},{3,19},{19,3},{4,20},{20... | collective-permute-start | bytes 36872 | tf_op jit(solution)/shard_map/cond/branch_1_fun/ppermute | solution.py:755
  223.7 16.7 %copy-start.20 = (bf16[48,128]{1,0:T(8,128)(2,1)S(1)}, bf16[48,128]{1,0:T(8,128)(2,1)}, u32[]{:S(2)}) copy-start(bf16[48,128]{1,0:T(8,128)(2,1)} %get-tuple-element.102) | copy-start | bytes 36868 | tf_op jit(solution)/shard_map/cond
  239.4 23.0 %collective-permute-start.21 = (bf16[4096,512]{1,0:T(8,128)(2,1)}, bf16[4096,512]{1,0:T(8,128)(2,1)}, u32[]{:S(2)}, u32[]{:S(2)}) collective-permute-start(bf16[4096,512]{1,0:T(8,128)(2,1)} %get-tuple-element.105), channel_id=1, source_target_pairs={{0,16},{16,0},{1,17},{17,1},{2,18},{18,2},{3,19},{19,3},{4,20},{20... | collective-permute-start | bytes 12582920 | tf_op jit(solution)/shard_map/cond/branch_1_fun/ppermute | solution.py:755
  240.4 6.2 %collective-permute-start.17 = (bf16[48,128]{1,0:T(8,128)(2,1)S(1)}, bf16[48,128]{1,0:T(8,128)(2,1)S(1)}, u32[]{:S(2)}, u32[]{:S(2)}) collective-permute-start(bf16[48,128]{1,0:T(8,128)(2,1)S(1)} %add_convert_fusion.4), channel_id=1, source_target_pairs={{0,3},{1,2},{2,1},{3,0},{4,7},{5,6},{6,5},{7,4},{8,11},{9,10},{10,... | collective-permute-start | bytes 36872 | tf_op jit(solution)/shard_map/cond/branch_1_fun/ppermute | solution.py:785
  243.1 5.4 %collective-permute-start.16 = (bf16[48,128]{1,0:T(8,128)(2,1)S(1)}, bf16[48,128]{1,0:T(8,128)(2,1)S(1)}, u32[]{:S(2)}, u32[]{:S(2)}) collective-permute-start(bf16[48,128]{1,0:T(8,128)(2,1)S(1)} %add_convert_fusion.4), channel_id=1, source_target_pairs={{0,2},{1,3},{2,0},{3,1},{4,6},{5,7},{6,4},{7,5},{8,10},{9,11},{10,... | collective-permute-start | bytes 36872 | tf_op jit(solution)/shard_map/cond/branch_1_fun/ppermute | solution.py:785
  243.6 6.7 %collective-permute-start.15 = (bf16[48,128]{1,0:T(8,128)(2,1)S(1)}, bf16[48,128]{1,0:T(8,128)(2,1)S(1)}, u32[]{:S(2)}, u32[]{:S(2)}) collective-permute-start(bf16[48,128]{1,0:T(8,128)(2,1)S(1)} %add_convert_fusion.4), channel_id=1, source_target_pairs={{0,1},{1,0},{2,3},{3,2},{4,5},{5,4},{6,7},{7,6},{8,9},{9,8},{10,11... | collective-permute-start | bytes 36872 | tf_op jit(solution)/shard_map/cond/branch_1_fun/ppermute | solution.py:785
  244.1 10.2 %collective-permute-start.10 = (bf16[256,128]{1,0:T(8,128)(2,1)S(1)}, bf16[256,128]{1,0:T(8,128)(2,1)S(1)}, u32[]{:S(2)}, u32[]{:S(2)}) collective-permute-start(bf16[256,128]{1,0:T(8,128)(2,1)S(1)} %get-tuple-element.278), channel_id=1, source_target_pairs={{0,8},{1,9},{2,10},{3,11},{4,12},{5,13},{6,14},{7,15},{8,0},{9,1},... | collective-permute-start | bytes 196616 | tf_op jit(solution)/shard_map/cond/branch_1_fun/ppermute | solution.py:785
  246.7 5.7 %collective-permute-start.9 = (bf16[256,128]{1,0:T(8,128)(2,1)S(1)}, bf16[256,128]{1,0:T(8,128)(2,1)S(1)}, u32[]{:S(2)}, u32[]{:S(2)}) collective-permute-start(bf16[256,128]{1,0:T(8,128)(2,1)S(1)} %get-tuple-element.278), channel_id=1, source_target_pairs={{0,4},{1,5},{2,6},{3,7},{4,0},{5,1},{6,2},{7,3},{8,12},{9,13},{10,... | collective-permute-start | bytes 196616 | tf_op jit(solution)/shard_map/cond/branch_1_fun/ppermute | solution.py:785
  248.4 6.5 %collective-permute-start.11 = (bf16[256,128]{1,0:T(8,128)(2,1)S(1)}, bf16[256,128]{1,0:T(8,128)(2,1)S(1)}, u32[]{:S(2)}, u32[]{:S(2)}) collective-permute-start(bf16[256,128]{1,0:T(8,128)(2,1)S(1)} %get-tuple-element.278), channel_id=1, source_target_pairs={{0,12},{1,13},{2,14},{3,15},{4,8},{5,9},{6,10},{7,11},{8,4},{9,5},... | collective-permute-start | bytes 196616 | tf_op jit(solution)/shard_map/cond/branch_1_fun/ppermute | solution.py:785
  250.4 11.5 %copy-start.15 = (bf16[48,128]{1,0:T(8,128)(2,1)}, bf16[48,128]{1,0:T(8,128)(2,1)S(1)}, u32[]{:S(2)}) copy-start(bf16[48,128]{1,0:T(8,128)(2,1)S(1)} %add_convert_fusion.3.v0) | copy-start | bytes 36868 | tf_op jit(solution)/shard_map/cond
  250.4 11.4 %collective-permute-start.20 = (bf16[48,128]{1,0:T(8,128)(2,1)S(1)}, bf16[48,128]{1,0:T(8,128)(2,1)S(1)}, u32[]{:S(2)}, u32[]{:S(2)}) collective-permute-start(bf16[48,128]{1,0:T(8,128)(2,1)S(1)} %add_convert_fusion.3.v0), channel_id=1, source_target_pairs={{0,12},{1,13},{2,14},{3,15},{4,8},{5,9},{6,10},{7,11},{8,4},{9,5},... | collective-permute-start | bytes 36872 | tf_op jit(solution)/shard_map/cond/branch_1_fun/ppermute | solution.py:785
  252.4 15.2 %collective-permute-start.19 = (bf16[48,128]{1,0:T(8,128)(2,1)S(1)}, bf16[48,128]{1,0:T(8,128)(2,1)S(1)}, u32[]{:S(2)}, u32[]{:S(2)}) collective-permute-start(bf16[48,128]{1,0:T(8,128)(2,1)S(1)} %add_convert_fusion.3.v0), channel_id=1, source_target_pairs={{0,8},{1,9},{2,10},{3,11},{4,12},{5,13},{6,14},{7,15},{8,0},{9,1},... | collective-permute-start | bytes 36872 | tf_op jit(solution)/shard_map/cond/branch_1_fun/ppermute | solution.py:785
  254.3 13.3 %collective-permute-start.18 = (bf16[48,128]{1,0:T(8,128)(2,1)S(1)}, bf16[48,128]{1,0:T(8,128)(2,1)S(1)}, u32[]{:S(2)}, u32[]{:S(2)}) collective-permute-start(bf16[48,128]{1,0:T(8,128)(2,1)S(1)} %add_convert_fusion.3.v0), channel_id=1, source_target_pairs={{0,4},{1,5},{2,6},{3,7},{4,0},{5,1},{6,2},{7,3},{8,12},{9,13},{10,... | collective-permute-start | bytes 36872 | tf_op jit(solution)/shard_map/cond/branch_1_fun/ppermute | solution.py:785
  255.0 7.5 %copy-start.10 = (bf16[4,256,128]{2,1,0:T(8,128)(2,1)}, bf16[4,256,128]{2,1,0:T(8,128)(2,1)S(1)}, u32[]{:S(2)}) copy-start(bf16[4,256,128]{2,1,0:T(8,128)(2,1)S(1)} %bitcast_dynamic-update-slice_fusion) | copy-start | bytes 786436 | tf_op jit(solution)/shard_map/cond
  255.0 12.6 %collective-permute-start.14 = (bf16[1024,128]{1,0:T(8,128)(2,1)S(1)}, bf16[1024,128]{1,0:T(8,128)(2,1)S(1)}, u32[]{:S(2)}, u32[]{:S(2)}) collective-permute-start(bf16[1024,128]{1,0:T(8,128)(2,1)S(1)} %bitcast.46), channel_id=1, source_target_pairs={{0,3},{1,2},{2,1},{3,0},{4,7},{5,6},{6,5},{7,4},{8,11},{9,10},{10,... | collective-permute-start | bytes 786440 | tf_op jit(solution)/shard_map/cond/branch_1_fun/ppermute | solution.py:785
  261.8 5.8 %copy-start.17 = (bf16[48,128]{1,0:T(8,128)(2,1)}, bf16[48,128]{1,0:T(8,128)(2,1)S(1)}, u32[]{:S(2)}) copy-start(bf16[48,128]{1,0:T(8,128)(2,1)S(1)} %collective-permute-done.20.v3) | copy-start | bytes 36868 | tf_op jit(solution)/shard_map/cond
  261.8 6.8 %collective-permute-start.13 = (bf16[1024,128]{1,0:T(8,128)(2,1)S(1)}, bf16[1024,128]{1,0:T(8,128)(2,1)S(1)}, u32[]{:S(2)}, u32[]{:S(2)}) collective-permute-start(bf16[1024,128]{1,0:T(8,128)(2,1)S(1)} %bitcast.47), channel_id=1, source_target_pairs={{0,2},{1,3},{2,0},{3,1},{4,6},{5,7},{6,4},{7,5},{8,10},{9,11},{10,... | collective-permute-start | bytes 786440 | tf_op jit(solution)/shard_map/cond/branch_1_fun/ppermute | solution.py:785
  262.5 6.5 %collective-permute-start.12 = (bf16[1024,128]{1,0:T(8,128)(2,1)S(1)}, bf16[1024,128]{1,0:T(8,128)(2,1)S(1)}, u32[]{:S(2)}, u32[]{:S(2)}) collective-permute-start(bf16[1024,128]{1,0:T(8,128)(2,1)S(1)} %bitcast.48), channel_id=1, source_target_pairs={{0,1},{1,0},{2,3},{3,2},{4,5},{5,4},{6,7},{7,6},{8,9},{9,8},{10,11... | collective-permute-start | bytes 786440 | tf_op jit(solution)/shard_map/cond/branch_1_fun/ppermute | solution.py:785
  267.6 1.3 copy-start.18
  267.6 1.3 copy-start.19
  267.6 1.3 copy-start.11
  268.6 0.7 copy-start.12
  269.3 0.7 copy-start.13
  272.7 3.8 %copy-start.22 = (f32[512]{0:T(512)}, f32[512]{0:T(512)S(1)}, u32[]{:S(2)}) copy-start(f32[512]{0:T(512)S(1)} %get-tuple-element.208) | copy-start | bytes 6148
  272.7 3.8 %copy-start.23 = (f32[512]{0:T(512)}, f32[512]{0:T(512)S(1)}, u32[]{:S(2)}) copy-start(f32[512]{0:T(512)S(1)} %get-tuple-element.207) | copy-start | bytes 6148
Sparse Core Ops, SparseCore 0:
  118.6 133.9 all-reduce.1

commit v6 on v4

--- a/solution.py
+++ b/solution.py
@@ -177,7 +177,8 @@
 
     def finish(s, mixed):
         x = tok[s * SEQ : (s + 1) * SEQ, :].astype(F32).T
-        hidden_o[s] = x + dot(wo_t[...], jnp.concatenate(mixed, axis=0)) + wide(vec[5 * dim : 6 * dim, :], SEQ)
+        made = x + dot(wo_t[...], jnp.concatenate(mixed, axis=0)) + wide(vec[5 * dim : 6 * dim, :], SEQ)
+        hidden_o[s] = made.astype(BF)
 
     first = prepare(0)
     ready = project(0, 0, first)
@@ -220,7 +221,7 @@
         gdown[...] = jnp.zeros_like(gdown)
         gvec[...] = jnp.zeros_like(gvec)
 
-    hidden = jnp.concatenate([hid[s] for s in range(seqs)], axis=1)
+    hidden = jnp.concatenate([hid[s] for s in range(seqs)], axis=1).astype(F32)
     grad_out = cot[...].astype(F32).T
     grad_low = grad_out.astype(BF)
     gain = wide(vec[0:dim, :], lanes)
@@ -283,7 +284,7 @@
 
     for s in range(seqs):
         rows = slice(s * SEQ, (s + 1) * SEQ)
-        out = hid[s] + dot(wd_t[...], act[s]) + wide(vec[...], SEQ)
+        out = hid[s].astype(F32) + dot(wd_t[...], act[s]) + wide(vec[...], SEQ)
         made = out.T.astype(BF)
         out_o[rows, :] = made
         whole_o[rows, :] = made
@@ -343,17 +344,30 @@
     first = jnp.concatenate([first_i[s] for s in range(seqs)], axis=1)
     low = jnp.concatenate([low_i[s] for s in range(seqs)], axis=1)
 
-    def pair(s, c, g, dm):
+    def mix_grad(s, g):
+        place = slice(g * LANES, (g + 1) * LANES)
+        spread = lambda c, e: jnp.broadcast_to(norm_i[s, c, g, e : e + 1, :], (HEAD_DIM, SEQ))
+        return [
+            (
+                dot(wo[place, :], low_i[s])
+                * jnp.concatenate([spread(c, e) for e in range(2)], axis=0)
+            ).astype(BF)
+            for c, wo in enumerate((wo0, wo1))
+        ]
+
+    def inner(s, g, c, dmixed):
+        dm = dmixed[c]
+        v_nat = turned(values_i[s, c, g])
+        near_m, far_m = pair_near_far(dm)
+        return dot(v_nat[:HALF], near_m), dot(v_nat, far_m), near_m, far_m
+
+    def outer(s, g, c, near_s, far_s, near_m, far_m):
         q, k = query_i[s, c, g], keys_i[s, c, g]
-        v_nat = turned(values_i[s, c, g])
         near_q, far_q = pair_near_far(q)
-        near_m, far_m = pair_near_far(dm)
         low_pair = []
-        for index in range(2):
-            keys = slice(0, HALF) if index == 0 else slice(0, SEQ)
+        for index, dsigned in enumerate((near_s, far_s)):
             block = slice(0, HALF) if index == 0 else slice(HALF, HALF + SEQ)
             lanes = slice(index * HALF, (index + 1) * HALF)
-            dsigned = dot(v_nat[keys], (near_m, far_m)[index])
             signed = signed_i[s, c, g, block].astype(F32)
             row_dot = jnp.sum(signed * dsigned, axis=0, keepdims=True)
             row_dot = row_dot * jnp.concatenate(
@@ -375,52 +389,43 @@
         near_p = tail_dot(signed_i[s, c, g, :HALF], near_m)
         far_p = tail_dot(signed_i[s, c, g, HALF:], far_m)
         dv = jnp.concatenate([far_p[:HALF] + near_p, far_p[HALF:]], axis=0)
-        return dq, dk, dv
-
-    for g in range(2):
-        place = slice(g * LANES, (g + 1) * LANES)
-        spread = lambda s, c, e: jnp.broadcast_to(norm_i[s, c, g, e : e + 1, :], (HEAD_DIM, SEQ))
-        norms = jnp.concatenate(
-            [
-                jnp.concatenate([spread(s, c, e) for c in range(2) for e in range(2)], axis=0)
-                for s in range(seqs)
-            ],
-            axis=1,
+        dq, dk, dv = (dq * scale).astype(BF), dk.astype(BF), dv.astype(BF)
+        dq_o, dk_o, dv_o = outs[3 * g : 3 * g + 3]
+        rows = slice(c * LANES, (c + 1) * LANES)
+        dq_o[s, rows, :], dk_o[s, :, rows], dv_o[s, :, rows] = dq, dk, dv
+        base = g * 4 * LANES
+        gb[base + c * LANES : base + (c + 1) * LANES, :] += lane_fold(dq.astype(F32))
+        for index, block in ((2, dk), (3, dv)):
+            at = base + index * LANES + 8 * c
+            gb[at : at + 8, :] += jnp.sum(block.astype(F32).reshape(-1, 8, LANES), axis=0)
+
+    def weight_grads(g):
+        mixed = jnp.concatenate(
+            [jnp.concatenate([mixed_i[s, 0, g], mixed_i[s, 1, g]], axis=0) for s in range(seqs)], axis=1
         )
-        dmixed = jnp.concatenate([dot(wo0[place, :], low), dot(wo1[place, :], low)], axis=0)
-        dmixed = (dmixed * norms).astype(BF)
-        mixed = jnp.concatenate(
-            [
-                jnp.concatenate([mixed_i[s, 0, g], mixed_i[s, 1, g]], axis=0)
-                for s in range(seqs)
-            ],
-            axis=1,
-        )
+        gout[g * part : (g + 1) * part, :] += tail_dot(mixed, low)
         dq_o, dk_o, dv_o = outs[3 * g : 3 * g + 3]
-        dq_all, dk_all, dv_all = [], [], []
-        for s in range(seqs):
-            span = slice(s * SEQ, (s + 1) * SEQ)
-            dq, dk, dv = zip(
-                *[pair(s, c, g, dmixed[c * LANES : (c + 1) * LANES, span]) for c in range(2)]
-            )
-            dq_all.append((jnp.concatenate(dq, axis=0) * scale).astype(BF))
-            dk_all.append(jnp.concatenate(dk, axis=1).astype(BF))
-            dv_all.append(jnp.concatenate(dv, axis=1).astype(BF))
-            dq_o[s], dk_o[s], dv_o[s] = dq_all[s], dk_all[s], dv_all[s]
-        gout[g * part : (g + 1) * part, :] += tail_dot(mixed, low)
-        dq = jnp.concatenate(dq_all, axis=1)
-        dk, dv = jnp.concatenate(dk_all, axis=0), jnp.concatenate(dv_all, axis=0)
+        dq = jnp.concatenate([dq_o[s] for s in range(seqs)], axis=1)
+        dk, dv = (jnp.concatenate([ref[s] for s in range(seqs)], axis=0) for ref in (dk_o, dv_o))
         at = 3 * g * part
         gqkv[:, at : at + part] += tail_dot(first, dq)
         gqkv[:, at + part : at + 2 * part] += dot(first, dk)
         gqkv[:, at + 2 * part : at + 3 * part] += dot(first, dv)
-        base = g * 4 * LANES
-        gb[base : base + part, :] += lane_fold(dq.astype(F32))
-        for index, block in ((2, dk), (3, dv)):
-            total = jnp.sum(block.astype(F32).reshape(-1, 8, part), axis=0)
-            rows = base + index * LANES
-            gb[rows : rows + 8, :] += total[:, :LANES]
-            gb[rows + 8 : rows + 16, :] += total[:, LANES:]
+
+    order = [(s, g, c) for g in range(2) for s in range(seqs) for c in range(2)]
+    made = mix_grad(0, 0)
+    ready = inner(*order[0], made)
+    for n, (s, g, c) in enumerate(order):
+        current = ready
+        if n + 1 < len(order):
+            following = order[n + 1]
+            if following[2] == 0:
+                made = mix_grad(*following[:2])
+            ready = inner(*following, made)
+        outer(s, g, c, *current)
+        if n == 2 * seqs:
+            weight_grads(0)
+    weight_grads(1)
 
     @pl.when(step == pl.num_programs(0) - 1)
     def _():
@@ -553,7 +558,7 @@
         out_shape=[shape((count,) + feat, BF)] * 4
         + [shape((count,) + wide_block, BF)] * 2
         + [shape((count, 2, 2, 8, SEQ), F32)]
-        + [shape((count, dim, SEQ), BF), shape((count, dim, SEQ), F32)],
+        + [shape((count, dim, SEQ), BF)] * 2,
         compiler_params=params(),
         cost_estimate=pl.CostEstimate(flops=1, bytes_accessed=1, transcendentals=0),
         name="attn_forward",
@@ -816,6 +821,7 @@
             )
             for c in range(2)
         ]
+    weights, smalls, wu, wd = tie((weights, smalls, wu, wd))
     mlp_weights = gathered(wu, mp, 1) + gathered(wd, mp, 0)
     gain1, shift1, bo, gain2, shift2, bd = (
         v.reshape(1, -1) for v in (gain1, shift1, bo, gain2, shift2, bd)
@@ -870,7 +876,6 @@
 
     def finish(low, act, grad_at):
         at = mp_send(lambda r: grad_at[r]) if per == 1 else []
-        low, at = tie((low, at))
         grow = -(-(6 * dim + 3 * local + units) // (16 * dp * LANES)) * 16 * dp
         tgrad, tgrad_full, vec_in, *vec_low = input_call(
             place,

time: 281 us -> 279 us (level)
  Pallas kernels: 196 us -> 189 us
  waiting for transfers between devices: 29.6 us -> 34.9 us
    pallas_call x1, Pallas kernels: 46.9 us -> 39.9 us  [grad_call(): pl.pallas_call(functools.partial(grad_kernel, seqs), grid=(steps,), in_sp...]
    ppermute x12, waiting for transfers between devices: 16.5 us -> 21.4 us  [swap(): lax.ppermute(value, 'dp', [(i, i ^ distance) for i in range(self.count)])]
    psum x1, waiting for transfers between devices: 0.02 us -> 4.5 us  [body(): ff = lax.psum(ff, 'dp')]
    ppermute x12, waiting for transfers between devices: 13.1 us -> 8.98 us  [shifted(): lax.ppermute(value, axis, [(i, (i + shift) % count) for i in range(count)])]
  transfers between devices with their start and end apart: 25 -> 25, of which waited for: 13 -> 9; matrix products, arithmetic and copies ran while one was open for 5% -> 5% of each run, Pallas kernels for 44% -> 42%
where the time goes in v6:
time: 279 us
  Pallas kernels  189 us (68%)
  waiting for transfers between devices  34.9 us (13%)
  starting transfers between devices  21.8 us (8%)
  between operations  14.3 us (5%)
  local copies, waits for them, and re-layouts  11.1 us (4%)
  other arithmetic  7.76 us (3%)
    pallas_call x1, Pallas kernels, mlp_call(): pl.pallas_call(functools.partial(mlp_kernel, seqs, block), grid_spec=pref...  68 us
    pallas_call x1, Pallas kernels, attn_call(): pl.pallas_call(functools.partial(attn_kernel, seqs), grid_spec=prefetch((...  42.3 us
    pallas_call x1, Pallas kernels, grad_call(): pl.pallas_call(functools.partial(grad_kernel, seqs), grid=(steps,), in_sp...  39.9 us
    ppermute x12, waiting for transfers between devices, swap(): lax.ppermute(value, 'dp', [(i, i ^ distance) for i in range(self.count)])  21.4 us
    ppermute x12, starting transfers between devices, swap(): lax.ppermute(value, 'dp', [(i, i ^ distance) for i in range(self.count)])  18.1 us
    pallas_call x1, Pallas kernels, input_call(): pl.pallas_call(functools.partial(input_kernel, seqs), grid_spec=prefetch(...  16.6 us
    pallas_call x1, Pallas kernels, out_call(): pl.pallas_call(functools.partial(out_kernel, seqs), grid_spec=prefetch((s...  15.6 us
    dynamic_update_slice x2, local copies, waits for them, and re-layouts, filled(): full = lax.dynamic_update_slice_in_dim(full, block, (me - r) % mp * own, 0)  9.24 us
  transfers between devices with their start and end apart: 25, of which 9 were waited for; matrix products, arithmetic and copies ran while one was open for 5% of the time, Pallas kernels for 42%

profile of v6, /device:TPU:0, one launch (start us, length us, event | category | flops | bytes accessed | tf_op | source)
XLA Modules:
  0.0 278.7 jit_solution(15759715924860808304)
XLA Ops:
  7.2 0.0 all-reduce.2.cloned.1.call-start
  7.2 0.5 collective-permute-start.16
  7.8 0.1 collective-permute-start.17
  7.8 0.4 collective-permute-start.18
  8.3 0.1 collective-permute-start.19
  8.3 0.7 pad_maximum_fusion.1
  9.1 0.5 collective-permute-start.20
  9.6 0.8 collective-permute-done.20.refs_13_.refs_9_
  10.4 0.0 copy-start.5
  10.5 0.0 copy-start.7
  10.5 0.4 collective-permute-start.21
  10.9 0.2 collective-permute-start.22
  11.1 0.2 copy-done.7
  11.2 42.3 %attn_forward.1 = (bf16[16,2,2,128,256]{4,3,2,1,0:T(8,128)(2,1)}, bf16[16,2,2,128,256]{4,3,2,1,0:T(8,128)(2,1)}, bf16[16,2,2,128,256]{4,3,2,1,0:T(8,128)(2,1)}, ...) custom-call(s32[1]{0:T(128)} %bitcast.27.place, ...), custom_call_target="tpu_custom_call" | custom-call | flops 1 | bytes 1 | tf_op jit(solution)/shard_map/attn_forward/pallas_call | solution.py:543
  53.5 68.0 %feed_forward.1 = (bf16[16,2048,256]{2,1,0:T(8,128)(2,1)}, bf16[16,512,256]{2,1,0:T(8,128)(2,1)}, bf16[2048,512]{1,0:T(8,128)(2,1)}, bf16[2048,512]{1,0:T(8,128)(2,1)}, f32[8,512]{1,0:T(8,128)S(1)}) custom-call(s32[1]{0:T(128)} %bitcast.27.place, bf16[16,512,256]{2,1,0:T(8,128)(2,1)} %get-tuple-element.208.refs_0_, bf16[8192,512]{1,0:T(8,128)(2,1)} %refs_1_.2, ...), custom_call_target="tpu_custom_call" | custom-call | flops 1 | bytes 1 | tf_op jit(solution)/shard_map/feed_forward/pallas_call | solution.py:652
  121.6 0.4 collective-permute-start.23
  122.0 4.0 %collective-permute-done.23 = bf16[2048,512]{1,0:T(8,128)(2,1)S(1)} collective-permute-done((bf16[2048,512]{1,0:T(8,128)(2,1)}, bf16[2048,512]{1,0:T(8,128)(2,1)S(1)}, u32[]{:S(2)}, u32[]{:S(2)}) %collective-permute-start.23) | collective-permute-done | bytes 2097184 | tf_op jit(solution)/shard_map/ppermute | solution.py:737
  126.0 3.5 %add_convert_fusion.3 = bf16[2048,512]{1,0:T(8,128)(2,1)} fusion(bf16[2048,512]{1,0:T(8,128)(2,1)S(1)} %collective-permute-done.23, bf16[2048,512]{1,0:T(8,128)(2,1)} %get-tuple-element.214), kind=kLoop, calls=%fused_computation.22 | loop fusion | flops 4194304 | bytes 6291456 | tf_op jit(solution)/shard_map/convert_element_type | solution.py:753
  129.5 0.0 all-reduce.2.cloned.1.call-update
  129.5 0.0 copy-start.2
  129.5 0.0 copy-start.3
  129.5 0.0 copy-start.4
  129.6 0.0 copy-start.13
  129.6 0.0 copy-start.16
  129.6 39.9 %attn_backward.1 = (bf16[16,256,256]{2,1,0:T(8,128)(2,1)}, bf16[16,256,256]{2,1,0:T(8,128)(2,1)}, bf16[16,256,256]{2,1,0:T(8,128)(2,1)}, bf16[16,256,256]{2,1,0:...) custom-call(bf16[16,512,256]{2,1,0:T(8,128)(2,1)} %get-tuple-element, ...), custom_call_target="tpu_custom_call" | custom-call | flops 1 | bytes 1 | tf_op jit(solution)/shard_map/attn_backward/pallas_call | solution.py:575
  169.6 94.0 %conditional.1 = (bf16[8192,512]{1,0:T(8,128)(2,1)}, bf16[8192,512]{1,0:T(8,128)(2,1)}, f32[512]{0:T(512)S(1)}, f32[512]{0:T(512)S(1)}, f32[512]{0:T(512)}, /*in...) conditional(s32[]{:T(128)} %convert_element_type.63, () %tuple.24, ...), branch_computations={%region_0.0_spmd, %region_1.0_spmd} | conditional | flops 5849172 | bytes 78395096 | solution.py:960
  169.6 0.4 collective-permute-start
  170.0 16.6 %input_grad.1 = (bf16[4096,512]{1,0:T(8,128)(2,1)}, bf16[8192,512]{1,0:T(8,128)(2,1)}, f32[8,512]{1,0:T(8,128)}, bf16[256,128]{1,0:T(8,128)(2,1)}, bf16[256,128]{1,0:T(8,128)(2,1)}) custom-call(s32[1]{0:T(128)} %get-tuple-element.56.place, bf16[8192,512]{1,0:T(8,128)(2,1)} %get-tuple-element.57.refs_0_, bf16[16,512,256]{2,1,0:T(8,128)(2,1)} %get-tuple-element.58.refs_1_, ...), custom_call_target="tpu_custom_call" | custom-call | flops 1 | bytes 1 | tf_op jit(solution)/shard_map/cond/branch_1_fun/input_grad/pallas_call | solution.py:616
  186.6 0.3 collective-permute-start.5
  186.8 0.3 collective-permute-start.1
  187.1 4.1 %collective-permute-done.1 = bf16[256,128]{1,0:T(8,128)(2,1)S(1)} collective-permute-done((bf16[256,128]{1,0:T(8,128)(2,1)}, bf16[256,128]{1,0:T(8,128)(2,1)S(1)}, u32[]{:S(2)}, u32[]{:S(2)}) %collective-permute-start.1) | collective-permute-done | bytes 65568 | tf_op jit(solution)/shard_map/cond/branch_1_fun/ppermute | solution.py:737
  191.3 0.9 add_convert_fusion.2
  192.1 1.8 add_convert_fusion
  193.9 0.1 pad_maximum_fusion
  194.0 0.1 dynamic-slice_bitcast_fusion
  194.1 3.3 %collective-permute-start.4 = (bf16[1088,128]{1,0:T(8,128)(2,1)S(1)}, bf16[1088,128]{1,0:T(8,128)(2,1)S(1)}, u32[]{:S(2)}, u32[]{:S(2)}) collective-permute-start(bf16[1088,128]{1,0:T(8,128)(2,1)S(1)} %get-tuple-element.257), channel_id=1, source_target_pairs={{0,3},{1,2},{2,1},{3,0},{4,7},{5,6},{6,5},{7,4},{8,11},{9,10},{10,... | collective-permute-start | bytes 835592 | tf_op jit(solution)/shard_map/cond/branch_1_fun/ppermute | solution.py:767
  197.4 0.6 collective-permute-start.3
  198.0 0.0 collective-permute-start.2
  198.1 15.6 %layer_out.1 = (bf16[4096,512]{1,0:T(8,128)(2,1)}, bf16[8192,512]{1,0:T(8,128)(2,1)}) custom-call(s32[1]{0:T(128)} %get-tuple-element.56.place, bf16[16,512,256]{2,1,0:T(8,128)(2,1)} %get-tuple-element.81.hid, bf16[16,2048,256]{2,1,0:T(8,128)(2,1)} %get-tuple-element.82.act, bf16[1024,512]{1,0:T(8,128)(2,1)S(1)} %get-tuple-element.83.wd0, ...), custom_call_target="tpu_custom_call" | custom-call | flops 1 | bytes 1 | tf_op jit(solution)/shard_map/cond/branch_1_fun/layer_out/pallas_call | solution.py:685
  213.7 0.1 collective-permute-start.15
  213.8 0.6 iota_xor_fusion.here
  214.4 0.1 add_convert_fusion.1
  214.6 2.5 collective-permute-start.6
  217.0 2.4 collective-permute-start.8
  219.4 0.5 collective-permute-start.7
  219.9 4.5 %constant_dynamic-update-slice_fusion.1 = bf16[8192,512]{1,0:T(8,128)(2,1)} fusion(bf16[8192,512]{1,0:T(8,128)(2,1)} %get-tuple-element.91, bf16[4096,512]{1,0:T(8,128)(2,1)} %collective-permute-done.5, s32[]{:T(128)S(6)} %select_n.62), kind=kLoop, calls=%fused_computation.20 | loop fusion | bytes 8388612 | tf_op jit(solution)/shard_map/cond/branch_1_fun/dynamic_update_slice | solution.py:832
  224.4 2.8 %collective-permute-done.7 = bf16[272,128]{1,0:T(8,128)(2,1)S(1)} collective-permute-done((bf16[272,128]{1,0:T(8,128)(2,1)S(1)}, bf16[272,128]{1,0:T(8,128)(2,1)S(1)}, u32[]{:S(2)}, u32[]{:S(2)}) %collective-permute-start.7) | collective-permute-done | bytes 69664 | tf_op jit(solution)/shard_map/cond/branch_1_fun/ppermute | solution.py:767
  227.3 4.6 %collective-permute-start.11 = (bf16[272,128]{1,0:T(8,128)(2,1)S(1)}, bf16[272,128]{1,0:T(8,128)(2,1)S(1)}, u32[]{:S(2)}, u32[]{:S(2)}) collective-permute-start(bf16[272,128]{1,0:T(8,128)(2,1)S(1)} %fusion.2), channel_id=1, source_target_pairs={{0,12},{1,13},{2,14},{3,15},{4,8},{5,9},{6,10},{7,11},{8,4},{9,5},... | collective-permute-start | bytes 208904 | tf_op jit(solution)/shard_map/cond/branch_1_fun/ppermute | solution.py:767
  231.9 0.6 collective-permute-start.9
  232.6 4.2 %collective-permute-done.9 = bf16[272,128]{1,0:T(8,128)(2,1)S(1)} collective-permute-done((bf16[272,128]{1,0:T(8,128)(2,1)S(1)}, bf16[272,128]{1,0:T(8,128)(2,1)S(1)}, u32[]{:S(2)}, u32[]{:S(2)}) %collective-permute-start.9) | collective-permute-done | bytes 69664 | tf_op jit(solution)/shard_map/cond/branch_1_fun/ppermute | solution.py:767
  236.8 2.0 collective-permute-done.10
  238.9 2.4 collective-permute-start.14
  241.3 0.8 collective-permute-start.13
  242.1 0.4 collective-permute-start.12
  242.4 4.7 %constant_dynamic-update-slice_fusion = bf16[8192,512]{1,0:T(8,128)(2,1)} fusion(bf16[8192,512]{1,0:T(8,128)(2,1)} %get-tuple-element.95, bf16[4096,512]{1,0:T(8,128)(2,1)} %collective-permute-done.15, s32[]{:T(128)S(6)} %select_n.62), kind=kLoop, calls=%fused_computation.19 | loop fusion | bytes 8388612 | tf_op jit(solution)/shard_map/cond/branch_1_fun/dynamic_update_slice | solution.py:832
  247.2 5.1 %collective-permute-done.14.b3 = bf16[1088,128]{1,0:T(8,128)(2,1)S(1)} collective-permute-done((bf16[1088,128]{1,0:T(8,128)(2,1)S(1)}, bf16[1088,128]{1,0:T(8,128)(2,1)S(1)}, u32[]{:S(2)}, u32[]{:S(2)}) %collective-permute-start.14) | collective-permute-done | bytes 278560 | tf_op jit(solution)/shard_map/cond/branch_1_fun/ppermute | solution.py:767
  252.2 7.2 %collective-permute-done.13.b2 = bf16[1088,128]{1,0:T(8,128)(2,1)S(1)} collective-permute-done((bf16[1088,128]{1,0:T(8,128)(2,1)S(1)}, bf16[1088,128]{1,0:T(8,128)(2,1)S(1)}, u32[]{:S(2)}, u32[]{:S(2)}) %collective-permute-start.13) | collective-permute-done | bytes 278560 | tf_op jit(solution)/shard_map/cond/branch_1_fun/ppermute | solution.py:767
  259.5 0.7 copy-done.9
  260.2 0.7 copy-done.10
  260.9 2.7 at_unpack.1
  263.6 0.0 copy-start.14
  263.6 0.0 copy-start.15
  263.6 4.5 %all-reduce.2.cloned.1.call-done.total = bf16[2048,512]{1,0:T(8,128)(2,1)} async-done(((bf16[2048,512]{1,0:T(8,128)(2,1)}), bf16[2048,512]{1,0:T(8,128)(2,1)}) %all-reduce.2.cloned.1.call-update) | async-done | bytes 2097168 | tf_op jit(solution)/shard_map/psum | solution.py:873
  268.1 3.7 %ff_unpack.1 = (f32[512,1024]{1,0:T(8,128)}, f32[1024,512]{1,0:T(8,128)}) custom-call(bf16[2048,512]{1,0:T(8,128)(2,1)} %all-reduce.2.cloned.1.call-done.total), custom_call_target="tpu_custom_call" | custom-call | tf_op jit(solution)/shard_map/ff_unpack/pallas_call | solution.py:708
  (47 shorter events, 0.3 us)
Async XLA Ops:
  7.2 260.9 %all-reduce.2.cloned.1.call-start = ((), (), s32[]{:S(2)}) async-start(), calls=%async_computation | async-start | bytes 4194304 | tf_op jit(solution)/shard_map/psum | solution.py:873
  7.2 3.2 %collective-permute-start.16 = (bf16[512,256]{1,0:T(8,128)(2,1)}, bf16[512,256]{1,0:T(8,128)(2,1)S(1)}, u32[]{:S(2)}, u32[]{:S(2)}) collective-permute-start(bf16[512,256]{1,0:T(8,128)(2,1)} %refs_1_.1), channel_id=1, source_target_pairs={{0,16},{16,0},{1,17},{17,1},{2,18},{18,2},{3,19},{19,3},{4,20},{20... | collective-permute-start | bytes 786440 | tf_op jit(solution)/shard_map/ppermute | solution.py:737
  7.8 2.7 collective-permute-start.17
  7.8 2.6 collective-permute-start.18
  8.3 2.2 collective-permute-start.19
  9.1 2.0 copy-start.11
  9.1 1.3 collective-permute-start.20
  10.4 0.6 copy-start.12
  10.4 43.1 %copy-start.5 = (bf16[512,256]{1,0:T(8,128)(2,1)}, bf16[512,256]{1,0:T(8,128)(2,1)S(1)}, u32[]{:S(2)}) copy-start(bf16[512,256]{1,0:T(8,128)(2,1)S(1)} %collective-permute-done.18.refs_6_) | copy-start | bytes 786436
  10.5 0.8 copy-start.7
  10.5 43.0 %collective-permute-start.21 = (bf16[512,1024]{1,0:T(8,128)(2,1)}, bf16[512,1024]{1,0:T(8,128)(2,1)}, u32[]{:S(2)}, u32[]{:S(2)}) collective-permute-start(bf16[512,1024]{1,0:T(8,128)(2,1)} %refs_2_), channel_id=1, source_target_pairs={{0,16},{16,0},{1,17},{17,1},{2,18},{18,2},{3,19},{19,3},{4,20},{20... | collective-permute-start | bytes 3145736 | tf_op jit(solution)/shard_map/ppermute | solution.py:737
  10.9 42.6 %collective-permute-start.22 = (bf16[1024,512]{1,0:T(8,128)(2,1)}, bf16[1024,512]{1,0:T(8,128)(2,1)S(1)}, u32[]{:S(2)}, u32[]{:S(2)}) collective-permute-start(bf16[1024,512]{1,0:T(8,128)(2,1)} %refs_4_), channel_id=1, source_target_pairs={{0,16},{16,0},{1,17},{17,1},{2,18},{18,2},{3,19},{19,3},{4,20},{20... | collective-permute-start | bytes 3145736 | tf_op jit(solution)/shard_map/ppermute | solution.py:737
  11.2 42.3 %copy-start = (bf16[1024,512]{1,0:T(8,128)(2,1)S(1)}, bf16[1024,512]{1,0:T(8,128)(2,1)}, u32[]{:S(2)}) copy-start(bf16[1024,512]{1,0:T(8,128)(2,1)} %refs_4_) | copy-start | bytes 3145732
  121.6 4.4 %collective-permute-start.23 = (bf16[2048,512]{1,0:T(8,128)(2,1)}, bf16[2048,512]{1,0:T(8,128)(2,1)S(1)}, u32[]{:S(2)}, u32[]{:S(2)}) collective-permute-start(bf16[2048,512]{1,0:T(8,128)(2,1)} %get-tuple-element.215), channel_id=1, source_target_pairs={{0,16},{16,0},{1,17},{17,1},{2,18},{18,2},{3,19},{19,3},{4,20},{20... | collective-permute-start | bytes 6291464 | tf_op jit(solution)/shard_map/ppermute | solution.py:737
  129.5 40.0 %copy-start.2 = (bf16[512,256]{1,0:T(8,128)(2,1)S(1)}, bf16[512,256]{1,0:T(8,128)(2,1)}, u32[]{:S(2)}) copy-start(bf16[512,256]{1,0:T(8,128)(2,1)} %refs_1_.1) | copy-start | bytes 786436
  129.5 40.0 %copy-start.3 = (bf16[512,256]{1,0:T(8,128)(2,1)S(1)}, bf16[512,256]{1,0:T(8,128)(2,1)}, u32[]{:S(2)}) copy-start(bf16[512,256]{1,0:T(8,128)(2,1)} %refs_3_) | copy-start | bytes 786436
  129.5 40.0 %copy-start.4 = (bf16[512,256]{1,0:T(8,128)(2,1)S(1)}, bf16[512,256]{1,0:T(8,128)(2,1)}, u32[]{:S(2)}) copy-start(bf16[512,256]{1,0:T(8,128)(2,1)} %refs_5_) | copy-start | bytes 786436
  129.6 40.0 %copy-start.6 = (bf16[512,256]{1,0:T(8,128)(2,1)S(1)}, bf16[512,256]{1,0:T(8,128)(2,1)}, u32[]{:S(2)}) copy-start(bf16[512,256]{1,0:T(8,128)(2,1)} %copy-done.5) | copy-start | bytes 786436
  129.6 40.0 %copy-start.13 = (f32[512]{0:T(512)S(1)}, f32[512]{0:T(512)}, u32[]{:S(2)}) copy-start(f32[512]{0:T(512)} %param.21) | copy-start | bytes 6148
  129.6 40.0 %copy-start.16 = (f32[512]{0:T(512)S(1)}, f32[512]{0:T(512)}, u32[]{:S(2)}) copy-start(f32[512]{0:T(512)} %param.36) | copy-start | bytes 6148
  169.6 17.0 %collective-permute-start = (bf16[4096,128]{1,0:T(8,128)(2,1)}, bf16[4096,128]{1,0:T(8,128)(2,1)}, u32[]{:S(2)}, u32[]{:S(2)}) collective-permute-start(bf16[4096,128]{1,0:T(8,128)(2,1)} %get-tuple-element.55), channel_id=1, source_target_pairs={{0,16},{16,0},{1,17},{17,1},{2,18},{18,2},{3,19},{19,3},{4,20},{20... | collective-permute-start | bytes 3145736 | tf_op jit(solution)/shard_map/cond/branch_1_fun/ppermute | solution.py:737
  186.6 27.1 %collective-permute-start.5 = (bf16[4096,512]{1,0:T(8,128)(2,1)}, bf16[4096,512]{1,0:T(8,128)(2,1)}, u32[]{:S(2)}, u32[]{:S(2)}) collective-permute-start(bf16[4096,512]{1,0:T(8,128)(2,1)} %get-tuple-element.79), channel_id=1, source_target_pairs={{0,16},{16,0},{1,17},{17,1},{2,18},{18,2},{3,19},{19,3},{4,20},{20... | collective-permute-start | bytes 12582920 | tf_op jit(solution)/shard_map/cond/branch_1_fun/ppermute | solution.py:737
  186.8 4.4 %collective-permute-start.1 = (bf16[256,128]{1,0:T(8,128)(2,1)}, bf16[256,128]{1,0:T(8,128)(2,1)S(1)}, u32[]{:S(2)}, u32[]{:S(2)}) collective-permute-start(bf16[256,128]{1,0:T(8,128)(2,1)} %get-tuple-element.78), channel_id=1, source_target_pairs={{0,16},{16,0},{1,17},{17,1},{2,18},{18,2},{3,19},{19,3},{4,20},{20... | collective-permute-start | bytes 196616 | tf_op jit(solution)/shard_map/cond/branch_1_fun/ppermute | solution.py:737
  194.1 19.5 %collective-permute-start.4 = (bf16[1088,128]{1,0:T(8,128)(2,1)S(1)}, bf16[1088,128]{1,0:T(8,128)(2,1)S(1)}, u32[]{:S(2)}, u32[]{:S(2)}) collective-permute-start(bf16[1088,128]{1,0:T(8,128)(2,1)S(1)} %get-tuple-element.257), channel_id=1, source_target_pairs={{0,3},{1,2},{2,1},{3,0},{4,7},{5,6},{6,5},{7,4},{8,11},{9,10},{10,... | collective-permute-start | bytes 835592 | tf_op jit(solution)/shard_map/cond/branch_1_fun/ppermute | solution.py:767
  197.4 16.2 %collective-permute-start.3 = (bf16[1088,128]{1,0:T(8,128)(2,1)S(1)}, bf16[1088,128]{1,0:T(8,128)(2,1)S(1)}, u32[]{:S(2)}, u32[]{:S(2)}) collective-permute-start(bf16[1088,128]{1,0:T(8,128)(2,1)S(1)} %get-tuple-element.258), channel_id=1, source_target_pairs={{0,2},{1,3},{2,0},{3,1},{4,6},{5,7},{6,4},{7,5},{8,10},{9,11},{10,... | collective-permute-start | bytes 835592 | tf_op jit(solution)/shard_map/cond/branch_1_fun/ppermute | solution.py:767
  198.0 15.6 %collective-permute-start.2 = (bf16[1088,128]{1,0:T(8,128)(2,1)S(1)}, bf16[1088,128]{1,0:T(8,128)(2,1)S(1)}, u32[]{:S(2)}, u32[]{:S(2)}) collective-permute-start(bf16[1088,128]{1,0:T(8,128)(2,1)S(1)} %get-tuple-element.259), channel_id=1, source_target_pairs={{0,1},{1,0},{2,3},{3,2},{4,5},{5,4},{6,7},{7,6},{8,9},{9,8},{10,11... | collective-permute-start | bytes 835592 | tf_op jit(solution)/shard_map/cond/branch_1_fun/ppermute | solution.py:767
  213.7 28.8 %collective-permute-start.15 = (bf16[4096,512]{1,0:T(8,128)(2,1)}, bf16[4096,512]{1,0:T(8,128)(2,1)}, u32[]{:S(2)}, u32[]{:S(2)}) collective-permute-start(bf16[4096,512]{1,0:T(8,128)(2,1)} %get-tuple-element.96), channel_id=1, source_target_pairs={{0,16},{16,0},{1,17},{17,1},{2,18},{18,2},{3,19},{19,3},{4,20},{20... | collective-permute-start | bytes 12582920 | tf_op jit(solution)/shard_map/cond/branch_1_fun/ppermute | solution.py:737
  214.6 9.8 %collective-permute-start.6 = (bf16[272,128]{1,0:T(8,128)(2,1)S(1)}, bf16[272,128]{1,0:T(8,128)(2,1)S(1)}, u32[]{:S(2)}, u32[]{:S(2)}) collective-permute-start(bf16[272,128]{1,0:T(8,128)(2,1)S(1)} %get-tuple-element.261), channel_id=1, source_target_pairs={{0,4},{1,5},{2,6},{3,7},{4,0},{5,1},{6,2},{7,3},{8,12},{9,13},{10,... | collective-permute-start | bytes 208904 | tf_op jit(solution)/shard_map/cond/branch_1_fun/ppermute | solution.py:767
  217.0 7.4 %collective-permute-start.8 = (bf16[272,128]{1,0:T(8,128)(2,1)S(1)}, bf16[272,128]{1,0:T(8,128)(2,1)S(1)}, u32[]{:S(2)}, u32[]{:S(2)}) collective-permute-start(bf16[272,128]{1,0:T(8,128)(2,1)S(1)} %get-tuple-element.262), channel_id=1, source_target_pairs={{0,12},{1,13},{2,14},{3,15},{4,8},{5,9},{6,10},{7,11},{8,4},{9,5},... | collective-permute-start | bytes 208904 | tf_op jit(solution)/shard_map/cond/branch_1_fun/ppermute | solution.py:767
  219.4 7.8 %collective-permute-start.7 = (bf16[272,128]{1,0:T(8,128)(2,1)S(1)}, bf16[272,128]{1,0:T(8,128)(2,1)S(1)}, u32[]{:S(2)}, u32[]{:S(2)}) collective-permute-start(bf16[272,128]{1,0:T(8,128)(2,1)S(1)} %get-tuple-element.263), channel_id=1, source_target_pairs={{0,8},{1,9},{2,10},{3,11},{4,12},{5,13},{6,14},{7,15},{8,0},{9,1},... | collective-permute-start | bytes 208904 | tf_op jit(solution)/shard_map/cond/branch_1_fun/ppermute | solution.py:767
  227.3 11.5 %collective-permute-start.11 = (bf16[272,128]{1,0:T(8,128)(2,1)S(1)}, bf16[272,128]{1,0:T(8,128)(2,1)S(1)}, u32[]{:S(2)}, u32[]{:S(2)}) collective-permute-start(bf16[272,128]{1,0:T(8,128)(2,1)S(1)} %fusion.2), channel_id=1, source_target_pairs={{0,12},{1,13},{2,14},{3,15},{4,8},{5,9},{6,10},{7,11},{8,4},{9,5},... | collective-permute-start | bytes 208904 | tf_op jit(solution)/shard_map/cond/branch_1_fun/ppermute | solution.py:767
  231.9 6.9 %collective-permute-start.10 = (bf16[272,128]{1,0:T(8,128)(2,1)S(1)}, bf16[272,128]{1,0:T(8,128)(2,1)S(1)}, u32[]{:S(2)}, u32[]{:S(2)}) collective-permute-start(bf16[272,128]{1,0:T(8,128)(2,1)S(1)} %fusion.2), channel_id=1, source_target_pairs={{0,8},{1,9},{2,10},{3,11},{4,12},{5,13},{6,14},{7,15},{8,0},{9,1},... | collective-permute-start | bytes 208904 | tf_op jit(solution)/shard_map/cond/branch_1_fun/ppermute | solution.py:767
  231.9 4.9 %collective-permute-start.9 = (bf16[272,128]{1,0:T(8,128)(2,1)S(1)}, bf16[272,128]{1,0:T(8,128)(2,1)S(1)}, u32[]{:S(2)}, u32[]{:S(2)}) collective-permute-start(bf16[272,128]{1,0:T(8,128)(2,1)S(1)} %fusion.2), channel_id=1, source_target_pairs={{0,4},{1,5},{2,6},{3,7},{4,0},{5,1},{6,2},{7,3},{8,12},{9,13},{10,... | collective-permute-start | bytes 208904 | tf_op jit(solution)/shard_map/cond/branch_1_fun/ppermute | solution.py:767
  238.9 8.3 %copy-start.1 = (bf16[4,272,128]{2,1,0:T(8,128)(2,1)}, bf16[4,272,128]{2,1,0:T(8,128)(2,1)S(1)}, u32[]{:S(2)}) copy-start(bf16[4,272,128]{2,1,0:T(8,128)(2,1)S(1)} %bitcast_dynamic-update-slice_fusion) | copy-start | bytes 835588 | tf_op jit(solution)/shard_map/cond
  238.9 13.4 %collective-permute-start.14 = (bf16[1088,128]{1,0:T(8,128)(2,1)S(1)}, bf16[1088,128]{1,0:T(8,128)(2,1)S(1)}, u32[]{:S(2)}, u32[]{:S(2)}) collective-permute-start(bf16[1088,128]{1,0:T(8,128)(2,1)S(1)} %bitcast.48), channel_id=1, source_target_pairs={{0,3},{1,2},{2,1},{3,0},{4,7},{5,6},{6,5},{7,4},{8,11},{9,10},{10,... | collective-permute-start | bytes 835592 | tf_op jit(solution)/shard_map/cond/branch_1_fun/ppermute | solution.py:767
  241.3 18.2 %collective-permute-start.13 = (bf16[1088,128]{1,0:T(8,128)(2,1)S(1)}, bf16[1088,128]{1,0:T(8,128)(2,1)S(1)}, u32[]{:S(2)}, u32[]{:S(2)}) collective-permute-start(bf16[1088,128]{1,0:T(8,128)(2,1)S(1)} %bitcast.49), channel_id=1, source_target_pairs={{0,2},{1,3},{2,0},{3,1},{4,6},{5,7},{6,4},{7,5},{8,10},{9,11},{10,... | collective-permute-start | bytes 835592 | tf_op jit(solution)/shard_map/cond/branch_1_fun/ppermute | solution.py:767
  242.1 17.4 %collective-permute-start.12 = (bf16[1088,128]{1,0:T(8,128)(2,1)S(1)}, bf16[1088,128]{1,0:T(8,128)(2,1)S(1)}, u32[]{:S(2)}, u32[]{:S(2)}) collective-permute-start(bf16[1088,128]{1,0:T(8,128)(2,1)S(1)} %bitcast.50), channel_id=1, source_target_pairs={{0,1},{1,0},{2,3},{3,2},{4,5},{5,4},{6,7},{7,6},{8,9},{9,8},{10,11... | collective-permute-start | bytes 835592 | tf_op jit(solution)/shard_map/cond/branch_1_fun/ppermute | solution.py:767
  252.2 7.3 %copy-start.8 = (bf16[1088,128]{1,0:T(8,128)(2,1)}, bf16[1088,128]{1,0:T(8,128)(2,1)S(1)}, u32[]{:S(2)}) copy-start(bf16[1088,128]{1,0:T(8,128)(2,1)S(1)} %collective-permute-done.14.b3) | copy-start | bytes 835588 | tf_op jit(solution)/shard_map/cond
  259.5 0.7 copy-start.9
  260.2 0.7 copy-start.10
  263.6 8.3 %copy-start.14 = (f32[512]{0:T(512)}, f32[512]{0:T(512)S(1)}, u32[]{:S(2)}) copy-start(f32[512]{0:T(512)S(1)} %get-tuple-element.190) | copy-start | bytes 6148
  263.6 8.3 %copy-start.15 = (f32[512]{0:T(512)}, f32[512]{0:T(512)S(1)}, u32[]{:S(2)}) copy-start(f32[512]{0:T(512)S(1)} %get-tuple-element.189) | copy-start | bytes 6148
Sparse Core Ops, SparseCore 0:
  129.6 138.4 all-reduce.1

commit v7 on v6

--- a/solution.py
+++ b/solution.py
@@ -101,14 +101,13 @@
     top = jnp.max(magnitude, axis=0, keepdims=True)
     expo = jnp.exp(magnitude - top)
     norm = 1.0 / jnp.sum(expo, axis=0, keepdims=True)
-    low_expo, sign, low = expo.astype(BF), (scores * inverse).astype(BF), inverse.astype(BF)
-    return sign * low_expo, (low * low * low + sign * sign) * low_expo, norm
+    return (scores * inverse).astype(BF), expo.astype(BF), norm
 
 
 def attn_kernel(seqs, place, *refs):
     (tok, wq0, wq1, wk0, wk1, wv0, wv1, wo0, wo1) = refs[:9]
     gain1, shift1, bout, small0, small1 = refs[9:14]
-    (query_o, keys_o, values_o, mixed_o, signed_o, slope_o, norm_o, first_o, hidden_o) = refs[14:23]
+    (query_o, keys_o, values_o, mixed_o, sign_o, expo_o, norm_o, first_o, hidden_o) = refs[14:23]
     wqkv_t, wo_t, vec = refs[23:26]
     dim = tok.shape[1]
     lanes = seqs * SEQ
@@ -154,14 +153,15 @@
 
     def mix(s, p, near_s, far_s, values):
         c, g = divmod(p, 2)
-        near, near_g, near_n = attend(near_s, mask)
-        far, far_g, far_n = attend(far_s, mask)
+        near_t, near_e, near_n = attend(near_s, mask)
+        far_t, far_e, far_n = attend(far_s, mask)
+        near, far = near_t * near_e, far_t * far_e
         norms = [
             jnp.concatenate([near_n[:, lanes], far_n[:, lanes]], axis=1)
             for lanes in (slice(0, HALF), slice(HALF, SEQ))
         ]
-        signed_o[s, c, g, :HALF], signed_o[s, c, g, HALF:] = near, far
-        slope_o[s, c, g, :HALF], slope_o[s, c, g, HALF:] = near_g, far_g
+        sign_o[s, c, g, :HALF], sign_o[s, c, g, HALF:] = near_t, far_t
+        expo_o[s, c, g, :HALF], expo_o[s, c, g, HALF:] = near_e, far_e
         near_m, far_m = dot(values[:, :HALF], near), dot(values, far)
         made = jnp.concatenate(
             [
@@ -202,8 +202,8 @@
 
 def mlp_kernel(seqs, block, place, *refs):
     (hid, cot, wu0, wu1, wd0, wd1, gain2, shift2, small0, small1) = refs[:10]
-    (act_o, low_o, own_o, other_o, gvec_o) = refs[10:15]
-    wu_t, gup, gdown, gvec, vec, bup = refs[15:21]
+    (act_o, low_o, own_up, own_down, other_up, other_down, gvec_o) = refs[10:17]
+    wu_t, gup, gdown, gvec, vec, bup = refs[17:23]
     dim = hid.shape[1]
     units = wu0.shape[1]
     lanes = seqs * SEQ
@@ -261,11 +261,11 @@
 
     @pl.when(step == pl.num_programs(0) - 1)
     def _():
-        for half, grad_o in enumerate((own_o, other_o)):
+        for half, (up_o, down_o) in enumerate(((own_up, own_down), (other_up, other_down))):
             for index in range(units // dim):
                 start = half * units + index * dim
-                grad_o[index * dim : (index + 1) * dim, :] = gup[:dim, start : start + dim].astype(BF)
-            grad_o[units:, :] = gdown[16 + half * units : 16 + (half + 1) * units, :].astype(BF)
+                up_o[index * dim : (index + 1) * dim, :] = gup[:dim, start : start + dim].astype(BF)
+            down_o[...] = gdown[16 + half * units : 16 + (half + 1) * units, :].astype(BF)
         for index, row in ((0, 0), (1, 1), (2, 3)):
             gvec_o[row : row + 1, :] = as_row(gvec[index * dim : (index + 1) * dim, :])
         gvec_o[2:3, :] = gdown[:1, :]
@@ -290,11 +290,11 @@
         whole_o[rows, :] = made
 
 
-def ff_unpack_kernel(total, up_o, down_o):
+def ff_unpack_kernel(up, down, up_o, down_o):
     dim, units = up_o.shape
     for start in range(0, units, dim):
-        up_o[:, start : start + dim] = total[start : start + dim, :].astype(F32)
-    down_o[...] = total[units:, :].astype(F32)
+        up_o[:, start : start + dim] = up[start : start + dim, :].astype(F32)
+    down_o[...] = down[...].astype(F32)
 
 
 def at_unpack_kernel(here, b0, b1, b2, b3, *refs):
@@ -325,7 +325,7 @@
 
 
 def grad_kernel(seqs, *refs):
-    (low_i, first_i, query_i, keys_i, values_i, mixed_i, signed_i, slope_i, norm_i) = refs[:9]
+    (low_i, first_i, query_i, keys_i, values_i, mixed_i, sign_i, expo_i, norm_i) = refs[:9]
     wo0, wo1 = refs[9:11]
     outs = refs[11:17]
     own_o, other_o, gvec_o = refs[17:20]
@@ -364,16 +364,21 @@
     def outer(s, g, c, near_s, far_s, near_m, far_m):
         q, k = query_i[s, c, g], keys_i[s, c, g]
         near_q, far_q = pair_near_far(q)
-        low_pair = []
+        low_pair, signed_pair = [], []
         for index, dsigned in enumerate((near_s, far_s)):
             block = slice(0, HALF) if index == 0 else slice(HALF, HALF + SEQ)
             lanes = slice(index * HALF, (index + 1) * HALF)
-            signed = signed_i[s, c, g, block].astype(F32)
+            sign, expo = sign_i[s, c, g, block], expo_i[s, c, g, block]
+            signed_pair.append(sign * expo)
+            signed = signed_pair[index].astype(F32)
+            square = sign * sign
+            rest = jnp.maximum(1.0 - square, 1e-6)
+            slope = (rest * rest * lax.rsqrt(rest) + square) * expo
             row_dot = jnp.sum(signed * dsigned, axis=0, keepdims=True)
             row_dot = row_dot * jnp.concatenate(
                 [norm_i[s, c, g, e : e + 1, lanes] for e in range(2)], axis=1
             )
-            dscores = slope_i[s, c, g, block].astype(F32) * dsigned - signed * row_dot
+            dscores = slope.astype(F32) * dsigned - signed * row_dot
             low_pair.append(dscores.astype(BF))
         near, far = low_pair
         near_p, far_p = dot(k[:, :HALF], near), dot(k, far)
@@ -386,8 +391,7 @@
         )
         near_p, far_p = tail_dot(near, near_q), tail_dot(far, far_q)
         dk = jnp.concatenate([far_p[:HALF] + near_p, far_p[HALF:]], axis=0)
-        near_p = tail_dot(signed_i[s, c, g, :HALF], near_m)
-        far_p = tail_dot(signed_i[s, c, g, HALF:], far_m)
+        near_p, far_p = tail_dot(signed_pair[0], near_m), tail_dot(signed_pair[1], far_m)
         dv = jnp.concatenate([far_p[:HALF] + near_p, far_p[HALF:]], axis=0)
         dq, dk, dv = (dq * scale).astype(BF), dk.astype(BF), dv.astype(BF)
         dq_o, dk_o, dv_o = outs[3 * g : 3 * g + 3]
@@ -655,7 +659,7 @@
             (steps,),
             [placed_seq_block(seqs, dim, SEQ), row_block(seqs, dim, steps)] + [whole_vmem()] * 8,
             [placed_seq_block(seqs, 2 * units, SEQ), placed_seq_block(seqs, dim, SEQ)]
-            + [whole_vmem()] * 3,
+            + [whole_vmem()] * 5,
             [
                 pltpu.VMEM((2 * units, dim), BF),
                 pltpu.VMEM((dim + 16, 2 * units), F32),
@@ -668,8 +672,10 @@
         out_shape=[
             shape((count, 2 * units, SEQ), BF),
             shape((count, dim, SEQ), BF),
-            shape((2 * units, dim), BF),
-            shape((2 * units, dim), BF),
+            shape((units, dim), BF),
+            shape((units, dim), BF),
+            shape((units, dim), BF),
+            shape((units, dim), BF),
             shape((8, dim), F32),
         ],
         compiler_params=params(),
@@ -703,11 +709,11 @@
     )(place, hidden, act, *weights, bdown)
 
 
-def ff_unpack_call(total, units):
-    dim = total.shape[1]
+def ff_unpack_call(up, down):
+    units, dim = up.shape
     return pl.pallas_call(
         ff_unpack_kernel,
-        in_specs=[whole_vmem()],
+        in_specs=[whole_vmem()] * 2,
         out_specs=[whole_vmem()] * 2,
         out_shape=[
             jax.ShapeDtypeStruct((dim, units), F32),
@@ -715,7 +721,7 @@
         ],
         compiler_params=pltpu.CompilerParams(vmem_limit_bytes=VMEM_LIMIT),
         name="ff_unpack",
-    )(total)
+    )(up, down)
 
 
 def at_unpack_call(here, blocks, dim, local, sizes):
@@ -868,7 +874,11 @@
     act, low, *grad_ff, vec_ff = mlp_call(
         place, hidden, cotangent, mlp_weights, [gain2, shift2] + smalls, SEQS["mlp"], 512
     )
-    ff = total_of(mp_send(lambda r: ff_piece(grad_ff, r)))
+    if per == 1:
+        ff = [total_of(mp_send(lambda r: grad_ff[2 * r + k])) for k in range(2)]
+    else:
+        grad_ff = [jnp.concatenate(grad_ff[2 * c : 2 * c + 2], axis=0) for c in range(2)]
+        ff = [total_of(mp_send(lambda r: ff_piece(grad_ff, r)))]
     low, ff = tie((low, ff))
     ff = lax.psum(ff, "dp")
     *pieces, grad_own, grad_other, vec_at = grad_call(low, first, saved, weights[6:], SEQS["grad"])
@@ -966,9 +976,9 @@
         grad_at,
     )
     if per == 1:
-        g_up, g_down = ff_unpack_call(ff, units)
+        g_up, g_down = ff_unpack_call(*ff)
     else:
-        ff = ff.astype(F32)
+        ff = ff[0].astype(F32)
         g_up = ff[:units].reshape(dim, units)
         g_down = ff[units:]
     return (

time: 279 us -> 278 us (level)
    convert_element_type x5 -> x6, other arithmetic: 6.38 us -> 7.98 us  [total_of(): return total.astype(BF)]
    ppermute x12 -> x13, waiting for transfers between devices: 8.98 us -> 7.6 us  [shifted(): lax.ppermute(value, axis, [(i, (i + shift) % count) for i in range(count)])]
  transfers between devices with their start and end apart: 25 -> 26, of which waited for: 9 -> 9; matrix products, arithmetic and copies ran while one was open for 5% -> 6% of each run, Pallas kernels for 42% -> 42%
where the time goes in v7:
time: 278 us; the launch traced here: 277 us
  Pallas kernels  187 us (67%)
  waiting for transfers between devices  33.9 us (12%)
  starting transfers between devices  21.4 us (8%)
  between operations  14.3 us (5%)
  local copies, waits for them, and re-layouts  11.2 us (4%)
  other arithmetic  9.31 us (3%)
    pallas_call x1, Pallas kernels, mlp_call(): pl.pallas_call(functools.partial(mlp_kernel, seqs, block), grid_spec=pref...  68 us
    pallas_call x1, Pallas kernels, grad_call(): pl.pallas_call(functools.partial(grad_kernel, seqs), grid=(steps,), in_sp...  40.4 us
    pallas_call x1, Pallas kernels, attn_call(): pl.pallas_call(functools.partial(attn_kernel, seqs), grid_spec=prefetch((...  40.2 us
    ppermute x12, waiting for transfers between devices, swap(): lax.ppermute(value, 'dp', [(i, i ^ distance) for i in range(self.count)])  21.7 us
    ppermute x12, starting transfers between devices, swap(): lax.ppermute(value, 'dp', [(i, i ^ distance) for i in range(self.count)])  17.6 us
    pallas_call x1, Pallas kernels, input_call(): pl.pallas_call(functools.partial(input_kernel, seqs), grid_spec=prefetch(...  16.6 us
    pallas_call x1, Pallas kernels, out_call(): pl.pallas_call(functools.partial(out_kernel, seqs), grid_spec=prefetch((s...  15.6 us
    dynamic_update_slice x2, local copies, waits for them, and re-layouts, filled(): full = lax.dynamic_update_slice_in_dim(full, block, (me - r) % mp * own, 0)  9.35 us
  transfers between devices with their start and end apart: 26, of which 9 were waited for; matrix products, arithmetic and copies ran while one was open for 6% of the time, Pallas kernels for 42%

profile of v7, /device:TPU:0, one launch (start us, length us, event | category | flops | bytes accessed | tf_op | source)
XLA Modules:
  0.0 277.5 jit_solution(6985665635058390418)
XLA Ops:
  7.2 0.0 all-reduce.3.cloned.1.call-start
  7.2 0.5 collective-permute-start.16
  7.8 0.1 collective-permute-start.17
  7.8 0.4 collective-permute-start.18
  8.3 0.1 collective-permute-start.19
  8.3 0.7 pad_maximum_fusion.1
  9.1 0.5 collective-permute-start.20
  9.6 0.8 collective-permute-done.20.refs_13_.refs_9_
  10.4 0.0 copy-start.5
  10.5 0.4 collective-permute-start.21
  10.9 0.2 collective-permute-start.22
  11.1 0.2 copy-done.7
  11.2 40.2 %attn_forward.1 = (bf16[16,2,2,128,256]{4,3,2,1,0:T(8,128)(2,1)}, bf16[16,2,2,128,256]{4,3,2,1,0:T(8,128)(2,1)}, bf16[16,2,2,128,256]{4,3,2,1,0:T(8,128)(2,1)}, ...) custom-call(s32[1]{0:T(128)} %bitcast.27.place, ...), custom_call_target="tpu_custom_call" | custom-call | flops 1 | bytes 1 | tf_op jit(solution)/shard_map/attn_forward/pallas_call | solution.py:547
  51.4 68.0 %feed_forward.1 = (bf16[16,2048,256]{2,1,0:T(8,128)(2,1)}, bf16[16,512,256]{2,1,0:T(8,128)(2,1)}, bf16[1024,512]{1,0:T(8,128)(2,1)}, bf16[1024,512]{1,0:T(8,128)...) custom-call(s32[1]{0:T(128)} %bitcast.27.place, ...), custom_call_target="tpu_custom_call" | custom-call | flops 1 | bytes 1 | tf_op jit(solution)/shard_map/feed_forward/pallas_call | solution.py:656
  119.5 0.4 collective-permute-start.23
  119.9 0.1 collective-permute-start.24
  120.1 2.4 collective-permute-done.23
  122.4 2.5 add_convert_fusion.4
  124.9 2.6 add_convert_fusion.3
  127.5 0.0 all-reduce.3.cloned.1.call-update
  127.6 0.0 copy-start.2
  127.6 0.0 copy-start.3
  127.6 0.0 copy-start.6
  127.6 0.0 copy-start.13
  127.6 40.4 %attn_backward.1 = (bf16[16,256,256]{2,1,0:T(8,128)(2,1)}, bf16[16,256,256]{2,1,0:T(8,128)(2,1)}, bf16[16,256,256]{2,1,0:T(8,128)(2,1)}, bf16[16,256,256]{2,1,0:...) custom-call(bf16[16,512,256]{2,1,0:T(8,128)(2,1)} %get-tuple-element, ...), custom_call_target="tpu_custom_call" | custom-call | flops 1 | bytes 1 | tf_op jit(solution)/shard_map/attn_backward/pallas_call | solution.py:579
  168.1 94.2 %conditional.1 = (bf16[8192,512]{1,0:T(8,128)(2,1)}, bf16[8192,512]{1,0:T(8,128)(2,1)}, f32[512]{0:T(512)S(1)}, f32[512]{0:T(512)S(1)}, f32[512]{0:T(512)}, /*in...) conditional(s32[]{:T(128)} %convert_element_type.72, () %tuple.24, ...), branch_computations={%region_0.0_spmd, %region_1.0_spmd} | conditional | flops 5849172 | bytes 78395096 | solution.py:970
  168.1 0.4 collective-permute-start
  168.5 16.6 %input_grad.1 = (bf16[4096,512]{1,0:T(8,128)(2,1)}, bf16[8192,512]{1,0:T(8,128)(2,1)}, f32[8,512]{1,0:T(8,128)}, bf16[256,128]{1,0:T(8,128)(2,1)}, bf16[256,128]{1,0:T(8,128)(2,1)}) custom-call(s32[1]{0:T(128)} %get-tuple-element.56.place, bf16[8192,512]{1,0:T(8,128)(2,1)} %get-tuple-element.57.refs_0_, bf16[16,512,256]{2,1,0:T(8,128)(2,1)} %get-tuple-element.58.refs_1_, ...), custom_call_target="tpu_custom_call" | custom-call | flops 1 | bytes 1 | tf_op jit(solution)/shard_map/cond/branch_1_fun/input_grad/pallas_call | solution.py:620
  185.1 0.2 collective-permute-start.5
  185.3 0.4 collective-permute-start.1
  185.7 4.4 %collective-permute-done.1 = bf16[256,128]{1,0:T(8,128)(2,1)S(1)} collective-permute-done((bf16[256,128]{1,0:T(8,128)(2,1)}, bf16[256,128]{1,0:T(8,128)(2,1)S(1)}, u32[]{:S(2)}, u32[]{:S(2)}) %collective-permute-start.1) | collective-permute-done | bytes 65568 | tf_op jit(solution)/shard_map/cond/branch_1_fun/ppermute | solution.py:743
  190.1 0.9 add_convert_fusion.2
  190.9 1.8 add_convert_fusion
  192.8 0.1 pad_maximum_fusion
  192.9 0.1 dynamic-slice_bitcast_fusion
  192.9 3.3 %collective-permute-start.4 = (bf16[1088,128]{1,0:T(8,128)(2,1)S(1)}, bf16[1088,128]{1,0:T(8,128)(2,1)S(1)}, u32[]{:S(2)}, u32[]{:S(2)}) collective-permute-start(bf16[1088,128]{1,0:T(8,128)(2,1)S(1)} %get-tuple-element.265), channel_id=1, source_target_pairs={{0,3},{1,2},{2,1},{3,0},{4,7},{5,6},{6,5},{7,4},{8,11},{9,10},{10,... | collective-permute-start | bytes 835592 | tf_op jit(solution)/shard_map/cond/branch_1_fun/ppermute | solution.py:773
  196.2 0.4 collective-permute-start.3
  196.6 0.3 collective-permute-start.2
  196.9 15.6 %layer_out.1 = (bf16[4096,512]{1,0:T(8,128)(2,1)}, bf16[8192,512]{1,0:T(8,128)(2,1)}) custom-call(s32[1]{0:T(128)} %get-tuple-element.56.place, bf16[16,512,256]{2,1,0:T(8,128)(2,1)} %get-tuple-element.81.hid, bf16[16,2048,256]{2,1,0:T(8,128)(2,1)} %get-tuple-element.82.act, bf16[1024,512]{1,0:T(8,128)(2,1)S(1)} %get-tuple-element.83.wd0, ...), custom_call_target="tpu_custom_call" | custom-call | flops 1 | bytes 1 | tf_op jit(solution)/shard_map/cond/branch_1_fun/layer_out/pallas_call | solution.py:691
  212.5 0.1 collective-permute-start.15
  212.6 0.5 iota_xor_fusion.here
  213.2 0.1 add_convert_fusion.1
  213.3 2.0 collective-permute-start.6
  215.4 2.7 collective-permute-start.8
  218.1 0.5 collective-permute-start.7
  218.6 4.5 %constant_dynamic-update-slice_fusion.1 = bf16[8192,512]{1,0:T(8,128)(2,1)} fusion(bf16[8192,512]{1,0:T(8,128)(2,1)} %get-tuple-element.91, bf16[4096,512]{1,0:T(8,128)(2,1)} %collective-permute-done.5, s32[]{:T(128)S(6)} %select_n.62), kind=kLoop, calls=%fused_computation.20 | loop fusion | bytes 8388612 | tf_op jit(solution)/shard_map/cond/branch_1_fun/dynamic_update_slice | solution.py:838
  223.1 3.1 %collective-permute-done.7 = bf16[272,128]{1,0:T(8,128)(2,1)S(1)} collective-permute-done((bf16[272,128]{1,0:T(8,128)(2,1)S(1)}, bf16[272,128]{1,0:T(8,128)(2,1)S(1)}, u32[]{:S(2)}, u32[]{:S(2)}) %collective-permute-start.7) | collective-permute-done | bytes 69664 | tf_op jit(solution)/shard_map/cond/branch_1_fun/ppermute | solution.py:773
  226.3 4.2 %collective-permute-start.11 = (bf16[272,128]{1,0:T(8,128)(2,1)S(1)}, bf16[272,128]{1,0:T(8,128)(2,1)S(1)}, u32[]{:S(2)}, u32[]{:S(2)}) collective-permute-start(bf16[272,128]{1,0:T(8,128)(2,1)S(1)} %fusion.2), channel_id=1, source_target_pairs={{0,12},{1,13},{2,14},{3,15},{4,8},{5,9},{6,10},{7,11},{8,4},{9,5},... | collective-permute-start | bytes 208904 | tf_op jit(solution)/shard_map/cond/branch_1_fun/ppermute | solution.py:773
  230.5 0.6 collective-permute-start.9
  231.2 3.9 %collective-permute-done.9 = bf16[272,128]{1,0:T(8,128)(2,1)S(1)} collective-permute-done((bf16[272,128]{1,0:T(8,128)(2,1)S(1)}, bf16[272,128]{1,0:T(8,128)(2,1)S(1)}, u32[]{:S(2)}, u32[]{:S(2)}) %collective-permute-start.9) | collective-permute-done | bytes 69664 | tf_op jit(solution)/shard_map/cond/branch_1_fun/ppermute | solution.py:773
  235.1 2.2 collective-permute-done.10
  237.4 1.9 collective-permute-start.14
  239.3 1.1 collective-permute-start.13
  240.5 0.5 collective-permute-start.12
  241.0 4.8 %constant_dynamic-update-slice_fusion = bf16[8192,512]{1,0:T(8,128)(2,1)} fusion(bf16[8192,512]{1,0:T(8,128)(2,1)} %get-tuple-element.95, bf16[4096,512]{1,0:T(8,128)(2,1)} %collective-permute-done.15, s32[]{:T(128)S(6)} %select_n.62), kind=kLoop, calls=%fused_computation.19 | loop fusion | bytes 8388612 | tf_op jit(solution)/shard_map/cond/branch_1_fun/dynamic_update_slice | solution.py:838
  245.8 4.4 %collective-permute-done.14.b3 = bf16[1088,128]{1,0:T(8,128)(2,1)S(1)} collective-permute-done((bf16[1088,128]{1,0:T(8,128)(2,1)S(1)}, bf16[1088,128]{1,0:T(8,128)(2,1)S(1)}, u32[]{:S(2)}, u32[]{:S(2)}) %collective-permute-start.14) | collective-permute-done | bytes 278560 | tf_op jit(solution)/shard_map/cond/branch_1_fun/ppermute | solution.py:773
  250.2 8.0 %collective-permute-done.13.b2 = bf16[1088,128]{1,0:T(8,128)(2,1)S(1)} collective-permute-done((bf16[1088,128]{1,0:T(8,128)(2,1)S(1)}, bf16[1088,128]{1,0:T(8,128)(2,1)S(1)}, u32[]{:S(2)}, u32[]{:S(2)}) %collective-permute-start.13) | collective-permute-done | bytes 278560 | tf_op jit(solution)/shard_map/cond/branch_1_fun/ppermute | solution.py:773
  258.2 0.7 copy-done.9
  258.9 0.7 copy-done.10
  259.6 2.7 at_unpack.1
  262.3 0.0 copy-start.14
  262.3 0.0 copy-start.15
  262.3 4.6 %all-reduce.3.cloned.1.call-done = (bf16[1024,512]{1,0:T(8,128)(2,1)}, bf16[1024,512]{1,0:T(8,128)(2,1)}) async-done(((bf16[1024,512]{1,0:T(8,128)(2,1)}, bf16[1024,512]{1,0:T(8,128)(2,1)}), (bf16[1024,512]{1,0:T(8,128)(2,1)}, bf16[1024,512]{1,0:T(8,128)(2,1)})) %all-reduce.3.cloned.1.call-update) | async-done | bytes 2097168 | tf_op jit(solution)/shard_map/psum | solution.py:883
  266.9 3.7 %ff_unpack.1 = (f32[512,1024]{1,0:T(8,128)}, f32[1024,512]{1,0:T(8,128)}) custom-call(bf16[1024,512]{1,0:T(8,128)(2,1)} %get-tuple-element.263.up, bf16[1024,512]{1,0:T(8,128)(2,1)} %get-tuple-element.264.down), custom_call_target="tpu_custom_call" | custom-call | tf_op jit(solution)/shard_map/ff_unpack/pallas_call | solution.py:714
  (50 shorter events, 0.3 us)
Async XLA Ops:
  7.2 259.7 %all-reduce.3.cloned.1.call-start = ((), (), s32[]{:S(2)}) async-start(), calls=%async_computation | async-start | bytes 4194304 | tf_op jit(solution)/shard_map/psum | solution.py:883
  7.2 3.2 %collective-permute-start.16 = (bf16[512,256]{1,0:T(8,128)(2,1)}, bf16[512,256]{1,0:T(8,128)(2,1)S(1)}, u32[]{:S(2)}, u32[]{:S(2)}) collective-permute-start(bf16[512,256]{1,0:T(8,128)(2,1)} %refs_1_.1), channel_id=1, source_target_pairs={{0,16},{16,0},{1,17},{17,1},{2,18},{18,2},{3,19},{19,3},{4,20},{20... | collective-permute-start | bytes 786440 | tf_op jit(solution)/shard_map/ppermute | solution.py:743
  7.8 2.7 collective-permute-start.17
  7.8 2.6 collective-permute-start.18
  8.3 2.2 collective-permute-start.19
  9.1 2.0 copy-start.11
  9.1 1.3 collective-permute-start.20
  10.4 0.6 copy-start.12
  10.4 41.0 %copy-start.5 = (bf16[512,256]{1,0:T(8,128)(2,1)}, bf16[512,256]{1,0:T(8,128)(2,1)S(1)}, u32[]{:S(2)}) copy-start(bf16[512,256]{1,0:T(8,128)(2,1)S(1)} %collective-permute-done.18.refs_6_) | copy-start | bytes 786436
  10.5 0.8 copy-start.7
  10.5 40.9 %collective-permute-start.21 = (bf16[512,1024]{1,0:T(8,128)(2,1)}, bf16[512,1024]{1,0:T(8,128)(2,1)}, u32[]{:S(2)}, u32[]{:S(2)}) collective-permute-start(bf16[512,1024]{1,0:T(8,128)(2,1)} %refs_2_), channel_id=1, source_target_pairs={{0,16},{16,0},{1,17},{17,1},{2,18},{18,2},{3,19},{19,3},{4,20},{20... | collective-permute-start | bytes 3145736 | tf_op jit(solution)/shard_map/ppermute | solution.py:743
  10.9 40.5 %collective-permute-start.22 = (bf16[1024,512]{1,0:T(8,128)(2,1)}, bf16[1024,512]{1,0:T(8,128)(2,1)S(1)}, u32[]{:S(2)}, u32[]{:S(2)}) collective-permute-start(bf16[1024,512]{1,0:T(8,128)(2,1)} %refs_4_), channel_id=1, source_target_pairs={{0,16},{16,0},{1,17},{17,1},{2,18},{18,2},{3,19},{19,3},{4,20},{20... | collective-permute-start | bytes 3145736 | tf_op jit(solution)/shard_map/ppermute | solution.py:743
  11.2 40.2 %copy-start = (bf16[1024,512]{1,0:T(8,128)(2,1)S(1)}, bf16[1024,512]{1,0:T(8,128)(2,1)}, u32[]{:S(2)}) copy-start(bf16[1024,512]{1,0:T(8,128)(2,1)} %refs_4_) | copy-start | bytes 3145732
  119.5 2.9 %collective-permute-start.23 = (bf16[1024,512]{1,0:T(8,128)(2,1)}, bf16[1024,512]{1,0:T(8,128)(2,1)S(1)}, u32[]{:S(2)}, u32[]{:S(2)}) collective-permute-start(bf16[1024,512]{1,0:T(8,128)(2,1)} %get-tuple-element.218), channel_id=1, source_target_pairs={{0,16},{16,0},{1,17},{17,1},{2,18},{18,2},{3,19},{19,3},{4,20},{20... | collective-permute-start | bytes 3145736 | tf_op jit(solution)/shard_map/ppermute | solution.py:743
  119.9 5.0 %collective-permute-start.24 = (bf16[1024,512]{1,0:T(8,128)(2,1)}, bf16[1024,512]{1,0:T(8,128)(2,1)S(1)}, u32[]{:S(2)}, u32[]{:S(2)}) collective-permute-start(bf16[1024,512]{1,0:T(8,128)(2,1)} %get-tuple-element.220), channel_id=1, source_target_pairs={{0,16},{16,0},{1,17},{17,1},{2,18},{18,2},{3,19},{19,3},{4,20},{20... | collective-permute-start | bytes 3145736 | tf_op jit(solution)/shard_map/ppermute | solution.py:743
  127.6 40.5 %copy-start.2 = (bf16[512,256]{1,0:T(8,128)(2,1)S(1)}, bf16[512,256]{1,0:T(8,128)(2,1)}, u32[]{:S(2)}) copy-start(bf16[512,256]{1,0:T(8,128)(2,1)} %refs_1_.1) | copy-start | bytes 786436
  127.6 40.5 %copy-start.3 = (bf16[512,256]{1,0:T(8,128)(2,1)S(1)}, bf16[512,256]{1,0:T(8,128)(2,1)}, u32[]{:S(2)}) copy-start(bf16[512,256]{1,0:T(8,128)(2,1)} %refs_3_) | copy-start | bytes 786436
  127.6 40.5 %copy-start.4 = (bf16[512,256]{1,0:T(8,128)(2,1)S(1)}, bf16[512,256]{1,0:T(8,128)(2,1)}, u32[]{:S(2)}) copy-start(bf16[512,256]{1,0:T(8,128)(2,1)} %refs_5_) | copy-start | bytes 786436
  127.6 40.4 %copy-start.6 = (bf16[512,256]{1,0:T(8,128)(2,1)S(1)}, bf16[512,256]{1,0:T(8,128)(2,1)}, u32[]{:S(2)}) copy-start(bf16[512,256]{1,0:T(8,128)(2,1)} %copy-done.5) | copy-start | bytes 786436
  127.6 40.4 %copy-start.13 = (f32[512]{0:T(512)S(1)}, f32[512]{0:T(512)}, u32[]{:S(2)}) copy-start(f32[512]{0:T(512)} %param.21) | copy-start | bytes 6148
  127.6 40.4 %copy-start.16 = (f32[512]{0:T(512)S(1)}, f32[512]{0:T(512)}, u32[]{:S(2)}) copy-start(f32[512]{0:T(512)} %param.36) | copy-start | bytes 6148
  168.1 17.0 %collective-permute-start = (bf16[4096,128]{1,0:T(8,128)(2,1)}, bf16[4096,128]{1,0:T(8,128)(2,1)}, u32[]{:S(2)}, u32[]{:S(2)}) collective-permute-start(bf16[4096,128]{1,0:T(8,128)(2,1)} %get-tuple-element.55), channel_id=1, source_target_pairs={{0,16},{16,0},{1,17},{17,1},{2,18},{18,2},{3,19},{19,3},{4,20},{20... | collective-permute-start | bytes 3145736 | tf_op jit(solution)/shard_map/cond/branch_1_fun/ppermute | solution.py:743
  185.1 27.3 %collective-permute-start.5 = (bf16[4096,512]{1,0:T(8,128)(2,1)}, bf16[4096,512]{1,0:T(8,128)(2,1)}, u32[]{:S(2)}, u32[]{:S(2)}) collective-permute-start(bf16[4096,512]{1,0:T(8,128)(2,1)} %get-tuple-element.79), channel_id=1, source_target_pairs={{0,16},{16,0},{1,17},{17,1},{2,18},{18,2},{3,19},{19,3},{4,20},{20... | collective-permute-start | bytes 12582920 | tf_op jit(solution)/shard_map/cond/branch_1_fun/ppermute | solution.py:743
  185.3 4.7 %collective-permute-start.1 = (bf16[256,128]{1,0:T(8,128)(2,1)}, bf16[256,128]{1,0:T(8,128)(2,1)S(1)}, u32[]{:S(2)}, u32[]{:S(2)}) collective-permute-start(bf16[256,128]{1,0:T(8,128)(2,1)} %get-tuple-element.78), channel_id=1, source_target_pairs={{0,16},{16,0},{1,17},{17,1},{2,18},{18,2},{3,19},{19,3},{4,20},{20... | collective-permute-start | bytes 196616 | tf_op jit(solution)/shard_map/cond/branch_1_fun/ppermute | solution.py:743
  192.9 19.5 %collective-permute-start.4 = (bf16[1088,128]{1,0:T(8,128)(2,1)S(1)}, bf16[1088,128]{1,0:T(8,128)(2,1)S(1)}, u32[]{:S(2)}, u32[]{:S(2)}) collective-permute-start(bf16[1088,128]{1,0:T(8,128)(2,1)S(1)} %get-tuple-element.265), channel_id=1, source_target_pairs={{0,3},{1,2},{2,1},{3,0},{4,7},{5,6},{6,5},{7,4},{8,11},{9,10},{10,... | collective-permute-start | bytes 835592 | tf_op jit(solution)/shard_map/cond/branch_1_fun/ppermute | solution.py:773
  196.2 16.2 %collective-permute-start.3 = (bf16[1088,128]{1,0:T(8,128)(2,1)S(1)}, bf16[1088,128]{1,0:T(8,128)(2,1)S(1)}, u32[]{:S(2)}, u32[]{:S(2)}) collective-permute-start(bf16[1088,128]{1,0:T(8,128)(2,1)S(1)} %get-tuple-element.266), channel_id=1, source_target_pairs={{0,2},{1,3},{2,0},{3,1},{4,6},{5,7},{6,4},{7,5},{8,10},{9,11},{10,... | collective-permute-start | bytes 835592 | tf_op jit(solution)/shard_map/cond/branch_1_fun/ppermute | solution.py:773
  196.6 15.8 %collective-permute-start.2 = (bf16[1088,128]{1,0:T(8,128)(2,1)S(1)}, bf16[1088,128]{1,0:T(8,128)(2,1)S(1)}, u32[]{:S(2)}, u32[]{:S(2)}) collective-permute-start(bf16[1088,128]{1,0:T(8,128)(2,1)S(1)} %get-tuple-element.267), channel_id=1, source_target_pairs={{0,1},{1,0},{2,3},{3,2},{4,5},{5,4},{6,7},{7,6},{8,9},{9,8},{10,11... | collective-permute-start | bytes 835592 | tf_op jit(solution)/shard_map/cond/branch_1_fun/ppermute | solution.py:773
  212.5 28.5 %collective-permute-start.15 = (bf16[4096,512]{1,0:T(8,128)(2,1)}, bf16[4096,512]{1,0:T(8,128)(2,1)}, u32[]{:S(2)}, u32[]{:S(2)}) collective-permute-start(bf16[4096,512]{1,0:T(8,128)(2,1)} %get-tuple-element.96), channel_id=1, source_target_pairs={{0,16},{16,0},{1,17},{17,1},{2,18},{18,2},{3,19},{19,3},{4,20},{20... | collective-permute-start | bytes 12582920 | tf_op jit(solution)/shard_map/cond/branch_1_fun/ppermute | solution.py:743
  213.3 9.8 %collective-permute-start.6 = (bf16[272,128]{1,0:T(8,128)(2,1)S(1)}, bf16[272,128]{1,0:T(8,128)(2,1)S(1)}, u32[]{:S(2)}, u32[]{:S(2)}) collective-permute-start(bf16[272,128]{1,0:T(8,128)(2,1)S(1)} %get-tuple-element.269), channel_id=1, source_target_pairs={{0,4},{1,5},{2,6},{3,7},{4,0},{5,1},{6,2},{7,3},{8,12},{9,13},{10,... | collective-permute-start | bytes 208904 | tf_op jit(solution)/shard_map/cond/branch_1_fun/ppermute | solution.py:773
  215.4 7.7 %collective-permute-start.8 = (bf16[272,128]{1,0:T(8,128)(2,1)S(1)}, bf16[272,128]{1,0:T(8,128)(2,1)S(1)}, u32[]{:S(2)}, u32[]{:S(2)}) collective-permute-start(bf16[272,128]{1,0:T(8,128)(2,1)S(1)} %get-tuple-element.270), channel_id=1, source_target_pairs={{0,12},{1,13},{2,14},{3,15},{4,8},{5,9},{6,10},{7,11},{8,4},{9,5},... | collective-permute-start | bytes 208904 | tf_op jit(solution)/shard_map/cond/branch_1_fun/ppermute | solution.py:773
  218.1 8.2 %collective-permute-start.7 = (bf16[272,128]{1,0:T(8,128)(2,1)S(1)}, bf16[272,128]{1,0:T(8,128)(2,1)S(1)}, u32[]{:S(2)}, u32[]{:S(2)}) collective-permute-start(bf16[272,128]{1,0:T(8,128)(2,1)S(1)} %get-tuple-element.271), channel_id=1, source_target_pairs={{0,8},{1,9},{2,10},{3,11},{4,12},{5,13},{6,14},{7,15},{8,0},{9,1},... | collective-permute-start | bytes 208904 | tf_op jit(solution)/shard_map/cond/branch_1_fun/ppermute | solution.py:773
  226.3 11.1 %collective-permute-start.11 = (bf16[272,128]{1,0:T(8,128)(2,1)S(1)}, bf16[272,128]{1,0:T(8,128)(2,1)S(1)}, u32[]{:S(2)}, u32[]{:S(2)}) collective-permute-start(bf16[272,128]{1,0:T(8,128)(2,1)S(1)} %fusion.2), channel_id=1, source_target_pairs={{0,12},{1,13},{2,14},{3,15},{4,8},{5,9},{6,10},{7,11},{8,4},{9,5},... | collective-permute-start | bytes 208904 | tf_op jit(solution)/shard_map/cond/branch_1_fun/ppermute | solution.py:773
  230.5 6.8 %collective-permute-start.10 = (bf16[272,128]{1,0:T(8,128)(2,1)S(1)}, bf16[272,128]{1,0:T(8,128)(2,1)S(1)}, u32[]{:S(2)}, u32[]{:S(2)}) collective-permute-start(bf16[272,128]{1,0:T(8,128)(2,1)S(1)} %fusion.2), channel_id=1, source_target_pairs={{0,8},{1,9},{2,10},{3,11},{4,12},{5,13},{6,14},{7,15},{8,0},{9,1},... | collective-permute-start | bytes 208904 | tf_op jit(solution)/shard_map/cond/branch_1_fun/ppermute | solution.py:773
  230.5 4.6 %collective-permute-start.9 = (bf16[272,128]{1,0:T(8,128)(2,1)S(1)}, bf16[272,128]{1,0:T(8,128)(2,1)S(1)}, u32[]{:S(2)}, u32[]{:S(2)}) collective-permute-start(bf16[272,128]{1,0:T(8,128)(2,1)S(1)} %fusion.2), channel_id=1, source_target_pairs={{0,4},{1,5},{2,6},{3,7},{4,0},{5,1},{6,2},{7,3},{8,12},{9,13},{10,... | collective-permute-start | bytes 208904 | tf_op jit(solution)/shard_map/cond/branch_1_fun/ppermute | solution.py:773
  237.4 8.4 %copy-start.1 = (bf16[4,272,128]{2,1,0:T(8,128)(2,1)}, bf16[4,272,128]{2,1,0:T(8,128)(2,1)S(1)}, u32[]{:S(2)}) copy-start(bf16[4,272,128]{2,1,0:T(8,128)(2,1)S(1)} %bitcast_dynamic-update-slice_fusion) | copy-start | bytes 835588 | tf_op jit(solution)/shard_map/cond
  237.4 12.8 %collective-permute-start.14 = (bf16[1088,128]{1,0:T(8,128)(2,1)S(1)}, bf16[1088,128]{1,0:T(8,128)(2,1)S(1)}, u32[]{:S(2)}, u32[]{:S(2)}) collective-permute-start(bf16[1088,128]{1,0:T(8,128)(2,1)S(1)} %bitcast.48), channel_id=1, source_target_pairs={{0,3},{1,2},{2,1},{3,0},{4,7},{5,6},{6,5},{7,4},{8,11},{9,10},{10,... | collective-permute-start | bytes 835592 | tf_op jit(solution)/shard_map/cond/branch_1_fun/ppermute | solution.py:773
  239.3 18.9 %collective-permute-start.13 = (bf16[1088,128]{1,0:T(8,128)(2,1)S(1)}, bf16[1088,128]{1,0:T(8,128)(2,1)S(1)}, u32[]{:S(2)}, u32[]{:S(2)}) collective-permute-start(bf16[1088,128]{1,0:T(8,128)(2,1)S(1)} %bitcast.49), channel_id=1, source_target_pairs={{0,2},{1,3},{2,0},{3,1},{4,6},{5,7},{6,4},{7,5},{8,10},{9,11},{10,... | collective-permute-start | bytes 835592 | tf_op jit(solution)/shard_map/cond/branch_1_fun/ppermute | solution.py:773
  240.5 17.7 %collective-permute-start.12 = (bf16[1088,128]{1,0:T(8,128)(2,1)S(1)}, bf16[1088,128]{1,0:T(8,128)(2,1)S(1)}, u32[]{:S(2)}, u32[]{:S(2)}) collective-permute-start(bf16[1088,128]{1,0:T(8,128)(2,1)S(1)} %bitcast.50), channel_id=1, source_target_pairs={{0,1},{1,0},{2,3},{3,2},{4,5},{5,4},{6,7},{7,6},{8,9},{9,8},{10,11... | collective-permute-start | bytes 835592 | tf_op jit(solution)/shard_map/cond/branch_1_fun/ppermute | solution.py:773
  250.2 8.0 %copy-start.8 = (bf16[1088,128]{1,0:T(8,128)(2,1)}, bf16[1088,128]{1,0:T(8,128)(2,1)S(1)}, u32[]{:S(2)}) copy-start(bf16[1088,128]{1,0:T(8,128)(2,1)S(1)} %collective-permute-done.14.b3) | copy-start | bytes 835588 | tf_op jit(solution)/shard_map/cond
  258.2 0.7 copy-start.9
  258.9 0.7 copy-start.10
  262.3 8.3 %copy-start.14 = (f32[512]{0:T(512)}, f32[512]{0:T(512)S(1)}, u32[]{:S(2)}) copy-start(f32[512]{0:T(512)S(1)} %get-tuple-element.193) | copy-start | bytes 6148
  262.3 8.3 %copy-start.15 = (f32[512]{0:T(512)}, f32[512]{0:T(512)S(1)}, u32[]{:S(2)}) copy-start(f32[512]{0:T(512)S(1)} %get-tuple-element.192) | copy-start | bytes 6148
Sparse Core Ops, SparseCore 0:
  127.7 139.2 all-reduce.2

commit v8 on v7

--- a/solution.py
+++ b/solution.py
@@ -291,9 +291,7 @@
 
 
 def ff_unpack_kernel(up, down, up_o, down_o):
-    dim, units = up_o.shape
-    for start in range(0, units, dim):
-        up_o[:, start : start + dim] = up[start : start + dim, :].astype(F32)
+    up_o[...] = up[...].astype(F32)
     down_o[...] = down[...].astype(F32)
 
 
@@ -711,15 +709,18 @@
 
 def ff_unpack_call(up, down):
     units, dim = up.shape
+    tall = dim // SEQ
+    block = pl.BlockSpec((SEQ, dim), lambda i: (i, 0))
     return pl.pallas_call(
         ff_unpack_kernel,
-        in_specs=[whole_vmem()] * 2,
-        out_specs=[whole_vmem()] * 2,
+        grid=(units // SEQ,),
+        in_specs=[block] * 2,
+        out_specs=[pl.BlockSpec((SEQ, dim), lambda i: (i % tall, i // tall)), block],
         out_shape=[
             jax.ShapeDtypeStruct((dim, units), F32),
             jax.ShapeDtypeStruct((units, dim), F32),
         ],
-        compiler_params=pltpu.CompilerParams(vmem_limit_bytes=VMEM_LIMIT),
+        compiler_params=params(),
         name="ff_unpack",
     )(up, down)
 

time: 278 us -> 278 us (level)
  no operation moved by 1% of the time
where the time goes in v8:
time: 278 us
  Pallas kernels  188 us (68%)
  waiting for transfers between devices  33.9 us (12%)
  starting transfers between devices  21.4 us (8%)
  between operations  14.3 us (5%)
  local copies, waits for them, and re-layouts  11.2 us (4%)
  other arithmetic  9.31 us (3%)
    pallas_call x1, Pallas kernels, mlp_call(): pl.pallas_call(functools.partial(mlp_kernel, seqs, block), grid_spec=pref...  68 us
    pallas_call x1, Pallas kernels, grad_call(): pl.pallas_call(functools.partial(grad_kernel, seqs), grid=(steps,), in_sp...  40.4 us
    pallas_call x1, Pallas kernels, attn_call(): pl.pallas_call(functools.partial(attn_kernel, seqs), grid_spec=prefetch((...  40.2 us
    ppermute x12, waiting for transfers between devices, swap(): lax.ppermute(value, 'dp', [(i, i ^ distance) for i in range(self.count)])  21.7 us
    ppermute x12, starting transfers between devices, swap(): lax.ppermute(value, 'dp', [(i, i ^ distance) for i in range(self.count)])  17.6 us
    pallas_call x1, Pallas kernels, input_call(): pl.pallas_call(functools.partial(input_kernel, seqs), grid_spec=prefetch(...  16.6 us
    pallas_call x1, Pallas kernels, out_call(): pl.pallas_call(functools.partial(out_kernel, seqs), grid_spec=prefetch((s...  15.6 us
    dynamic_update_slice x2, local copies, waits for them, and re-layouts, filled(): full = lax.dynamic_update_slice_in_dim(full, block, (me - r) % mp * own, 0)  9.35 us
  transfers between devices with their start and end apart: 26, of which 9 were waited for; matrix products, arithmetic and copies ran while one was open for 6% of the time, Pallas kernels for 42%

profile of v8, /device:TPU:0, one launch (start us, length us, event | category | flops | bytes accessed | tf_op | source)
XLA Modules:
  0.0 277.9 jit_solution(16812083294789083663)
XLA Ops:
  7.2 0.0 all-reduce.3.cloned.1.call-start
  7.2 0.5 collective-permute-start.16
  7.8 0.1 collective-permute-start.17
  7.8 0.4 collective-permute-start.18
  8.3 0.1 collective-permute-start.19
  8.3 0.7 pad_maximum_fusion.1
  9.1 0.5 collective-permute-start.20
  9.6 0.8 collective-permute-done.20.refs_13_.refs_9_
  10.4 0.0 copy-start.5
  10.5 0.4 collective-permute-start.21
  10.9 0.2 collective-permute-start.22
  11.1 0.2 copy-done.7
  11.2 40.2 %attn_forward.1 = (bf16[16,2,2,128,256]{4,3,2,1,0:T(8,128)(2,1)}, bf16[16,2,2,128,256]{4,3,2,1,0:T(8,128)(2,1)}, bf16[16,2,2,128,256]{4,3,2,1,0:T(8,128)(2,1)}, ...) custom-call(s32[1]{0:T(128)} %bitcast.27.place, ...), custom_call_target="tpu_custom_call" | custom-call | flops 1 | bytes 1 | tf_op jit(solution)/shard_map/attn_forward/pallas_call | solution.py:545
  51.4 68.0 %feed_forward.1 = (bf16[16,2048,256]{2,1,0:T(8,128)(2,1)}, bf16[16,512,256]{2,1,0:T(8,128)(2,1)}, bf16[1024,512]{1,0:T(8,128)(2,1)}, bf16[1024,512]{1,0:T(8,128)...) custom-call(s32[1]{0:T(128)} %bitcast.27.place, ...), custom_call_target="tpu_custom_call" | custom-call | flops 1 | bytes 1 | tf_op jit(solution)/shard_map/feed_forward/pallas_call | solution.py:654
  119.5 0.4 collective-permute-start.23
  119.9 0.1 collective-permute-start.24
  120.1 2.4 collective-permute-done.23
  122.4 2.5 add_convert_fusion.4
  124.9 2.6 add_convert_fusion.3
  127.5 0.0 all-reduce.3.cloned.1.call-update
  127.6 0.0 copy-start.2
  127.6 0.0 copy-start.3
  127.6 0.0 copy-start.6
  127.6 0.0 copy-start.13
  127.6 40.4 %attn_backward.1 = (bf16[16,256,256]{2,1,0:T(8,128)(2,1)}, bf16[16,256,256]{2,1,0:T(8,128)(2,1)}, bf16[16,256,256]{2,1,0:T(8,128)(2,1)}, bf16[16,256,256]{2,1,0:...) custom-call(bf16[16,512,256]{2,1,0:T(8,128)(2,1)} %get-tuple-element, ...), custom_call_target="tpu_custom_call" | custom-call | flops 1 | bytes 1 | tf_op jit(solution)/shard_map/attn_backward/pallas_call | solution.py:577
  168.1 94.2 %conditional.1 = (bf16[8192,512]{1,0:T(8,128)(2,1)}, bf16[8192,512]{1,0:T(8,128)(2,1)}, f32[512]{0:T(512)S(1)}, f32[512]{0:T(512)S(1)}, f32[512]{0:T(512)}, /*in...) conditional(s32[]{:T(128)} %convert_element_type.72, () %tuple.24, ...), branch_computations={%region_0.0_spmd, %region_1.0_spmd} | conditional | flops 5849172 | bytes 78395096 | solution.py:971
  168.1 0.4 collective-permute-start
  168.5 16.6 %input_grad.1 = (bf16[4096,512]{1,0:T(8,128)(2,1)}, bf16[8192,512]{1,0:T(8,128)(2,1)}, f32[8,512]{1,0:T(8,128)}, bf16[256,128]{1,0:T(8,128)(2,1)}, bf16[256,128]{1,0:T(8,128)(2,1)}) custom-call(s32[1]{0:T(128)} %get-tuple-element.56.place, bf16[8192,512]{1,0:T(8,128)(2,1)} %get-tuple-element.57.refs_0_, bf16[16,512,256]{2,1,0:T(8,128)(2,1)} %get-tuple-element.58.refs_1_, ...), custom_call_target="tpu_custom_call" | custom-call | flops 1 | bytes 1 | tf_op jit(solution)/shard_map/cond/branch_1_fun/input_grad/pallas_call | solution.py:618
  185.1 0.2 collective-permute-start.5
  185.3 0.4 collective-permute-start.1
  185.7 4.4 %collective-permute-done.1 = bf16[256,128]{1,0:T(8,128)(2,1)S(1)} collective-permute-done((bf16[256,128]{1,0:T(8,128)(2,1)}, bf16[256,128]{1,0:T(8,128)(2,1)S(1)}, u32[]{:S(2)}, u32[]{:S(2)}) %collective-permute-start.1) | collective-permute-done | bytes 65568 | tf_op jit(solution)/shard_map/cond/branch_1_fun/ppermute | solution.py:744
  190.1 0.9 add_convert_fusion.2
  190.9 1.8 add_convert_fusion
  192.8 0.1 pad_maximum_fusion
  192.9 0.1 dynamic-slice_bitcast_fusion
  192.9 3.3 %collective-permute-start.4 = (bf16[1088,128]{1,0:T(8,128)(2,1)S(1)}, bf16[1088,128]{1,0:T(8,128)(2,1)S(1)}, u32[]{:S(2)}, u32[]{:S(2)}) collective-permute-start(bf16[1088,128]{1,0:T(8,128)(2,1)S(1)} %get-tuple-element.265), channel_id=1, source_target_pairs={{0,3},{1,2},{2,1},{3,0},{4,7},{5,6},{6,5},{7,4},{8,11},{9,10},{10,... | collective-permute-start | bytes 835592 | tf_op jit(solution)/shard_map/cond/branch_1_fun/ppermute | solution.py:774
  196.2 0.4 collective-permute-start.3
  196.6 0.3 collective-permute-start.2
  196.9 15.6 %layer_out.1 = (bf16[4096,512]{1,0:T(8,128)(2,1)}, bf16[8192,512]{1,0:T(8,128)(2,1)}) custom-call(s32[1]{0:T(128)} %get-tuple-element.56.place, bf16[16,512,256]{2,1,0:T(8,128)(2,1)} %get-tuple-element.81.hid, bf16[16,2048,256]{2,1,0:T(8,128)(2,1)} %get-tuple-element.82.act, bf16[1024,512]{1,0:T(8,128)(2,1)S(1)} %get-tuple-element.83.wd0, ...), custom_call_target="tpu_custom_call" | custom-call | flops 1 | bytes 1 | tf_op jit(solution)/shard_map/cond/branch_1_fun/layer_out/pallas_call | solution.py:689
  212.5 0.1 collective-permute-start.15
  212.6 0.5 iota_xor_fusion.here
  213.2 0.1 add_convert_fusion.1
  213.3 2.0 collective-permute-start.6
  215.4 2.7 collective-permute-start.8
  218.1 0.5 collective-permute-start.7
  218.6 4.5 %constant_dynamic-update-slice_fusion.1 = bf16[8192,512]{1,0:T(8,128)(2,1)} fusion(bf16[8192,512]{1,0:T(8,128)(2,1)} %get-tuple-element.91, bf16[4096,512]{1,0:T(8,128)(2,1)} %collective-permute-done.5, s32[]{:T(128)S(6)} %select_n.62), kind=kLoop, calls=%fused_computation.20 | loop fusion | bytes 8388612 | tf_op jit(solution)/shard_map/cond/branch_1_fun/dynamic_update_slice | solution.py:839
  223.1 3.1 %collective-permute-done.7 = bf16[272,128]{1,0:T(8,128)(2,1)S(1)} collective-permute-done((bf16[272,128]{1,0:T(8,128)(2,1)S(1)}, bf16[272,128]{1,0:T(8,128)(2,1)S(1)}, u32[]{:S(2)}, u32[]{:S(2)}) %collective-permute-start.7) | collective-permute-done | bytes 69664 | tf_op jit(solution)/shard_map/cond/branch_1_fun/ppermute | solution.py:774
  226.3 4.2 %collective-permute-start.11 = (bf16[272,128]{1,0:T(8,128)(2,1)S(1)}, bf16[272,128]{1,0:T(8,128)(2,1)S(1)}, u32[]{:S(2)}, u32[]{:S(2)}) collective-permute-start(bf16[272,128]{1,0:T(8,128)(2,1)S(1)} %fusion.2), channel_id=1, source_target_pairs={{0,12},{1,13},{2,14},{3,15},{4,8},{5,9},{6,10},{7,11},{8,4},{9,5},... | collective-permute-start | bytes 208904 | tf_op jit(solution)/shard_map/cond/branch_1_fun/ppermute | solution.py:774
  230.5 0.6 collective-permute-start.9
  231.2 3.9 %collective-permute-done.9 = bf16[272,128]{1,0:T(8,128)(2,1)S(1)} collective-permute-done((bf16[272,128]{1,0:T(8,128)(2,1)S(1)}, bf16[272,128]{1,0:T(8,128)(2,1)S(1)}, u32[]{:S(2)}, u32[]{:S(2)}) %collective-permute-start.9) | collective-permute-done | bytes 69664 | tf_op jit(solution)/shard_map/cond/branch_1_fun/ppermute | solution.py:774
  235.1 2.2 collective-permute-done.10
  237.4 1.9 collective-permute-start.14
  239.3 1.1 collective-permute-start.13
  240.5 0.5 collective-permute-start.12
  241.0 4.8 %constant_dynamic-update-slice_fusion = bf16[8192,512]{1,0:T(8,128)(2,1)} fusion(bf16[8192,512]{1,0:T(8,128)(2,1)} %get-tuple-element.95, bf16[4096,512]{1,0:T(8,128)(2,1)} %collective-permute-done.15, s32[]{:T(128)S(6)} %select_n.62), kind=kLoop, calls=%fused_computation.19 | loop fusion | bytes 8388612 | tf_op jit(solution)/shard_map/cond/branch_1_fun/dynamic_update_slice | solution.py:839
  245.8 4.4 %collective-permute-done.14.b3 = bf16[1088,128]{1,0:T(8,128)(2,1)S(1)} collective-permute-done((bf16[1088,128]{1,0:T(8,128)(2,1)S(1)}, bf16[1088,128]{1,0:T(8,128)(2,1)S(1)}, u32[]{:S(2)}, u32[]{:S(2)}) %collective-permute-start.14) | collective-permute-done | bytes 278560 | tf_op jit(solution)/shard_map/cond/branch_1_fun/ppermute | solution.py:774
  250.2 8.0 %collective-permute-done.13.b2 = bf16[1088,128]{1,0:T(8,128)(2,1)S(1)} collective-permute-done((bf16[1088,128]{1,0:T(8,128)(2,1)S(1)}, bf16[1088,128]{1,0:T(8,128)(2,1)S(1)}, u32[]{:S(2)}, u32[]{:S(2)}) %collective-permute-start.13) | collective-permute-done | bytes 278560 | tf_op jit(solution)/shard_map/cond/branch_1_fun/ppermute | solution.py:774
  258.2 0.7 copy-done.9
  258.9 0.7 copy-done.10
  259.6 2.7 at_unpack.1
  262.3 0.0 copy-start.14
  262.3 0.0 copy-start.15
  262.3 4.6 %all-reduce.3.cloned.1.call-done = (bf16[1024,512]{1,0:T(8,128)(2,1)}, bf16[1024,512]{1,0:T(8,128)(2,1)}) async-done(((bf16[1024,512]{1,0:T(8,128)(2,1)}, bf16[1024,512]{1,0:T(8,128)(2,1)}), (bf16[1024,512]{1,0:T(8,128)(2,1)}, bf16[1024,512]{1,0:T(8,128)(2,1)})) %all-reduce.3.cloned.1.call-update) | async-done | bytes 2097168 | tf_op jit(solution)/shard_map/psum | solution.py:884
  266.9 4.1 %ff_unpack.1 = (f32[512,1024]{1,0:T(8,128)}, f32[1024,512]{1,0:T(8,128)}) custom-call(bf16[1024,512]{1,0:T(8,128)(2,1)} %get-tuple-element.263.up, bf16[1024,512]{1,0:T(8,128)(2,1)} %get-tuple-element.264.down), custom_call_target="tpu_custom_call" | custom-call | tf_op jit(solution)/shard_map/ff_unpack/pallas_call | solution.py:714
  (50 shorter events, 0.3 us)
Async XLA Ops:
  7.2 259.7 %all-reduce.3.cloned.1.call-start = ((), (), s32[]{:S(2)}) async-start(), calls=%async_computation | async-start | bytes 4194304 | tf_op jit(solution)/shard_map/psum | solution.py:884
  7.2 3.2 %collective-permute-start.16 = (bf16[512,256]{1,0:T(8,128)(2,1)}, bf16[512,256]{1,0:T(8,128)(2,1)S(1)}, u32[]{:S(2)}, u32[]{:S(2)}) collective-permute-start(bf16[512,256]{1,0:T(8,128)(2,1)} %refs_1_.1), channel_id=1, source_target_pairs={{0,16},{16,0},{1,17},{17,1},{2,18},{18,2},{3,19},{19,3},{4,20},{20... | collective-permute-start | bytes 786440 | tf_op jit(solution)/shard_map/ppermute | solution.py:744
  7.8 2.7 collective-permute-start.17
  7.8 2.6 collective-permute-start.18
  8.3 2.2 collective-permute-start.19
  9.1 2.0 copy-start.11
  9.1 1.3 collective-permute-start.20
  10.4 0.6 copy-start.12
  10.4 41.0 %copy-start.5 = (bf16[512,256]{1,0:T(8,128)(2,1)}, bf16[512,256]{1,0:T(8,128)(2,1)S(1)}, u32[]{:S(2)}) copy-start(bf16[512,256]{1,0:T(8,128)(2,1)S(1)} %collective-permute-done.18.refs_6_) | copy-start | bytes 786436
  10.5 0.8 copy-start.7
  10.5 40.9 %collective-permute-start.21 = (bf16[512,1024]{1,0:T(8,128)(2,1)}, bf16[512,1024]{1,0:T(8,128)(2,1)}, u32[]{:S(2)}, u32[]{:S(2)}) collective-permute-start(bf16[512,1024]{1,0:T(8,128)(2,1)} %refs_2_), channel_id=1, source_target_pairs={{0,16},{16,0},{1,17},{17,1},{2,18},{18,2},{3,19},{19,3},{4,20},{20... | collective-permute-start | bytes 3145736 | tf_op jit(solution)/shard_map/ppermute | solution.py:744
  10.9 40.5 %collective-permute-start.22 = (bf16[1024,512]{1,0:T(8,128)(2,1)}, bf16[1024,512]{1,0:T(8,128)(2,1)S(1)}, u32[]{:S(2)}, u32[]{:S(2)}) collective-permute-start(bf16[1024,512]{1,0:T(8,128)(2,1)} %refs_4_), channel_id=1, source_target_pairs={{0,16},{16,0},{1,17},{17,1},{2,18},{18,2},{3,19},{19,3},{4,20},{20... | collective-permute-start | bytes 3145736 | tf_op jit(solution)/shard_map/ppermute | solution.py:744
  11.2 40.2 %copy-start = (bf16[1024,512]{1,0:T(8,128)(2,1)S(1)}, bf16[1024,512]{1,0:T(8,128)(2,1)}, u32[]{:S(2)}) copy-start(bf16[1024,512]{1,0:T(8,128)(2,1)} %refs_4_) | copy-start | bytes 3145732
  119.5 2.9 %collective-permute-start.23 = (bf16[1024,512]{1,0:T(8,128)(2,1)}, bf16[1024,512]{1,0:T(8,128)(2,1)S(1)}, u32[]{:S(2)}, u32[]{:S(2)}) collective-permute-start(bf16[1024,512]{1,0:T(8,128)(2,1)} %get-tuple-element.218), channel_id=1, source_target_pairs={{0,16},{16,0},{1,17},{17,1},{2,18},{18,2},{3,19},{19,3},{4,20},{20... | collective-permute-start | bytes 3145736 | tf_op jit(solution)/shard_map/ppermute | solution.py:744
  119.9 5.0 %collective-permute-start.24 = (bf16[1024,512]{1,0:T(8,128)(2,1)}, bf16[1024,512]{1,0:T(8,128)(2,1)S(1)}, u32[]{:S(2)}, u32[]{:S(2)}) collective-permute-start(bf16[1024,512]{1,0:T(8,128)(2,1)} %get-tuple-element.220), channel_id=1, source_target_pairs={{0,16},{16,0},{1,17},{17,1},{2,18},{18,2},{3,19},{19,3},{4,20},{20... | collective-permute-start | bytes 3145736 | tf_op jit(solution)/shard_map/ppermute | solution.py:744
  127.6 40.5 %copy-start.2 = (bf16[512,256]{1,0:T(8,128)(2,1)S(1)}, bf16[512,256]{1,0:T(8,128)(2,1)}, u32[]{:S(2)}) copy-start(bf16[512,256]{1,0:T(8,128)(2,1)} %refs_1_.1) | copy-start | bytes 786436
  127.6 40.5 %copy-start.3 = (bf16[512,256]{1,0:T(8,128)(2,1)S(1)}, bf16[512,256]{1,0:T(8,128)(2,1)}, u32[]{:S(2)}) copy-start(bf16[512,256]{1,0:T(8,128)(2,1)} %refs_3_) | copy-start | bytes 786436
  127.6 40.5 %copy-start.4 = (bf16[512,256]{1,0:T(8,128)(2,1)S(1)}, bf16[512,256]{1,0:T(8,128)(2,1)}, u32[]{:S(2)}) copy-start(bf16[512,256]{1,0:T(8,128)(2,1)} %refs_5_) | copy-start | bytes 786436
  127.6 40.4 %copy-start.6 = (bf16[512,256]{1,0:T(8,128)(2,1)S(1)}, bf16[512,256]{1,0:T(8,128)(2,1)}, u32[]{:S(2)}) copy-start(bf16[512,256]{1,0:T(8,128)(2,1)} %copy-done.5) | copy-start | bytes 786436
  127.6 40.4 %copy-start.13 = (f32[512]{0:T(512)S(1)}, f32[512]{0:T(512)}, u32[]{:S(2)}) copy-start(f32[512]{0:T(512)} %param.21) | copy-start | bytes 6148
  127.6 40.4 %copy-start.16 = (f32[512]{0:T(512)S(1)}, f32[512]{0:T(512)}, u32[]{:S(2)}) copy-start(f32[512]{0:T(512)} %param.36) | copy-start | bytes 6148
  168.1 17.0 %collective-permute-start = (bf16[4096,128]{1,0:T(8,128)(2,1)}, bf16[4096,128]{1,0:T(8,128)(2,1)}, u32[]{:S(2)}, u32[]{:S(2)}) collective-permute-start(bf16[4096,128]{1,0:T(8,128)(2,1)} %get-tuple-element.55), channel_id=1, source_target_pairs={{0,16},{16,0},{1,17},{17,1},{2,18},{18,2},{3,19},{19,3},{4,20},{20... | collective-permute-start | bytes 3145736 | tf_op jit(solution)/shard_map/cond/branch_1_fun/ppermute | solution.py:744
  185.1 27.3 %collective-permute-start.5 = (bf16[4096,512]{1,0:T(8,128)(2,1)}, bf16[4096,512]{1,0:T(8,128)(2,1)}, u32[]{:S(2)}, u32[]{:S(2)}) collective-permute-start(bf16[4096,512]{1,0:T(8,128)(2,1)} %get-tuple-element.79), channel_id=1, source_target_pairs={{0,16},{16,0},{1,17},{17,1},{2,18},{18,2},{3,19},{19,3},{4,20},{20... | collective-permute-start | bytes 12582920 | tf_op jit(solution)/shard_map/cond/branch_1_fun/ppermute | solution.py:744
  185.3 4.7 %collective-permute-start.1 = (bf16[256,128]{1,0:T(8,128)(2,1)}, bf16[256,128]{1,0:T(8,128)(2,1)S(1)}, u32[]{:S(2)}, u32[]{:S(2)}) collective-permute-start(bf16[256,128]{1,0:T(8,128)(2,1)} %get-tuple-element.78), channel_id=1, source_target_pairs={{0,16},{16,0},{1,17},{17,1},{2,18},{18,2},{3,19},{19,3},{4,20},{20... | collective-permute-start | bytes 196616 | tf_op jit(solution)/shard_map/cond/branch_1_fun/ppermute | solution.py:744
  192.9 19.5 %collective-permute-start.4 = (bf16[1088,128]{1,0:T(8,128)(2,1)S(1)}, bf16[1088,128]{1,0:T(8,128)(2,1)S(1)}, u32[]{:S(2)}, u32[]{:S(2)}) collective-permute-start(bf16[1088,128]{1,0:T(8,128)(2,1)S(1)} %get-tuple-element.265), channel_id=1, source_target_pairs={{0,3},{1,2},{2,1},{3,0},{4,7},{5,6},{6,5},{7,4},{8,11},{9,10},{10,... | collective-permute-start | bytes 835592 | tf_op jit(solution)/shard_map/cond/branch_1_fun/ppermute | solution.py:774
  196.2 16.2 %collective-permute-start.3 = (bf16[1088,128]{1,0:T(8,128)(2,1)S(1)}, bf16[1088,128]{1,0:T(8,128)(2,1)S(1)}, u32[]{:S(2)}, u32[]{:S(2)}) collective-permute-start(bf16[1088,128]{1,0:T(8,128)(2,1)S(1)} %get-tuple-element.266), channel_id=1, source_target_pairs={{0,2},{1,3},{2,0},{3,1},{4,6},{5,7},{6,4},{7,5},{8,10},{9,11},{10,... | collective-permute-start | bytes 835592 | tf_op jit(solution)/shard_map/cond/branch_1_fun/ppermute | solution.py:774
  196.6 15.8 %collective-permute-start.2 = (bf16[1088,128]{1,0:T(8,128)(2,1)S(1)}, bf16[1088,128]{1,0:T(8,128)(2,1)S(1)}, u32[]{:S(2)}, u32[]{:S(2)}) collective-permute-start(bf16[1088,128]{1,0:T(8,128)(2,1)S(1)} %get-tuple-element.267), channel_id=1, source_target_pairs={{0,1},{1,0},{2,3},{3,2},{4,5},{5,4},{6,7},{7,6},{8,9},{9,8},{10,11... | collective-permute-start | bytes 835592 | tf_op jit(solution)/shard_map/cond/branch_1_fun/ppermute | solution.py:774
  212.5 28.5 %collective-permute-start.15 = (bf16[4096,512]{1,0:T(8,128)(2,1)}, bf16[4096,512]{1,0:T(8,128)(2,1)}, u32[]{:S(2)}, u32[]{:S(2)}) collective-permute-start(bf16[4096,512]{1,0:T(8,128)(2,1)} %get-tuple-element.96), channel_id=1, source_target_pairs={{0,16},{16,0},{1,17},{17,1},{2,18},{18,2},{3,19},{19,3},{4,20},{20... | collective-permute-start | bytes 12582920 | tf_op jit(solution)/shard_map/cond/branch_1_fun/ppermute | solution.py:744
  213.3 9.8 %collective-permute-start.6 = (bf16[272,128]{1,0:T(8,128)(2,1)S(1)}, bf16[272,128]{1,0:T(8,128)(2,1)S(1)}, u32[]{:S(2)}, u32[]{:S(2)}) collective-permute-start(bf16[272,128]{1,0:T(8,128)(2,1)S(1)} %get-tuple-element.269), channel_id=1, source_target_pairs={{0,4},{1,5},{2,6},{3,7},{4,0},{5,1},{6,2},{7,3},{8,12},{9,13},{10,... | collective-permute-start | bytes 208904 | tf_op jit(solution)/shard_map/cond/branch_1_fun/ppermute | solution.py:774
  215.4 7.7 %collective-permute-start.8 = (bf16[272,128]{1,0:T(8,128)(2,1)S(1)}, bf16[272,128]{1,0:T(8,128)(2,1)S(1)}, u32[]{:S(2)}, u32[]{:S(2)}) collective-permute-start(bf16[272,128]{1,0:T(8,128)(2,1)S(1)} %get-tuple-element.270), channel_id=1, source_target_pairs={{0,12},{1,13},{2,14},{3,15},{4,8},{5,9},{6,10},{7,11},{8,4},{9,5},... | collective-permute-start | bytes 208904 | tf_op jit(solution)/shard_map/cond/branch_1_fun/ppermute | solution.py:774
  218.1 8.2 %collective-permute-start.7 = (bf16[272,128]{1,0:T(8,128)(2,1)S(1)}, bf16[272,128]{1,0:T(8,128)(2,1)S(1)}, u32[]{:S(2)}, u32[]{:S(2)}) collective-permute-start(bf16[272,128]{1,0:T(8,128)(2,1)S(1)} %get-tuple-element.271), channel_id=1, source_target_pairs={{0,8},{1,9},{2,10},{3,11},{4,12},{5,13},{6,14},{7,15},{8,0},{9,1},... | collective-permute-start | bytes 208904 | tf_op jit(solution)/shard_map/cond/branch_1_fun/ppermute | solution.py:774
  226.3 11.1 %collective-permute-start.11 = (bf16[272,128]{1,0:T(8,128)(2,1)S(1)}, bf16[272,128]{1,0:T(8,128)(2,1)S(1)}, u32[]{:S(2)}, u32[]{:S(2)}) collective-permute-start(bf16[272,128]{1,0:T(8,128)(2,1)S(1)} %fusion.2), channel_id=1, source_target_pairs={{0,12},{1,13},{2,14},{3,15},{4,8},{5,9},{6,10},{7,11},{8,4},{9,5},... | collective-permute-start | bytes 208904 | tf_op jit(solution)/shard_map/cond/branch_1_fun/ppermute | solution.py:774
  230.5 6.8 %collective-permute-start.10 = (bf16[272,128]{1,0:T(8,128)(2,1)S(1)}, bf16[272,128]{1,0:T(8,128)(2,1)S(1)}, u32[]{:S(2)}, u32[]{:S(2)}) collective-permute-start(bf16[272,128]{1,0:T(8,128)(2,1)S(1)} %fusion.2), channel_id=1, source_target_pairs={{0,8},{1,9},{2,10},{3,11},{4,12},{5,13},{6,14},{7,15},{8,0},{9,1},... | collective-permute-start | bytes 208904 | tf_op jit(solution)/shard_map/cond/branch_1_fun/ppermute | solution.py:774
  230.5 4.6 %collective-permute-start.9 = (bf16[272,128]{1,0:T(8,128)(2,1)S(1)}, bf16[272,128]{1,0:T(8,128)(2,1)S(1)}, u32[]{:S(2)}, u32[]{:S(2)}) collective-permute-start(bf16[272,128]{1,0:T(8,128)(2,1)S(1)} %fusion.2), channel_id=1, source_target_pairs={{0,4},{1,5},{2,6},{3,7},{4,0},{5,1},{6,2},{7,3},{8,12},{9,13},{10,... | collective-permute-start | bytes 208904 | tf_op jit(solution)/shard_map/cond/branch_1_fun/ppermute | solution.py:774
  237.4 8.4 %copy-start.1 = (bf16[4,272,128]{2,1,0:T(8,128)(2,1)}, bf16[4,272,128]{2,1,0:T(8,128)(2,1)S(1)}, u32[]{:S(2)}) copy-start(bf16[4,272,128]{2,1,0:T(8,128)(2,1)S(1)} %bitcast_dynamic-update-slice_fusion) | copy-start | bytes 835588 | tf_op jit(solution)/shard_map/cond
  237.4 12.8 %collective-permute-start.14 = (bf16[1088,128]{1,0:T(8,128)(2,1)S(1)}, bf16[1088,128]{1,0:T(8,128)(2,1)S(1)}, u32[]{:S(2)}, u32[]{:S(2)}) collective-permute-start(bf16[1088,128]{1,0:T(8,128)(2,1)S(1)} %bitcast.48), channel_id=1, source_target_pairs={{0,3},{1,2},{2,1},{3,0},{4,7},{5,6},{6,5},{7,4},{8,11},{9,10},{10,... | collective-permute-start | bytes 835592 | tf_op jit(solution)/shard_map/cond/branch_1_fun/ppermute | solution.py:774
  239.3 18.9 %collective-permute-start.13 = (bf16[1088,128]{1,0:T(8,128)(2,1)S(1)}, bf16[1088,128]{1,0:T(8,128)(2,1)S(1)}, u32[]{:S(2)}, u32[]{:S(2)}) collective-permute-start(bf16[1088,128]{1,0:T(8,128)(2,1)S(1)} %bitcast.49), channel_id=1, source_target_pairs={{0,2},{1,3},{2,0},{3,1},{4,6},{5,7},{6,4},{7,5},{8,10},{9,11},{10,... | collective-permute-start | bytes 835592 | tf_op jit(solution)/shard_map/cond/branch_1_fun/ppermute | solution.py:774
  240.5 17.7 %collective-permute-start.12 = (bf16[1088,128]{1,0:T(8,128)(2,1)S(1)}, bf16[1088,128]{1,0:T(8,128)(2,1)S(1)}, u32[]{:S(2)}, u32[]{:S(2)}) collective-permute-start(bf16[1088,128]{1,0:T(8,128)(2,1)S(1)} %bitcast.50), channel_id=1, source_target_pairs={{0,1},{1,0},{2,3},{3,2},{4,5},{5,4},{6,7},{7,6},{8,9},{9,8},{10,11... | collective-permute-start | bytes 835592 | tf_op jit(solution)/shard_map/cond/branch_1_fun/ppermute | solution.py:774
  250.2 8.0 %copy-start.8 = (bf16[1088,128]{1,0:T(8,128)(2,1)}, bf16[1088,128]{1,0:T(8,128)(2,1)S(1)}, u32[]{:S(2)}) copy-start(bf16[1088,128]{1,0:T(8,128)(2,1)S(1)} %collective-permute-done.14.b3) | copy-start | bytes 835588 | tf_op jit(solution)/shard_map/cond
  258.2 0.7 copy-start.9
  258.9 0.7 copy-start.10
  262.3 8.8 %copy-start.14 = (f32[512]{0:T(512)}, f32[512]{0:T(512)S(1)}, u32[]{:S(2)}) copy-start(f32[512]{0:T(512)S(1)} %get-tuple-element.193) | copy-start | bytes 6148
  262.3 8.8 %copy-start.15 = (f32[512]{0:T(512)}, f32[512]{0:T(512)S(1)}, u32[]{:S(2)}) copy-start(f32[512]{0:T(512)S(1)} %get-tuple-element.192) | copy-start | bytes 6148
Sparse Core Ops, SparseCore 0:
  127.7 139.2 all-reduce.2
